TPU v7x, 32 devices: a whole 2x2x4 slice. The times are simulated.
32 devices in a mesh: tgroup: 4 (over z), chan: 8 (over y, x, core).
Axes of the slice: x: 2, y: 2, z: 4, core: 2. Of those that a mesh axis runs over, the one named last changes fastest.
Arguments:
- raw_strain: float32 [16384, 10240], P(('tgroup', 'chan')), may hold values from -6 to 6
- whitening_taps: float32 [255], replicated, may hold values from -0.375 to 0.375
- first_block: int32 [16], P('chan'), may hold values from 0 to 159, as said below
- pair_owner: int32 [128, 1], P('chan'), may hold values from 0 to 3; in each aligned block of 16 rows (0 to 15, 16 to 31, ...) at most 5 rows name the same one
Outputs:
- stacks: float32 [160, 8, 8, 1001], P(('tgroup', 'chan'))
Inputs may be any that keep to these rules, and one draw needn't show every extreme that they name: `first_block`: each chan index lists 2 stripes; its first stripe starts within the last 7 of its 160 blocks; chan index 0 lists block 159 first and block 0 second. `pair_owner`: pair blocks are ordered by chan index, stripe, then partner offset. Among the 16 pair blocks of one chan index at most 5 share an owner, and exactly 5 do in some chan index.
All inputs are finite; a program needn't handle non-finite values.
Results may differ from a plain program's by a relative error of at most 0.02.
Values may be sent and summed in bfloat16 or wider, within the bound.
No kernel may reach another device: no remote copies, remote signals or barrier semaphores. Data moves between devices by JAX's collectives and lax.ppermute only.
A program may use at most 192 MiB of HBM per device.

v0:
```python
import math

import jax
import jax.numpy as jnp
from jax import lax
from jax.sharding import PartitionSpec as P

MAXLAG = 500
CB = 8
K = 8
STRIPES = 2
SLOTS = 5


def from_behind(value, axis, steps):
    count = lax.axis_size(axis)
    first, last = (max(0, -steps), min(count, count - steps))
    return lax.ppermute(value, axis, [(source, source + steps) for source in range(first, last)])


def fir_matrix(whitening_taps, out_rows):
    padded = jnp.concatenate([whitening_taps, jnp.zeros((2 * out_rows,), whitening_taps.dtype)])
    length = padded.shape[0]
    tiled_taps = jnp.tile(padded, out_rows + 1)[: out_rows * (length - 2)]
    return tiled_taps.reshape(out_rows, length - 2)


def whiten(padded, whitening_taps):
    row_count = padded.shape[0] - whitening_taps.shape[0] + 1
    out_rows = min(256, row_count // 2)
    blocks = row_count // (2 * out_rows)
    matrix = fir_matrix(whitening_taps, out_rows)
    span_cols = matrix.shape[1]
    starts = jnp.arange(blocks, dtype=jnp.int32) * (2 * out_rows)

    def take_window(offset_row):
        return lax.dynamic_slice_in_dim(padded, offset_row, span_cols, 0)

    windows = jax.vmap(take_window)(starts)
    result = jnp.einsum("jq,bqc->cbj", matrix, windows, precision=lax.Precision.HIGHEST)
    return result.reshape(result.shape[0], blocks * out_rows).astype(jnp.bfloat16)


def correlate(source, offset_row, factor):
    lag_count = 2 * MAXLAG + 1
    lag_block = 128
    lag_blocks = (lag_count + lag_block - 1) // lag_block
    sample_count = source.shape[1]
    span_width = sample_count + lag_block
    leading = lax.dynamic_slice_in_dim(source, offset_row, CB, 0)
    partners = lax.dynamic_slice_in_dim(source, offset_row, K * CB, 0)
    lead_padded = jnp.pad(leading, ((0, 0), (lag_block - 1, lag_block + 1)))

    def shifted_copy(shift_count):
        return lax.dynamic_slice_in_dim(lead_padded, lag_block - 1 - shift_count, span_width, 1)

    shifted = jax.vmap(shifted_copy)(jnp.arange(lag_block, dtype=jnp.int32))
    extra_right = MAXLAG + lag_blocks * lag_block - lag_count + 1
    partner_padded = jnp.pad(partners, ((0, 0), (MAXLAG, extra_right)))
    windows = jnp.stack(
        [
            partner_padded[:, block_index * lag_block : block_index * lag_block + span_width]
            for block_index in range(lag_blocks)
        ],
        0,
    )
    summed = jnp.einsum("raj,nbj->banr", shifted, windows, preferred_element_type=jnp.float32)
    summed = summed.reshape(K * CB, CB, lag_blocks * lag_block)[:, :, :lag_count]
    scaled = (summed * factor).astype(jnp.bfloat16)
    return scaled.reshape(K, CB, CB, lag_count).transpose(0, 2, 1, 3)


def local(raw_strain, whitening_taps, first_block, pair_owner):
    half_taps = (whitening_taps.shape[0] - 1) // 2
    chan_count = lax.axis_size("chan")
    local_rows = raw_strain.shape[0]
    grouped = raw_strain.reshape(local_rows, chan_count, raw_strain.shape[1] // chan_count)
    series = lax.all_to_all(
        grouped.astype(jnp.bfloat16), "chan", split_axis=1, concat_axis=0, tiled=True
    ).astype(grouped.dtype)[:, 0, :]
    padded = jnp.pad(series, ((half_taps, half_taps), (0, 0)))
    filtered = whiten(padded, whitening_taps)
    rim_rows = from_behind(filtered[: (K - 1) * CB], "chan", -1)
    extended = jnp.concatenate([filtered, rim_rows], 0)
    offsets = [first_block[stripe] * CB for stripe in range(STRIPES)]
    factor = 1.0 / math.sqrt(extended.shape[1])
    lag_count = 2 * MAXLAG + 1
    partial_value = jnp.concatenate(
        [correlate(extended, offset_row, factor) for offset_row in offsets], 0
    )
    pair_count = partial_value.shape[0]
    flat_partial = partial_value.reshape(pair_count, CB * CB * lag_count)
    group_count = lax.axis_size("tgroup")
    owners_vec = pair_owner[:, 0]
    owner_hot = (owners_vec[:, None] == jnp.arange(group_count, dtype=jnp.int32)[None, :]).astype(
        jnp.int32
    )
    earlier = (
        jnp.arange(pair_count, dtype=jnp.int32)[None, :]
        < jnp.arange(pair_count, dtype=jnp.int32)[:, None]
    ).astype(jnp.int32)
    before_count = jnp.dot(earlier, owner_hot)
    slot_index = jnp.sum(before_count * owner_hot, 1)
    target = owners_vec * SLOTS + slot_index
    placement = jnp.arange(group_count * SLOTS, dtype=jnp.int32)[:, None] == target[None, :]
    placement_half = placement.astype(jnp.bfloat16)
    mine = lax.psum_scatter(
        jnp.dot(placement_half, flat_partial, preferred_element_type=jnp.float32).astype(
            jnp.bfloat16
        ),
        "tgroup",
        scatter_dimension=0,
        tiled=True,
    ).astype(jnp.float32)
    return mine.reshape(SLOTS, CB, CB, lag_count)


def solution(mesh):
    in_specs = (P(("tgroup", "chan"), None), P(), P("chan"), P("chan", None))
    out_specs = P(("tgroup", "chan"), None, None, None)
    return jax.shard_map(local, mesh=mesh, in_specs=in_specs, out_specs=out_specs, check_vma=False)
```

profile of v0, /device:TPU:0, one launch (start us, length us, event | category | flops | bytes accessed | tf_op | source)
XLA Modules:
  0.0 886.6 jit_solution(11197838399652786586)
XLA Ops:
  6.5 12.3 %convert_element_type.49 = bf16[512,10240]{1,0:T(8,128)(2,1)} convert(f32[512,10240]{1,0:T(8,128)} %param.4) | non-fusion elementwise | flops 5242880 | bytes 31457280 | tf_op jit(solution)/shard_map/convert_element_type | solution.py:79
  18.9 8.6 copy.51
  27.5 5.3 all-to-all-start
  35.2 114.7 %all-to-all-done = bf16[512,8,1280]{2,0,1:T(8,128)(2,1)} async-done(((bf16[512,8,1280]{2,0,1:T(8,128)(2,1)}), bf16[512,8,1280]{2,0,1:T(8,128)(2,1)}, u32[]{:S(2)}, u32[]{:S(2)}) %all-to-all-start) | async-done | bytes 10485792 | tf_op jit(solution)/shard_map/all_to_all | solution.py:78
  150.0 11.2 %pad.24 = bf16[4350,1280]{1,0:T(8,128)(2,1)} pad(bf16[4096,1280]{1,0:T(8,128)(2,1)} %bitcast.3, bf16[]{:T(256)} %constant.13.clone.1), padding=127_127x0_0 | pad | bytes 21621762 | tf_op jit(solution)/shard_map/jit(_pad)/pad | solution.py:81
  161.1 35.7 %while.3 = (s32[]{:T(128)}, bf16[4350,1280]{1,0:T(8,128)(2,1)}, s32[8,2]{0,1:T(2,128)S(1)}, bf16[8,765,1280]{2,1,0:T(8,128)(2,1)}, s32[]{:T(128)}) while((s32[]{:T(128)}, bf16[4350,1280]{1,0:T(8,128)(2,1)}, s32[8,2]{0,1:T(2,128)S(1)}, bf16[8,765,1280]{2,1,0:T(8,128)(2,1)}, s32[]{:T(128)}) %tuple.42), condition=%wide.while_cond, body=%wide.while_body.sunk | while | flops 2 | bytes 3933273 | solution.py:37
  161.7 3.9 bitcast_dynamic-update-slice_fusion.6
  166.2 3.8 bitcast_dynamic-update-slice_fusion.6
  170.6 3.9 bitcast_dynamic-update-slice_fusion.6
  175.1 3.8 bitcast_dynamic-update-slice_fusion.6
  179.5 3.9 bitcast_dynamic-update-slice_fusion.6
  184.0 3.8 bitcast_dynamic-update-slice_fusion.6
  188.5 3.9 bitcast_dynamic-update-slice_fusion.6
  193.0 3.8 bitcast_dynamic-update-slice_fusion.6
  196.8 21.2 %fusion.6 = bf16[1280,8,256]{2,0,1:T(8,128)(2,1)S(1)} fusion(bf16[8,765,1280]{2,1,0:T(8,128)(2,1)} %get-tuple-element.12, f32[256,765,1]{1,0,2:T(8,128)S(1)} %reshape.152), kind=kOutput, calls=%fused_computation.19 | convolution fusion | flops 24067440640 | bytes 21693440 | tf_op jit(solution)/shard_map/jq,bqc->cbj/dot_general | solution.py:40
  218.0 2.3 copy-done.1
  223.1 8.1 copy.22
  231.2 7.9 copy.24
  239.1 1.3 fusion.54
  242.5 2.4 broadcast.106.clone.1
  244.9 230.3 %while.4 = (s32[]{:T(128)}, bf16[8,2304]{1,0:T(8,128)(2,1)S(1)}, s32[128,2]{0,1:T(2,128)S(1)}, bf16[128,8,2176]{2,1,0:T(8,128)(2,1)}, s32[]{:T(128)}) while((s32[]{:T(128)}, bf16[8,2304]{1,0:T(8,128)(2,1)S(1)}, s32[128,2]{0,1:T(2,128)S(1)}, bf16[128,8,2176]{2,1,0:T(8,128)(2,1)}, s32[]{:T(128)}) %tuple.48), condition=%wide.while_cond.1, body=%wide.while_body.1.sunk | while | flops 2 | bytes 70745 | solution.py:55
  475.1 4.9 fusion.11
  481.3 1.5 reshape.86
  482.8 2.0 fusion.10
  486.4 1.4 copy-done.3
  487.9 2.4 broadcast.106.clone
  490.3 246.0 %while.5 = (s32[]{:T(128)}, bf16[8,2304]{1,0:T(8,128)(2,1)S(1)}, s32[128,2]{0,1:T(2,128)S(1)}, bf16[128,8,2176]{2,1,0:T(8,128)(2,1)}, s32[]{:T(128)}) while((s32[]{:T(128)}, bf16[8,2304]{1,0:T(8,128)(2,1)S(1)}, s32[128,2]{0,1:T(2,128)S(1)}, bf16[128,8,2176]{2,1,0:T(8,128)(2,1)}, s32[]{:T(128)}) %tuple.53), condition=%wide.while_cond.2, body=%wide.while_body.2.sunk | while | flops 2 | bytes 70745 | solution.py:55
  508.2 1.3 bitcast_dynamic-update-slice_fusion.8
  525.4 1.3 bitcast_dynamic-update-slice_fusion.8
  527.4 1.3 bitcast_dynamic-update-slice_fusion.8
  537.0 1.3 bitcast_dynamic-update-slice_fusion.8
  558.1 1.3 bitcast_dynamic-update-slice_fusion.8
  588.9 1.3 bitcast_dynamic-update-slice_fusion.8
  602.4 1.3 bitcast_dynamic-update-slice_fusion.8
  619.6 1.3 bitcast_dynamic-update-slice_fusion.8
  633.1 1.3 bitcast_dynamic-update-slice_fusion.8
  652.3 1.3 bitcast_dynamic-update-slice_fusion.8
  658.1 1.3 bitcast_dynamic-update-slice_fusion.8
  667.7 1.3 bitcast_dynamic-update-slice_fusion.8
  686.9 1.3 bitcast_dynamic-update-slice_fusion.8
  736.3 5.6 fusion.16
  743.1 1.5 reshape.88
  744.6 1.8 fusion.9
  747.3 3.6 reshape.90
  750.8 4.1 convolution_convert_fusion
  756.8 119.0 %all-reduce.11.cloned.1.call-done = bf16[20,64064]{1,0:T(8,128)(2,1)} async-done(((bf16[20,64064]{1,0:T(8,128)(2,1)}), bf16[20,64064]{1,0:T(8,128)(2,1)}) %all-reduce.11.cloned.1.call-update) | async-done | bytes 2562576
  875.9 1.8 dynamic-slice_convert_fusion
  877.7 2.1 reshape.151
  (828 shorter events, 475.1 us)
Async XLA Ops:
  27.5 5.4 copy-start.5
  27.5 122.5 %all-to-all-start = ((bf16[512,8,1280]{2,0,1:T(8,128)(2,1)}), bf16[512,8,1280]{2,0,1:T(8,128)(2,1)}, u32[]{:S(2)}, u32[]{:S(2)}) async-start(bf16[512,8,1280]{2,0,1:T(8,128)(2,1)} %bitcast.150), calls=%async_computation | async-start | bytes 20971520 | tf_op jit(solution)/shard_map/all_to_all | solution.py:78
  32.8 843.1 %all-reduce.11.cloned.1.call-start = ((), (), s32[]{:S(2)}) async-start(), calls=%async_computation.1 | async-start | bytes 6156288
  32.9 1.5 copy-start.4
  33.0 2.1 copy-start.6
  218.0 2.3 copy-start.1
  220.4 18.7 %collective-permute-start = (bf16[56,2048]{1,0:T(8,128)(2,1)S(1)}, bf16[56,2048]{1,0:T(8,128)(2,1)S(1)}, u32[]{:S(2)}, u32[]{:S(2)}) collective-permute-start(bf16[56,2048]{1,0:T(8,128)(2,1)S(1)} %bitcast.157), channel_id=1, source_target_pairs={{1,0},{2,1},{3,2},{4,3},{5,4},{6,5},{7,6},{9,8},{10,9},{11,10},{12... | collective-permute-start | bytes 688136 | tf_op jit(solution)/shard_map/ppermute | solution.py:18
  239.1 3.3 copy-start
  482.8 2.6 copy-start.2
  486.4 1.4 copy-start.3
  754.9 0.7 copy-start.7
Sparse Core Ops, SparseCore 0:
  755.1 120.7 all-reduce.10
where the time goes:
time: 890 us; the launch traced here: 887 us
  local copies, waits for them, and re-layouts  575 us (65%)
  waiting for transfers between devices  234 us (26%)
  matrix products  35.9 us (4%)
  other arithmetic  19.6 us (2%)
  between operations  15.7 us (2%)
    gather x792, local copies, waits for them, and re-layouts  512 us
    unnamed x2, waiting for transfers between devices  119 us
    all_to_all x1, waiting for transfers between devices, local(): lax.all_to_all(grouped.astype(jnp.bfloat16), 'chan', split_axis=1, concat...  115 us
    dot_general x1, matrix products, whiten(): jnp.einsum('jq,bqc->cbj', matrix, windows, precision=lax.Precision.HIGHEST)  21.2 us
  transfers between devices with their start and end apart: 3, of which 2 were waited for; matrix products, arithmetic and copies ran while one was open for 2% of the time, Pallas kernels for 0%

commit v1 on v0

v1 whole, which is shorter than its diff:
```python
import functools
import math

import jax
import jax.numpy as jnp
from jax import lax
from jax.experimental import pallas as pl
from jax.experimental.pallas import tpu as pltpu
from jax.sharding import PartitionSpec as P

MAXLAG = 500
LAGS = 2 * MAXLAG + 1
CB = 8
K = 8
STRIPES = 2
SLOTS = 5
PAIRS = STRIPES * K
BLOCKS = STRIPES + SLOTS
WIDE = K * CB
SPILL = 64
LANES = 128
SHIFTS = 32
FRONT = -(-MAXLAG // LANES) * LANES
NT = (((1,), (1,)), ((), ()))


def params(megabytes):
    return pltpu.CompilerParams(vmem_limit_bytes=megabytes << 20)


def vmem():
    return pl.BlockSpec(memory_space=pltpu.VMEM)


def smem():
    return pl.BlockSpec(memory_space=pltpu.SMEM)


def from_behind(value, axis, steps):
    count = lax.axis_size(axis)
    first, last = (max(0, -steps), min(count, count - steps))
    return lax.ppermute(value, axis, [(source, source + steps) for source in range(first, last)])


def fir_matrix(taps, rows, outs):
    all_outs = outs + 2 * SPILL
    padded = jnp.concatenate(
        [jnp.zeros((1,), taps.dtype), taps, jnp.zeros((2 * all_outs,), taps.dtype)]
    )
    length = padded.shape[0]
    tiled = jnp.tile(padded, all_outs + 1)[: all_outs * (length - 2)]
    matrix = tiled.reshape(all_outs, length - 2)[:, 4 * SPILL : 4 * SPILL + rows]
    matrix = matrix.astype(jnp.bfloat16)
    spills = jnp.concatenate([matrix[:SPILL], matrix[SPILL + outs :]], 0)
    return matrix[SPILL : SPILL + outs], spills


def select_kernel(n_chan, n_tgroup, meta, raw, main_taps, spill_taps, main, left, right, table, window, picked, sems):
    rows, channels = raw.shape
    stripes = n_chan * STRIPES
    blocks_per = channels // n_chan // CB
    span = window.shape[2]

    def place(p):
        c, k = p // STRIPES, p % STRIPES
        start = (meta[c, k] + c * blocks_per) * CB
        base = jnp.minimum(start - lax.rem(start, LANES), channels - span)
        return start, pl.multiple_of(base, LANES)

    def copy(p):
        base = place(p)[1]
        return pltpu.make_async_copy(raw.at[:, pl.ds(base, span)], window.at[p], sems.at[p])

    for p in range(stripes):
        copy(p).start()

    def slots(c, carry):
        counts = jnp.int32(0)
        for q in range(PAIRS):
            owner = meta[c, STRIPES + q]
            slot = (counts >> (3 * owner)) & 7
            counts = counts + (jnp.int32(1) << (3 * owner))
            table[c * PAIRS + q] = (owner * n_chan + c) * BLOCKS + STRIPES + slot
        return carry

    lax.fori_loop(0, n_chan, slots, 0)

    row = lax.broadcasted_iota(jnp.int32, (WIDE, span), 0)
    lane = lax.broadcasted_iota(jnp.int32, (WIDE, span), 1)
    for p in range(stripes):
        copy(p).wait()
        start, base = place(p)
        hot = (lane == row + (start - base)) & (row < channels - start)
        hot = jnp.where(hot, 1.0, 0.0).astype(jnp.bfloat16)
        block = window[p].astype(jnp.bfloat16)
        chosen = lax.dot_general(hot, block, NT, preferred_element_type=jnp.float32)
        picked[p * WIDE : (p + 1) * WIDE, :] = chosen.astype(jnp.bfloat16)

    taken = picked[...]
    main[...] = lax.dot_general(taken, main_taps[...], NT, preferred_element_type=jnp.float32)
    spilled = lax.dot_general(taken, spill_taps[...], NT, preferred_element_type=jnp.float32)
    half = spilled.shape[0] // 2
    low, high = spilled[:half], spilled[half:]
    low_turned, high_turned = pltpu.roll(low, SPILL, 1), pltpu.roll(high, SPILL, 1)
    early = lax.broadcasted_iota(jnp.int32, low.shape, 1) < SPILL
    left[...] = jnp.where(early, low, high_turned).astype(jnp.bfloat16)
    right[...] = jnp.where(early, low_turned, high).astype(jnp.bfloat16)


def place_kernel(n_chan, n_tgroup, table, main, from_left, from_right, payload, total):
    count, outs = main.shape
    half = count // 2
    lanes = payload.shape[2]
    zero = jnp.zeros(payload.shape[1:], payload.dtype)

    total[...] = main[...]
    left, right = from_left[...].astype(jnp.float32), from_right[...].astype(jnp.float32)
    left_turned, right_turned = pltpu.roll(left, SPILL, 1), pltpu.roll(right, SPILL, 1)
    if outs >= LANES:
        early = lax.broadcasted_iota(jnp.int32, left.shape, 1) < SPILL
        total[:half, :LANES] += jnp.where(early, left, 0.0)
        total[half:, :LANES] += jnp.where(early, left_turned, 0.0)
        total[:half, outs - LANES :] += jnp.where(early, 0.0, right_turned)
        total[half:, outs - LANES :] += jnp.where(early, 0.0, right)
    else:
        total[:half, :] += (left + right)[:, :outs]
        total[half:, :] += (left_turned + right_turned)[:, :outs]

    def folded(block):
        value = total[pl.ds(pl.multiple_of(block * CB, CB), CB), :]
        parts = [value[:, at : at + lanes] for at in range(0, outs, lanes)]
        return jnp.concatenate(parts, 0).astype(payload.dtype)

    def one(c, carry):
        leads = [folded(c * PAIRS + p * K) for p in range(STRIPES)]
        for g in range(n_tgroup):
            at = (g * n_chan + c) * BLOCKS
            for p in range(STRIPES):
                payload[at + p] = leads[p]
            for s in range(SLOTS):
                payload[at + STRIPES + s] = zero
        for q in range(PAIRS):
            payload[table[c * PAIRS + q]] = folded(c * PAIRS + q)
        return carry

    lax.fori_loop(0, n_chan, one, 0)


def correlate_kernel(n_chan, n_tgroup, factor, first_count, arrived, out, lead, window_a, window_b):
    samples = lead.shape[2] // n_tgroup - LANES
    span = samples + LANES
    cols = span // LANES
    lag_blocks = -(-LAGS // LANES)
    step = LANES // SHIFTS
    high = step * CB
    ahead = FRONT // LANES - 1
    windows = (window_a, window_b)

    def series(g, block):
        if arrived.shape[0] == n_tgroup * BLOCKS:
            value = arrived[g * BLOCKS + block].astype(jnp.float32)
        else:
            parts = []
            for c in range(n_chan):
                piece = arrived[(g * n_chan + c) * BLOCKS + block].astype(jnp.float32)
                parts += [piece[at : at + CB] for at in range(0, piece.shape[0], CB)]
            value = jnp.concatenate(parts, 1)
        return jnp.concatenate([value, jnp.zeros((CB, LANES), jnp.float32)], 1)

    for p in range(STRIPES):
        for g in range(n_tgroup):
            value = series(g, p)
            for a in range(CB):
                spread = jnp.broadcast_to(value[a : a + 1], (SHIFTS, span))
                turned = pltpu.roll(spread, 0, 1, stride=1, stride_axis=0)
                lead[p, a * SHIFTS : (a + 1) * SHIFTS, g * span : (g + 1) * span] = turned.astype(
                    jnp.bfloat16
                )

    def bounds(i):
        return max(0, ahead - i), min(cols, ahead + cols - i)

    for window in windows:
        for g in range(n_tgroup):
            for i in range(lag_blocks):
                first, last = bounds(i)
                rows = slice(i * high, (i + 1) * high)
                if first > 0:
                    window[rows, g * span : g * span + first * LANES] = jnp.zeros(
                        (high, first * LANES), jnp.bfloat16
                    )
                if last < cols:
                    window[rows, g * span + last * LANES : (g + 1) * span] = jnp.zeros(
                        (high, (cols - last) * LANES), jnp.bfloat16
                    )

    group = lax.broadcasted_iota(jnp.int32, (CB, LANES), 1) // SHIFTS
    for s in range(SLOTS):
        window = windows[s % 2]
        for g in range(n_tgroup):
            value = series(g, STRIPES + s)
            turned = [
                pltpu.roll(value, span - (FRONT - MAXLAG + SHIFTS * n), 1) for n in range(step)
            ]
            stacked = jnp.concatenate(turned, 0).astype(jnp.bfloat16)
            stacked = jnp.concatenate([stacked[:, samples:], stacked[:, :samples]], 1)
            for i in range(lag_blocks):
                first, last = bounds(i)
                window[
                    i * high : (i + 1) * high, g * span + first * LANES : g * span + last * LANES
                ] = stacked[:, (first + i - ahead) * LANES : (last + i - ahead) * LANES]
        which = jnp.where(s < first_count[0], 0, 1)
        summed = lax.dot_general(window[...], lead[which], NT, preferred_element_type=jnp.float32)
        summed = summed * factor
        for i in range(lag_blocks):
            width = min(LANES, LAGS - i * LANES)
            for h in range(CB // step):
                parts = [
                    summed[(i * step + n) * CB : (i * step + n + 1) * CB, h * LANES : (h + 1) * LANES]
                    for n in range(step)
                ]
                for a in range(step):
                    value = parts[a]
                    for n in range(step):
                        if n != a:
                            moved = pltpu.roll(parts[n], (SHIFTS * (n - a)) % LANES, 1)
                            value = jnp.where(group == n, moved, value)
                    out[s, h * step + a, :, i * LANES : i * LANES + width] = value[:, :width]


def local(raw_strain, whitening_taps, first_block, pair_owner):
    n_chan, n_tgroup = lax.axis_size("chan"), lax.axis_size("tgroup")
    n_dev = n_chan * n_tgroup
    rows, channels = raw_strain.shape
    outs = rows // 2
    samples = outs * n_chan
    count = n_chan * STRIPES * WIDE
    span = 2 * LANES

    own = jnp.concatenate([first_block, pair_owner[:, 0]])
    meta = lax.all_gather(own, "chan")
    me = lax.axis_index("tgroup")
    first_count = jnp.sum((pair_owner[:K, 0] == me).astype(jnp.int32)).reshape(1)
    main_taps, spill_taps = fir_matrix(whitening_taps, rows, outs)

    main, left, right, table = pl.pallas_call(
        functools.partial(select_kernel, n_chan, n_tgroup),
        out_shape=(
            jax.ShapeDtypeStruct((count, outs), jnp.float32),
            jax.ShapeDtypeStruct((count // 2, LANES), jnp.bfloat16),
            jax.ShapeDtypeStruct((count // 2, LANES), jnp.bfloat16),
            jax.ShapeDtypeStruct((n_chan * PAIRS,), jnp.int32),
        ),
        in_specs=[smem(), pl.BlockSpec(memory_space=pl.ANY), vmem(), vmem()],
        out_specs=(vmem(), vmem(), vmem(), smem()),
        scratch_shapes=[
            pltpu.VMEM((n_chan * STRIPES, rows, span), jnp.float32),
            pltpu.VMEM((count, rows), jnp.bfloat16),
            pltpu.SemaphoreType.DMA((n_chan * STRIPES,)),
        ],
        compiler_params=params(40),
        name="select_filter",
    )(meta, raw_strain, main_taps, spill_taps)

    from_right = from_behind(left, "chan", -1)
    from_left = from_behind(right, "chan", 1)

    lanes = min(LANES, outs)
    fold = CB * (outs // lanes)
    payload = pl.pallas_call(
        functools.partial(place_kernel, n_chan, n_tgroup),
        out_shape=jax.ShapeDtypeStruct((n_dev * BLOCKS, fold, lanes), jnp.bfloat16),
        in_specs=[smem(), vmem(), vmem(), vmem()],
        out_specs=vmem(),
        scratch_shapes=[pltpu.VMEM((count, outs), jnp.float32)],
        compiler_params=params(40),
        name="place_blocks",
    )(table, main, from_left, from_right)

    arrived = lax.all_to_all(
        payload.reshape(n_dev, BLOCKS, fold, lanes),
        ("tgroup", "chan"),
        split_axis=0,
        concat_axis=0,
        tiled=True,
    )
    if lanes == LANES:
        arrived = arrived.reshape(n_dev * BLOCKS, fold, lanes)
    else:
        arrived = arrived.reshape(n_tgroup, n_chan, BLOCKS, CB, lanes)
        arrived = arrived.transpose(0, 2, 3, 1, 4).reshape(n_tgroup * BLOCKS, CB, samples)

    depth = n_tgroup * (samples + LANES)
    return pl.pallas_call(
        functools.partial(correlate_kernel, n_chan, n_tgroup, 1.0 / math.sqrt(samples)),
        out_shape=jax.ShapeDtypeStruct((SLOTS, CB, CB, LAGS), jnp.float32),
        in_specs=[smem(), vmem()],
        out_specs=vmem(),
        scratch_shapes=[
            pltpu.VMEM((STRIPES, CB * SHIFTS, depth), jnp.bfloat16),
            pltpu.VMEM((-(-LAGS // SHIFTS) * CB, depth), jnp.bfloat16),
            pltpu.VMEM((-(-LAGS // SHIFTS) * CB, depth), jnp.bfloat16),
        ],
        compiler_params=params(56),
        name="correlate",
    )(first_count, arrived)


def solution(mesh):
    in_specs = (P(("tgroup", "chan"), None), P(), P("chan"), P("chan", None))
    out_specs = P(("tgroup", "chan"), None, None, None)
    return jax.shard_map(local, mesh=mesh, in_specs=in_specs, out_specs=out_specs, check_vma=False)
```

time: 890 us -> 74.4 us (0.08)
  local copies, waits for them, and re-layouts: 575 us -> 4.14 us
  waiting for transfers between devices: 234 us -> 25.6 us
  matrix products: 35.9 us -> 0 us
  Pallas kernels: 0 us -> 20.5 us
  other arithmetic: 19.6 us -> 2.28 us
  between operations: 15.7 us -> 0.78 us
  blocking collectives: 0 us -> 9.46 us
    gather x792 -> x0, local copies, waits for them, and re-layouts: 512 us -> none
    unnamed x2 -> x0, waiting for transfers between devices: 119 us -> none
    all_to_all x1, waiting for transfers between devices: 115 us -> 22.6 us  [local(): lax.all_to_all(payload.reshape(n_dev, BLOCKS, fold, lanes), ('tgroup', 'c...]
    dot_general x5 -> x0, matrix products: 35.9 us -> none  [the longest x1 21.2 us: whiten(): jnp.einsum('jq,bqc->cbj', matrix, windows, precision=lax.Precision.HIGHEST)]
    convert_element_type x3 -> x0, local copies, waits for them, and re-layouts: 24.7 us -> none  [the longest x2 16 us: whiten(): result.reshape(result.shape[0], blocks * out_rows).astype(jnp.bfloat16)]
    pallas_call x0 -> x3, Pallas kernels: none -> 20.5 us  [the longest x1 12.7 us: local(): pl.pallas_call(functools.partial(correlate_kernel, n_chan, n_tgroup, 1.0...]
    convert_element_type x3 -> x0, other arithmetic: 16.2 us -> none  [the longest x1 12.3 us: local(): grouped.astype(jnp.bfloat16)]
    pad x3 -> x0, local copies, waits for them, and re-layouts: 11.3 us -> none  [the longest x1 11.2 us: local(): padded = jnp.pad(series, ((half_taps, half_taps), (0, 0)))]
  transfers between devices with their start and end apart: 3 -> 3, of which waited for: 2 -> 2; matrix products, arithmetic and copies ran while one was open for 2% -> 1% of each run, Pallas kernels for 0% -> 0%
where the time goes in v1:
time: 74.4 us; the launch traced here: 74.1 us
  waiting for transfers between devices  25.6 us (34%)
  Pallas kernels  20.5 us (28%)
  starting transfers between devices  11.3 us (15%)
  blocking collectives  9.46 us (13%)
  local copies, waits for them, and re-layouts  4.14 us (6%)
  other arithmetic  2.28 us (3%)
  between operations  0.78 us (1%)
    all_to_all x1, waiting for transfers between devices, local(): lax.all_to_all(payload.reshape(n_dev, BLOCKS, fold, lanes), ('tgroup', 'c...  22.6 us
    pallas_call x1, Pallas kernels, local(): pl.pallas_call(functools.partial(correlate_kernel, n_chan, n_tgroup, 1.0...  12.7 us
    unnamed x1, blocking collectives  9.46 us
    all_to_all x1, starting transfers between devices, local(): lax.all_to_all(payload.reshape(n_dev, BLOCKS, fold, lanes), ('tgroup', 'c...  8.74 us
    pallas_call x1, Pallas kernels, local(): pl.pallas_call(functools.partial(select_kernel, n_chan, n_tgroup), out_sh...  5.79 us
    ppermute x2, waiting for transfers between devices, from_behind(): lax.ppermute(value, axis, [(source, source + steps) for source in range(f...  3.03 us
    ppermute x2, starting transfers between devices, from_behind(): lax.ppermute(value, axis, [(source, source + steps) for source in range(f...  2.59 us
    unnamed x6, local copies, waits for them, and re-layouts  2.17 us
  transfers between devices with their start and end apart: 3, of which 2 were waited for; matrix products, arithmetic and copies ran while one was open for 1% of the time, Pallas kernels for 0%

profile of v1, /device:TPU:0, one launch (start us, length us, event | category | flops | bytes accessed | tf_op | source)
XLA Modules:
  0.0 74.1 jit_solution(3660821298655066534)
XLA Ops:
  0.0 0.0 copy-start.1
  0.0 0.8 %maximum_convert_fusion = bf16[1024]{0:T(1024)(128)(2,1)S(1)} fusion(bf16[768]{0:T(1024)(128)(2,1)S(1)} %broadcast_in_dim.3, f32[255]{0:T(256)} %param.5, bf16[1]{0:T(256)(128)(2,1)} %constant.25), kind=kLoop, calls=%fused_computation.1 | loop fusion | flops 6144 | bytes 4606 | tf_op jit(solution)/shard_map/convert.4
  0.8 0.1 tile.10
  0.9 0.3 tile.11
  1.2 0.1 slice.26
  1.3 1.4 %reshape.18 = bf16[384,1022]{1,0:T(8,128)(2,1)S(1)} reshape(bf16[392448]{0:T(1024)(128)(2,1)S(1)} %slice.26) | data formatting | bytes 1569792 | tf_op jit(solution)/shard_map/reshape | solution.py:52
  2.7 1.2 %dynamic-slice = u32[1]{0:T(128)} dynamic-slice(u32[32]{0:T(128)} %constant.14, u32[]{:T(128)S(6)} %add), dynamic_slice_sizes={1} | dynamic-slice | bytes 12
  4.6 0.8 %add_dynamic-update-slice_fusion = s32[144]{0:T(256)S(1)} fusion(s32[144]{0:T(256)S(1)} %broadcast.4, u32[]{:T(128)} %bitcast.2, s32[16]{0:T(128)} %bitcast.6, s32[2]{0:T(128)} %param.6), kind=kLoop, calls=%fused_computation.4 | loop fusion | flops 18 | bytes 588
  5.5 9.5 %all-reduce = s32[144]{0:T(256)S(1)} all-reduce(s32[144]{0:T(256)S(1)} %add_dynamic-update-slice_fusion), channel_id=2, replica_groups=mesh['tgroup'=4,'chan'=8] {'chan'}, use_global_device_ids=true, to_apply=%add | all-reduce | flops 144 | bytes 1152
  14.9 0.1 reshape.21.meta
  15.0 5.8 %select_filter.1 = (f32[1024,256]{1,0:T(8,128)S(1)}, bf16[512,128]{1,0:T(8,128)(2,1)S(1)}, bf16[512,128]{1,0:T(8,128)(2,1)S(1)}, s32[128]{0:T(128)S(1)}) custom-call(s32[8,18]{1,0:T(8,128)S(1)} %reshape.21.meta, f32[512,10240]{1,0:T(8,128)} %raw.1, bf16[256,512]{1,0:T(8,128)(2,1)S(1)} %slice.27.main_taps, bf16[128,512]{1,0:T(8,128)(2,1)S(1)} %pad_maximum_fusion.spill_taps), custom_call_target="tpu_custom_call" | custom-call | tf_op jit(solution)/shard_map/select_filter/pallas_call | solution.py:246
  20.8 1.3 %collective-permute-start = (bf16[512,128]{1,0:T(8,128)(2,1)S(1)}, bf16[512,128]{1,0:T(8,128)(2,1)S(1)}, u32[]{:S(2)}, u32[]{:S(2)}) collective-permute-start(bf16[512,128]{1,0:T(8,128)(2,1)S(1)} %get-tuple-element.11), channel_id=1, source_target_pairs={{0,1},{1,2},{2,3},{3,4},{4,5},{5,6},{6,7},{8,9},{9,10},{10,11},{11... | collective-permute-start | bytes 393224 | tf_op jit(solution)/shard_map/ppermute | solution.py:42
  22.1 1.3 %collective-permute-start.1 = (bf16[512,128]{1,0:T(8,128)(2,1)S(1)}, bf16[512,128]{1,0:T(8,128)(2,1)S(1)}, u32[]{:S(2)}, u32[]{:S(2)}) collective-permute-start(bf16[512,128]{1,0:T(8,128)(2,1)S(1)} %get-tuple-element.12), channel_id=1, source_target_pairs={{1,0},{2,1},{3,2},{4,3},{5,4},{6,5},{7,6},{9,8},{10,9},{11,10},{12... | collective-permute-start | bytes 393224 | tf_op jit(solution)/shard_map/ppermute | solution.py:42
  23.4 0.0 collective-permute-done.from_left
  23.4 3.0 %collective-permute-done.1.from_right = bf16[512,128]{1,0:T(8,128)(2,1)S(1)} collective-permute-done((bf16[512,128]{1,0:T(8,128)(2,1)S(1)}, bf16[512,128]{1,0:T(8,128)(2,1)S(1)}, u32[]{:S(2)}, u32[]{:S(2)}) %collective-permute-start.1) | collective-permute-done | bytes 131104 | tf_op jit(solution)/shard_map/ppermute | solution.py:42
  26.5 2.0 %place_blocks.1 = bf16[224,16,128]{2,1,0:T(8,128)(2,1)} custom-call(s32[128]{0:T(128)S(1)} %get-tuple-element.9.table, f32[1024,256]{1,0:T(8,128)S(1)} %get-tuple-element.10.main, bf16[512,128]{1,0:T(8,128)(2,1)S(1)} %collective-permute-done.from_left, bf16[512,128]{1,0:T(8,128)(2,1)S(1)} %collective-permute-done.1.from_right), custom_call_target="tpu_custom_call" | custom-call | tf_op jit(solution)/shard_map/place_blocks/pallas_call | solution.py:270
  28.5 8.7 %all-to-all-start = ((bf16[32,7,16,128]{3,2,1,0:T(8,128)(2,1)}), bf16[32,7,16,128]{3,2,1,0:T(8,128)(2,1)S(1)}, u32[]{:S(2)}, u32[]{:S(2)}) async-start(bf16[32,7,16,128]{3,2,1,0:T(8,128)(2,1)} %bitcast.3), calls=%async_computation | async-start | bytes 1835008 | tf_op jit(solution)/shard_map/all_to_all | solution.py:280
  37.2 0.0 copy-done.1
  37.2 0.7 fusion
  37.9 22.6 %all-to-all-done = bf16[32,7,16,128]{3,2,1,0:T(8,128)(2,1)S(1)} async-done(((bf16[32,7,16,128]{3,2,1,0:T(8,128)(2,1)}), bf16[32,7,16,128]{3,2,1,0:T(8,128)(2,1)S(1)}, u32[]{:S(2)}, u32[]{:S(2)}) %all-to-all-start) | async-done | bytes 917536 | tf_op jit(solution)/shard_map/all_to_all | solution.py:280
  60.4 0.0 copy-start
  60.4 0.9 %copy-done = bf16[32,7,16,128]{3,2,1,0:T(8,128)(2,1)} copy-done((bf16[32,7,16,128]{3,2,1,0:T(8,128)(2,1)}, bf16[32,7,16,128]{3,2,1,0:T(8,128)(2,1)S(1)}, u32[]{:S(2)}) %copy-start) | copy-done | bytes 917528
  61.4 12.7 %correlate.1 = f32[5,8,8,1001]{3,2,1,0:T(8,128)} custom-call(s32[1]{0:T(128)} %bitcast.first_count, bf16[224,16,128]{2,1,0:T(8,128)(2,1)} %bitcast.5), custom_call_target="tpu_custom_call" | custom-call | tf_op jit(solution)/shard_map/correlate/pallas_call | solution.py:294
  (5 shorter events, 0.0 us)
Async XLA Ops:
  0.0 37.2 %copy-start.1 = (s32[16,1]{0,1:T(1,128)S(1)}, s32[16,1]{0,1:T(1,128)}, u32[]{:S(2)}) copy-start(s32[16,1]{0,1:T(1,128)} %param.7) | copy-start | bytes 196
  20.8 2.6 %collective-permute-start = (bf16[512,128]{1,0:T(8,128)(2,1)S(1)}, bf16[512,128]{1,0:T(8,128)(2,1)S(1)}, u32[]{:S(2)}, u32[]{:S(2)}) collective-permute-start(bf16[512,128]{1,0:T(8,128)(2,1)S(1)} %get-tuple-element.11), channel_id=1, source_target_pairs={{0,1},{1,2},{2,3},{3,4},{4,5},{5,6},{6,7},{8,9},{9,10},{10,11},{11... | collective-permute-start | bytes 393224 | tf_op jit(solution)/shard_map/ppermute | solution.py:42
  22.1 4.3 %collective-permute-start.1 = (bf16[512,128]{1,0:T(8,128)(2,1)S(1)}, bf16[512,128]{1,0:T(8,128)(2,1)S(1)}, u32[]{:S(2)}, u32[]{:S(2)}) collective-permute-start(bf16[512,128]{1,0:T(8,128)(2,1)S(1)} %get-tuple-element.12), channel_id=1, source_target_pairs={{1,0},{2,1},{3,2},{4,3},{5,4},{6,5},{7,6},{9,8},{10,9},{11,10},{12... | collective-permute-start | bytes 393224 | tf_op jit(solution)/shard_map/ppermute | solution.py:42
  28.5 32.0 %all-to-all-start = ((bf16[32,7,16,128]{3,2,1,0:T(8,128)(2,1)}), bf16[32,7,16,128]{3,2,1,0:T(8,128)(2,1)S(1)}, u32[]{:S(2)}, u32[]{:S(2)}) async-start(bf16[32,7,16,128]{3,2,1,0:T(8,128)(2,1)} %bitcast.3), calls=%async_computation | async-start | bytes 1835008 | tf_op jit(solution)/shard_map/all_to_all | solution.py:280
  60.4 0.9 %copy-start = (bf16[32,7,16,128]{3,2,1,0:T(8,128)(2,1)}, bf16[32,7,16,128]{3,2,1,0:T(8,128)(2,1)S(1)}, u32[]{:S(2)}) copy-start(bf16[32,7,16,128]{3,2,1,0:T(8,128)(2,1)S(1)} %all-to-all-done) | copy-start | bytes 2752516

commit v2 on v0

v2 whole, which is shorter than its diff:
```python
import functools
import math

import jax
import jax.numpy as jnp
from jax import lax
from jax.experimental import pallas as pl
from jax.experimental.pallas import tpu as pltpu
from jax.sharding import PartitionSpec as P

MAXLAG = 500
LAGS = 2 * MAXLAG + 1
TAPS = 255
CB = 8
K = 8
STRIPES = 2
SLOTS = 5
PAIRS = STRIPES * K
BLOCKS = STRIPES + SLOTS
WIDE = K * CB
SPILL = 64
LANES = 128
SHIFTS = 32
STEP = LANES // SHIFTS
LAG_BLOCKS = -(-LAGS // LANES)
FRONT = -(-MAXLAG // LANES) * LANES
NT = (((1,), (1,)), ((), ()))


def params(megabytes):
    return pltpu.CompilerParams(vmem_limit_bytes=megabytes << 20)


def vmem():
    return pl.BlockSpec(memory_space=pltpu.VMEM)


def smem():
    return pl.BlockSpec(memory_space=pltpu.SMEM)


def select_kernel(n_chan, firsts, raw, taps, sent, window, picked, line, sems):
    rows, channels = raw.shape
    outs = rows // 2
    stripes = n_chan * STRIPES
    blocks_per = channels // n_chan // CB
    span = window.shape[2]

    def place(p):
        c, k = p // STRIPES, p % STRIPES
        start = (firsts[c, k] + c * blocks_per) * CB
        base = jnp.minimum(start - lax.rem(start, LANES), channels - span)
        return start, pl.multiple_of(base, LANES)

    def copy(p):
        base = place(p)[1]
        return pltpu.make_async_copy(raw.at[:, pl.ds(base, span)], window.at[p], sems.at[p])

    for p in range(stripes):
        copy(p).start()

    width = line.shape[1]
    line[...] = jnp.zeros_like(line)
    line[0:1, :TAPS] = taps[...]
    spread = jnp.broadcast_to(line[0:1, :], (outs + 2 * SPILL, width))
    weights = pltpu.roll(spread, width - 4 * SPILL + 1, 1, stride=2, stride_axis=0)[:, :rows]
    weights = weights.astype(jnp.bfloat16)
    weights = jnp.concatenate(
        [weights[SPILL : SPILL + outs], weights[SPILL + outs :], weights[:SPILL]], 0
    )

    row = lax.broadcasted_iota(jnp.int32, (WIDE, span), 0)
    lane = lax.broadcasted_iota(jnp.int32, (WIDE, span), 1)
    batch = 4
    for first in range(0, stripes, batch):
        for p in range(first, first + batch):
            copy(p).wait()
            start, base = place(p)
            hot = (lane == row + (start - base)) & (row < channels - start)
            hot = jnp.where(hot, 1.0, 0.0).astype(jnp.bfloat16)
            block = window[p].astype(jnp.bfloat16)
            chosen = lax.dot_general(hot, block, NT, preferred_element_type=jnp.float32)
            picked[p * WIDE : (p + 1) * WIDE, :] = chosen.astype(jnp.bfloat16)
        part = slice(first * WIDE, (first + batch) * WIDE)
        result = lax.dot_general(picked[part, :], weights, NT, preferred_element_type=jnp.float32)
        sent[part, :] = result.astype(jnp.bfloat16)


def add_spills(n_chan, outs, got, total):
    count = total.shape[0]
    early = lax.broadcasted_iota(jnp.int32, (count, LANES), 1) < SPILL

    def spill(c):
        return got[c * count : (c + 1) * count, outs:].astype(jnp.float32)

    spills = [spill(c) for c in range(n_chan)]
    for c in range(n_chan):
        value = got[c * count : (c + 1) * count, :outs].astype(jnp.float32)
        parts = [value[:, at : at + LANES] for at in range(0, outs, LANES)]
        if c > 0:
            parts[0] = parts[0] + jnp.where(early, spills[c - 1], 0.0)
        if c < n_chan - 1:
            parts[-1] = parts[-1] + jnp.where(early, 0.0, spills[c + 1])
        for at, part in enumerate(parts):
            total[:, c * outs + at * LANES : c * outs + (at + 1) * LANES] = part


def place_kernel(n_chan, n_tgroup, outs, owners, got, *refs):
    sends, (total, pairs) = refs[:n_tgroup], refs[n_tgroup:]
    me = lax.axis_index("tgroup")
    if got.dtype == jnp.float32:
        total[...] = got[...]
    else:
        add_spills(n_chan, outs, got, total)

    for at in range(n_tgroup * SLOTS):
        pairs[at] = -1
    counts = jnp.int32(0)
    for q in range(PAIRS):
        owner = owners[q]
        slot = (counts >> (3 * owner)) & 7
        counts = counts + (jnp.int32(1) << (3 * owner))
        pairs[lax.rem(owner - me + n_tgroup, n_tgroup) * SLOTS + slot] = q

    half = total.shape[1] // 2

    def folded(q):
        value = total[pl.ds(pl.multiple_of(q * CB, CB), CB), :]
        return jnp.concatenate([value[:, :half], value[:, half:]], 0)

    leads = [folded(p * K).astype(jnp.bfloat16) for p in range(STRIPES)]
    for shift in range(n_tgroup):
        for p in range(STRIPES):
            sends[shift][p] = leads[p]
        for s in range(SLOTS):
            q = pairs[shift * SLOTS + s]
            value = jnp.where(q >= 0, folded(jnp.maximum(q, 0)), 0.0)
            sends[shift][STRIPES + s] = value.astype(jnp.bfloat16)


def correlate_kernel(factor, last, owners, *refs):
    lead, window_a, window_b = refs[-3:]
    out = refs[-4]
    arrived, before = refs[0], (refs[1] if len(refs) == 6 else None)
    windows = (window_a, window_b)
    span = lead.shape[2]
    samples = span - LANES
    cols = span // LANES
    high = STEP * CB
    ahead = FRONT // LANES - 1
    me = lax.axis_index("tgroup")
    first_count = jnp.int32(0)
    for q in range(K):
        first_count += jnp.where(owners[q] == me, 1, 0)

    def series(block):
        value = arrived[block].astype(jnp.float32)
        return jnp.concatenate([value[:CB], value[CB:], jnp.zeros((CB, LANES), jnp.float32)], 1)

    for p in range(STRIPES):
        value = series(p)
        for a in range(CB):
            spread = jnp.broadcast_to(value[a : a + 1], (SHIFTS, span))
            turned = pltpu.roll(spread, 0, 1, stride=1, stride_axis=0)
            lead[p, a * SHIFTS : (a + 1) * SHIFTS, :] = turned.astype(jnp.bfloat16)

    def bounds(i):
        return max(0, ahead - i), min(cols, ahead + cols - i)

    for window in windows:
        for i in range(LAG_BLOCKS):
            first, end = bounds(i)
            rows = slice(i * high, (i + 1) * high)
            if first > 0:
                window[rows, : first * LANES] = jnp.zeros((high, first * LANES), jnp.bfloat16)
            if end < cols:
                window[rows, end * LANES :] = jnp.zeros((high, (cols - end) * LANES), jnp.bfloat16)

    group = lax.broadcasted_iota(jnp.int32, (CB, LANES), 1) // SHIFTS
    for s in range(SLOTS):
        window = windows[s % 2]
        value = series(STRIPES + s)
        turned = [pltpu.roll(value, span - (FRONT - MAXLAG + SHIFTS * n), 1) for n in range(STEP)]
        stacked = jnp.concatenate(turned, 0).astype(jnp.bfloat16)
        stacked = jnp.concatenate([stacked[:, samples:], stacked[:, :samples]], 1)
        for i in range(LAG_BLOCKS):
            first, end = bounds(i)
            window[i * high : (i + 1) * high, first * LANES : end * LANES] = stacked[
                :, (first + i - ahead) * LANES : (end + i - ahead) * LANES
            ]
        which = jnp.where(s < first_count, 0, 1)
        summed = lax.dot_general(window[...], lead[which], NT, preferred_element_type=jnp.float32)
        if before is not None:
            summed = summed + before[s]
        if not last:
            out[s] = summed
            continue
        summed = summed * factor
        for i in range(LAG_BLOCKS):
            width = min(LANES, LAGS - i * LANES)
            for h in range(CB // STEP):
                parts = [
                    summed[(i * STEP + n) * CB : (i * STEP + n + 1) * CB, h * LANES : (h + 1) * LANES]
                    for n in range(STEP)
                ]
                for a in range(STEP):
                    value = parts[a]
                    for n in range(STEP):
                        if n != a:
                            moved = pltpu.roll(parts[n], (SHIFTS * (n - a)) % LANES, 1)
                            value = jnp.where(group == n, moved, value)
                    out[s, h * STEP + a, :, i * LANES : i * LANES + width] = value[:, :width]


def correlate(owners, arrived, before, factor, last, samples):
    high, wide = STEP * LAG_BLOCKS * CB, CB * SHIFTS
    if last:
        shape = jax.ShapeDtypeStruct((SLOTS, CB, CB, LAGS), jnp.float32)
    else:
        shape = jax.ShapeDtypeStruct((SLOTS, high, wide), jnp.float32)
    operands = (owners, arrived) + (() if before is None else (before,))
    return pl.pallas_call(
        functools.partial(correlate_kernel, factor, last),
        out_shape=shape,
        in_specs=[smem()] + [vmem()] * (len(operands) - 1),
        out_specs=vmem(),
        scratch_shapes=[
            pltpu.VMEM((STRIPES, wide, samples + LANES), jnp.bfloat16),
            pltpu.VMEM((high, samples + LANES), jnp.bfloat16),
            pltpu.VMEM((high, samples + LANES), jnp.bfloat16),
        ],
        compiler_params=params(40),
        name="correlate_last" if last else "correlate",
    )(*operands)


def local(raw_strain, whitening_taps, first_block, pair_owner):
    n_chan, n_tgroup = lax.axis_size("chan"), lax.axis_size("tgroup")
    rows, channels = raw_strain.shape
    outs = rows // 2
    samples = outs * n_chan
    count = PAIRS * CB
    owners = pair_owner[:, 0]

    firsts = lax.all_to_all(
        jnp.broadcast_to(first_block[None, :], (n_chan, STRIPES)),
        "chan",
        split_axis=0,
        concat_axis=0,
        tiled=True,
    )
    line = -(-(rows + 2 * outs + 4 * SPILL) // (2 * LANES)) * 2 * LANES
    sent = pl.pallas_call(
        functools.partial(select_kernel, n_chan),
        out_shape=jax.ShapeDtypeStruct((n_chan * count, outs + 2 * SPILL), jnp.bfloat16),
        in_specs=[smem(), pl.BlockSpec(memory_space=pl.ANY), vmem()],
        out_specs=vmem(),
        scratch_shapes=[
            pltpu.VMEM((n_chan * STRIPES, rows, 2 * LANES), jnp.float32),
            pltpu.VMEM((n_chan * count, rows), jnp.bfloat16),
            pltpu.VMEM((8, line), jnp.float32),
            pltpu.SemaphoreType.DMA((n_chan * STRIPES,)),
        ],
        compiler_params=params(40),
        name="select_filter",
    )(firsts, raw_strain, whitening_taps.reshape(1, TAPS))

    got = lax.all_to_all(
        sent.reshape(n_chan, count, outs + 2 * SPILL),
        "chan",
        split_axis=0,
        concat_axis=0,
        tiled=True,
    )
    if outs % LANES == 0:
        got = got.reshape(n_chan * count, outs + 2 * SPILL)
    else:
        wide = got.astype(jnp.float32)
        none = jnp.zeros((1, count, outs - SPILL), jnp.float32)
        zero = jnp.zeros((1, count, SPILL), jnp.float32)
        right = jnp.concatenate([zero, wide[:-1, :, outs : outs + SPILL]], 0)
        left = jnp.concatenate([wide[1:, :, outs + SPILL :], zero], 0)
        none = jnp.broadcast_to(none, (n_chan,) + none.shape[1:])
        added = wide[:, :, :outs] + jnp.concatenate([right, none], 2) + jnp.concatenate([none, left], 2)
        got = added.transpose(1, 0, 2).reshape(count, samples)

    packed = jax.ShapeDtypeStruct((BLOCKS, 2 * CB, samples // 2), jnp.bfloat16)
    sends = pl.pallas_call(
        functools.partial(place_kernel, n_chan, n_tgroup, outs),
        out_shape=(packed,) * n_tgroup,
        in_specs=[smem(), vmem()],
        out_specs=(vmem(),) * n_tgroup,
        scratch_shapes=[
            pltpu.VMEM((count, samples), jnp.float32),
            pltpu.SMEM((n_tgroup * SLOTS,), jnp.int32),
        ],
        compiler_params=params(40),
        name="place_blocks",
    )(owners, got)

    order = sorted(range(1, n_tgroup), key=lambda s: min(s, n_tgroup - s))
    arrived = [sends[0]]
    for shift in order:
        route = [(g, (g + shift) % n_tgroup) for g in range(n_tgroup)]
        arrived.append(lax.ppermute(sends[shift], "tgroup", route))

    value = None
    factor = 1.0 / math.sqrt(samples)
    for at, block in enumerate(arrived):
        value = correlate(owners, block, value, factor, at == n_tgroup - 1, samples)
    return value


def solution(mesh):
    in_specs = (P(("tgroup", "chan"), None), P(), P("chan"), P("chan", None))
    out_specs = P(("tgroup", "chan"), None, None, None)
    return jax.shard_map(local, mesh=mesh, in_specs=in_specs, out_specs=out_specs, check_vma=False)
```

time: 890 us -> 61.3 us (0.07)
  local copies, waits for them, and re-layouts: 575 us -> 1.34 us
  waiting for transfers between devices: 234 us -> 8.72 us
  matrix products: 35.9 us -> 0 us
  blocking collectives: 0 us -> 24.6 us
  Pallas kernels: 0 us -> 21.4 us
  other arithmetic: 19.6 us -> 0 us
  between operations: 15.7 us -> 0.06 us
    gather x792 -> x0, local copies, waits for them, and re-layouts: 512 us -> none
    unnamed x2 -> x0, waiting for transfers between devices: 119 us -> none
    all_to_all x1 -> x0, waiting for transfers between devices: 115 us -> none  [local(): lax.all_to_all(grouped.astype(jnp.bfloat16), 'chan', split_axis=1, concat...]
    dot_general x5 -> x0, matrix products: 35.9 us -> none  [the longest x1 21.2 us: whiten(): jnp.einsum('jq,bqc->cbj', matrix, windows, precision=lax.Precision.HIGHEST)]
    convert_element_type x3 -> x0, local copies, waits for them, and re-layouts: 24.7 us -> none  [the longest x2 16 us: whiten(): result.reshape(result.shape[0], blocks * out_rows).astype(jnp.bfloat16)]
    all_to_all x0 -> x2, blocking collectives: none -> 24.6 us  [the longest x1 15 us: local(): lax.all_to_all(sent.reshape(n_chan, count, outs + 2 * SPILL), 'chan', spl...]
    pallas_call x0 -> x6, Pallas kernels: none -> 21.4 us  [the longest x4 14.6 us: correlate(): pl.pallas_call(functools.partial(correlate_kernel, factor, last), out_sha...]
    convert_element_type x3 -> x0, other arithmetic: 16.2 us -> none  [the longest x1 12.3 us: local(): grouped.astype(jnp.bfloat16)]
  transfers between devices with their start and end apart: 3 -> 3, of which waited for: 2 -> 2; matrix products, arithmetic and copies ran while one was open for 2% -> 0% of each run, Pallas kernels for 0% -> 16%
where the time goes in v2:
time: 61.3 us; the launch traced here: 60.8 us
  blocking collectives  24.6 us (40%)
  Pallas kernels  21.4 us (35%)
  waiting for transfers between devices  8.72 us (14%)
  starting transfers between devices  4.67 us (8%)
  local copies, waits for them, and re-layouts  1.34 us (2%)
    all_to_all x1, blocking collectives, local(): lax.all_to_all(sent.reshape(n_chan, count, outs + 2 * SPILL), 'chan', spl...  15 us
    pallas_call x4, Pallas kernels, correlate(): pl.pallas_call(functools.partial(correlate_kernel, factor, last), out_sha...  14.6 us
    all_to_all x1, blocking collectives, local(): lax.all_to_all(jnp.broadcast_to(first_block[None, :], (n_chan, STRIPES)),...  9.62 us
    ppermute x3, waiting for transfers between devices, local(): arrived.append(lax.ppermute(sends[shift], 'tgroup', route))  8.72 us
    pallas_call x1, Pallas kernels, local(): pl.pallas_call(functools.partial(select_kernel, n_chan), out_shape=jax.Sh...  5.94 us
    ppermute x3, starting transfers between devices, local(): arrived.append(lax.ppermute(sends[shift], 'tgroup', route))  4.67 us
  transfers between devices with their start and end apart: 3, of which 2 were waited for; matrix products, arithmetic and copies ran while one was open for 0% of the time, Pallas kernels for 16%

profile of v2, /device:TPU:0, one launch (start us, length us, event | category | flops | bytes accessed | tf_op | source)
XLA Modules:
  0.0 60.8 jit_solution(13936039146960187215)
XLA Ops:
  0.0 0.7 %broadcast_in_dim.2 = s32[8,1,2]{2,1,0:T(1,128)S(1)} broadcast(s32[2]{0:T(128)} %param.6), dimensions={2} | broadcast | bytes 72 | tf_op jit(solution)/shard_map/broadcast_in_dim | solution.py:246
  0.7 9.6 %all_to_all.13 = s32[8,1,2]{2,1,0:T(1,128)S(1)} all-to-all(s32[8,1,2]{2,1,0:T(1,128)S(1)} %broadcast_in_dim.2), channel_id=1, replica_groups=mesh['tgroup'=4,'chan'=8] {'chan'}, dimensions={0} | all-to-all | bytes 128 | tf_op jit(solution)/shard_map/all_to_all | solution.py:245
  10.3 0.0 copy-start.1
  10.3 0.7 %copy-done.1 = f32[255]{0:T(256)S(1)} copy-done((f32[255]{0:T(256)S(1)}, f32[255]{0:T(256)}, u32[]{:S(2)}) %copy-start.1) | copy-done | bytes 1044
  11.0 5.9 %select_filter.1 = bf16[1024,384]{1,0:T(8,128)(2,1)S(1)} custom-call(s32[8,2]{1,0:T(8,128)S(1)} %bitcast.7, f32[512,10240]{1,0:T(8,128)} %raw.1, f32[1,255]{1,0:T(1,128)S(1)} %bitcast.13), custom_call_target="tpu_custom_call" | custom-call | tf_op jit(solution)/shard_map/select_filter/pallas_call | solution.py:253
  16.9 0.0 copy-start
  16.9 15.0 %all_to_all.14 = bf16[8,128,384]{2,1,0:T(8,128)(2,1)S(1)} all-to-all(bf16[8,128,384]{2,1,0:T(8,128)(2,1)S(1)} %bitcast.5), channel_id=1, replica_groups=mesh['tgroup'=4,'chan'=8] {'chan'}, dimensions={0} | all-to-all | bytes 1572864 | tf_op jit(solution)/shard_map/all_to_all | solution.py:268
  31.9 0.0 copy-done
  31.9 0.9 %place_blocks.1 = (bf16[7,16,1024]{2,1,0:T(8,128)(2,1)S(1)}, bf16[7,16,1024]{2,1,0:T(8,128)(2,1)S(1)}, bf16[7,16,1024]{2,1,0:T(8,128)(2,1)S(1)}, bf16[7,16,1024]{2,1,0:T(8,128)(2,1)S(1)}) custom-call(s32[16]{0:T(128)S(1)} %bitcast.8, bf16[1024,384]{1,0:T(8,128)(2,1)S(1)} %bitcast.6), custom_call_target="tpu_custom_call" | custom-call | tf_op jit(solution)/shard_map/place_blocks/pallas_call | solution.py:288
  32.7 1.6 %collective-permute-start.2 = (bf16[7,16,1024]{2,1,0:T(8,128)(2,1)S(1)}, bf16[7,16,1024]{2,1,0:T(8,128)(2,1)S(1)}, u32[]{:S(2)}, u32[]{:S(2)}) collective-permute-start(bf16[7,16,1024]{2,1,0:T(8,128)(2,1)S(1)} %get-tuple-element.11), channel_id=1, source_target_pairs={{0,8},{8,16},{16,24},{24,0},{1,9},{9,17},{17,25},{25,1},{2,10},{10... | collective-permute-start | bytes 688136 | tf_op jit(solution)/shard_map/ppermute | solution.py:305
  34.4 2.3 %collective-permute-start.1 = (bf16[7,16,1024]{2,1,0:T(8,128)(2,1)S(1)}, bf16[7,16,1024]{2,1,0:T(8,128)(2,1)S(1)}, u32[]{:S(2)}, u32[]{:S(2)}) collective-permute-start(bf16[7,16,1024]{2,1,0:T(8,128)(2,1)S(1)} %get-tuple-element.10), channel_id=1, source_target_pairs={{0,24},{8,0},{16,8},{24,16},{1,25},{9,1},{17,9},{25,17},{2,26},{10... | collective-permute-start | bytes 688136 | tf_op jit(solution)/shard_map/ppermute | solution.py:305
  36.7 0.8 %collective-permute-start = (bf16[7,16,1024]{2,1,0:T(8,128)(2,1)S(1)}, bf16[7,16,1024]{2,1,0:T(8,128)(2,1)S(1)}, u32[]{:S(2)}, u32[]{:S(2)}) collective-permute-start(bf16[7,16,1024]{2,1,0:T(8,128)(2,1)S(1)} %get-tuple-element.9), channel_id=1, source_target_pairs={{0,16},{8,24},{16,0},{24,8},{1,17},{9,25},{17,1},{25,9},{2,18},{10... | collective-permute-start | bytes 688136 | tf_op jit(solution)/shard_map/ppermute | solution.py:305
  37.4 3.3 %correlate.3.refs_1_ = f32[5,256,256]{2,1,0:T(8,128)S(1)} custom-call(s32[16]{0:T(128)S(1)} %bitcast.9, bf16[7,16,1024]{2,1,0:T(8,128)(2,1)S(1)} %get-tuple-element.12.refs_0_), custom_call_target="tpu_custom_call" | custom-call | tf_op jit(solution)/shard_map/correlate/pallas_call | solution.py:222
  40.7 2.5 %collective-permute-done.2.refs_0_ = bf16[7,16,1024]{2,1,0:T(8,128)(2,1)S(1)} collective-permute-done((bf16[7,16,1024]{2,1,0:T(8,128)(2,1)S(1)}, bf16[7,16,1024]{2,1,0:T(8,128)(2,1)S(1)}, u32[]{:S(2)}, u32[]{:S(2)}) %collective-permute-start.2) | collective-permute-done | bytes 229408 | tf_op jit(solution)/shard_map/ppermute | solution.py:305
  43.2 3.3 %correlate.4.refs_1_ = f32[5,256,256]{2,1,0:T(8,128)S(1)} custom-call(s32[16]{0:T(128)S(1)} %bitcast.10, bf16[7,16,1024]{2,1,0:T(8,128)(2,1)S(1)} %collective-permute-done.2.refs_0_, f32[5,256,256]{2,1,0:T(8,128)S(1)} %correlate.3.refs_1_), custom_call_target="tpu_custom_call" | custom-call | tf_op jit(solution)/shard_map/correlate/pallas_call | solution.py:222
  46.5 0.0 collective-permute-done.1.refs_0_
  46.5 3.3 %correlate.5.refs_1_ = f32[5,256,256]{2,1,0:T(8,128)S(1)} custom-call(s32[16]{0:T(128)S(1)} %bitcast.11, bf16[7,16,1024]{2,1,0:T(8,128)(2,1)S(1)} %collective-permute-done.1.refs_0_, f32[5,256,256]{2,1,0:T(8,128)S(1)} %correlate.4.refs_1_), custom_call_target="tpu_custom_call" | custom-call | tf_op jit(solution)/shard_map/correlate/pallas_call | solution.py:222
  49.9 6.3 %collective-permute-done.refs_0_ = bf16[7,16,1024]{2,1,0:T(8,128)(2,1)S(1)} collective-permute-done((bf16[7,16,1024]{2,1,0:T(8,128)(2,1)S(1)}, bf16[7,16,1024]{2,1,0:T(8,128)(2,1)S(1)}, u32[]{:S(2)}, u32[]{:S(2)}) %collective-permute-start) | collective-permute-done | bytes 229408 | tf_op jit(solution)/shard_map/ppermute | solution.py:305
  56.1 4.7 %correlate_last.1 = f32[5,8,8,1001]{3,2,1,0:T(8,128)} custom-call(s32[16]{0:T(128)S(1)} %bitcast.12, bf16[7,16,1024]{2,1,0:T(8,128)(2,1)S(1)} %collective-permute-done.refs_0_, f32[5,256,256]{2,1,0:T(8,128)S(1)} %correlate.5.refs_1_), custom_call_target="tpu_custom_call" | custom-call | tf_op jit(solution)/shard_map/correlate_last/pallas_call | solution.py:222
Async XLA Ops:
  10.3 0.7 %copy-start.1 = (f32[255]{0:T(256)S(1)}, f32[255]{0:T(256)}, u32[]{:S(2)}) copy-start(f32[255]{0:T(256)} %param.5) | copy-start | bytes 3064
  16.9 15.0 %copy-start = (s32[16,1]{0,1:T(1,128)S(1)}, s32[16,1]{0,1:T(1,128)}, u32[]{:S(2)}) copy-start(s32[16,1]{0,1:T(1,128)} %param.7) | copy-start | bytes 196
  32.7 10.4 %collective-permute-start.2 = (bf16[7,16,1024]{2,1,0:T(8,128)(2,1)S(1)}, bf16[7,16,1024]{2,1,0:T(8,128)(2,1)S(1)}, u32[]{:S(2)}, u32[]{:S(2)}) collective-permute-start(bf16[7,16,1024]{2,1,0:T(8,128)(2,1)S(1)} %get-tuple-element.11), channel_id=1, source_target_pairs={{0,8},{8,16},{16,24},{24,0},{1,9},{9,17},{17,25},{25,1},{2,10},{10... | collective-permute-start | bytes 688136 | tf_op jit(solution)/shard_map/ppermute | solution.py:305
  34.4 12.1 %collective-permute-start.1 = (bf16[7,16,1024]{2,1,0:T(8,128)(2,1)S(1)}, bf16[7,16,1024]{2,1,0:T(8,128)(2,1)S(1)}, u32[]{:S(2)}, u32[]{:S(2)}) collective-permute-start(bf16[7,16,1024]{2,1,0:T(8,128)(2,1)S(1)} %get-tuple-element.10), channel_id=1, source_target_pairs={{0,24},{8,0},{16,8},{24,16},{1,25},{9,1},{17,9},{25,17},{2,26},{10... | collective-permute-start | bytes 688136 | tf_op jit(solution)/shard_map/ppermute | solution.py:305
  36.7 19.5 %collective-permute-start = (bf16[7,16,1024]{2,1,0:T(8,128)(2,1)S(1)}, bf16[7,16,1024]{2,1,0:T(8,128)(2,1)S(1)}, u32[]{:S(2)}, u32[]{:S(2)}) collective-permute-start(bf16[7,16,1024]{2,1,0:T(8,128)(2,1)S(1)} %get-tuple-element.9), channel_id=1, source_target_pairs={{0,16},{8,24},{16,0},{24,8},{1,17},{9,25},{17,1},{25,9},{2,18},{10... | collective-permute-start | bytes 688136 | tf_op jit(solution)/shard_map/ppermute | solution.py:305

commit v3 on v2

--- a/solution.py
+++ b/solution.py
@@ -39,15 +39,17 @@
     return pl.BlockSpec(memory_space=pltpu.SMEM)
 
 
-def select_kernel(n_chan, firsts, raw, taps, sent, window, picked, line, sems):
+def select_kernel(n_chan, firsts, raw, taps, *refs):
+    sends, (window, picked, line, tap_sem, sems) = refs[:n_chan], refs[n_chan:]
     rows, channels = raw.shape
     outs = rows // 2
     stripes = n_chan * STRIPES
     blocks_per = channels // n_chan // CB
     span = window.shape[2]
+    me = lax.axis_index("chan")
 
     def place(p):
-        c, k = p // STRIPES, p % STRIPES
+        c, k = me ^ (p // STRIPES), p % STRIPES
         start = (firsts[c, k] + c * blocks_per) * CB
         base = jnp.minimum(start - lax.rem(start, LANES), channels - span)
         return start, pl.multiple_of(base, LANES)
@@ -56,12 +58,14 @@
         base = place(p)[1]
         return pltpu.make_async_copy(raw.at[:, pl.ds(base, span)], window.at[p], sems.at[p])
 
+    line[...] = jnp.zeros_like(line)
+    tap_copy = pltpu.make_async_copy(taps, line.at[0:1, : taps.shape[1]], tap_sem)
+    tap_copy.start()
     for p in range(stripes):
         copy(p).start()
 
     width = line.shape[1]
-    line[...] = jnp.zeros_like(line)
-    line[0:1, :TAPS] = taps[...]
+    tap_copy.wait()
     spread = jnp.broadcast_to(line[0:1, :], (outs + 2 * SPILL, width))
     weights = pltpu.roll(spread, width - 4 * SPILL + 1, 1, stride=2, stride_axis=0)[:, :rows]
     weights = weights.astype(jnp.bfloat16)
@@ -71,7 +75,7 @@
 
     row = lax.broadcasted_iota(jnp.int32, (WIDE, span), 0)
     lane = lax.broadcasted_iota(jnp.int32, (WIDE, span), 1)
-    batch = 4
+    batch = 2 * STRIPES
     for first in range(0, stripes, batch):
         for p in range(first, first + batch):
             copy(p).wait()
@@ -83,33 +87,45 @@
             picked[p * WIDE : (p + 1) * WIDE, :] = chosen.astype(jnp.bfloat16)
         part = slice(first * WIDE, (first + batch) * WIDE)
         result = lax.dot_general(picked[part, :], weights, NT, preferred_element_type=jnp.float32)
-        sent[part, :] = result.astype(jnp.bfloat16)
+        result = result.astype(jnp.bfloat16)
+        for at in range(batch // STRIPES):
+            sends[first // STRIPES + at][...] = result[at * STRIPES * WIDE : (at + 1) * STRIPES * WIDE]
 
 
 def add_spills(n_chan, outs, got, total):
     count = total.shape[0]
     early = lax.broadcasted_iota(jnp.int32, (count, LANES), 1) < SPILL
-
-    def spill(c):
-        return got[c * count : (c + 1) * count, outs:].astype(jnp.float32)
-
-    spills = [spill(c) for c in range(n_chan)]
-    for c in range(n_chan):
-        value = got[c * count : (c + 1) * count, :outs].astype(jnp.float32)
-        parts = [value[:, at : at + LANES] for at in range(0, outs, LANES)]
-        if c > 0:
-            parts[0] = parts[0] + jnp.where(early, spills[c - 1], 0.0)
-        if c < n_chan - 1:
-            parts[-1] = parts[-1] + jnp.where(early, 0.0, spills[c + 1])
-        for at, part in enumerate(parts):
-            total[:, c * outs + at * LANES : c * outs + (at + 1) * LANES] = part
-
-
-def place_kernel(n_chan, n_tgroup, outs, owners, got, *refs):
-    sends, (total, pairs) = refs[:n_tgroup], refs[n_tgroup:]
+    chunks = [lax.axis_index("chan") ^ k for k in range(n_chan)]
+    for chunk, value in zip(chunks, got):
+        at = pl.ds(pl.multiple_of(chunk * outs, LANES), outs)
+        total[:, at] = value[:, :outs].astype(jnp.float32)
+    for chunk, value in zip(chunks, got):
+        spill = value[:, outs:].astype(jnp.float32)
+        after = jnp.minimum(chunk + 1, n_chan - 1) * outs
+        after = pl.ds(pl.multiple_of(after, LANES), LANES)
+        total[:, after] += jnp.where(early & (chunk < n_chan - 1), spill, 0.0)
+        before = jnp.maximum(chunk * outs, LANES) - LANES
+        before = pl.ds(pl.multiple_of(before, LANES), LANES)
+        total[:, before] += jnp.where(early | (chunk == 0), 0.0, spill)
+
+
+def tile_of(group, width, vectors):
+    half = vectors // 2
+    if group == 0:
+        return jnp.where(width == 0, 0, half + 1), half - 1
+    return jnp.where(width == 0, half - 1, 0), half + 1
+
+
+def own_half(n_chan):
+    return jnp.where(lax.axis_index("chan") < n_chan // 2, 0, 1)
+
+
+def place_kernel(n_chan, n_tgroup, outs, group, owners, *refs):
+    got, (total, pairs) = refs[: -n_tgroup - 2], refs[-2:]
+    sends = refs[-n_tgroup - 2 : -2]
     me = lax.axis_index("tgroup")
-    if got.dtype == jnp.float32:
-        total[...] = got[...]
+    if len(got) == 1:
+        total[...] = got[0][...]
     else:
         add_spills(n_chan, outs, got, total)
 
@@ -122,26 +138,31 @@
         counts = counts + (jnp.int32(1) << (3 * owner))
         pairs[lax.rem(owner - me + n_tgroup, n_tgroup) * SLOTS + slot] = q
 
-    half = total.shape[1] // 2
-
-    def folded(q):
-        value = total[pl.ds(pl.multiple_of(q * CB, CB), CB), :]
-        return jnp.concatenate([value[:, :half], value[:, half:]], 0)
-
-    leads = [folded(p * K).astype(jnp.bfloat16) for p in range(STRIPES)]
+    base, per = tile_of(group, own_half(n_chan), total.shape[1] // LANES)
+
+    def tiles(q):
+        rows = pl.ds(pl.multiple_of(q * CB, CB), CB)
+        return [
+            total[rows, pl.ds(pl.multiple_of((base + j) * LANES, LANES), LANES)] for j in range(per)
+        ]
+
+    zero = jnp.zeros((CB, LANES), jnp.float32)
+    leads = sum([tiles(p * K) for p in range(STRIPES)], [])
     for shift in range(n_tgroup):
-        for p in range(STRIPES):
-            sends[shift][p] = leads[p]
+        parts = list(leads)
         for s in range(SLOTS):
             q = pairs[shift * SLOTS + s]
-            value = jnp.where(q >= 0, folded(jnp.maximum(q, 0)), 0.0)
-            sends[shift][STRIPES + s] = value.astype(jnp.bfloat16)
-
-
-def correlate_kernel(factor, last, owners, *refs):
-    lead, window_a, window_b = refs[-3:]
-    out = refs[-4]
-    arrived, before = refs[0], (refs[1] if len(refs) == 6 else None)
+            parts += [jnp.where(q >= 0, tile, 0.0) for tile in tiles(jnp.maximum(q, 0))]
+        parts += [zero] * (len(parts) % 2)
+        for at in range(0, len(parts), 2):
+            value = jnp.concatenate(parts[at : at + 2], 0)
+            sends[shift][at // 2] = value.astype(jnp.bfloat16)
+
+
+def correlate_kernel(n_chan, factor, last, owners, *refs):
+    lead, window_a, window_b, whole = refs[-4:]
+    out = refs[-5]
+    arrived, before = refs[:2], (refs[2] if len(refs) == 8 else None)
     windows = (window_a, window_b)
     span = lead.shape[2]
     samples = span - LANES
@@ -153,9 +174,18 @@
     for q in range(K):
         first_count += jnp.where(owners[q] == me, 1, 0)
 
+    for group in range(2):
+        base, per = tile_of(group, own_half(n_chan), samples // LANES)
+        for at in range(arrived[group].shape[0]):
+            value = arrived[group][at].astype(jnp.float32)
+            for part in range(2):
+                block, j = (2 * at + part) // per, (2 * at + part) % per
+                if block < BLOCKS:
+                    lanes = pl.ds(pl.multiple_of((base + j) * LANES, LANES), LANES)
+                    whole[block, :, lanes] = value[part * CB : (part + 1) * CB]
+
     def series(block):
-        value = arrived[block].astype(jnp.float32)
-        return jnp.concatenate([value[:CB], value[CB:], jnp.zeros((CB, LANES), jnp.float32)], 1)
+        return jnp.concatenate([whole[block], jnp.zeros((CB, LANES), jnp.float32)], 1)
 
     for p in range(STRIPES):
         value = series(p)
@@ -212,15 +242,15 @@
                     out[s, h * STEP + a, :, i * LANES : i * LANES + width] = value[:, :width]
 
 
-def correlate(owners, arrived, before, factor, last, samples):
+def correlate(n_chan, owners, arrived, before, factor, last, samples):
     high, wide = STEP * LAG_BLOCKS * CB, CB * SHIFTS
     if last:
         shape = jax.ShapeDtypeStruct((SLOTS, CB, CB, LAGS), jnp.float32)
     else:
         shape = jax.ShapeDtypeStruct((SLOTS, high, wide), jnp.float32)
-    operands = (owners, arrived) + (() if before is None else (before,))
+    operands = (owners,) + arrived + (() if before is None else (before,))
     return pl.pallas_call(
-        functools.partial(correlate_kernel, factor, last),
+        functools.partial(correlate_kernel, n_chan, factor, last),
         out_shape=shape,
         in_specs=[smem()] + [vmem()] * (len(operands) - 1),
         out_specs=vmem(),
@@ -228,6 +258,7 @@
             pltpu.VMEM((STRIPES, wide, samples + LANES), jnp.bfloat16),
             pltpu.VMEM((high, samples + LANES), jnp.bfloat16),
             pltpu.VMEM((high, samples + LANES), jnp.bfloat16),
+            pltpu.VMEM((BLOCKS, CB, samples), jnp.float32),
         ],
         compiler_params=params(40),
         name="correlate_last" if last else "correlate",
@@ -250,64 +281,66 @@
         tiled=True,
     )
     line = -(-(rows + 2 * outs + 4 * SPILL) // (2 * LANES)) * 2 * LANES
-    sent = pl.pallas_call(
+    sends = pl.pallas_call(
         functools.partial(select_kernel, n_chan),
-        out_shape=jax.ShapeDtypeStruct((n_chan * count, outs + 2 * SPILL), jnp.bfloat16),
-        in_specs=[smem(), pl.BlockSpec(memory_space=pl.ANY), vmem()],
-        out_specs=vmem(),
+        out_shape=(jax.ShapeDtypeStruct((count, outs + 2 * SPILL), jnp.bfloat16),) * n_chan,
+        in_specs=[smem(), pl.BlockSpec(memory_space=pl.ANY), pl.BlockSpec(memory_space=pl.ANY)],
+        out_specs=(vmem(),) * n_chan,
         scratch_shapes=[
             pltpu.VMEM((n_chan * STRIPES, rows, 2 * LANES), jnp.float32),
             pltpu.VMEM((n_chan * count, rows), jnp.bfloat16),
             pltpu.VMEM((8, line), jnp.float32),
+            pltpu.SemaphoreType.DMA,
             pltpu.SemaphoreType.DMA((n_chan * STRIPES,)),
         ],
         compiler_params=params(40),
         name="select_filter",
-    )(firsts, raw_strain, whitening_taps.reshape(1, TAPS))
-
-    got = lax.all_to_all(
-        sent.reshape(n_chan, count, outs + 2 * SPILL),
-        "chan",
-        split_axis=0,
-        concat_axis=0,
-        tiled=True,
-    )
-    if outs % LANES == 0:
-        got = got.reshape(n_chan * count, outs + 2 * SPILL)
-    else:
-        wide = got.astype(jnp.float32)
-        none = jnp.zeros((1, count, outs - SPILL), jnp.float32)
+    )(firsts, raw_strain, jnp.pad(whitening_taps, (0, 1)).reshape(1, TAPS + 1))
+
+    got = [sends[0]]
+    for k in range(1, n_chan):
+        got.append(lax.ppermute(sends[k], "chan", [(c, c ^ k) for c in range(n_chan)]))
+    if outs % LANES:
+        wide = jnp.stack(got).astype(jnp.float32)
+        wide = jnp.take(wide, lax.axis_index("chan") ^ jnp.arange(n_chan), axis=0)
+        none = jnp.zeros((n_chan, count, outs - SPILL), jnp.float32)
         zero = jnp.zeros((1, count, SPILL), jnp.float32)
         right = jnp.concatenate([zero, wide[:-1, :, outs : outs + SPILL]], 0)
         left = jnp.concatenate([wide[1:, :, outs + SPILL :], zero], 0)
-        none = jnp.broadcast_to(none, (n_chan,) + none.shape[1:])
         added = wide[:, :, :outs] + jnp.concatenate([right, none], 2) + jnp.concatenate([none, left], 2)
         got = added.transpose(1, 0, 2).reshape(count, samples)
 
-    packed = jax.ShapeDtypeStruct((BLOCKS, 2 * CB, samples // 2), jnp.bfloat16)
-    sends = pl.pallas_call(
-        functools.partial(place_kernel, n_chan, n_tgroup, outs),
-        out_shape=(packed,) * n_tgroup,
-        in_specs=[smem(), vmem()],
-        out_specs=(vmem(),) * n_tgroup,
-        scratch_shapes=[
-            pltpu.VMEM((count, samples), jnp.float32),
-            pltpu.SMEM((n_tgroup * SLOTS,), jnp.int32),
-        ],
-        compiler_params=params(40),
-        name="place_blocks",
-    )(owners, got)
-
     order = sorted(range(1, n_tgroup), key=lambda s: min(s, n_tgroup - s))
-    arrived = [sends[0]]
-    for shift in order:
-        route = [(g, (g + shift) % n_tgroup) for g in range(n_tgroup)]
-        arrived.append(lax.ppermute(sends[shift], "tgroup", route))
+    arrived = [[] for _ in range(n_tgroup)]
+    for group in range(2):
+        if outs % LANES:
+            use = [got]
+        else:
+            use = got[: n_chan // 2] if group == 0 else got
+        vectors = samples // LANES // 2 + (1 if group else -1)
+        packed = jax.ShapeDtypeStruct((-(-BLOCKS * vectors // 2), 2 * CB, LANES), jnp.bfloat16)
+        sends = pl.pallas_call(
+            functools.partial(place_kernel, n_chan, n_tgroup, outs, group),
+            out_shape=(packed,) * n_tgroup,
+            in_specs=[smem()] + [vmem()] * len(use),
+            out_specs=(vmem(),) * n_tgroup,
+            scratch_shapes=[
+                pltpu.VMEM((count, samples), jnp.float32),
+                pltpu.SMEM((n_tgroup * SLOTS,), jnp.int32),
+            ],
+            compiler_params=params(40),
+            name="place_first" if group == 0 else "place_second",
+        )(owners, *use)
+        arrived[0].append(sends[0])
+        for shift in order:
+            route = [(g, (g + shift) % n_tgroup) for g in range(n_tgroup)]
+            arrived[shift].append(lax.ppermute(sends[shift], "tgroup", route))
 
     value = None
     factor = 1.0 / math.sqrt(samples)
-    for at, block in enumerate(arrived):
-        value = correlate(owners, block, value, factor, at == n_tgroup - 1, samples)
+    for at, shift in enumerate([0] + order):
+        last = at == n_tgroup - 1
+        value = correlate(n_chan, owners, tuple(arrived[shift]), value, factor, last, samples)
     return value
 
 

time: 61.3 us -> 58.7 us (0.958)
  blocking collectives: 24.6 us -> 0 us
  starting transfers between devices: 4.67 us -> 19.3 us
  waiting for transfers between devices: 8.72 us -> 14.6 us
  Pallas kernels: 21.4 us -> 22.6 us
    all_to_all x2 -> x0, blocking collectives: 24.6 us -> none  [the longest x1 15 us: local(): lax.all_to_all(sent.reshape(n_chan, count, outs + 2 * SPILL), 'chan', spl...]
    ppermute x3 -> x13, starting transfers between devices: 4.67 us -> 14.1 us  [the longest x6 9.35 us: local(): arrived[shift].append(lax.ppermute(sends[shift], 'tgroup', route))]
    all_to_all x0 -> x1, starting transfers between devices: none -> 5.17 us  [local(): lax.all_to_all(jnp.broadcast_to(first_block[None, :], (n_chan, STRIPES)),...]
    all_to_all x0 -> x1, waiting for transfers between devices: none -> 3.9 us  [local(): lax.all_to_all(jnp.broadcast_to(first_block[None, :], (n_chan, STRIPES)),...]
    ppermute x3 -> x13, waiting for transfers between devices: 8.72 us -> 10.7 us  [the longest x7 5.39 us: local(): lax.ppermute(sends[k], 'chan', [(c, c ^ k) for c in range(n_chan)])]
    pallas_call x6 -> x7, Pallas kernels: 21.4 us -> 22.6 us  [the longest x4 14.6 us: correlate(): pl.pallas_call(functools.partial(correlate_kernel, n_chan, factor, last),...]
    unnamed x4 -> x2, local copies, waits for them, and re-layouts: 0.69 us -> 0.01 us
    pad x0 -> x1, local copies, waits for them, and re-layouts: none -> 0.68 us  [local(): jnp.pad(whitening_taps, (0, 1)).reshape(1, TAPS + 1)]
  transfers between devices with their start and end apart: 3 -> 14, of which waited for: 2 -> 5; matrix products, arithmetic and copies ran while one was open for 0% -> 1% of each run, Pallas kernels for 16% -> 20%
where the time goes in v3:
time: 58.7 us; the launch traced here: 58.5 us
  Pallas kernels  22.6 us (39%)
  starting transfers between devices  19.3 us (33%)
  waiting for transfers between devices  14.6 us (25%)
  local copies, waits for them, and re-layouts  1.93 us (3%)
    pallas_call x4, Pallas kernels, correlate(): pl.pallas_call(functools.partial(correlate_kernel, n_chan, factor, last),...  14.6 us
    ppermute x6, starting transfers between devices, local(): arrived[shift].append(lax.ppermute(sends[shift], 'tgroup', route))  9.35 us
    pallas_call x1, Pallas kernels, local(): pl.pallas_call(functools.partial(select_kernel, n_chan), out_shape=(jax.S...  5.95 us
    ppermute x7, waiting for transfers between devices, local(): lax.ppermute(sends[k], 'chan', [(c, c ^ k) for c in range(n_chan)])  5.39 us
    ppermute x6, waiting for transfers between devices, local(): arrived[shift].append(lax.ppermute(sends[shift], 'tgroup', route))  5.35 us
    all_to_all x1, starting transfers between devices, local(): lax.all_to_all(jnp.broadcast_to(first_block[None, :], (n_chan, STRIPES)),...  5.17 us
    ppermute x7, starting transfers between devices, local(): lax.ppermute(sends[k], 'chan', [(c, c ^ k) for c in range(n_chan)])  4.79 us
    all_to_all x1, waiting for transfers between devices, local(): lax.all_to_all(jnp.broadcast_to(first_block[None, :], (n_chan, STRIPES)),...  3.9 us
  transfers between devices with their start and end apart: 14, of which 5 were waited for; matrix products, arithmetic and copies ran while one was open for 1% of the time, Pallas kernels for 20%

profile of v3, /device:TPU:0, one launch (start us, length us, event | category | flops | bytes accessed | tf_op | source)
XLA Modules:
  0.0 58.5 jit_solution(4829177841137621616)
XLA Ops:
  0.0 1.2 %broadcast_in_dim.2 = s32[8,1,2]{2,1,0:T(1,128)} broadcast(s32[2]{0:T(128)} %param.6), dimensions={2} | broadcast | bytes 72 | tf_op jit(solution)/shard_map/broadcast_in_dim | solution.py:277
  1.2 5.2 %all-to-all-start = ((s32[8,1,2]{2,1,0:T(1,128)}), s32[8,1,2]{2,1,0:T(1,128)S(1)}, u32[]{:S(2)}, u32[]{:S(2)}) async-start(s32[8,1,2]{2,1,0:T(1,128)} %broadcast_in_dim.2), calls=%async_computation | async-start | bytes 8192 | tf_op jit(solution)/shard_map/all_to_all | solution.py:276
  6.4 0.7 %pad.4 = f32[256]{0:T(256)S(1)} pad(f32[255]{0:T(256)} %param.5, f32[]{:T(128)} %constant.2.clone.1), padding=0_1 | pad | bytes 2048 | tf_op jit(solution)/shard_map/jit(_pad)/pad | solution.py:298
  7.1 3.9 %all-to-all-done = s32[8,1,2]{2,1,0:T(1,128)S(1)} async-done(((s32[8,1,2]{2,1,0:T(1,128)}), s32[8,1,2]{2,1,0:T(1,128)S(1)}, u32[]{:S(2)}, u32[]{:S(2)}) %all-to-all-start) | async-done | bytes 96 | tf_op jit(solution)/shard_map/all_to_all | solution.py:276
  11.0 0.0 copy-start
  11.0 6.0 %select_filter.1 = (bf16[128,384]{1,0:T(8,128)(2,1)S(1)}, bf16[128,384]{1,0:T(8,128)(2,1)S(1)}, bf16[128,384]{1,0:T(8,128)(2,1)S(1)}, bf16[128,384]{1,0:T(8,128)...) custom-call(s32[8,2]{1,0:T(8,128)S(1)} %bitcast.9, ...), custom_call_target="tpu_custom_call" | custom-call | tf_op jit(solution)/shard_map/select_filter/pallas_call | solution.py:284
  17.0 0.1 collective-permute-start
  17.0 0.6 %collective-permute-start.1 = (bf16[128,384]{1,0:T(8,128)(2,1)S(1)}, bf16[128,384]{1,0:T(8,128)(2,1)S(1)}, u32[]{:S(2)}, u32[]{:S(2)}) collective-permute-start(bf16[128,384]{1,0:T(8,128)(2,1)S(1)} %get-tuple-element.23), channel_id=1, source_target_pairs={{0,2},{1,3},{2,0},{3,1},{4,6},{5,7},{6,4},{7,5},{8,10},{9,11},{10,... | collective-permute-start | bytes 294920 | tf_op jit(solution)/shard_map/ppermute | solution.py:302
  17.7 1.2 %collective-permute-start.2 = (bf16[128,384]{1,0:T(8,128)(2,1)S(1)}, bf16[128,384]{1,0:T(8,128)(2,1)S(1)}, u32[]{:S(2)}, u32[]{:S(2)}) collective-permute-start(bf16[128,384]{1,0:T(8,128)(2,1)S(1)} %get-tuple-element.24), channel_id=1, source_target_pairs={{0,3},{1,2},{2,1},{3,0},{4,7},{5,6},{6,5},{7,4},{8,11},{9,10},{10,... | collective-permute-start | bytes 294920 | tf_op jit(solution)/shard_map/ppermute | solution.py:302
  18.9 0.6 collective-permute-start.4
  19.5 1.1 %collective-permute-start.5 = (bf16[128,384]{1,0:T(8,128)(2,1)S(1)}, bf16[128,384]{1,0:T(8,128)(2,1)S(1)}, u32[]{:S(2)}, u32[]{:S(2)}) collective-permute-start(bf16[128,384]{1,0:T(8,128)(2,1)S(1)} %get-tuple-element.27), channel_id=1, source_target_pairs={{0,5},{1,4},{2,7},{3,6},{4,1},{5,0},{6,3},{7,2},{8,13},{9,12},{10,... | collective-permute-start | bytes 294920 | tf_op jit(solution)/shard_map/ppermute | solution.py:302
  20.6 0.0 collective-permute-done.refs_1_
  20.6 0.6 collective-permute-start.6
  21.2 1.5 %collective-permute-done.1.refs_2_ = bf16[128,384]{1,0:T(8,128)(2,1)S(1)} collective-permute-done((bf16[128,384]{1,0:T(8,128)(2,1)S(1)}, bf16[128,384]{1,0:T(8,128)(2,1)S(1)}, u32[]{:S(2)}, u32[]{:S(2)}) %collective-permute-start.1) | collective-permute-done | bytes 98336 | tf_op jit(solution)/shard_map/ppermute | solution.py:302
  22.7 0.6 %collective-permute-start.7 = (bf16[128,384]{1,0:T(8,128)(2,1)S(1)}, bf16[128,384]{1,0:T(8,128)(2,1)S(1)}, u32[]{:S(2)}, u32[]{:S(2)}) collective-permute-start(bf16[128,384]{1,0:T(8,128)(2,1)S(1)} %get-tuple-element.29), channel_id=1, source_target_pairs={{0,7},{1,6},{2,5},{3,4},{4,3},{5,2},{6,1},{7,0},{8,15},{9,14},{10,... | collective-permute-start | bytes 294920 | tf_op jit(solution)/shard_map/ppermute | solution.py:302
  23.3 0.6 %collective-permute-done.2.refs_3_ = bf16[128,384]{1,0:T(8,128)(2,1)S(1)} collective-permute-done((bf16[128,384]{1,0:T(8,128)(2,1)S(1)}, bf16[128,384]{1,0:T(8,128)(2,1)S(1)}, u32[]{:S(2)}, u32[]{:S(2)}) %collective-permute-start.2) | collective-permute-done | bytes 98336 | tf_op jit(solution)/shard_map/ppermute | solution.py:302
  23.9 0.0 copy-done
  23.9 0.9 %place_first.1 = (bf16[25,16,128]{2,1,0:T(8,128)(2,1)S(1)}, bf16[25,16,128]{2,1,0:T(8,128)(2,1)S(1)}, bf16[25,16,128]{2,1,0:T(8,128)(2,1)S(1)}, bf16[25,16,128]{2,1,0:T(8,128)(2,1)S(1)}) custom-call(s32[16]{0:T(128)S(1)} %bitcast.3, bf16[128,384]{1,0:T(8,128)(2,1)S(1)} %get-tuple-element.21.refs_0_, bf16[128,384]{1,0:T(8,128)(2,1)S(1)} %collective-permute-done.refs_1_, ...), custom_call_target="tpu_custom_call" | custom-call | tf_op jit(solution)/shard_map/place_first/pallas_call | solution.py:322
  24.8 1.6 %collective-permute-start.11 = (bf16[25,16,128]{2,1,0:T(8,128)(2,1)S(1)}, bf16[25,16,128]{2,1,0:T(8,128)(2,1)S(1)}, u32[]{:S(2)}, u32[]{:S(2)}) collective-permute-start(bf16[25,16,128]{2,1,0:T(8,128)(2,1)S(1)} %get-tuple-element.33), channel_id=1, source_target_pairs={{0,8},{8,16},{16,24},{24,0},{1,9},{9,17},{17,25},{25,1},{2,10},{10... | collective-permute-start | bytes 307208 | tf_op jit(solution)/shard_map/ppermute | solution.py:337
  26.5 0.0 collective-permute-done.4.refs_4_
  26.5 3.2 %collective-permute-done.5.refs_5_ = bf16[128,384]{1,0:T(8,128)(2,1)S(1)} collective-permute-done((bf16[128,384]{1,0:T(8,128)(2,1)S(1)}, bf16[128,384]{1,0:T(8,128)(2,1)S(1)}, u32[]{:S(2)}, u32[]{:S(2)}) %collective-permute-start.5) | collective-permute-done | bytes 98336 | tf_op jit(solution)/shard_map/ppermute | solution.py:302
  29.7 0.0 collective-permute-done.6.refs_6_
  29.7 0.0 collective-permute-done.7.refs_7_
  29.7 1.1 %place_second.1 = (bf16[32,16,128]{2,1,0:T(8,128)(2,1)S(1)}, bf16[32,16,128]{2,1,0:T(8,128)(2,1)S(1)}, bf16[32,16,128]{2,1,0:T(8,128)(2,1)S(1)}, bf16[32,16,128]{2,1,0:T(8,128)(2,1)S(1)}) custom-call(s32[16]{0:T(128)S(1)} %bitcast.4, bf16[128,384]{1,0:T(8,128)(2,1)S(1)} %get-tuple-element.21.refs_0_, bf16[128,384]{1,0:T(8,128)(2,1)S(1)} %collective-permute-done.refs_1_, ...), custom_call_target="tpu_custom_call" | custom-call | tf_op jit(solution)/shard_map/place_second/pallas_call | solution.py:322
  30.8 1.6 %collective-permute-start.12 = (bf16[32,16,128]{2,1,0:T(8,128)(2,1)S(1)}, bf16[32,16,128]{2,1,0:T(8,128)(2,1)S(1)}, u32[]{:S(2)}, u32[]{:S(2)}) collective-permute-start(bf16[32,16,128]{2,1,0:T(8,128)(2,1)S(1)} %get-tuple-element.34), channel_id=1, source_target_pairs={{0,8},{8,16},{16,24},{24,0},{1,9},{9,17},{17,25},{25,1},{2,10},{10... | collective-permute-start | bytes 393224 | tf_op jit(solution)/shard_map/ppermute | solution.py:337
  32.4 2.2 %collective-permute-start.10 = (bf16[32,16,128]{2,1,0:T(8,128)(2,1)S(1)}, bf16[32,16,128]{2,1,0:T(8,128)(2,1)S(1)}, u32[]{:S(2)}, u32[]{:S(2)}) collective-permute-start(bf16[32,16,128]{2,1,0:T(8,128)(2,1)S(1)} %get-tuple-element.32), channel_id=1, source_target_pairs={{0,24},{8,0},{16,8},{24,16},{1,25},{9,1},{17,9},{25,17},{2,26},{10... | collective-permute-start | bytes 393224 | tf_op jit(solution)/shard_map/ppermute | solution.py:337
  34.7 0.8 %collective-permute-start.8 = (bf16[32,16,128]{2,1,0:T(8,128)(2,1)S(1)}, bf16[32,16,128]{2,1,0:T(8,128)(2,1)S(1)}, u32[]{:S(2)}, u32[]{:S(2)}) collective-permute-start(bf16[32,16,128]{2,1,0:T(8,128)(2,1)S(1)} %get-tuple-element.30), channel_id=1, source_target_pairs={{0,16},{8,24},{16,0},{24,8},{1,17},{9,25},{17,1},{25,9},{2,18},{10... | collective-permute-start | bytes 393224 | tf_op jit(solution)/shard_map/ppermute | solution.py:337
  35.4 1.3 %collective-permute-start.9 = (bf16[25,16,128]{2,1,0:T(8,128)(2,1)S(1)}, bf16[25,16,128]{2,1,0:T(8,128)(2,1)S(1)}, u32[]{:S(2)}, u32[]{:S(2)}) collective-permute-start(bf16[25,16,128]{2,1,0:T(8,128)(2,1)S(1)} %get-tuple-element.31), channel_id=1, source_target_pairs={{0,24},{8,0},{16,8},{24,16},{1,25},{9,1},{17,9},{25,17},{2,26},{10... | collective-permute-start | bytes 307208 | tf_op jit(solution)/shard_map/ppermute | solution.py:337
  36.8 0.0 collective-permute-done.11.refs_0_
  36.8 1.7 %collective-permute-start.3 = (bf16[25,16,128]{2,1,0:T(8,128)(2,1)S(1)}, bf16[25,16,128]{2,1,0:T(8,128)(2,1)S(1)}, u32[]{:S(2)}, u32[]{:S(2)}) collective-permute-start(bf16[25,16,128]{2,1,0:T(8,128)(2,1)S(1)} %get-tuple-element.25), channel_id=1, source_target_pairs={{0,16},{8,24},{16,0},{24,8},{1,17},{9,25},{17,1},{25,9},{2,18},{10... | collective-permute-start | bytes 307208 | tf_op jit(solution)/shard_map/ppermute | solution.py:337
  38.5 3.3 %correlate.3.refs_2_ = f32[5,256,256]{2,1,0:T(8,128)S(1)} custom-call(s32[16]{0:T(128)S(1)} %bitcast.5, bf16[25,16,128]{2,1,0:T(8,128)(2,1)S(1)} %get-tuple-element.35.refs_0_, bf16[32,16,128]{2,1,0:T(8,128)(2,1)S(1)} %get-tuple-element.36.refs_1_), custom_call_target="tpu_custom_call" | custom-call | tf_op jit(solution)/shard_map/correlate/pallas_call | solution.py:252
  41.8 0.0 collective-permute-done.12.refs_1_
  41.8 3.3 %correlate.4.refs_2_ = f32[5,256,256]{2,1,0:T(8,128)S(1)} custom-call(s32[16]{0:T(128)S(1)} %bitcast.6, bf16[25,16,128]{2,1,0:T(8,128)(2,1)S(1)} %collective-permute-done.11.refs_0_, bf16[32,16,128]{2,1,0:T(8,128)(2,1)S(1)} %collective-permute-done.12.refs_1_, f32[5,256,256]{2,1,0:T(8,128)S(1)} %correlate.3.refs_2_), custom_call_target="tpu_custom_call" | custom-call | tf_op jit(solution)/shard_map/correlate/pallas_call | solution.py:252
  45.1 0.0 collective-permute-done.9.refs_0_
  45.1 0.0 collective-permute-done.10.refs_1_
  45.1 3.3 %correlate.5.refs_2_ = f32[5,256,256]{2,1,0:T(8,128)S(1)} custom-call(s32[16]{0:T(128)S(1)} %bitcast.7, bf16[25,16,128]{2,1,0:T(8,128)(2,1)S(1)} %collective-permute-done.9.refs_0_, bf16[32,16,128]{2,1,0:T(8,128)(2,1)S(1)} %collective-permute-done.10.refs_1_, f32[5,256,256]{2,1,0:T(8,128)S(1)} %correlate.4.refs_2_), custom_call_target="tpu_custom_call" | custom-call | tf_op jit(solution)/shard_map/correlate/pallas_call | solution.py:252
  48.5 5.3 %collective-permute-done.3.refs_0_ = bf16[25,16,128]{2,1,0:T(8,128)(2,1)S(1)} collective-permute-done((bf16[25,16,128]{2,1,0:T(8,128)(2,1)S(1)}, bf16[25,16,128]{2,1,0:T(8,128)(2,1)S(1)}, u32[]{:S(2)}, u32[]{:S(2)}) %collective-permute-start.3) | collective-permute-done | bytes 102432 | tf_op jit(solution)/shard_map/ppermute | solution.py:337
  53.8 0.0 collective-permute-done.8.refs_1_
  53.8 4.7 %correlate_last.1 = f32[5,8,8,1001]{3,2,1,0:T(8,128)} custom-call(s32[16]{0:T(128)S(1)} %bitcast.8, bf16[25,16,128]{2,1,0:T(8,128)(2,1)S(1)} %collective-permute-done.3.refs_0_, bf16[32,16,128]{2,1,0:T(8,128)(2,1)S(1)} %collective-permute-done.8.refs_1_, f32[5,256,256]{2,1,0:T(8,128)S(1)} %correlate.5.refs_2_), custom_call_target="tpu_custom_call" | custom-call | tf_op jit(solution)/shard_map/correlate_last/pallas_call | solution.py:252
Async XLA Ops:
  1.2 9.8 %all-to-all-start = ((s32[8,1,2]{2,1,0:T(1,128)}), s32[8,1,2]{2,1,0:T(1,128)S(1)}, u32[]{:S(2)}, u32[]{:S(2)}) async-start(s32[8,1,2]{2,1,0:T(1,128)} %broadcast_in_dim.2), calls=%async_computation | async-start | bytes 8192 | tf_op jit(solution)/shard_map/all_to_all | solution.py:276
  11.0 12.9 %copy-start = (s32[16,1]{0,1:T(1,128)S(1)}, s32[16,1]{0,1:T(1,128)}, u32[]{:S(2)}) copy-start(s32[16,1]{0,1:T(1,128)} %param.7) | copy-start | bytes 196
  17.0 3.6 %collective-permute-start = (bf16[128,384]{1,0:T(8,128)(2,1)S(1)}, bf16[128,384]{1,0:T(8,128)(2,1)S(1)}, u32[]{:S(2)}, u32[]{:S(2)}) collective-permute-start(bf16[128,384]{1,0:T(8,128)(2,1)S(1)} %get-tuple-element.22), channel_id=1, source_target_pairs={{0,1},{1,0},{2,3},{3,2},{4,5},{5,4},{6,7},{7,6},{8,9},{9,8},{10,11... | collective-permute-start | bytes 294920 | tf_op jit(solution)/shard_map/ppermute | solution.py:302
  17.0 5.7 %collective-permute-start.1 = (bf16[128,384]{1,0:T(8,128)(2,1)S(1)}, bf16[128,384]{1,0:T(8,128)(2,1)S(1)}, u32[]{:S(2)}, u32[]{:S(2)}) collective-permute-start(bf16[128,384]{1,0:T(8,128)(2,1)S(1)} %get-tuple-element.23), channel_id=1, source_target_pairs={{0,2},{1,3},{2,0},{3,1},{4,6},{5,7},{6,4},{7,5},{8,10},{9,11},{10,... | collective-permute-start | bytes 294920 | tf_op jit(solution)/shard_map/ppermute | solution.py:302
  17.7 6.2 %collective-permute-start.2 = (bf16[128,384]{1,0:T(8,128)(2,1)S(1)}, bf16[128,384]{1,0:T(8,128)(2,1)S(1)}, u32[]{:S(2)}, u32[]{:S(2)}) collective-permute-start(bf16[128,384]{1,0:T(8,128)(2,1)S(1)} %get-tuple-element.24), channel_id=1, source_target_pairs={{0,3},{1,2},{2,1},{3,0},{4,7},{5,6},{6,5},{7,4},{8,11},{9,10},{10,... | collective-permute-start | bytes 294920 | tf_op jit(solution)/shard_map/ppermute | solution.py:302
  18.9 7.5 %collective-permute-start.4 = (bf16[128,384]{1,0:T(8,128)(2,1)S(1)}, bf16[128,384]{1,0:T(8,128)(2,1)S(1)}, u32[]{:S(2)}, u32[]{:S(2)}) collective-permute-start(bf16[128,384]{1,0:T(8,128)(2,1)S(1)} %get-tuple-element.26), channel_id=1, source_target_pairs={{0,4},{1,5},{2,6},{3,7},{4,0},{5,1},{6,2},{7,3},{8,12},{9,13},{10,... | collective-permute-start | bytes 294920 | tf_op jit(solution)/shard_map/ppermute | solution.py:302
  19.5 10.2 %collective-permute-start.5 = (bf16[128,384]{1,0:T(8,128)(2,1)S(1)}, bf16[128,384]{1,0:T(8,128)(2,1)S(1)}, u32[]{:S(2)}, u32[]{:S(2)}) collective-permute-start(bf16[128,384]{1,0:T(8,128)(2,1)S(1)} %get-tuple-element.27), channel_id=1, source_target_pairs={{0,5},{1,4},{2,7},{3,6},{4,1},{5,0},{6,3},{7,2},{8,13},{9,12},{10,... | collective-permute-start | bytes 294920 | tf_op jit(solution)/shard_map/ppermute | solution.py:302
  20.6 9.1 %collective-permute-start.6 = (bf16[128,384]{1,0:T(8,128)(2,1)S(1)}, bf16[128,384]{1,0:T(8,128)(2,1)S(1)}, u32[]{:S(2)}, u32[]{:S(2)}) collective-permute-start(bf16[128,384]{1,0:T(8,128)(2,1)S(1)} %get-tuple-element.28), channel_id=1, source_target_pairs={{0,6},{1,7},{2,4},{3,5},{4,2},{5,3},{6,0},{7,1},{8,14},{9,15},{10,... | collective-permute-start | bytes 294920 | tf_op jit(solution)/shard_map/ppermute | solution.py:302
  22.7 7.0 %collective-permute-start.7 = (bf16[128,384]{1,0:T(8,128)(2,1)S(1)}, bf16[128,384]{1,0:T(8,128)(2,1)S(1)}, u32[]{:S(2)}, u32[]{:S(2)}) collective-permute-start(bf16[128,384]{1,0:T(8,128)(2,1)S(1)} %get-tuple-element.29), channel_id=1, source_target_pairs={{0,7},{1,6},{2,5},{3,4},{4,3},{5,2},{6,1},{7,0},{8,15},{9,14},{10,... | collective-permute-start | bytes 294920 | tf_op jit(solution)/shard_map/ppermute | solution.py:302
  24.8 12.0 %collective-permute-start.11 = (bf16[25,16,128]{2,1,0:T(8,128)(2,1)S(1)}, bf16[25,16,128]{2,1,0:T(8,128)(2,1)S(1)}, u32[]{:S(2)}, u32[]{:S(2)}) collective-permute-start(bf16[25,16,128]{2,1,0:T(8,128)(2,1)S(1)} %get-tuple-element.33), channel_id=1, source_target_pairs={{0,8},{8,16},{16,24},{24,0},{1,9},{9,17},{17,25},{25,1},{2,10},{10... | collective-permute-start | bytes 307208 | tf_op jit(solution)/shard_map/ppermute | solution.py:337
  30.8 11.0 %collective-permute-start.12 = (bf16[32,16,128]{2,1,0:T(8,128)(2,1)S(1)}, bf16[32,16,128]{2,1,0:T(8,128)(2,1)S(1)}, u32[]{:S(2)}, u32[]{:S(2)}) collective-permute-start(bf16[32,16,128]{2,1,0:T(8,128)(2,1)S(1)} %get-tuple-element.34), channel_id=1, source_target_pairs={{0,8},{8,16},{16,24},{24,0},{1,9},{9,17},{17,25},{25,1},{2,10},{10... | collective-permute-start | bytes 393224 | tf_op jit(solution)/shard_map/ppermute | solution.py:337
  32.4 12.7 %collective-permute-start.10 = (bf16[32,16,128]{2,1,0:T(8,128)(2,1)S(1)}, bf16[32,16,128]{2,1,0:T(8,128)(2,1)S(1)}, u32[]{:S(2)}, u32[]{:S(2)}) collective-permute-start(bf16[32,16,128]{2,1,0:T(8,128)(2,1)S(1)} %get-tuple-element.32), channel_id=1, source_target_pairs={{0,24},{8,0},{16,8},{24,16},{1,25},{9,1},{17,9},{25,17},{2,26},{10... | collective-permute-start | bytes 393224 | tf_op jit(solution)/shard_map/ppermute | solution.py:337
  34.7 19.1 %collective-permute-start.8 = (bf16[32,16,128]{2,1,0:T(8,128)(2,1)S(1)}, bf16[32,16,128]{2,1,0:T(8,128)(2,1)S(1)}, u32[]{:S(2)}, u32[]{:S(2)}) collective-permute-start(bf16[32,16,128]{2,1,0:T(8,128)(2,1)S(1)} %get-tuple-element.30), channel_id=1, source_target_pairs={{0,16},{8,24},{16,0},{24,8},{1,17},{9,25},{17,1},{25,9},{2,18},{10... | collective-permute-start | bytes 393224 | tf_op jit(solution)/shard_map/ppermute | solution.py:337
  35.4 9.7 %collective-permute-start.9 = (bf16[25,16,128]{2,1,0:T(8,128)(2,1)S(1)}, bf16[25,16,128]{2,1,0:T(8,128)(2,1)S(1)}, u32[]{:S(2)}, u32[]{:S(2)}) collective-permute-start(bf16[25,16,128]{2,1,0:T(8,128)(2,1)S(1)} %get-tuple-element.31), channel_id=1, source_target_pairs={{0,24},{8,0},{16,8},{24,16},{1,25},{9,1},{17,9},{25,17},{2,26},{10... | collective-permute-start | bytes 307208 | tf_op jit(solution)/shard_map/ppermute | solution.py:337
  36.8 17.0 %collective-permute-start.3 = (bf16[25,16,128]{2,1,0:T(8,128)(2,1)S(1)}, bf16[25,16,128]{2,1,0:T(8,128)(2,1)S(1)}, u32[]{:S(2)}, u32[]{:S(2)}) collective-permute-start(bf16[25,16,128]{2,1,0:T(8,128)(2,1)S(1)} %get-tuple-element.25), channel_id=1, source_target_pairs={{0,16},{8,24},{16,0},{24,8},{1,17},{9,25},{17,1},{25,9},{2,18},{10... | collective-permute-start | bytes 307208 | tf_op jit(solution)/shard_map/ppermute | solution.py:337

commit v4 on v3

--- a/solution.py
+++ b/solution.py
@@ -121,9 +121,12 @@
 
 
 def place_kernel(n_chan, n_tgroup, outs, group, owners, *refs):
-    got, (total, pairs) = refs[: -n_tgroup - 2], refs[-2:]
-    sends = refs[-n_tgroup - 2 : -2]
-    me = lax.axis_index("tgroup")
+    total, pairs = refs[-2:]
+    if group == 0:
+        got, sends, me = refs[:-3], refs[-3], 0
+    else:
+        got, sends = refs[: -n_tgroup - 2], refs[-n_tgroup - 2 : -2]
+        me = lax.axis_index("tgroup")
     if len(got) == 1:
         total[...] = got[0][...]
     else:
@@ -156,10 +159,13 @@
         parts += [zero] * (len(parts) % 2)
         for at in range(0, len(parts), 2):
             value = jnp.concatenate(parts[at : at + 2], 0)
-            sends[shift][at // 2] = value.astype(jnp.bfloat16)
-
-
-def correlate_kernel(n_chan, factor, last, owners, *refs):
+            if group == 0:
+                sends[shift, at // 2] = value.astype(jnp.bfloat16)
+            else:
+                sends[shift][at // 2] = value.astype(jnp.bfloat16)
+
+
+def correlate_kernel(n_chan, n_tgroup, shift, factor, last, owners, *refs):
     lead, window_a, window_b, whole = refs[-4:]
     out = refs[-5]
     arrived, before = refs[:2], (refs[2] if len(refs) == 8 else None)
@@ -174,10 +180,12 @@
     for q in range(K):
         first_count += jnp.where(owners[q] == me, 1, 0)
 
+    source = lax.rem(lax.axis_index("tgroup") + n_tgroup - shift, n_tgroup)
     for group in range(2):
         base, per = tile_of(group, own_half(n_chan), samples // LANES)
-        for at in range(arrived[group].shape[0]):
-            value = arrived[group][at].astype(jnp.float32)
+        for at in range(arrived[group].shape[-3]):
+            value = arrived[0][source, at] if group == 0 else arrived[1][at]
+            value = value.astype(jnp.float32)
             for part in range(2):
                 block, j = (2 * at + part) // per, (2 * at + part) % per
                 if block < BLOCKS:
@@ -242,7 +250,7 @@
                     out[s, h * STEP + a, :, i * LANES : i * LANES + width] = value[:, :width]
 
 
-def correlate(n_chan, owners, arrived, before, factor, last, samples):
+def correlate(n_chan, n_tgroup, shift, owners, arrived, before, factor, last, samples):
     high, wide = STEP * LAG_BLOCKS * CB, CB * SHIFTS
     if last:
         shape = jax.ShapeDtypeStruct((SLOTS, CB, CB, LAGS), jnp.float32)
@@ -250,7 +258,7 @@
         shape = jax.ShapeDtypeStruct((SLOTS, high, wide), jnp.float32)
     operands = (owners,) + arrived + (() if before is None else (before,))
     return pl.pallas_call(
-        functools.partial(correlate_kernel, n_chan, factor, last),
+        functools.partial(correlate_kernel, n_chan, n_tgroup, shift, factor, last),
         out_shape=shape,
         in_specs=[smem()] + [vmem()] * (len(operands) - 1),
         out_specs=vmem(),
@@ -311,19 +319,22 @@
         got = added.transpose(1, 0, 2).reshape(count, samples)
 
     order = sorted(range(1, n_tgroup), key=lambda s: min(s, n_tgroup - s))
-    arrived = [[] for _ in range(n_tgroup)]
     for group in range(2):
         if outs % LANES:
             use = [got]
         else:
             use = got[: n_chan // 2] if group == 0 else got
         vectors = samples // LANES // 2 + (1 if group else -1)
-        packed = jax.ShapeDtypeStruct((-(-BLOCKS * vectors // 2), 2 * CB, LANES), jnp.bfloat16)
+        shape = (-(-BLOCKS * vectors // 2), 2 * CB, LANES)
+        if group == 0:
+            packed, specs = jax.ShapeDtypeStruct((n_tgroup,) + shape, jnp.bfloat16), vmem()
+        else:
+            packed, specs = (jax.ShapeDtypeStruct(shape, jnp.bfloat16),) * n_tgroup, (vmem(),) * n_tgroup
         sends = pl.pallas_call(
             functools.partial(place_kernel, n_chan, n_tgroup, outs, group),
-            out_shape=(packed,) * n_tgroup,
+            out_shape=packed,
             in_specs=[smem()] + [vmem()] * len(use),
-            out_specs=(vmem(),) * n_tgroup,
+            out_specs=specs,
             scratch_shapes=[
                 pltpu.VMEM((count, samples), jnp.float32),
                 pltpu.SMEM((n_tgroup * SLOTS,), jnp.int32),
@@ -331,6 +342,10 @@
             compiler_params=params(40),
             name="place_first" if group == 0 else "place_second",
         )(owners, *use)
+        if group == 0:
+            moved = lax.all_to_all(sends, "tgroup", split_axis=0, concat_axis=0, tiled=True)
+            arrived = [[sends]] + [[moved] for _ in order]
+            continue
         arrived[0].append(sends[0])
         for shift in order:
             route = [(g, (g + shift) % n_tgroup) for g in range(n_tgroup)]
@@ -340,7 +355,8 @@
     factor = 1.0 / math.sqrt(samples)
     for at, shift in enumerate([0] + order):
         last = at == n_tgroup - 1
-        value = correlate(n_chan, owners, tuple(arrived[shift]), value, factor, last, samples)
+        operands = (owners, tuple(arrived[shift]), value)
+        value = correlate(n_chan, n_tgroup, shift, *operands, factor, last, samples)
     return value
 
 

time: 58.7 us -> 64 us (1.090); the launches traced: 58.5 us -> 62.9 us
  starting transfers between devices: 19.3 us -> 21.2 us
  waiting for transfers between devices: 14.6 us -> 16 us
  Pallas kernels: 22.6 us -> 23.7 us
    ppermute x7, waiting for transfers between devices: 5.39 us -> 10.7 us  [local(): lax.ppermute(sends[k], 'chan', [(c, c ^ k) for c in range(n_chan)])]
    all_to_all x0 -> x1, starting transfers between devices: none -> 4.88 us  [local(): lax.all_to_all(sends, 'tgroup', split_axis=0, concat_axis=0, tiled=True)]
    ppermute x6 -> x3, starting transfers between devices: 9.35 us -> 4.82 us  [local(): arrived[shift].append(lax.ppermute(sends[shift], 'tgroup', route))]
    ppermute x6 -> x3, waiting for transfers between devices: 5.35 us -> 1.4 us  [local(): arrived[shift].append(lax.ppermute(sends[shift], 'tgroup', route))]
    ppermute x7, starting transfers between devices: 4.79 us -> 6.32 us  [local(): lax.ppermute(sends[k], 'chan', [(c, c ^ k) for c in range(n_chan)])]
    pallas_call x2, Pallas kernels: 1.95 us -> 2.69 us  [local(): pl.pallas_call(functools.partial(place_kernel, n_chan, n_tgroup, outs, gr...]
  transfers between devices with their start and end apart: 14 -> 12, of which waited for: 5 -> 6; matrix products, arithmetic and copies ran while one was open for 1% -> 1% of each run, Pallas kernels for 20% -> 18%
where the time goes in v4:
time: 64 us; the launch traced here: 62.9 us
  Pallas kernels  23.7 us (37%)
  starting transfers between devices  21.2 us (33%)
  waiting for transfers between devices  16 us (25%)
  local copies, waits for them, and re-layouts  1.93 us (3%)
    pallas_call x4, Pallas kernels, correlate(): pl.pallas_call(functools.partial(correlate_kernel, n_chan, n_tgroup, shif...  15.1 us
    ppermute x7, waiting for transfers between devices, local(): lax.ppermute(sends[k], 'chan', [(c, c ^ k) for c in range(n_chan)])  10.7 us
    ppermute x7, starting transfers between devices, local(): lax.ppermute(sends[k], 'chan', [(c, c ^ k) for c in range(n_chan)])  6.32 us
    pallas_call x1, Pallas kernels, local(): pl.pallas_call(functools.partial(select_kernel, n_chan), out_shape=(jax.S...  5.95 us
    all_to_all x1, starting transfers between devices, local(): lax.all_to_all(jnp.broadcast_to(first_block[None, :], (n_chan, STRIPES)),...  5.17 us
    all_to_all x1, starting transfers between devices, local(): lax.all_to_all(sends, 'tgroup', split_axis=0, concat_axis=0, tiled=True)  4.88 us
    ppermute x3, starting transfers between devices, local(): arrived[shift].append(lax.ppermute(sends[shift], 'tgroup', route))  4.82 us
    all_to_all x1, waiting for transfers between devices, local(): lax.all_to_all(jnp.broadcast_to(first_block[None, :], (n_chan, STRIPES)),...  3.9 us
  transfers between devices with their start and end apart: 12, of which 6 were waited for; matrix products, arithmetic and copies ran while one was open for 1% of the time, Pallas kernels for 18%

profile of v4, /device:TPU:0, one launch (start us, length us, event | category | flops | bytes accessed | tf_op | source)
XLA Modules:
  0.0 62.9 jit_solution(5939934837543398056)
XLA Ops:
  0.0 1.2 %broadcast_in_dim.2 = s32[8,1,2]{2,1,0:T(1,128)} broadcast(s32[2]{0:T(128)} %param.6), dimensions={2} | broadcast | bytes 72 | tf_op jit(solution)/shard_map/broadcast_in_dim | solution.py:285
  1.2 5.2 %all-to-all-start = ((s32[8,1,2]{2,1,0:T(1,128)}), s32[8,1,2]{2,1,0:T(1,128)S(1)}, u32[]{:S(2)}, u32[]{:S(2)}) async-start(s32[8,1,2]{2,1,0:T(1,128)} %broadcast_in_dim.2), calls=%async_computation | async-start | bytes 8192 | tf_op jit(solution)/shard_map/all_to_all | solution.py:284
  6.4 0.7 %pad.4 = f32[256]{0:T(256)S(1)} pad(f32[255]{0:T(256)} %param.5, f32[]{:T(128)} %constant.2.clone.1), padding=0_1 | pad | bytes 2048 | tf_op jit(solution)/shard_map/jit(_pad)/pad | solution.py:306
  7.1 3.9 %all-to-all-done = s32[8,1,2]{2,1,0:T(1,128)S(1)} async-done(((s32[8,1,2]{2,1,0:T(1,128)}), s32[8,1,2]{2,1,0:T(1,128)S(1)}, u32[]{:S(2)}, u32[]{:S(2)}) %all-to-all-start) | async-done | bytes 96 | tf_op jit(solution)/shard_map/all_to_all | solution.py:284
  11.0 0.0 copy-start
  11.0 6.0 %select_filter.1 = (bf16[128,384]{1,0:T(8,128)(2,1)S(1)}, bf16[128,384]{1,0:T(8,128)(2,1)S(1)}, bf16[128,384]{1,0:T(8,128)(2,1)S(1)}, bf16[128,384]{1,0:T(8,128)...) custom-call(s32[8,2]{1,0:T(8,128)S(1)} %bitcast.9, ...), custom_call_target="tpu_custom_call" | custom-call | tf_op jit(solution)/shard_map/select_filter/pallas_call | solution.py:292
  17.0 0.1 collective-permute-start
  17.0 0.6 collective-permute-start.1
  17.7 1.2 %collective-permute-start.2 = (bf16[128,384]{1,0:T(8,128)(2,1)S(1)}, bf16[128,384]{1,0:T(8,128)(2,1)S(1)}, u32[]{:S(2)}, u32[]{:S(2)}) collective-permute-start(bf16[128,384]{1,0:T(8,128)(2,1)S(1)} %get-tuple-element.20), channel_id=1, source_target_pairs={{0,3},{1,2},{2,1},{3,0},{4,7},{5,6},{6,5},{7,4},{8,11},{9,10},{10,... | collective-permute-start | bytes 294920 | tf_op jit(solution)/shard_map/ppermute | solution.py:310
  18.9 0.0 collective-permute-done.refs_1_
  18.9 3.8 %collective-permute-done.1.refs_2_ = bf16[128,384]{1,0:T(8,128)(2,1)S(1)} collective-permute-done((bf16[128,384]{1,0:T(8,128)(2,1)S(1)}, bf16[128,384]{1,0:T(8,128)(2,1)S(1)}, u32[]{:S(2)}, u32[]{:S(2)}) %collective-permute-start.1) | collective-permute-done | bytes 98336 | tf_op jit(solution)/shard_map/ppermute | solution.py:310
  22.7 1.2 %collective-permute-done.2.refs_3_ = bf16[128,384]{1,0:T(8,128)(2,1)S(1)} collective-permute-done((bf16[128,384]{1,0:T(8,128)(2,1)S(1)}, bf16[128,384]{1,0:T(8,128)(2,1)S(1)}, u32[]{:S(2)}, u32[]{:S(2)}) %collective-permute-start.2) | collective-permute-done | bytes 98336 | tf_op jit(solution)/shard_map/ppermute | solution.py:310
  23.9 0.0 copy-done
  23.9 1.6 %place_first.1.refs_0_ = bf16[4,25,16,128]{3,2,1,0:T(8,128)(2,1)} custom-call(s32[16]{0:T(128)S(1)} %bitcast.3, bf16[128,384]{1,0:T(8,128)(2,1)S(1)} %get-tuple-element.17.refs_0_, bf16[128,384]{1,0:T(8,128)(2,1)S(1)} %collective-permute-done.refs_1_, bf16[128,384]{1,0:T(8,128)(2,1)S(1)} %collective-permute-done.1.refs_2_, ...), custom_call_target="tpu_custom_call" | custom-call | tf_op jit(solution)/shard_map/place_first/pallas_call | solution.py:333
  25.6 4.9 %all-to-all-start.1 = ((bf16[4,25,16,128]{3,2,1,0:T(8,128)(2,1)}), bf16[4,25,16,128]{3,2,1,0:T(8,128)(2,1)S(1)}, u32[]{:S(2)}, u32[]{:S(2)}) async-start(bf16[4,25,16,128]{3,2,1,0:T(8,128)(2,1)} %place_first.1.refs_0_), calls=%async_computation.1 | async-start | bytes 819200 | tf_op jit(solution)/shard_map/all_to_all | solution.py:346
  30.4 0.6 collective-permute-start.3
  31.0 0.8 %collective-permute-start.4 = (bf16[128,384]{1,0:T(8,128)(2,1)S(1)}, bf16[128,384]{1,0:T(8,128)(2,1)S(1)}, u32[]{:S(2)}, u32[]{:S(2)}) collective-permute-start(bf16[128,384]{1,0:T(8,128)(2,1)S(1)} %get-tuple-element.22), channel_id=1, source_target_pairs={{0,5},{1,4},{2,7},{3,6},{4,1},{5,0},{6,3},{7,2},{8,13},{9,12},{10,... | collective-permute-start | bytes 294920 | tf_op jit(solution)/shard_map/ppermute | solution.py:310
  31.8 0.7 %collective-permute-start.5 = (bf16[128,384]{1,0:T(8,128)(2,1)S(1)}, bf16[128,384]{1,0:T(8,128)(2,1)S(1)}, u32[]{:S(2)}, u32[]{:S(2)}) collective-permute-start(bf16[128,384]{1,0:T(8,128)(2,1)S(1)} %get-tuple-element.23), channel_id=1, source_target_pairs={{0,6},{1,7},{2,4},{3,5},{4,2},{5,3},{6,0},{7,1},{8,14},{9,15},{10,... | collective-permute-start | bytes 294920 | tf_op jit(solution)/shard_map/ppermute | solution.py:310
  32.5 2.4 %collective-permute-start.6 = (bf16[128,384]{1,0:T(8,128)(2,1)S(1)}, bf16[128,384]{1,0:T(8,128)(2,1)S(1)}, u32[]{:S(2)}, u32[]{:S(2)}) collective-permute-start(bf16[128,384]{1,0:T(8,128)(2,1)S(1)} %get-tuple-element.24), channel_id=1, source_target_pairs={{0,7},{1,6},{2,5},{3,4},{4,3},{5,2},{6,1},{7,0},{8,15},{9,14},{10,... | collective-permute-start | bytes 294920 | tf_op jit(solution)/shard_map/ppermute | solution.py:310
  34.8 1.3 %collective-permute-done.3.refs_4_ = bf16[128,384]{1,0:T(8,128)(2,1)S(1)} collective-permute-done((bf16[128,384]{1,0:T(8,128)(2,1)S(1)}, bf16[128,384]{1,0:T(8,128)(2,1)S(1)}, u32[]{:S(2)}, u32[]{:S(2)}) %collective-permute-start.3) | collective-permute-done | bytes 98336 | tf_op jit(solution)/shard_map/ppermute | solution.py:310
  36.1 4.4 %collective-permute-done.4.refs_5_ = bf16[128,384]{1,0:T(8,128)(2,1)S(1)} collective-permute-done((bf16[128,384]{1,0:T(8,128)(2,1)S(1)}, bf16[128,384]{1,0:T(8,128)(2,1)S(1)}, u32[]{:S(2)}, u32[]{:S(2)}) %collective-permute-start.4) | collective-permute-done | bytes 98336 | tf_op jit(solution)/shard_map/ppermute | solution.py:310
  40.5 0.0 collective-permute-done.5.refs_6_
  40.5 0.0 collective-permute-done.6.refs_7_
  40.5 1.1 %place_second.1 = (bf16[32,16,128]{2,1,0:T(8,128)(2,1)S(1)}, bf16[32,16,128]{2,1,0:T(8,128)(2,1)S(1)}, bf16[32,16,128]{2,1,0:T(8,128)(2,1)S(1)}, bf16[32,16,128]{2,1,0:T(8,128)(2,1)S(1)}) custom-call(s32[16]{0:T(128)S(1)} %bitcast.4, bf16[128,384]{1,0:T(8,128)(2,1)S(1)} %get-tuple-element.17.refs_0_, bf16[128,384]{1,0:T(8,128)(2,1)S(1)} %collective-permute-done.refs_1_, ...), custom_call_target="tpu_custom_call" | custom-call | tf_op jit(solution)/shard_map/place_second/pallas_call | solution.py:333
  41.6 1.9 %collective-permute-start.9 = (bf16[32,16,128]{2,1,0:T(8,128)(2,1)S(1)}, bf16[32,16,128]{2,1,0:T(8,128)(2,1)S(1)}, u32[]{:S(2)}, u32[]{:S(2)}) collective-permute-start(bf16[32,16,128]{2,1,0:T(8,128)(2,1)S(1)} %get-tuple-element.27), channel_id=1, source_target_pairs={{0,8},{8,16},{16,24},{24,0},{1,9},{9,17},{17,25},{25,1},{2,10},{10... | collective-permute-start | bytes 393224 | tf_op jit(solution)/shard_map/ppermute | solution.py:352
  43.5 2.0 %collective-permute-start.8 = (bf16[32,16,128]{2,1,0:T(8,128)(2,1)S(1)}, bf16[32,16,128]{2,1,0:T(8,128)(2,1)S(1)}, u32[]{:S(2)}, u32[]{:S(2)}) collective-permute-start(bf16[32,16,128]{2,1,0:T(8,128)(2,1)S(1)} %get-tuple-element.26), channel_id=1, source_target_pairs={{0,24},{8,0},{16,8},{24,16},{1,25},{9,1},{17,9},{25,17},{2,26},{10... | collective-permute-start | bytes 393224 | tf_op jit(solution)/shard_map/ppermute | solution.py:352
  45.5 0.9 %collective-permute-start.7 = (bf16[32,16,128]{2,1,0:T(8,128)(2,1)S(1)}, bf16[32,16,128]{2,1,0:T(8,128)(2,1)S(1)}, u32[]{:S(2)}, u32[]{:S(2)}) collective-permute-start(bf16[32,16,128]{2,1,0:T(8,128)(2,1)S(1)} %get-tuple-element.25), channel_id=1, source_target_pairs={{0,16},{8,24},{16,0},{24,8},{1,17},{9,25},{17,1},{25,9},{2,18},{10... | collective-permute-start | bytes 393224 | tf_op jit(solution)/shard_map/ppermute | solution.py:352
  46.4 3.7 %correlate.3.refs_2_ = f32[5,256,256]{2,1,0:T(8,128)S(1)} custom-call(s32[16]{0:T(128)S(1)} %bitcast.5, bf16[4,25,16,128]{3,2,1,0:T(8,128)(2,1)} %place_first.1.refs_0_, bf16[32,16,128]{2,1,0:T(8,128)(2,1)S(1)} %get-tuple-element.28.refs_1_), custom_call_target="tpu_custom_call" | custom-call | tf_op jit(solution)/shard_map/correlate/pallas_call | solution.py:260
  50.1 0.0 collective-permute-done.9.refs_1_
  50.1 0.0 all-to-all-done.1.refs_0_
  50.2 3.3 %correlate.4.refs_2_ = f32[5,256,256]{2,1,0:T(8,128)S(1)} custom-call(s32[16]{0:T(128)S(1)} %bitcast.6, bf16[4,25,16,128]{3,2,1,0:T(8,128)(2,1)S(1)} %all-to-all-done.1.refs_0_, bf16[32,16,128]{2,1,0:T(8,128)(2,1)S(1)} %collective-permute-done.9.refs_1_, f32[5,256,256]{2,1,0:T(8,128)S(1)} %correlate.3.refs_2_), custom_call_target="tpu_custom_call" | custom-call | tf_op jit(solution)/shard_map/correlate/pallas_call | solution.py:260
  53.4 0.0 collective-permute-done.8.refs_1_
  53.4 3.4 %correlate.5.refs_2_ = f32[5,256,256]{2,1,0:T(8,128)S(1)} custom-call(s32[16]{0:T(128)S(1)} %bitcast.7, bf16[4,25,16,128]{3,2,1,0:T(8,128)(2,1)S(1)} %all-to-all-done.1.refs_0_, bf16[32,16,128]{2,1,0:T(8,128)(2,1)S(1)} %collective-permute-done.8.refs_1_, f32[5,256,256]{2,1,0:T(8,128)S(1)} %correlate.4.refs_2_), custom_call_target="tpu_custom_call" | custom-call | tf_op jit(solution)/shard_map/correlate/pallas_call | solution.py:260
  56.8 1.4 %collective-permute-done.7.refs_1_ = bf16[32,16,128]{2,1,0:T(8,128)(2,1)S(1)} collective-permute-done((bf16[32,16,128]{2,1,0:T(8,128)(2,1)S(1)}, bf16[32,16,128]{2,1,0:T(8,128)(2,1)S(1)}, u32[]{:S(2)}, u32[]{:S(2)}) %collective-permute-start.7) | collective-permute-done | bytes 131104 | tf_op jit(solution)/shard_map/ppermute | solution.py:352
  58.2 4.7 %correlate_last.1 = f32[5,8,8,1001]{3,2,1,0:T(8,128)} custom-call(s32[16]{0:T(128)S(1)} %bitcast.8, bf16[4,25,16,128]{3,2,1,0:T(8,128)(2,1)S(1)} %all-to-all-done.1.refs_0_, bf16[32,16,128]{2,1,0:T(8,128)(2,1)S(1)} %collective-permute-done.7.refs_1_, f32[5,256,256]{2,1,0:T(8,128)S(1)} %correlate.5.refs_2_), custom_call_target="tpu_custom_call" | custom-call | tf_op jit(solution)/shard_map/correlate_last/pallas_call | solution.py:260
Async XLA Ops:
  1.2 9.8 %all-to-all-start = ((s32[8,1,2]{2,1,0:T(1,128)}), s32[8,1,2]{2,1,0:T(1,128)S(1)}, u32[]{:S(2)}, u32[]{:S(2)}) async-start(s32[8,1,2]{2,1,0:T(1,128)} %broadcast_in_dim.2), calls=%async_computation | async-start | bytes 8192 | tf_op jit(solution)/shard_map/all_to_all | solution.py:284
  11.0 12.9 %copy-start = (s32[16,1]{0,1:T(1,128)S(1)}, s32[16,1]{0,1:T(1,128)}, u32[]{:S(2)}) copy-start(s32[16,1]{0,1:T(1,128)} %param.7) | copy-start | bytes 196
  17.0 1.9 %collective-permute-start = (bf16[128,384]{1,0:T(8,128)(2,1)S(1)}, bf16[128,384]{1,0:T(8,128)(2,1)S(1)}, u32[]{:S(2)}, u32[]{:S(2)}) collective-permute-start(bf16[128,384]{1,0:T(8,128)(2,1)S(1)} %get-tuple-element.18), channel_id=1, source_target_pairs={{0,1},{1,0},{2,3},{3,2},{4,5},{5,4},{6,7},{7,6},{8,9},{9,8},{10,11... | collective-permute-start | bytes 294920 | tf_op jit(solution)/shard_map/ppermute | solution.py:310
  17.0 5.7 %collective-permute-start.1 = (bf16[128,384]{1,0:T(8,128)(2,1)S(1)}, bf16[128,384]{1,0:T(8,128)(2,1)S(1)}, u32[]{:S(2)}, u32[]{:S(2)}) collective-permute-start(bf16[128,384]{1,0:T(8,128)(2,1)S(1)} %get-tuple-element.19), channel_id=1, source_target_pairs={{0,2},{1,3},{2,0},{3,1},{4,6},{5,7},{6,4},{7,5},{8,10},{9,11},{10,... | collective-permute-start | bytes 294920 | tf_op jit(solution)/shard_map/ppermute | solution.py:310
  17.7 6.2 %collective-permute-start.2 = (bf16[128,384]{1,0:T(8,128)(2,1)S(1)}, bf16[128,384]{1,0:T(8,128)(2,1)S(1)}, u32[]{:S(2)}, u32[]{:S(2)}) collective-permute-start(bf16[128,384]{1,0:T(8,128)(2,1)S(1)} %get-tuple-element.20), channel_id=1, source_target_pairs={{0,3},{1,2},{2,1},{3,0},{4,7},{5,6},{6,5},{7,4},{8,11},{9,10},{10,... | collective-permute-start | bytes 294920 | tf_op jit(solution)/shard_map/ppermute | solution.py:310
  25.6 24.6 %all-to-all-start.1 = ((bf16[4,25,16,128]{3,2,1,0:T(8,128)(2,1)}), bf16[4,25,16,128]{3,2,1,0:T(8,128)(2,1)S(1)}, u32[]{:S(2)}, u32[]{:S(2)}) async-start(bf16[4,25,16,128]{3,2,1,0:T(8,128)(2,1)} %place_first.1.refs_0_), calls=%async_computation.1 | async-start | bytes 819200 | tf_op jit(solution)/shard_map/all_to_all | solution.py:346
  30.4 5.7 %collective-permute-start.3 = (bf16[128,384]{1,0:T(8,128)(2,1)S(1)}, bf16[128,384]{1,0:T(8,128)(2,1)S(1)}, u32[]{:S(2)}, u32[]{:S(2)}) collective-permute-start(bf16[128,384]{1,0:T(8,128)(2,1)S(1)} %get-tuple-element.21), channel_id=1, source_target_pairs={{0,4},{1,5},{2,6},{3,7},{4,0},{5,1},{6,2},{7,3},{8,12},{9,13},{10,... | collective-permute-start | bytes 294920 | tf_op jit(solution)/shard_map/ppermute | solution.py:310
  31.0 9.5 %collective-permute-start.4 = (bf16[128,384]{1,0:T(8,128)(2,1)S(1)}, bf16[128,384]{1,0:T(8,128)(2,1)S(1)}, u32[]{:S(2)}, u32[]{:S(2)}) collective-permute-start(bf16[128,384]{1,0:T(8,128)(2,1)S(1)} %get-tuple-element.22), channel_id=1, source_target_pairs={{0,5},{1,4},{2,7},{3,6},{4,1},{5,0},{6,3},{7,2},{8,13},{9,12},{10,... | collective-permute-start | bytes 294920 | tf_op jit(solution)/shard_map/ppermute | solution.py:310
  31.8 8.7 %collective-permute-start.5 = (bf16[128,384]{1,0:T(8,128)(2,1)S(1)}, bf16[128,384]{1,0:T(8,128)(2,1)S(1)}, u32[]{:S(2)}, u32[]{:S(2)}) collective-permute-start(bf16[128,384]{1,0:T(8,128)(2,1)S(1)} %get-tuple-element.23), channel_id=1, source_target_pairs={{0,6},{1,7},{2,4},{3,5},{4,2},{5,3},{6,0},{7,1},{8,14},{9,15},{10,... | collective-permute-start | bytes 294920 | tf_op jit(solution)/shard_map/ppermute | solution.py:310
  32.5 8.0 %collective-permute-start.6 = (bf16[128,384]{1,0:T(8,128)(2,1)S(1)}, bf16[128,384]{1,0:T(8,128)(2,1)S(1)}, u32[]{:S(2)}, u32[]{:S(2)}) collective-permute-start(bf16[128,384]{1,0:T(8,128)(2,1)S(1)} %get-tuple-element.24), channel_id=1, source_target_pairs={{0,7},{1,6},{2,5},{3,4},{4,3},{5,2},{6,1},{7,0},{8,15},{9,14},{10,... | collective-permute-start | bytes 294920 | tf_op jit(solution)/shard_map/ppermute | solution.py:310
  41.6 8.6 %collective-permute-start.9 = (bf16[32,16,128]{2,1,0:T(8,128)(2,1)S(1)}, bf16[32,16,128]{2,1,0:T(8,128)(2,1)S(1)}, u32[]{:S(2)}, u32[]{:S(2)}) collective-permute-start(bf16[32,16,128]{2,1,0:T(8,128)(2,1)S(1)} %get-tuple-element.27), channel_id=1, source_target_pairs={{0,8},{8,16},{16,24},{24,0},{1,9},{9,17},{17,25},{25,1},{2,10},{10... | collective-permute-start | bytes 393224 | tf_op jit(solution)/shard_map/ppermute | solution.py:352
  43.5 10.0 %collective-permute-start.8 = (bf16[32,16,128]{2,1,0:T(8,128)(2,1)S(1)}, bf16[32,16,128]{2,1,0:T(8,128)(2,1)S(1)}, u32[]{:S(2)}, u32[]{:S(2)}) collective-permute-start(bf16[32,16,128]{2,1,0:T(8,128)(2,1)S(1)} %get-tuple-element.26), channel_id=1, source_target_pairs={{0,24},{8,0},{16,8},{24,16},{1,25},{9,1},{17,9},{25,17},{2,26},{10... | collective-permute-start | bytes 393224 | tf_op jit(solution)/shard_map/ppermute | solution.py:352
  45.5 12.7 %collective-permute-start.7 = (bf16[32,16,128]{2,1,0:T(8,128)(2,1)S(1)}, bf16[32,16,128]{2,1,0:T(8,128)(2,1)S(1)}, u32[]{:S(2)}, u32[]{:S(2)}) collective-permute-start(bf16[32,16,128]{2,1,0:T(8,128)(2,1)S(1)} %get-tuple-element.25), channel_id=1, source_target_pairs={{0,16},{8,24},{16,0},{24,8},{1,17},{9,25},{17,1},{25,9},{2,18},{10... | collective-permute-start | bytes 393224 | tf_op jit(solution)/shard_map/ppermute | solution.py:352

commit v5 on v3

--- a/solution.py
+++ b/solution.py
@@ -39,17 +39,32 @@
     return pl.BlockSpec(memory_space=pltpu.SMEM)
 
 
-def select_kernel(n_chan, firsts, raw, taps, *refs):
-    sends, (window, picked, line, tap_sem, sems) = refs[:n_chan], refs[n_chan:]
+def weights_kernel(taps, weights, held, line, sem):
+    copy = pltpu.make_async_copy(taps, held, sem)
+    copy.start()
+    rows, outs, width = weights.shape[1], weights.shape[0] - 2 * SPILL, line.shape[1]
+    line[...] = jnp.zeros_like(line)
+    copy.wait()
+    line[0:1, :TAPS] = held[...]
+    spread = jnp.broadcast_to(line[0:1, :], (outs + 2 * SPILL, width))
+    value = pltpu.roll(spread, width - 4 * SPILL + 1, 1, stride=2, stride_axis=0)[:, :rows]
+    value = value.astype(jnp.bfloat16)
+    weights[:outs, :] = value[SPILL : SPILL + outs]
+    weights[outs : outs + SPILL, :] = value[SPILL + outs :]
+    weights[outs + SPILL :, :] = value[:SPILL]
+
+
+def select_kernel(n_chan, groups, firsts, raw, weights, *refs):
+    sends, (window, picked, sems) = refs[: len(groups)], refs[len(groups) :]
     rows, channels = raw.shape
-    outs = rows // 2
+    steps = [k for group in groups for k in group]
     stripes = n_chan * STRIPES
     blocks_per = channels // n_chan // CB
     span = window.shape[2]
     me = lax.axis_index("chan")
 
     def place(p):
-        c, k = me ^ (p // STRIPES), p % STRIPES
+        c, k = me ^ steps[p // STRIPES], p % STRIPES
         start = (firsts[c, k] + c * blocks_per) * CB
         base = jnp.minimum(start - lax.rem(start, LANES), channels - span)
         return start, pl.multiple_of(base, LANES)
@@ -58,20 +73,8 @@
         base = place(p)[1]
         return pltpu.make_async_copy(raw.at[:, pl.ds(base, span)], window.at[p], sems.at[p])
 
-    line[...] = jnp.zeros_like(line)
-    tap_copy = pltpu.make_async_copy(taps, line.at[0:1, : taps.shape[1]], tap_sem)
-    tap_copy.start()
     for p in range(stripes):
         copy(p).start()
-
-    width = line.shape[1]
-    tap_copy.wait()
-    spread = jnp.broadcast_to(line[0:1, :], (outs + 2 * SPILL, width))
-    weights = pltpu.roll(spread, width - 4 * SPILL + 1, 1, stride=2, stride_axis=0)[:, :rows]
-    weights = weights.astype(jnp.bfloat16)
-    weights = jnp.concatenate(
-        [weights[SPILL : SPILL + outs], weights[SPILL + outs :], weights[:SPILL]], 0
-    )
 
     row = lax.broadcasted_iota(jnp.int32, (WIDE, span), 0)
     lane = lax.broadcasted_iota(jnp.int32, (WIDE, span), 1)
@@ -86,20 +89,29 @@
             chosen = lax.dot_general(hot, block, NT, preferred_element_type=jnp.float32)
             picked[p * WIDE : (p + 1) * WIDE, :] = chosen.astype(jnp.bfloat16)
         part = slice(first * WIDE, (first + batch) * WIDE)
-        result = lax.dot_general(picked[part, :], weights, NT, preferred_element_type=jnp.float32)
-        result = result.astype(jnp.bfloat16)
+        result = lax.dot_general(
+            picked[part, :], weights[...], NT, preferred_element_type=jnp.float32
+        ).astype(jnp.bfloat16)
+        height = STRIPES * WIDE
         for at in range(batch // STRIPES):
-            sends[first // STRIPES + at][...] = result[at * STRIPES * WIDE : (at + 1) * STRIPES * WIDE]
-
-
-def add_spills(n_chan, outs, got, total):
+            k = steps[first // STRIPES + at]
+            out, where = [(o, g.index(k)) for o, g in enumerate(groups) if k in g][0]
+            sends[out][where * height : (where + 1) * height, :] = result[at * height : (at + 1) * height]
+
+
+def add_spills(n_chan, outs, steps, got, total):
     count = total.shape[0]
     early = lax.broadcasted_iota(jnp.int32, (count, LANES), 1) < SPILL
-    chunks = [lax.axis_index("chan") ^ k for k in range(n_chan)]
-    for chunk, value in zip(chunks, got):
+    me = lax.axis_index("chan")
+    pieces = [
+        (me ^ k, ref.at[at * count : (at + 1) * count])
+        for ks, ref in zip(steps, got)
+        for at, k in enumerate(ks)
+    ]
+    for chunk, value in pieces:
         at = pl.ds(pl.multiple_of(chunk * outs, LANES), outs)
         total[:, at] = value[:, :outs].astype(jnp.float32)
-    for chunk, value in zip(chunks, got):
+    for chunk, value in pieces:
         spill = value[:, outs:].astype(jnp.float32)
         after = jnp.minimum(chunk + 1, n_chan - 1) * outs
         after = pl.ds(pl.multiple_of(after, LANES), LANES)
@@ -120,14 +132,14 @@
     return jnp.where(lax.axis_index("chan") < n_chan // 2, 0, 1)
 
 
-def place_kernel(n_chan, n_tgroup, outs, group, owners, *refs):
+def place_kernel(n_chan, n_tgroup, outs, group, steps, owners, *refs):
     got, (total, pairs) = refs[: -n_tgroup - 2], refs[-2:]
     sends = refs[-n_tgroup - 2 : -2]
     me = lax.axis_index("tgroup")
     if len(got) == 1:
         total[...] = got[0][...]
     else:
-        add_spills(n_chan, outs, got, total)
+        add_spills(n_chan, outs, steps, got, total)
 
     for at in range(n_tgroup * SLOTS):
         pairs[at] = -1
@@ -281,25 +293,57 @@
         tiled=True,
     )
     line = -(-(rows + 2 * outs + 4 * SPILL) // (2 * LANES)) * 2 * LANES
+    weights = pl.pallas_call(
+        weights_kernel,
+        out_shape=jax.ShapeDtypeStruct((outs + 2 * SPILL, rows), jnp.bfloat16),
+        in_specs=[pl.BlockSpec(memory_space=pl.ANY)],
+        out_specs=vmem(),
+        scratch_shapes=[
+            pltpu.VMEM((1, TAPS), jnp.float32),
+            pltpu.VMEM((8, line), jnp.float32),
+            pltpu.SemaphoreType.DMA,
+        ],
+        compiler_params=params(40),
+        name="fir_weights",
+    )(whitening_taps.reshape(1, TAPS))
+
+    relayed = n_chan == 8 and outs % LANES == 0
+    groups = [[2], [3], [1, 5, 7], [4], [6], [0]] if relayed else [[k] for k in range(n_chan)]
     sends = pl.pallas_call(
-        functools.partial(select_kernel, n_chan),
-        out_shape=(jax.ShapeDtypeStruct((count, outs + 2 * SPILL), jnp.bfloat16),) * n_chan,
-        in_specs=[smem(), pl.BlockSpec(memory_space=pl.ANY), pl.BlockSpec(memory_space=pl.ANY)],
-        out_specs=(vmem(),) * n_chan,
+        functools.partial(select_kernel, n_chan, groups),
+        out_shape=[
+            jax.ShapeDtypeStruct((len(group) * count, outs + 2 * SPILL), jnp.bfloat16)
+            for group in groups
+        ],
+        in_specs=[smem(), pl.BlockSpec(memory_space=pl.ANY), vmem()],
+        out_specs=[vmem()] * len(groups),
         scratch_shapes=[
             pltpu.VMEM((n_chan * STRIPES, rows, 2 * LANES), jnp.float32),
             pltpu.VMEM((n_chan * count, rows), jnp.bfloat16),
-            pltpu.VMEM((8, line), jnp.float32),
-            pltpu.SemaphoreType.DMA,
             pltpu.SemaphoreType.DMA((n_chan * STRIPES,)),
         ],
         compiler_params=params(40),
         name="select_filter",
-    )(firsts, raw_strain, jnp.pad(whitening_taps, (0, 1)).reshape(1, TAPS + 1))
-
-    got = [sends[0]]
-    for k in range(1, n_chan):
-        got.append(lax.ppermute(sends[k], "chan", [(c, c ^ k) for c in range(n_chan)]))
+    )(firsts, raw_strain, weights)
+
+    def exchange(value, k):
+        return lax.ppermute(value, "chan", [(c, c ^ k) for c in range(n_chan)])
+
+    if relayed:
+        got = [sends[5], exchange(sends[0], 2), exchange(sends[1], 3), exchange(sends[2], 1)]
+        across = [
+            jnp.concatenate([sends[3 + at], got[3][(1 + at) * count : (2 + at) * count]], 0)
+            for at in range(2)
+        ]
+        across, got[1] = lax.optimization_barrier((across, got[1]))
+        across = [exchange(value, 4 + 2 * at) for at, value in enumerate(across)]
+        early, late = got, got + across
+        early_steps, late_steps = [[0], [2], [3], [1]], [[0], [2], [3], [1], [4, 5], [6, 7]]
+    else:
+        got = [sends[0]] + [exchange(sends[k], k) for k in range(1, n_chan)]
+        half = n_chan // 2
+        early, late = got[:half], got
+        early_steps, late_steps = [[k] for k in range(half)], [[k] for k in range(n_chan)]
     if outs % LANES:
         wide = jnp.stack(got).astype(jnp.float32)
         wide = jnp.take(wide, lax.axis_index("chan") ^ jnp.arange(n_chan), axis=0)
@@ -308,19 +352,16 @@
         right = jnp.concatenate([zero, wide[:-1, :, outs : outs + SPILL]], 0)
         left = jnp.concatenate([wide[1:, :, outs + SPILL :], zero], 0)
         added = wide[:, :, :outs] + jnp.concatenate([right, none], 2) + jnp.concatenate([none, left], 2)
-        got = added.transpose(1, 0, 2).reshape(count, samples)
+        early = late = [added.transpose(1, 0, 2).reshape(count, samples)]
 
     order = sorted(range(1, n_tgroup), key=lambda s: min(s, n_tgroup - s))
     arrived = [[] for _ in range(n_tgroup)]
     for group in range(2):
-        if outs % LANES:
-            use = [got]
-        else:
-            use = got[: n_chan // 2] if group == 0 else got
+        use, steps = (early, early_steps) if group == 0 else (late, late_steps)
         vectors = samples // LANES // 2 + (1 if group else -1)
         packed = jax.ShapeDtypeStruct((-(-BLOCKS * vectors // 2), 2 * CB, LANES), jnp.bfloat16)
         sends = pl.pallas_call(
-            functools.partial(place_kernel, n_chan, n_tgroup, outs, group),
+            functools.partial(place_kernel, n_chan, n_tgroup, outs, group, steps),
             out_shape=(packed,) * n_tgroup,
             in_specs=[smem()] + [vmem()] * len(use),
             out_specs=(vmem(),) * n_tgroup,
@@ -332,9 +373,12 @@
             name="place_first" if group == 0 else "place_second",
         )(owners, *use)
         arrived[0].append(sends[0])
-        for shift in order:
+        for at, shift in enumerate(order):
             route = [(g, (g + shift) % n_tgroup) for g in range(n_tgroup)]
-            arrived[shift].append(lax.ppermute(sends[shift], "tgroup", route))
+            value = sends[shift]
+            if group == 1:
+                value, arrived[shift][0] = lax.optimization_barrier((value, arrived[shift][0]))
+            arrived[shift].append(lax.ppermute(value, "tgroup", route))
 
     value = None
     factor = 1.0 / math.sqrt(samples)

time: 58.7 us -> 56.2 us (0.957)
  starting transfers between devices: 19.3 us -> 17.6 us
  waiting for transfers between devices: 14.6 us -> 13.3 us
    ppermute x13 -> x11, starting transfers between devices: 14.1 us -> 12.5 us  [the longest x6 8.5 us: local(): arrived[shift].append(lax.ppermute(value, 'tgroup', route))]
    ppermute x13 -> x11, waiting for transfers between devices: 10.7 us -> 9.51 us  [the longest x5 6.35 us: exchange(): return lax.ppermute(value, 'chan', [(c, c ^ k) for c in range(n_chan)])]
    pad x1 -> x0, local copies, waits for them, and re-layouts: 0.68 us -> none  [local(): jnp.pad(whitening_taps, (0, 1)).reshape(1, TAPS + 1)]
    unnamed x2 -> x4, local copies, waits for them, and re-layouts: 0.01 us -> 0.68 us
    pallas_call x1 -> x2, Pallas kernels: 5.95 us -> 6.06 us  [the longest x1 5.93 us: local(): pl.pallas_call(functools.partial(select_kernel, n_chan, groups), out_shap...]
  transfers between devices with their start and end apart: 14 -> 12, of which waited for: 5 -> 6; matrix products, arithmetic and copies ran while one was open for 1% -> 0% of each run, Pallas kernels for 20% -> 22%
where the time goes in v5:
time: 56.2 us; the launch traced here: 55.7 us
  Pallas kernels  22.7 us (40%)
  starting transfers between devices  17.6 us (31%)
  waiting for transfers between devices  13.3 us (24%)
  local copies, waits for them, and re-layouts  1.95 us (3%)
    pallas_call x4, Pallas kernels, correlate(): pl.pallas_call(functools.partial(correlate_kernel, n_chan, factor, last),...  14.6 us
    ppermute x6, starting transfers between devices, local(): arrived[shift].append(lax.ppermute(value, 'tgroup', route))  8.5 us
    ppermute x5, waiting for transfers between devices, exchange(): return lax.ppermute(value, 'chan', [(c, c ^ k) for c in range(n_chan)])  6.35 us
    pallas_call x1, Pallas kernels, local(): pl.pallas_call(functools.partial(select_kernel, n_chan, groups), out_shap...  5.93 us
    all_to_all x1, starting transfers between devices, local(): lax.all_to_all(jnp.broadcast_to(first_block[None, :], (n_chan, STRIPES)),...  5.17 us
    ppermute x5, starting transfers between devices, exchange(): return lax.ppermute(value, 'chan', [(c, c ^ k) for c in range(n_chan)])  3.96 us
    all_to_all x1, waiting for transfers between devices, local(): lax.all_to_all(jnp.broadcast_to(first_block[None, :], (n_chan, STRIPES)),...  3.76 us
    ppermute x6, waiting for transfers between devices, local(): arrived[shift].append(lax.ppermute(value, 'tgroup', route))  3.16 us
  transfers between devices with their start and end apart: 12, of which 6 were waited for; matrix products, arithmetic and copies ran while one was open for 0% of the time, Pallas kernels for 22%

profile of v5, /device:TPU:0, one launch (start us, length us, event | category | flops | bytes accessed | tf_op | source)
XLA Modules:
  0.0 55.7 jit_solution(609822562565846820)
XLA Ops:
  0.0 1.2 %broadcast_in_dim.2 = s32[8,1,2]{2,1,0:T(1,128)} broadcast(s32[2]{0:T(128)} %param.6), dimensions={2} | broadcast | bytes 72 | tf_op jit(solution)/shard_map/broadcast_in_dim | solution.py:289
  1.2 5.2 %all-to-all-start = ((s32[8,1,2]{2,1,0:T(1,128)}), s32[8,1,2]{2,1,0:T(1,128)S(1)}, u32[]{:S(2)}, u32[]{:S(2)}) async-start(s32[8,1,2]{2,1,0:T(1,128)} %broadcast_in_dim.2), calls=%async_computation | async-start | bytes 8192 | tf_op jit(solution)/shard_map/all_to_all | solution.py:288
  6.4 0.0 copy-start.1
  6.4 0.7 %copy-done.1 = f32[255]{0:T(256)S(1)} copy-done((f32[255]{0:T(256)S(1)}, f32[255]{0:T(256)}, u32[]{:S(2)}) %copy-start.1) | copy-done | bytes 1044
  7.1 0.1 fir_weights.1.weights
  7.2 3.8 %all-to-all-done = s32[8,1,2]{2,1,0:T(1,128)S(1)} async-done(((s32[8,1,2]{2,1,0:T(1,128)}), s32[8,1,2]{2,1,0:T(1,128)S(1)}, u32[]{:S(2)}, u32[]{:S(2)}) %all-to-all-start) | async-done | bytes 96 | tf_op jit(solution)/shard_map/all_to_all | solution.py:288
  11.0 0.0 copy-start
  11.0 5.9 %select_filter.1 = (bf16[128,384]{1,0:T(8,128)(2,1)S(1)}, bf16[128,384]{1,0:T(8,128)(2,1)S(1)}, bf16[384,384]{1,0:T(8,128)(2,1)S(1)}, bf16[128,384]{1,0:T(8,128)...) custom-call(s32[8,2]{1,0:T(8,128)S(1)} %bitcast.9, f32[512,10240]{1,0:T(8,128)} %raw.1, ...), custom_call_target="tpu_custom_call" | custom-call | tf_op jit(solution)/shard_map/select_filter/pallas_call | solution.py:312
  16.9 0.1 collective-permute-start
  17.0 0.6 %collective-permute-start.1 = (bf16[128,384]{1,0:T(8,128)(2,1)S(1)}, bf16[128,384]{1,0:T(8,128)(2,1)S(1)}, u32[]{:S(2)}, u32[]{:S(2)}) collective-permute-start(bf16[128,384]{1,0:T(8,128)(2,1)S(1)} %get-tuple-element.32), channel_id=1, source_target_pairs={{0,2},{1,3},{2,0},{3,1},{4,6},{5,7},{6,4},{7,5},{8,10},{9,11},{10,... | collective-permute-start | bytes 294920 | tf_op jit(solution)/shard_map/ppermute | solution.py:330
  17.6 1.2 %collective-permute-start.2 = (bf16[128,384]{1,0:T(8,128)(2,1)S(1)}, bf16[128,384]{1,0:T(8,128)(2,1)S(1)}, u32[]{:S(2)}, u32[]{:S(2)}) collective-permute-start(bf16[128,384]{1,0:T(8,128)(2,1)S(1)} %get-tuple-element.34), channel_id=1, source_target_pairs={{0,3},{1,2},{2,1},{3,0},{4,7},{5,6},{6,5},{7,4},{8,11},{9,10},{10,... | collective-permute-start | bytes 294920 | tf_op jit(solution)/shard_map/ppermute | solution.py:330
  18.9 0.0 collective-permute-done.refs_3_
  19.0 3.7 %collective-permute-done.1.refs_1_ = bf16[128,384]{1,0:T(8,128)(2,1)S(1)} collective-permute-done((bf16[128,384]{1,0:T(8,128)(2,1)S(1)}, bf16[128,384]{1,0:T(8,128)(2,1)S(1)}, u32[]{:S(2)}, u32[]{:S(2)}) %collective-permute-start.1) | collective-permute-done | bytes 98336 | tf_op jit(solution)/shard_map/ppermute | solution.py:330
  22.7 0.6 %collective-permute-start.3 = (bf16[256,384]{1,0:T(8,128)(2,1)S(1)}, bf16[256,384]{1,0:T(8,128)(2,1)S(1)}, u32[]{:S(2)}, u32[]{:S(2)}) collective-permute-start(bf16[256,384]{1,0:T(8,128)(2,1)S(1)} %get-tuple-element.35), channel_id=1, source_target_pairs={{0,4},{1,5},{2,6},{3,7},{4,0},{5,1},{6,2},{7,3},{8,12},{9,13},{10,... | collective-permute-start | bytes 589832 | tf_op jit(solution)/shard_map/ppermute | solution.py:330
  23.3 1.5 %collective-permute-start.4 = (bf16[256,384]{1,0:T(8,128)(2,1)S(1)}, bf16[256,384]{1,0:T(8,128)(2,1)S(1)}, u32[]{:S(2)}, u32[]{:S(2)}) collective-permute-start(bf16[256,384]{1,0:T(8,128)(2,1)S(1)} %get-tuple-element.36), channel_id=1, source_target_pairs={{0,6},{1,7},{2,4},{3,5},{4,2},{5,3},{6,0},{7,1},{8,14},{9,15},{10,... | collective-permute-start | bytes 589832 | tf_op jit(solution)/shard_map/ppermute | solution.py:330
  24.7 0.0 collective-permute-done.2.refs_2_
  24.7 0.0 copy-done
  24.7 0.9 %place_first.1 = (bf16[25,16,128]{2,1,0:T(8,128)(2,1)S(1)}, bf16[25,16,128]{2,1,0:T(8,128)(2,1)S(1)}, bf16[25,16,128]{2,1,0:T(8,128)(2,1)S(1)}, bf16[25,16,128]{2,1,0:T(8,128)(2,1)S(1)}) custom-call(s32[16]{0:T(128)S(1)} %bitcast.3, bf16[128,384]{1,0:T(8,128)(2,1)S(1)} %get-tuple-element.28.refs_0_, bf16[128,384]{1,0:T(8,128)(2,1)S(1)} %collective-permute-done.1.refs_1_, ...), custom_call_target="tpu_custom_call" | custom-call | tf_op jit(solution)/shard_map/place_first/pallas_call | solution.py:363
  25.6 3.7 %collective-permute-start.7 = (bf16[25,16,128]{2,1,0:T(8,128)(2,1)S(1)}, bf16[25,16,128]{2,1,0:T(8,128)(2,1)S(1)}, u32[]{:S(2)}, u32[]{:S(2)}) collective-permute-start(bf16[25,16,128]{2,1,0:T(8,128)(2,1)S(1)} %get-tuple-element.42), channel_id=1, source_target_pairs={{0,24},{8,0},{16,8},{24,16},{1,25},{9,1},{17,9},{25,17},{2,26},{10... | collective-permute-start | bytes 307208 | tf_op jit(solution)/shard_map/ppermute | solution.py:381
  29.3 0.0 collective-permute-start.9
  29.3 1.0 %collective-permute-start.5 = (bf16[25,16,128]{2,1,0:T(8,128)(2,1)S(1)}, bf16[25,16,128]{2,1,0:T(8,128)(2,1)S(1)}, u32[]{:S(2)}, u32[]{:S(2)}) collective-permute-start(bf16[25,16,128]{2,1,0:T(8,128)(2,1)S(1)} %get-tuple-element.38), channel_id=1, source_target_pairs={{0,16},{8,24},{16,0},{24,8},{1,17},{9,25},{17,1},{25,9},{2,18},{10... | collective-permute-start | bytes 307208 | tf_op jit(solution)/shard_map/ppermute | solution.py:381
  30.3 2.6 %collective-permute-done.3.refs_4_ = bf16[256,384]{1,0:T(8,128)(2,1)S(1)} collective-permute-done((bf16[256,384]{1,0:T(8,128)(2,1)S(1)}, bf16[256,384]{1,0:T(8,128)(2,1)S(1)}, u32[]{:S(2)}, u32[]{:S(2)}) %collective-permute-start.3) | collective-permute-done | bytes 196640 | tf_op jit(solution)/shard_map/ppermute | solution.py:330
  32.9 0.0 collective-permute-done.4.refs_5_
  32.9 1.1 %place_second.1 = (bf16[32,16,128]{2,1,0:T(8,128)(2,1)S(1)}, bf16[32,16,128]{2,1,0:T(8,128)(2,1)S(1)}, bf16[32,16,128]{2,1,0:T(8,128)(2,1)S(1)}, bf16[32,16,128]{2,1,0:T(8,128)(2,1)S(1)}) custom-call(s32[16]{0:T(128)S(1)} %bitcast.4, bf16[128,384]{1,0:T(8,128)(2,1)S(1)} %get-tuple-element.28.refs_0_, bf16[128,384]{1,0:T(8,128)(2,1)S(1)} %collective-permute-done.1.refs_1_, ...), custom_call_target="tpu_custom_call" | custom-call | tf_op jit(solution)/shard_map/place_second/pallas_call | solution.py:363
  34.0 0.0 collective-permute-done.7.refs_0_
  34.0 2.2 %collective-permute-done.9.refs_0_ = bf16[25,16,128]{2,1,0:T(8,128)(2,1)S(1)} collective-permute-done((bf16[25,16,128]{2,1,0:T(8,128)(2,1)S(1)}, bf16[25,16,128]{2,1,0:T(8,128)(2,1)S(1)}, u32[]{:S(2)}, u32[]{:S(2)}) %collective-permute-start.9) | collective-permute-done | bytes 102432 | tf_op jit(solution)/shard_map/ppermute | solution.py:381
  36.2 0.6 %collective-permute-start.10 = (bf16[32,16,128]{2,1,0:T(8,128)(2,1)S(1)}, bf16[32,16,128]{2,1,0:T(8,128)(2,1)S(1)}, u32[]{:S(2)}, u32[]{:S(2)}) collective-permute-start(bf16[32,16,128]{2,1,0:T(8,128)(2,1)S(1)} %get-tuple-element.48), channel_id=1, source_target_pairs={{0,8},{8,16},{16,24},{24,0},{1,9},{9,17},{17,25},{25,1},{2,10},{10... | collective-permute-start | bytes 393224 | tf_op jit(solution)/shard_map/ppermute | solution.py:381
  36.8 3.3 %collective-permute-start.8 = (bf16[32,16,128]{2,1,0:T(8,128)(2,1)S(1)}, bf16[32,16,128]{2,1,0:T(8,128)(2,1)S(1)}, u32[]{:S(2)}, u32[]{:S(2)}) collective-permute-start(bf16[32,16,128]{2,1,0:T(8,128)(2,1)S(1)} %get-tuple-element.44), channel_id=1, source_target_pairs={{0,24},{8,0},{16,8},{24,16},{1,25},{9,1},{17,9},{25,17},{2,26},{10... | collective-permute-start | bytes 393224 | tf_op jit(solution)/shard_map/ppermute | solution.py:381
  40.1 0.7 %collective-permute-done.5.refs_0_ = bf16[25,16,128]{2,1,0:T(8,128)(2,1)S(1)} collective-permute-done((bf16[25,16,128]{2,1,0:T(8,128)(2,1)S(1)}, bf16[25,16,128]{2,1,0:T(8,128)(2,1)S(1)}, u32[]{:S(2)}, u32[]{:S(2)}) %collective-permute-start.5) | collective-permute-done | bytes 102432 | tf_op jit(solution)/shard_map/ppermute | solution.py:381
  40.7 0.0 collective-permute-start.6
  40.7 3.3 %correlate.3.refs_2_ = f32[5,256,256]{2,1,0:T(8,128)S(1)} custom-call(s32[16]{0:T(128)S(1)} %bitcast.5, bf16[25,16,128]{2,1,0:T(8,128)(2,1)S(1)} %get-tuple-element.49.refs_0_, bf16[32,16,128]{2,1,0:T(8,128)(2,1)S(1)} %get-tuple-element.50.refs_1_), custom_call_target="tpu_custom_call" | custom-call | tf_op jit(solution)/shard_map/correlate/pallas_call | solution.py:264
  44.0 0.2 collective-permute-done.10.refs_1_
  44.3 3.3 %correlate.4.refs_2_ = f32[5,256,256]{2,1,0:T(8,128)S(1)} custom-call(s32[16]{0:T(128)S(1)} %bitcast.6, bf16[25,16,128]{2,1,0:T(8,128)(2,1)S(1)} %collective-permute-done.9.refs_0_, bf16[32,16,128]{2,1,0:T(8,128)(2,1)S(1)} %collective-permute-done.10.refs_1_, f32[5,256,256]{2,1,0:T(8,128)S(1)} %correlate.3.refs_2_), custom_call_target="tpu_custom_call" | custom-call | tf_op jit(solution)/shard_map/correlate/pallas_call | solution.py:264
  47.6 0.0 collective-permute-done.8.refs_1_
  47.6 3.3 %correlate.5.refs_2_ = f32[5,256,256]{2,1,0:T(8,128)S(1)} custom-call(s32[16]{0:T(128)S(1)} %bitcast.7, bf16[25,16,128]{2,1,0:T(8,128)(2,1)S(1)} %collective-permute-done.7.refs_0_, bf16[32,16,128]{2,1,0:T(8,128)(2,1)S(1)} %collective-permute-done.8.refs_1_, f32[5,256,256]{2,1,0:T(8,128)S(1)} %correlate.4.refs_2_), custom_call_target="tpu_custom_call" | custom-call | tf_op jit(solution)/shard_map/correlate/pallas_call | solution.py:264
  50.9 0.0 collective-permute-done.6.refs_1_
  50.9 4.7 %correlate_last.1 = f32[5,8,8,1001]{3,2,1,0:T(8,128)} custom-call(s32[16]{0:T(128)S(1)} %bitcast.8, bf16[25,16,128]{2,1,0:T(8,128)(2,1)S(1)} %collective-permute-done.5.refs_0_, bf16[32,16,128]{2,1,0:T(8,128)(2,1)S(1)} %collective-permute-done.6.refs_1_, f32[5,256,256]{2,1,0:T(8,128)S(1)} %correlate.5.refs_2_), custom_call_target="tpu_custom_call" | custom-call | tf_op jit(solution)/shard_map/correlate_last/pallas_call | solution.py:264
  (2 shorter events, 0.1 us)
Async XLA Ops:
  1.2 9.8 %all-to-all-start = ((s32[8,1,2]{2,1,0:T(1,128)}), s32[8,1,2]{2,1,0:T(1,128)S(1)}, u32[]{:S(2)}, u32[]{:S(2)}) async-start(s32[8,1,2]{2,1,0:T(1,128)} %broadcast_in_dim.2), calls=%async_computation | async-start | bytes 8192 | tf_op jit(solution)/shard_map/all_to_all | solution.py:288
  6.4 0.7 %copy-start.1 = (f32[255]{0:T(256)S(1)}, f32[255]{0:T(256)}, u32[]{:S(2)}) copy-start(f32[255]{0:T(256)} %param.5) | copy-start | bytes 3064
  11.0 13.7 %copy-start = (s32[16,1]{0,1:T(1,128)S(1)}, s32[16,1]{0,1:T(1,128)}, u32[]{:S(2)}) copy-start(s32[16,1]{0,1:T(1,128)} %param.7) | copy-start | bytes 196
  16.9 1.9 %collective-permute-start = (bf16[384,384]{1,0:T(8,128)(2,1)S(1)}, bf16[384,384]{1,0:T(8,128)(2,1)S(1)}, u32[]{:S(2)}, u32[]{:S(2)}) collective-permute-start(bf16[384,384]{1,0:T(8,128)(2,1)S(1)} %get-tuple-element.30), channel_id=1, source_target_pairs={{0,1},{1,0},{2,3},{3,2},{4,5},{5,4},{6,7},{7,6},{8,9},{9,8},{10,11... | collective-permute-start | bytes 884744 | tf_op jit(solution)/shard_map/ppermute | solution.py:330
  17.0 5.7 %collective-permute-start.1 = (bf16[128,384]{1,0:T(8,128)(2,1)S(1)}, bf16[128,384]{1,0:T(8,128)(2,1)S(1)}, u32[]{:S(2)}, u32[]{:S(2)}) collective-permute-start(bf16[128,384]{1,0:T(8,128)(2,1)S(1)} %get-tuple-element.32), channel_id=1, source_target_pairs={{0,2},{1,3},{2,0},{3,1},{4,6},{5,7},{6,4},{7,5},{8,10},{9,11},{10,... | collective-permute-start | bytes 294920 | tf_op jit(solution)/shard_map/ppermute | solution.py:330
  17.6 7.1 %collective-permute-start.2 = (bf16[128,384]{1,0:T(8,128)(2,1)S(1)}, bf16[128,384]{1,0:T(8,128)(2,1)S(1)}, u32[]{:S(2)}, u32[]{:S(2)}) collective-permute-start(bf16[128,384]{1,0:T(8,128)(2,1)S(1)} %get-tuple-element.34), channel_id=1, source_target_pairs={{0,3},{1,2},{2,1},{3,0},{4,7},{5,6},{6,5},{7,4},{8,11},{9,10},{10,... | collective-permute-start | bytes 294920 | tf_op jit(solution)/shard_map/ppermute | solution.py:330
  22.7 10.2 %collective-permute-start.3 = (bf16[256,384]{1,0:T(8,128)(2,1)S(1)}, bf16[256,384]{1,0:T(8,128)(2,1)S(1)}, u32[]{:S(2)}, u32[]{:S(2)}) collective-permute-start(bf16[256,384]{1,0:T(8,128)(2,1)S(1)} %get-tuple-element.35), channel_id=1, source_target_pairs={{0,4},{1,5},{2,6},{3,7},{4,0},{5,1},{6,2},{7,3},{8,12},{9,13},{10,... | collective-permute-start | bytes 589832 | tf_op jit(solution)/shard_map/ppermute | solution.py:330
  23.3 9.7 %collective-permute-start.4 = (bf16[256,384]{1,0:T(8,128)(2,1)S(1)}, bf16[256,384]{1,0:T(8,128)(2,1)S(1)}, u32[]{:S(2)}, u32[]{:S(2)}) collective-permute-start(bf16[256,384]{1,0:T(8,128)(2,1)S(1)} %get-tuple-element.36), channel_id=1, source_target_pairs={{0,6},{1,7},{2,4},{3,5},{4,2},{5,3},{6,0},{7,1},{8,14},{9,15},{10,... | collective-permute-start | bytes 589832 | tf_op jit(solution)/shard_map/ppermute | solution.py:330
  25.6 8.4 %collective-permute-start.7 = (bf16[25,16,128]{2,1,0:T(8,128)(2,1)S(1)}, bf16[25,16,128]{2,1,0:T(8,128)(2,1)S(1)}, u32[]{:S(2)}, u32[]{:S(2)}) collective-permute-start(bf16[25,16,128]{2,1,0:T(8,128)(2,1)S(1)} %get-tuple-element.42), channel_id=1, source_target_pairs={{0,24},{8,0},{16,8},{24,16},{1,25},{9,1},{17,9},{25,17},{2,26},{10... | collective-permute-start | bytes 307208 | tf_op jit(solution)/shard_map/ppermute | solution.py:381
  29.3 7.0 %collective-permute-start.9 = (bf16[25,16,128]{2,1,0:T(8,128)(2,1)S(1)}, bf16[25,16,128]{2,1,0:T(8,128)(2,1)S(1)}, u32[]{:S(2)}, u32[]{:S(2)}) collective-permute-start(bf16[25,16,128]{2,1,0:T(8,128)(2,1)S(1)} %get-tuple-element.46), channel_id=1, source_target_pairs={{0,8},{8,16},{16,24},{24,0},{1,9},{9,17},{17,25},{25,1},{2,10},{10... | collective-permute-start | bytes 307208 | tf_op jit(solution)/shard_map/ppermute | solution.py:381
  29.3 11.4 %collective-permute-start.5 = (bf16[25,16,128]{2,1,0:T(8,128)(2,1)S(1)}, bf16[25,16,128]{2,1,0:T(8,128)(2,1)S(1)}, u32[]{:S(2)}, u32[]{:S(2)}) collective-permute-start(bf16[25,16,128]{2,1,0:T(8,128)(2,1)S(1)} %get-tuple-element.38), channel_id=1, source_target_pairs={{0,16},{8,24},{16,0},{24,8},{1,17},{9,25},{17,1},{25,9},{2,18},{10... | collective-permute-start | bytes 307208 | tf_op jit(solution)/shard_map/ppermute | solution.py:381
  36.2 8.0 %collective-permute-start.10 = (bf16[32,16,128]{2,1,0:T(8,128)(2,1)S(1)}, bf16[32,16,128]{2,1,0:T(8,128)(2,1)S(1)}, u32[]{:S(2)}, u32[]{:S(2)}) collective-permute-start(bf16[32,16,128]{2,1,0:T(8,128)(2,1)S(1)} %get-tuple-element.48), channel_id=1, source_target_pairs={{0,8},{8,16},{16,24},{24,0},{1,9},{9,17},{17,25},{25,1},{2,10},{10... | collective-permute-start | bytes 393224 | tf_op jit(solution)/shard_map/ppermute | solution.py:381
  36.8 10.8 %collective-permute-start.8 = (bf16[32,16,128]{2,1,0:T(8,128)(2,1)S(1)}, bf16[32,16,128]{2,1,0:T(8,128)(2,1)S(1)}, u32[]{:S(2)}, u32[]{:S(2)}) collective-permute-start(bf16[32,16,128]{2,1,0:T(8,128)(2,1)S(1)} %get-tuple-element.44), channel_id=1, source_target_pairs={{0,24},{8,0},{16,8},{24,16},{1,25},{9,1},{17,9},{25,17},{2,26},{10... | collective-permute-start | bytes 393224 | tf_op jit(solution)/shard_map/ppermute | solution.py:381
  40.7 10.2 %collective-permute-start.6 = (bf16[32,16,128]{2,1,0:T(8,128)(2,1)S(1)}, bf16[32,16,128]{2,1,0:T(8,128)(2,1)S(1)}, u32[]{:S(2)}, u32[]{:S(2)}) collective-permute-start(bf16[32,16,128]{2,1,0:T(8,128)(2,1)S(1)} %get-tuple-element.40), channel_id=1, source_target_pairs={{0,16},{8,24},{16,0},{24,8},{1,17},{9,25},{17,1},{25,9},{2,18},{10... | collective-permute-start | bytes 393224 | tf_op jit(solution)/shard_map/ppermute | solution.py:381

commit v6 on v5

--- a/solution.py
+++ b/solution.py
@@ -58,7 +58,7 @@
     sends, (window, picked, sems) = refs[: len(groups)], refs[len(groups) :]
     rows, channels = raw.shape
     steps = [k for group in groups for k in group]
-    stripes = n_chan * STRIPES
+    stripes = len(steps) * STRIPES
     blocks_per = channels // n_chan // CB
     span = window.shape[2]
     me = lax.axis_index("chan")
@@ -66,24 +66,44 @@
     def place(p):
         c, k = me ^ steps[p // STRIPES], p % STRIPES
         start = (firsts[c, k] + c * blocks_per) * CB
-        base = jnp.minimum(start - lax.rem(start, LANES), channels - span)
-        return start, pl.multiple_of(base, LANES)
-
-    def copy(p):
-        base = place(p)[1]
-        return pltpu.make_async_copy(raw.at[:, pl.ds(base, span)], window.at[p], sems.at[p])
+        offset = lax.rem(start, LANES)
+        base = pl.multiple_of(start - offset, LANES)
+        return start, offset, base, (offset > LANES - WIDE) & (base < channels - LANES)
+
+    def copy(p, tile):
+        base = place(p)[2]
+        if tile:
+            base = pl.multiple_of(jnp.minimum(base + LANES, channels - LANES), LANES)
+        return pltpu.make_async_copy(
+            raw.at[:, pl.ds(base, LANES)],
+            window.at[p, :, pl.ds(tile * LANES, LANES)],
+            sems.at[p, tile],
+        )
 
     for p in range(stripes):
-        copy(p).start()
+        copy(p, 0).start()
+
+        @pl.when(place(p)[3])
+        def _(p=p):
+            copy(p, 1).start()
 
     row = lax.broadcasted_iota(jnp.int32, (WIDE, span), 0)
     lane = lax.broadcasted_iota(jnp.int32, (WIDE, span), 1)
     batch = 2 * STRIPES
     for first in range(0, stripes, batch):
         for p in range(first, first + batch):
-            copy(p).wait()
-            start, base = place(p)
-            hot = (lane == row + (start - base)) & (row < channels - start)
+            start, offset, _, both = place(p)
+            copy(p, 0).wait()
+
+            @pl.when(both)
+            def _(p=p):
+                copy(p, 1).wait()
+
+            @pl.when(jnp.logical_not(both))
+            def _(p=p):
+                window[p, :, LANES:] = jnp.zeros((rows, LANES), jnp.float32)
+
+            hot = (lane == row + offset) & (row < channels - start)
             hot = jnp.where(hot, 1.0, 0.0).astype(jnp.bfloat16)
             block = window[p].astype(jnp.bfloat16)
             chosen = lax.dot_general(hot, block, NT, preferred_element_type=jnp.float32)
@@ -308,29 +328,38 @@
     )(whitening_taps.reshape(1, TAPS))
 
     relayed = n_chan == 8 and outs % LANES == 0
-    groups = [[2], [3], [1, 5, 7], [4], [6], [0]] if relayed else [[k] for k in range(n_chan)]
-    sends = pl.pallas_call(
-        functools.partial(select_kernel, n_chan, groups),
-        out_shape=[
-            jax.ShapeDtypeStruct((len(group) * count, outs + 2 * SPILL), jnp.bfloat16)
-            for group in groups
-        ],
-        in_specs=[smem(), pl.BlockSpec(memory_space=pl.ANY), vmem()],
-        out_specs=[vmem()] * len(groups),
-        scratch_shapes=[
-            pltpu.VMEM((n_chan * STRIPES, rows, 2 * LANES), jnp.float32),
-            pltpu.VMEM((n_chan * count, rows), jnp.bfloat16),
-            pltpu.SemaphoreType.DMA((n_chan * STRIPES,)),
-        ],
-        compiler_params=params(40),
-        name="select_filter",
-    )(firsts, raw_strain, weights)
+    if relayed:
+        parts = [[[2], [3]], [[1, 5, 7], [4], [6], [0]]]
+    else:
+        parts = [[[k] for k in range(n_chan)]]
+    sends = []
+    for groups in parts:
+        steps = sum(len(group) for group in groups)
+        sends += pl.pallas_call(
+            functools.partial(select_kernel, n_chan, groups),
+            out_shape=[
+                jax.ShapeDtypeStruct((len(group) * count, outs + 2 * SPILL), jnp.bfloat16)
+                for group in groups
+            ],
+            in_specs=[smem(), pl.BlockSpec(memory_space=pl.ANY), vmem()],
+            out_specs=[vmem()] * len(groups),
+            scratch_shapes=[
+                pltpu.VMEM((steps * STRIPES, rows, 2 * LANES), jnp.float32),
+                pltpu.VMEM((steps * count, rows), jnp.bfloat16),
+                pltpu.SemaphoreType.DMA((steps * STRIPES, 2)),
+            ],
+            compiler_params=params(40),
+            name="select_filter",
+        )(firsts, raw_strain, weights)
+        weights, sends = lax.optimization_barrier((weights, sends))
 
     def exchange(value, k):
         return lax.ppermute(value, "chan", [(c, c ^ k) for c in range(n_chan)])
 
     if relayed:
-        got = [sends[5], exchange(sends[0], 2), exchange(sends[1], 3), exchange(sends[2], 1)]
+        near = exchange(sends[0], 2)
+        handed, near = lax.optimization_barrier((sends[2], near))
+        got = [sends[5], near, exchange(sends[1], 3), exchange(handed, 1)]
         across = [
             jnp.concatenate([sends[3 + at], got[3][(1 + at) * count : (2 + at) * count]], 0)
             for at in range(2)

time: 56.2 us -> 60.1 us (1.069)
  waiting for transfers between devices: 13.3 us -> 16.2 us
  Pallas kernels: 22.7 us -> 24.5 us
    ppermute x5, waiting for transfers between devices: 6.35 us -> 8.51 us  [exchange(): return lax.ppermute(value, 'chan', [(c, c ^ k) for c in range(n_chan)])]
    pallas_call x1 -> x2, Pallas kernels: 5.93 us -> 7.78 us  [local(): pl.pallas_call(functools.partial(select_kernel, n_chan, groups), out_shap...]
    ppermute x6, waiting for transfers between devices: 3.16 us -> 3.91 us  [local(): arrived[shift].append(lax.ppermute(value, 'tgroup', route))]
  transfers between devices with their start and end apart: 12 -> 12, of which waited for: 6 -> 8; matrix products, arithmetic and copies ran while one was open for 0% -> 0% of each run, Pallas kernels for 22% -> 20%
where the time goes in v6:
time: 60.1 us; the launch traced here: 59.9 us
  Pallas kernels  24.5 us (41%)
  starting transfers between devices  17.1 us (28%)
  waiting for transfers between devices  16.2 us (27%)
  local copies, waits for them, and re-layouts  1.95 us (3%)
    pallas_call x4, Pallas kernels, correlate(): pl.pallas_call(functools.partial(correlate_kernel, n_chan, factor, last),...  14.6 us
    ppermute x5, waiting for transfers between devices, exchange(): return lax.ppermute(value, 'chan', [(c, c ^ k) for c in range(n_chan)])  8.51 us
    ppermute x6, starting transfers between devices, local(): arrived[shift].append(lax.ppermute(value, 'tgroup', route))  8.5 us
    pallas_call x2, Pallas kernels, local(): pl.pallas_call(functools.partial(select_kernel, n_chan, groups), out_shap...  7.78 us
    all_to_all x1, starting transfers between devices, local(): lax.all_to_all(jnp.broadcast_to(first_block[None, :], (n_chan, STRIPES)),...  5.17 us
    ppermute x6, waiting for transfers between devices, local(): arrived[shift].append(lax.ppermute(value, 'tgroup', route))  3.91 us
    all_to_all x1, waiting for transfers between devices, local(): lax.all_to_all(jnp.broadcast_to(first_block[None, :], (n_chan, STRIPES)),...  3.76 us
    ppermute x5, starting transfers between devices, exchange(): return lax.ppermute(value, 'chan', [(c, c ^ k) for c in range(n_chan)])  3.4 us
  transfers between devices with their start and end apart: 12, of which 8 were waited for; matrix products, arithmetic and copies ran while one was open for 0% of the time, Pallas kernels for 20%

profile of v6, /device:TPU:0, one launch (start us, length us, event | category | flops | bytes accessed | tf_op | source)
XLA Modules:
  0.0 59.9 jit_solution(2588861646757139895)
XLA Ops:
  0.0 1.2 %broadcast_in_dim.2 = s32[8,1,2]{2,1,0:T(1,128)} broadcast(s32[2]{0:T(128)} %param.6), dimensions={2} | broadcast | bytes 72 | tf_op jit(solution)/shard_map/broadcast_in_dim | solution.py:309
  1.2 5.2 %all-to-all-start = ((s32[8,1,2]{2,1,0:T(1,128)}), s32[8,1,2]{2,1,0:T(1,128)S(1)}, u32[]{:S(2)}, u32[]{:S(2)}) async-start(s32[8,1,2]{2,1,0:T(1,128)} %broadcast_in_dim.2), calls=%async_computation | async-start | bytes 8192 | tf_op jit(solution)/shard_map/all_to_all | solution.py:308
  6.4 0.0 copy-start.1
  6.4 0.7 %copy-done.1 = f32[255]{0:T(256)S(1)} copy-done((f32[255]{0:T(256)S(1)}, f32[255]{0:T(256)}, u32[]{:S(2)}) %copy-start.1) | copy-done | bytes 1044
  7.1 0.1 fir_weights.1.weights
  7.2 3.8 %all-to-all-done = s32[8,1,2]{2,1,0:T(1,128)S(1)} async-done(((s32[8,1,2]{2,1,0:T(1,128)}), s32[8,1,2]{2,1,0:T(1,128)S(1)}, u32[]{:S(2)}, u32[]{:S(2)}) %all-to-all-start) | async-done | bytes 96 | tf_op jit(solution)/shard_map/all_to_all | solution.py:308
  11.0 2.8 %select_filter.2 = (bf16[128,384]{1,0:T(8,128)(2,1)S(1)}, bf16[128,384]{1,0:T(8,128)(2,1)S(1)}) custom-call(s32[8,2]{1,0:T(8,128)S(1)} %bitcast.3, f32[512,10240]{1,0:T(8,128)} %raw.3, bf16[384,512]{1,0:T(8,128)(2,1)S(1)} %fir_weights.1.weights), custom_call_target="tpu_custom_call" | custom-call | tf_op jit(solution)/shard_map/select_filter/pallas_call | solution.py:338
  13.8 0.0 copy-start
  13.8 5.0 %select_filter.3 = (bf16[384,384]{1,0:T(8,128)(2,1)S(1)}, bf16[128,384]{1,0:T(8,128)(2,1)S(1)}, bf16[128,384]{1,0:T(8,128)(2,1)S(1)}, bf16[128,384]{1,0:T(8,128)(2,1)S(1)}) custom-call(s32[8,2]{1,0:T(8,128)S(1)} %bitcast.4, f32[512,10240]{1,0:T(8,128)} %raw.3, bf16[384,512]{1,0:T(8,128)(2,1)S(1)} %fir_weights.1.weights), custom_call_target="tpu_custom_call" | custom-call | tf_op jit(solution)/shard_map/select_filter/pallas_call | solution.py:338
  18.8 0.6 %collective-permute-start = (bf16[128,384]{1,0:T(8,128)(2,1)S(1)}, bf16[128,384]{1,0:T(8,128)(2,1)S(1)}, u32[]{:S(2)}, u32[]{:S(2)}) collective-permute-start(bf16[128,384]{1,0:T(8,128)(2,1)S(1)} %get-tuple-element.51), channel_id=1, source_target_pairs={{0,2},{1,3},{2,0},{3,1},{4,6},{5,7},{6,4},{7,5},{8,10},{9,11},{10,... | collective-permute-start | bytes 294920 | tf_op jit(solution)/shard_map/ppermute | solution.py:357
  19.4 4.1 %collective-permute-done.refs_1_ = bf16[128,384]{1,0:T(8,128)(2,1)S(1)} collective-permute-done((bf16[128,384]{1,0:T(8,128)(2,1)S(1)}, bf16[128,384]{1,0:T(8,128)(2,1)S(1)}, u32[]{:S(2)}, u32[]{:S(2)}) %collective-permute-start) | collective-permute-done | bytes 98336 | tf_op jit(solution)/shard_map/ppermute | solution.py:357
  23.5 0.0 collective-permute-start.1
  23.5 0.7 %collective-permute-start.2 = (bf16[128,384]{1,0:T(8,128)(2,1)S(1)}, bf16[128,384]{1,0:T(8,128)(2,1)S(1)}, u32[]{:S(2)}, u32[]{:S(2)}) collective-permute-start(bf16[128,384]{1,0:T(8,128)(2,1)S(1)} %get-tuple-element.56), channel_id=1, source_target_pairs={{0,3},{1,2},{2,1},{3,0},{4,7},{5,6},{6,5},{7,4},{8,11},{9,10},{10,... | collective-permute-start | bytes 294920 | tf_op jit(solution)/shard_map/ppermute | solution.py:357
  24.2 0.9 %collective-permute-done.1.refs_3_ = bf16[384,384]{1,0:T(8,128)(2,1)S(1)} collective-permute-done((bf16[384,384]{1,0:T(8,128)(2,1)S(1)}, bf16[384,384]{1,0:T(8,128)(2,1)S(1)}, u32[]{:S(2)}, u32[]{:S(2)}) %collective-permute-start.1) | collective-permute-done | bytes 294944 | tf_op jit(solution)/shard_map/ppermute | solution.py:357
  25.2 0.6 %collective-permute-start.3 = (bf16[256,384]{1,0:T(8,128)(2,1)S(1)}, bf16[256,384]{1,0:T(8,128)(2,1)S(1)}, u32[]{:S(2)}, u32[]{:S(2)}) collective-permute-start(bf16[256,384]{1,0:T(8,128)(2,1)S(1)} %get-tuple-element.57), channel_id=1, source_target_pairs={{0,4},{1,5},{2,6},{3,7},{4,0},{5,1},{6,2},{7,3},{8,12},{9,13},{10,... | collective-permute-start | bytes 589832 | tf_op jit(solution)/shard_map/ppermute | solution.py:357
  25.8 1.5 %collective-permute-start.4 = (bf16[256,384]{1,0:T(8,128)(2,1)S(1)}, bf16[256,384]{1,0:T(8,128)(2,1)S(1)}, u32[]{:S(2)}, u32[]{:S(2)}) collective-permute-start(bf16[256,384]{1,0:T(8,128)(2,1)S(1)} %get-tuple-element.58), channel_id=1, source_target_pairs={{0,6},{1,7},{2,4},{3,5},{4,2},{5,3},{6,0},{7,1},{8,14},{9,15},{10,... | collective-permute-start | bytes 589832 | tf_op jit(solution)/shard_map/ppermute | solution.py:357
  27.2 0.7 %collective-permute-done.2.refs_2_ = bf16[128,384]{1,0:T(8,128)(2,1)S(1)} collective-permute-done((bf16[128,384]{1,0:T(8,128)(2,1)S(1)}, bf16[128,384]{1,0:T(8,128)(2,1)S(1)}, u32[]{:S(2)}, u32[]{:S(2)}) %collective-permute-start.2) | collective-permute-done | bytes 98336 | tf_op jit(solution)/shard_map/ppermute | solution.py:357
  27.9 0.0 copy-done
  27.9 0.9 %place_first.1 = (bf16[25,16,128]{2,1,0:T(8,128)(2,1)S(1)}, bf16[25,16,128]{2,1,0:T(8,128)(2,1)S(1)}, bf16[25,16,128]{2,1,0:T(8,128)(2,1)S(1)}, bf16[25,16,128]{2,1,0:T(8,128)(2,1)S(1)}) custom-call(s32[16]{0:T(128)S(1)} %bitcast.5, bf16[128,384]{1,0:T(8,128)(2,1)S(1)} %get-tuple-element.48.refs_0_, bf16[128,384]{1,0:T(8,128)(2,1)S(1)} %collective-permute-done.refs_1_, ...), custom_call_target="tpu_custom_call" | custom-call | tf_op jit(solution)/shard_map/place_first/pallas_call | solution.py:392
  28.9 3.7 %collective-permute-start.7 = (bf16[25,16,128]{2,1,0:T(8,128)(2,1)S(1)}, bf16[25,16,128]{2,1,0:T(8,128)(2,1)S(1)}, u32[]{:S(2)}, u32[]{:S(2)}) collective-permute-start(bf16[25,16,128]{2,1,0:T(8,128)(2,1)S(1)} %get-tuple-element.64), channel_id=1, source_target_pairs={{0,24},{8,0},{16,8},{24,16},{1,25},{9,1},{17,9},{25,17},{2,26},{10... | collective-permute-start | bytes 307208 | tf_op jit(solution)/shard_map/ppermute | solution.py:410
  32.5 0.0 collective-permute-start.9
  32.5 1.0 %collective-permute-start.5 = (bf16[25,16,128]{2,1,0:T(8,128)(2,1)S(1)}, bf16[25,16,128]{2,1,0:T(8,128)(2,1)S(1)}, u32[]{:S(2)}, u32[]{:S(2)}) collective-permute-start(bf16[25,16,128]{2,1,0:T(8,128)(2,1)S(1)} %get-tuple-element.60), channel_id=1, source_target_pairs={{0,16},{8,24},{16,0},{24,8},{1,17},{9,25},{17,1},{25,9},{2,18},{10... | collective-permute-start | bytes 307208 | tf_op jit(solution)/shard_map/ppermute | solution.py:410
  33.5 2.8 %collective-permute-done.3.refs_4_ = bf16[256,384]{1,0:T(8,128)(2,1)S(1)} collective-permute-done((bf16[256,384]{1,0:T(8,128)(2,1)S(1)}, bf16[256,384]{1,0:T(8,128)(2,1)S(1)}, u32[]{:S(2)}, u32[]{:S(2)}) %collective-permute-start.3) | collective-permute-done | bytes 196640 | tf_op jit(solution)/shard_map/ppermute | solution.py:357
  36.4 0.0 collective-permute-done.4.refs_5_
  36.4 1.1 %place_second.1 = (bf16[32,16,128]{2,1,0:T(8,128)(2,1)S(1)}, bf16[32,16,128]{2,1,0:T(8,128)(2,1)S(1)}, bf16[32,16,128]{2,1,0:T(8,128)(2,1)S(1)}, bf16[32,16,128]{2,1,0:T(8,128)(2,1)S(1)}) custom-call(s32[16]{0:T(128)S(1)} %bitcast.6, bf16[128,384]{1,0:T(8,128)(2,1)S(1)} %get-tuple-element.48.refs_0_, bf16[128,384]{1,0:T(8,128)(2,1)S(1)} %collective-permute-done.refs_1_, ...), custom_call_target="tpu_custom_call" | custom-call | tf_op jit(solution)/shard_map/place_second/pallas_call | solution.py:392
  37.4 0.0 collective-permute-done.7.refs_0_
  37.4 2.7 %collective-permute-done.9.refs_0_ = bf16[25,16,128]{2,1,0:T(8,128)(2,1)S(1)} collective-permute-done((bf16[25,16,128]{2,1,0:T(8,128)(2,1)S(1)}, bf16[25,16,128]{2,1,0:T(8,128)(2,1)S(1)}, u32[]{:S(2)}, u32[]{:S(2)}) %collective-permute-start.9) | collective-permute-done | bytes 102432 | tf_op jit(solution)/shard_map/ppermute | solution.py:410
  40.1 0.3 collective-permute-start.10
  40.4 3.5 %collective-permute-start.8 = (bf16[32,16,128]{2,1,0:T(8,128)(2,1)S(1)}, bf16[32,16,128]{2,1,0:T(8,128)(2,1)S(1)}, u32[]{:S(2)}, u32[]{:S(2)}) collective-permute-start(bf16[32,16,128]{2,1,0:T(8,128)(2,1)S(1)} %get-tuple-element.66), channel_id=1, source_target_pairs={{0,24},{8,0},{16,8},{24,16},{1,25},{9,1},{17,9},{25,17},{2,26},{10... | collective-permute-start | bytes 393224 | tf_op jit(solution)/shard_map/ppermute | solution.py:410
  44.0 1.0 %collective-permute-done.5.refs_0_ = bf16[25,16,128]{2,1,0:T(8,128)(2,1)S(1)} collective-permute-done((bf16[25,16,128]{2,1,0:T(8,128)(2,1)S(1)}, bf16[25,16,128]{2,1,0:T(8,128)(2,1)S(1)}, u32[]{:S(2)}, u32[]{:S(2)}) %collective-permute-start.5) | collective-permute-done | bytes 102432 | tf_op jit(solution)/shard_map/ppermute | solution.py:410
  44.9 0.0 collective-permute-start.6
  44.9 3.3 %correlate.3.refs_2_ = f32[5,256,256]{2,1,0:T(8,128)S(1)} custom-call(s32[16]{0:T(128)S(1)} %bitcast.7, bf16[25,16,128]{2,1,0:T(8,128)(2,1)S(1)} %get-tuple-element.71.refs_0_, bf16[32,16,128]{2,1,0:T(8,128)(2,1)S(1)} %get-tuple-element.72.refs_1_), custom_call_target="tpu_custom_call" | custom-call | tf_op jit(solution)/shard_map/correlate/pallas_call | solution.py:284
  48.2 0.2 collective-permute-done.10.refs_1_
  48.5 3.3 %correlate.4.refs_2_ = f32[5,256,256]{2,1,0:T(8,128)S(1)} custom-call(s32[16]{0:T(128)S(1)} %bitcast.8, bf16[25,16,128]{2,1,0:T(8,128)(2,1)S(1)} %collective-permute-done.9.refs_0_, bf16[32,16,128]{2,1,0:T(8,128)(2,1)S(1)} %collective-permute-done.10.refs_1_, f32[5,256,256]{2,1,0:T(8,128)S(1)} %correlate.3.refs_2_), custom_call_target="tpu_custom_call" | custom-call | tf_op jit(solution)/shard_map/correlate/pallas_call | solution.py:284
  51.8 0.0 collective-permute-done.8.refs_1_
  51.8 3.3 %correlate.5.refs_2_ = f32[5,256,256]{2,1,0:T(8,128)S(1)} custom-call(s32[16]{0:T(128)S(1)} %bitcast.9, bf16[25,16,128]{2,1,0:T(8,128)(2,1)S(1)} %collective-permute-done.7.refs_0_, bf16[32,16,128]{2,1,0:T(8,128)(2,1)S(1)} %collective-permute-done.8.refs_1_, f32[5,256,256]{2,1,0:T(8,128)S(1)} %correlate.4.refs_2_), custom_call_target="tpu_custom_call" | custom-call | tf_op jit(solution)/shard_map/correlate/pallas_call | solution.py:284
  55.1 0.0 collective-permute-done.6.refs_1_
  55.1 4.7 %correlate_last.1 = f32[5,8,8,1001]{3,2,1,0:T(8,128)} custom-call(s32[16]{0:T(128)S(1)} %bitcast.10, bf16[25,16,128]{2,1,0:T(8,128)(2,1)S(1)} %collective-permute-done.5.refs_0_, bf16[32,16,128]{2,1,0:T(8,128)(2,1)S(1)} %collective-permute-done.6.refs_1_, f32[5,256,256]{2,1,0:T(8,128)S(1)} %correlate.5.refs_2_), custom_call_target="tpu_custom_call" | custom-call | tf_op jit(solution)/shard_map/correlate_last/pallas_call | solution.py:284
  (2 shorter events, 0.1 us)
Async XLA Ops:
  1.2 9.8 %all-to-all-start = ((s32[8,1,2]{2,1,0:T(1,128)}), s32[8,1,2]{2,1,0:T(1,128)S(1)}, u32[]{:S(2)}, u32[]{:S(2)}) async-start(s32[8,1,2]{2,1,0:T(1,128)} %broadcast_in_dim.2), calls=%async_computation | async-start | bytes 8192 | tf_op jit(solution)/shard_map/all_to_all | solution.py:308
  6.4 0.7 %copy-start.1 = (f32[255]{0:T(256)S(1)}, f32[255]{0:T(256)}, u32[]{:S(2)}) copy-start(f32[255]{0:T(256)} %param.5) | copy-start | bytes 3064
  13.8 14.2 %copy-start = (s32[16,1]{0,1:T(1,128)S(1)}, s32[16,1]{0,1:T(1,128)}, u32[]{:S(2)}) copy-start(s32[16,1]{0,1:T(1,128)} %param.7) | copy-start | bytes 196
  18.8 4.7 %collective-permute-start = (bf16[128,384]{1,0:T(8,128)(2,1)S(1)}, bf16[128,384]{1,0:T(8,128)(2,1)S(1)}, u32[]{:S(2)}, u32[]{:S(2)}) collective-permute-start(bf16[128,384]{1,0:T(8,128)(2,1)S(1)} %get-tuple-element.51), channel_id=1, source_target_pairs={{0,2},{1,3},{2,0},{3,1},{4,6},{5,7},{6,4},{7,5},{8,10},{9,11},{10,... | collective-permute-start | bytes 294920 | tf_op jit(solution)/shard_map/ppermute | solution.py:357
  23.5 1.6 %collective-permute-start.1 = (bf16[384,384]{1,0:T(8,128)(2,1)S(1)}, bf16[384,384]{1,0:T(8,128)(2,1)S(1)}, u32[]{:S(2)}, u32[]{:S(2)}) collective-permute-start(bf16[384,384]{1,0:T(8,128)(2,1)S(1)} %get-tuple-element.52), channel_id=1, source_target_pairs={{0,1},{1,0},{2,3},{3,2},{4,5},{5,4},{6,7},{7,6},{8,9},{9,8},{10,11... | collective-permute-start | bytes 884744 | tf_op jit(solution)/shard_map/ppermute | solution.py:357
  23.5 4.4 %collective-permute-start.2 = (bf16[128,384]{1,0:T(8,128)(2,1)S(1)}, bf16[128,384]{1,0:T(8,128)(2,1)S(1)}, u32[]{:S(2)}, u32[]{:S(2)}) collective-permute-start(bf16[128,384]{1,0:T(8,128)(2,1)S(1)} %get-tuple-element.56), channel_id=1, source_target_pairs={{0,3},{1,2},{2,1},{3,0},{4,7},{5,6},{6,5},{7,4},{8,11},{9,10},{10,... | collective-permute-start | bytes 294920 | tf_op jit(solution)/shard_map/ppermute | solution.py:357
  25.2 11.2 %collective-permute-start.3 = (bf16[256,384]{1,0:T(8,128)(2,1)S(1)}, bf16[256,384]{1,0:T(8,128)(2,1)S(1)}, u32[]{:S(2)}, u32[]{:S(2)}) collective-permute-start(bf16[256,384]{1,0:T(8,128)(2,1)S(1)} %get-tuple-element.57), channel_id=1, source_target_pairs={{0,4},{1,5},{2,6},{3,7},{4,0},{5,1},{6,2},{7,3},{8,12},{9,13},{10,... | collective-permute-start | bytes 589832 | tf_op jit(solution)/shard_map/ppermute | solution.py:357
  25.8 10.6 %collective-permute-start.4 = (bf16[256,384]{1,0:T(8,128)(2,1)S(1)}, bf16[256,384]{1,0:T(8,128)(2,1)S(1)}, u32[]{:S(2)}, u32[]{:S(2)}) collective-permute-start(bf16[256,384]{1,0:T(8,128)(2,1)S(1)} %get-tuple-element.58), channel_id=1, source_target_pairs={{0,6},{1,7},{2,4},{3,5},{4,2},{5,3},{6,0},{7,1},{8,14},{9,15},{10,... | collective-permute-start | bytes 589832 | tf_op jit(solution)/shard_map/ppermute | solution.py:357
  28.9 8.6 %collective-permute-start.7 = (bf16[25,16,128]{2,1,0:T(8,128)(2,1)S(1)}, bf16[25,16,128]{2,1,0:T(8,128)(2,1)S(1)}, u32[]{:S(2)}, u32[]{:S(2)}) collective-permute-start(bf16[25,16,128]{2,1,0:T(8,128)(2,1)S(1)} %get-tuple-element.64), channel_id=1, source_target_pairs={{0,24},{8,0},{16,8},{24,16},{1,25},{9,1},{17,9},{25,17},{2,26},{10... | collective-permute-start | bytes 307208 | tf_op jit(solution)/shard_map/ppermute | solution.py:410
  32.5 7.6 %collective-permute-start.9 = (bf16[25,16,128]{2,1,0:T(8,128)(2,1)S(1)}, bf16[25,16,128]{2,1,0:T(8,128)(2,1)S(1)}, u32[]{:S(2)}, u32[]{:S(2)}) collective-permute-start(bf16[25,16,128]{2,1,0:T(8,128)(2,1)S(1)} %get-tuple-element.68), channel_id=1, source_target_pairs={{0,8},{8,16},{16,24},{24,0},{1,9},{9,17},{17,25},{25,1},{2,10},{10... | collective-permute-start | bytes 307208 | tf_op jit(solution)/shard_map/ppermute | solution.py:410
  32.5 12.4 %collective-permute-start.5 = (bf16[25,16,128]{2,1,0:T(8,128)(2,1)S(1)}, bf16[25,16,128]{2,1,0:T(8,128)(2,1)S(1)}, u32[]{:S(2)}, u32[]{:S(2)}) collective-permute-start(bf16[25,16,128]{2,1,0:T(8,128)(2,1)S(1)} %get-tuple-element.60), channel_id=1, source_target_pairs={{0,16},{8,24},{16,0},{24,8},{1,17},{9,25},{17,1},{25,9},{2,18},{10... | collective-permute-start | bytes 307208 | tf_op jit(solution)/shard_map/ppermute | solution.py:410
  40.1 8.3 %collective-permute-start.10 = (bf16[32,16,128]{2,1,0:T(8,128)(2,1)S(1)}, bf16[32,16,128]{2,1,0:T(8,128)(2,1)S(1)}, u32[]{:S(2)}, u32[]{:S(2)}) collective-permute-start(bf16[32,16,128]{2,1,0:T(8,128)(2,1)S(1)} %get-tuple-element.70), channel_id=1, source_target_pairs={{0,8},{8,16},{16,24},{24,0},{1,9},{9,17},{17,25},{25,1},{2,10},{10... | collective-permute-start | bytes 393224 | tf_op jit(solution)/shard_map/ppermute | solution.py:410
  40.4 11.4 %collective-permute-start.8 = (bf16[32,16,128]{2,1,0:T(8,128)(2,1)S(1)}, bf16[32,16,128]{2,1,0:T(8,128)(2,1)S(1)}, u32[]{:S(2)}, u32[]{:S(2)}) collective-permute-start(bf16[32,16,128]{2,1,0:T(8,128)(2,1)S(1)} %get-tuple-element.66), channel_id=1, source_target_pairs={{0,24},{8,0},{16,8},{24,16},{1,25},{9,1},{17,9},{25,17},{2,26},{10... | collective-permute-start | bytes 393224 | tf_op jit(solution)/shard_map/ppermute | solution.py:410
  44.9 10.2 %collective-permute-start.6 = (bf16[32,16,128]{2,1,0:T(8,128)(2,1)S(1)}, bf16[32,16,128]{2,1,0:T(8,128)(2,1)S(1)}, u32[]{:S(2)}, u32[]{:S(2)}) collective-permute-start(bf16[32,16,128]{2,1,0:T(8,128)(2,1)S(1)} %get-tuple-element.62), channel_id=1, source_target_pairs={{0,16},{8,24},{16,0},{24,8},{1,17},{9,25},{17,1},{25,9},{2,18},{10... | collective-permute-start | bytes 393224 | tf_op jit(solution)/shard_map/ppermute | solution.py:410

commit v7 on v5

--- a/solution.py
+++ b/solution.py
@@ -24,7 +24,6 @@
 STEP = LANES // SHIFTS
 LAG_BLOCKS = -(-LAGS // LANES)
 FRONT = -(-MAXLAG // LANES) * LANES
-NT = (((1,), (1,)), ((), ()))
 
 
 def params(megabytes):
@@ -55,7 +54,7 @@
 
 
 def select_kernel(n_chan, groups, firsts, raw, weights, *refs):
-    sends, (window, picked, sems) = refs[: len(groups)], refs[len(groups) :]
+    sends, (window, sems) = refs[: len(groups)], refs[len(groups) :]
     rows, channels = raw.shape
     steps = [k for group in groups for k in group]
     stripes = n_chan * STRIPES
@@ -76,27 +75,30 @@
     for p in range(stripes):
         copy(p).start()
 
-    row = lax.broadcasted_iota(jnp.int32, (WIDE, span), 0)
-    lane = lax.broadcasted_iota(jnp.int32, (WIDE, span), 1)
-    batch = 2 * STRIPES
-    for first in range(0, stripes, batch):
-        for p in range(first, first + batch):
+    row = lax.broadcasted_iota(jnp.int32, (span, STRIPES * WIDE), 0)
+    column = lax.broadcasted_iota(jnp.int32, (span, STRIPES * WIDE), 1)
+    height = STRIPES * WIDE
+    for at, k in enumerate(steps):
+        hots, blocks = [], []
+        for i in range(STRIPES):
+            p = at * STRIPES + i
             copy(p).wait()
             start, base = place(p)
-            hot = (lane == row + (start - base)) & (row < channels - start)
-            hot = jnp.where(hot, 1.0, 0.0).astype(jnp.bfloat16)
-            block = window[p].astype(jnp.bfloat16)
-            chosen = lax.dot_general(hot, block, NT, preferred_element_type=jnp.float32)
-            picked[p * WIDE : (p + 1) * WIDE, :] = chosen.astype(jnp.bfloat16)
-        part = slice(first * WIDE, (first + batch) * WIDE)
-        result = lax.dot_general(
-            picked[part, :], weights[...], NT, preferred_element_type=jnp.float32
-        ).astype(jnp.bfloat16)
-        height = STRIPES * WIDE
-        for at in range(batch // STRIPES):
-            k = steps[first // STRIPES + at]
-            out, where = [(o, g.index(k)) for o, g in enumerate(groups) if k in g][0]
-            sends[out][where * height : (where + 1) * height, :] = result[at * height : (at + 1) * height]
+            channel = column - i * WIDE
+            hot = (row == channel + (start - base)) & (channel < channels - start)
+            hot = hot & (channel >= 0) & (channel < WIDE)
+            hots.append(jnp.where(hot, 1.0, 0.0).astype(jnp.bfloat16))
+            blocks.append(window[p].astype(jnp.bfloat16))
+        chosen = jnp.dot(
+            jnp.concatenate(blocks, 1),
+            jnp.concatenate(hots, 0),
+            preferred_element_type=jnp.float32,
+        )
+        result = jnp.dot(
+            weights[...], chosen.astype(jnp.bfloat16), preferred_element_type=jnp.float32
+        )
+        out, where = [(o, g.index(k)) for o, g in enumerate(groups) if k in g][0]
+        sends[out][where * height : (where + 1) * height, :] = result.T.astype(jnp.bfloat16)
 
 
 def add_spills(n_chan, outs, steps, got, total):
@@ -176,7 +178,7 @@
     out = refs[-5]
     arrived, before = refs[:2], (refs[2] if len(refs) == 8 else None)
     windows = (window_a, window_b)
-    span = lead.shape[2]
+    span = lead.shape[1]
     samples = span - LANES
     cols = span // LANES
     high = STEP * CB
@@ -201,10 +203,15 @@
 
     for p in range(STRIPES):
         value = series(p)
-        for a in range(CB):
-            spread = jnp.broadcast_to(value[a : a + 1], (SHIFTS, span))
-            turned = pltpu.roll(spread, 0, 1, stride=1, stride_axis=0)
-            lead[p, a * SHIFTS : (a + 1) * SHIFTS, :] = turned.astype(jnp.bfloat16)
+        for first in range(0, CB, STEP):
+            turned = [
+                pltpu.roll(
+                    jnp.broadcast_to(value[a : a + 1], (SHIFTS, span)), 0, 1, stride=1, stride_axis=0
+                )
+                for a in range(first, first + STEP)
+            ]
+            turned = jnp.concatenate(turned, 0).T.astype(jnp.bfloat16)
+            lead[p, :, first * SHIFTS : (first + STEP) * SHIFTS] = turned
 
     def bounds(i):
         return max(0, ahead - i), min(cols, ahead + cols - i)
@@ -218,7 +225,15 @@
             if end < cols:
                 window[rows, end * LANES :] = jnp.zeros((high, (cols - end) * LANES), jnp.bfloat16)
 
-    group = lax.broadcasted_iota(jnp.int32, (CB, LANES), 1) // SHIFTS
+    lane = lax.broadcasted_iota(jnp.int32, (CB, LANES), 1)
+    left, even = lane < 2 * SHIFTS, (lane // SHIFTS) % 2 == 0
+
+    def swap(one, two, keep, by):
+        return (
+            jnp.where(keep, one, pltpu.roll(two, by, 1)),
+            jnp.where(keep, pltpu.roll(one, LANES - by, 1), two),
+        )
+
     for s in range(SLOTS):
         window = windows[s % 2]
         value = series(STRIPES + s)
@@ -231,7 +246,7 @@
                 :, (first + i - ahead) * LANES : (end + i - ahead) * LANES
             ]
         which = jnp.where(s < first_count, 0, 1)
-        summed = lax.dot_general(window[...], lead[which], NT, preferred_element_type=jnp.float32)
+        summed = jnp.dot(window[...], lead[which], preferred_element_type=jnp.float32)
         if before is not None:
             summed = summed + before[s]
         if not last:
@@ -242,16 +257,15 @@
             width = min(LANES, LAGS - i * LANES)
             for h in range(CB // STEP):
                 parts = [
-                    summed[(i * STEP + n) * CB : (i * STEP + n + 1) * CB, h * LANES : (h + 1) * LANES]
+                    summed[i * high + n * CB : i * high + (n + 1) * CB, h * LANES : (h + 1) * LANES]
                     for n in range(STEP)
                 ]
+                parts[0], parts[2] = swap(parts[0], parts[2], left, 2 * SHIFTS)
+                parts[1], parts[3] = swap(parts[1], parts[3], left, 2 * SHIFTS)
+                parts[0], parts[1] = swap(parts[0], parts[1], even, SHIFTS)
+                parts[2], parts[3] = swap(parts[2], parts[3], even, SHIFTS)
                 for a in range(STEP):
-                    value = parts[a]
-                    for n in range(STEP):
-                        if n != a:
-                            moved = pltpu.roll(parts[n], (SHIFTS * (n - a)) % LANES, 1)
-                            value = jnp.where(group == n, moved, value)
-                    out[s, h * STEP + a, :, i * LANES : i * LANES + width] = value[:, :width]
+                    out[s, h * STEP + a, :, i * LANES : i * LANES + width] = parts[a][:, :width]
 
 
 def correlate(n_chan, owners, arrived, before, factor, last, samples):
@@ -267,7 +281,7 @@
         in_specs=[smem()] + [vmem()] * (len(operands) - 1),
         out_specs=vmem(),
         scratch_shapes=[
-            pltpu.VMEM((STRIPES, wide, samples + LANES), jnp.bfloat16),
+            pltpu.VMEM((STRIPES, samples + LANES, wide), jnp.bfloat16),
             pltpu.VMEM((high, samples + LANES), jnp.bfloat16),
             pltpu.VMEM((high, samples + LANES), jnp.bfloat16),
             pltpu.VMEM((BLOCKS, CB, samples), jnp.float32),
@@ -319,7 +333,6 @@
         out_specs=[vmem()] * len(groups),
         scratch_shapes=[
             pltpu.VMEM((n_chan * STRIPES, rows, 2 * LANES), jnp.float32),
-            pltpu.VMEM((n_chan * count, rows), jnp.bfloat16),
             pltpu.SemaphoreType.DMA((n_chan * STRIPES,)),
         ],
         compiler_params=params(40),

time: 56.2 us -> 62.2 us (1.11)
  Pallas kernels: 22.7 us -> 29.2 us
    pallas_call x4, Pallas kernels: 14.6 us -> 19 us  [correlate(): pl.pallas_call(functools.partial(correlate_kernel, n_chan, factor, last),...]
    pallas_call x1, Pallas kernels: 5.93 us -> 8.09 us  [local(): pl.pallas_call(functools.partial(select_kernel, n_chan, groups), out_shap...]
  transfers between devices with their start and end apart: 12 -> 12, of which waited for: 6 -> 5; matrix products, arithmetic and copies ran while one was open for 0% -> 0% of each run, Pallas kernels for 22% -> 23%
where the time goes in v7:
time: 62.2 us; the launch traced here: 62 us
  Pallas kernels  29.2 us (47%)
  starting transfers between devices  17.6 us (28%)
  waiting for transfers between devices  13 us (21%)
  local copies, waits for them, and re-layouts  1.95 us (3%)
    pallas_call x4, Pallas kernels, correlate(): pl.pallas_call(functools.partial(correlate_kernel, n_chan, factor, last),...  19 us
    ppermute x6, starting transfers between devices, local(): arrived[shift].append(lax.ppermute(value, 'tgroup', route))  8.49 us
    pallas_call x1, Pallas kernels, local(): pl.pallas_call(functools.partial(select_kernel, n_chan, groups), out_shap...  8.09 us
    ppermute x5, waiting for transfers between devices, exchange(): return lax.ppermute(value, 'chan', [(c, c ^ k) for c in range(n_chan)])  6.35 us
    all_to_all x1, starting transfers between devices, local(): lax.all_to_all(jnp.broadcast_to(first_block[None, :], (n_chan, STRIPES)),...  5.17 us
    ppermute x5, starting transfers between devices, exchange(): return lax.ppermute(value, 'chan', [(c, c ^ k) for c in range(n_chan)])  3.96 us
    all_to_all x1, waiting for transfers between devices, local(): lax.all_to_all(jnp.broadcast_to(first_block[None, :], (n_chan, STRIPES)),...  3.76 us
    ppermute x6, waiting for transfers between devices, local(): arrived[shift].append(lax.ppermute(value, 'tgroup', route))  2.93 us
  transfers between devices with their start and end apart: 12, of which 5 were waited for; matrix products, arithmetic and copies ran while one was open for 0% of the time, Pallas kernels for 23%

profile of v7, /device:TPU:0, one launch (start us, length us, event | category | flops | bytes accessed | tf_op | source)
XLA Modules:
  0.0 62.0 jit_solution(17550136863323813060)
XLA Ops:
  0.0 1.2 %broadcast_in_dim.2 = s32[8,1,2]{2,1,0:T(1,128)} broadcast(s32[2]{0:T(128)} %param.6), dimensions={2} | broadcast | bytes 72 | tf_op jit(solution)/shard_map/broadcast_in_dim | solution.py:303
  1.2 5.2 %all-to-all-start = ((s32[8,1,2]{2,1,0:T(1,128)}), s32[8,1,2]{2,1,0:T(1,128)S(1)}, u32[]{:S(2)}, u32[]{:S(2)}) async-start(s32[8,1,2]{2,1,0:T(1,128)} %broadcast_in_dim.2), calls=%async_computation | async-start | bytes 8192 | tf_op jit(solution)/shard_map/all_to_all | solution.py:302
  6.4 0.0 copy-start.1
  6.4 0.7 %copy-done.1 = f32[255]{0:T(256)S(1)} copy-done((f32[255]{0:T(256)S(1)}, f32[255]{0:T(256)}, u32[]{:S(2)}) %copy-start.1) | copy-done | bytes 1044
  7.1 0.1 fir_weights.1.weights
  7.2 3.8 %all-to-all-done = s32[8,1,2]{2,1,0:T(1,128)S(1)} async-done(((s32[8,1,2]{2,1,0:T(1,128)}), s32[8,1,2]{2,1,0:T(1,128)S(1)}, u32[]{:S(2)}, u32[]{:S(2)}) %all-to-all-start) | async-done | bytes 96 | tf_op jit(solution)/shard_map/all_to_all | solution.py:302
  11.0 0.0 copy-start
  11.0 8.1 %select_filter.1 = (bf16[128,384]{1,0:T(8,128)(2,1)S(1)}, bf16[128,384]{1,0:T(8,128)(2,1)S(1)}, bf16[384,384]{1,0:T(8,128)(2,1)S(1)}, bf16[128,384]{1,0:T(8,128)...) custom-call(s32[8,2]{1,0:T(8,128)S(1)} %bitcast.9, f32[512,10240]{1,0:T(8,128)} %raw.1, ...), custom_call_target="tpu_custom_call" | custom-call | tf_op jit(solution)/shard_map/select_filter/pallas_call | solution.py:326
  19.1 0.1 collective-permute-start
  19.2 0.6 %collective-permute-start.1 = (bf16[128,384]{1,0:T(8,128)(2,1)S(1)}, bf16[128,384]{1,0:T(8,128)(2,1)S(1)}, u32[]{:S(2)}, u32[]{:S(2)}) collective-permute-start(bf16[128,384]{1,0:T(8,128)(2,1)S(1)} %get-tuple-element.32), channel_id=1, source_target_pairs={{0,2},{1,3},{2,0},{3,1},{4,6},{5,7},{6,4},{7,5},{8,10},{9,11},{10,... | collective-permute-start | bytes 294920 | tf_op jit(solution)/shard_map/ppermute | solution.py:343
  19.8 1.2 %collective-permute-start.2 = (bf16[128,384]{1,0:T(8,128)(2,1)S(1)}, bf16[128,384]{1,0:T(8,128)(2,1)S(1)}, u32[]{:S(2)}, u32[]{:S(2)}) collective-permute-start(bf16[128,384]{1,0:T(8,128)(2,1)S(1)} %get-tuple-element.34), channel_id=1, source_target_pairs={{0,3},{1,2},{2,1},{3,0},{4,7},{5,6},{6,5},{7,4},{8,11},{9,10},{10,... | collective-permute-start | bytes 294920 | tf_op jit(solution)/shard_map/ppermute | solution.py:343
  21.0 0.0 collective-permute-done.refs_3_
  21.1 3.7 %collective-permute-done.1.refs_1_ = bf16[128,384]{1,0:T(8,128)(2,1)S(1)} collective-permute-done((bf16[128,384]{1,0:T(8,128)(2,1)S(1)}, bf16[128,384]{1,0:T(8,128)(2,1)S(1)}, u32[]{:S(2)}, u32[]{:S(2)}) %collective-permute-start.1) | collective-permute-done | bytes 98336 | tf_op jit(solution)/shard_map/ppermute | solution.py:343
  24.8 0.6 collective-permute-start.3
  25.4 1.5 %collective-permute-start.4 = (bf16[256,384]{1,0:T(8,128)(2,1)S(1)}, bf16[256,384]{1,0:T(8,128)(2,1)S(1)}, u32[]{:S(2)}, u32[]{:S(2)}) collective-permute-start(bf16[256,384]{1,0:T(8,128)(2,1)S(1)} %get-tuple-element.36), channel_id=1, source_target_pairs={{0,6},{1,7},{2,4},{3,5},{4,2},{5,3},{6,0},{7,1},{8,14},{9,15},{10,... | collective-permute-start | bytes 589832 | tf_op jit(solution)/shard_map/ppermute | solution.py:343
  26.9 0.0 collective-permute-done.2.refs_2_
  26.9 0.0 copy-done
  26.9 0.9 %place_first.1 = (bf16[25,16,128]{2,1,0:T(8,128)(2,1)S(1)}, bf16[25,16,128]{2,1,0:T(8,128)(2,1)S(1)}, bf16[25,16,128]{2,1,0:T(8,128)(2,1)S(1)}, bf16[25,16,128]{2,1,0:T(8,128)(2,1)S(1)}) custom-call(s32[16]{0:T(128)S(1)} %bitcast.3, bf16[128,384]{1,0:T(8,128)(2,1)S(1)} %get-tuple-element.28.refs_0_, bf16[128,384]{1,0:T(8,128)(2,1)S(1)} %collective-permute-done.1.refs_1_, ...), custom_call_target="tpu_custom_call" | custom-call | tf_op jit(solution)/shard_map/place_first/pallas_call | solution.py:376
  27.8 3.7 %collective-permute-start.7 = (bf16[25,16,128]{2,1,0:T(8,128)(2,1)S(1)}, bf16[25,16,128]{2,1,0:T(8,128)(2,1)S(1)}, u32[]{:S(2)}, u32[]{:S(2)}) collective-permute-start(bf16[25,16,128]{2,1,0:T(8,128)(2,1)S(1)} %get-tuple-element.42), channel_id=1, source_target_pairs={{0,24},{8,0},{16,8},{24,16},{1,25},{9,1},{17,9},{25,17},{2,26},{10... | collective-permute-start | bytes 307208 | tf_op jit(solution)/shard_map/ppermute | solution.py:394
  31.4 0.0 collective-permute-start.9
  31.4 1.0 %collective-permute-start.5 = (bf16[25,16,128]{2,1,0:T(8,128)(2,1)S(1)}, bf16[25,16,128]{2,1,0:T(8,128)(2,1)S(1)}, u32[]{:S(2)}, u32[]{:S(2)}) collective-permute-start(bf16[25,16,128]{2,1,0:T(8,128)(2,1)S(1)} %get-tuple-element.38), channel_id=1, source_target_pairs={{0,16},{8,24},{16,0},{24,8},{1,17},{9,25},{17,1},{25,9},{2,18},{10... | collective-permute-start | bytes 307208 | tf_op jit(solution)/shard_map/ppermute | solution.py:394
  32.5 2.6 %collective-permute-done.3.refs_4_ = bf16[256,384]{1,0:T(8,128)(2,1)S(1)} collective-permute-done((bf16[256,384]{1,0:T(8,128)(2,1)S(1)}, bf16[256,384]{1,0:T(8,128)(2,1)S(1)}, u32[]{:S(2)}, u32[]{:S(2)}) %collective-permute-start.3) | collective-permute-done | bytes 196640 | tf_op jit(solution)/shard_map/ppermute | solution.py:343
  35.1 0.0 collective-permute-done.4.refs_5_
  35.1 1.1 %place_second.1 = (bf16[32,16,128]{2,1,0:T(8,128)(2,1)S(1)}, bf16[32,16,128]{2,1,0:T(8,128)(2,1)S(1)}, bf16[32,16,128]{2,1,0:T(8,128)(2,1)S(1)}, bf16[32,16,128]{2,1,0:T(8,128)(2,1)S(1)}) custom-call(s32[16]{0:T(128)S(1)} %bitcast.4, bf16[128,384]{1,0:T(8,128)(2,1)S(1)} %get-tuple-element.28.refs_0_, bf16[128,384]{1,0:T(8,128)(2,1)S(1)} %collective-permute-done.1.refs_1_, ...), custom_call_target="tpu_custom_call" | custom-call | tf_op jit(solution)/shard_map/place_second/pallas_call | solution.py:376
  36.1 0.0 collective-permute-done.7.refs_0_
  36.2 2.2 %collective-permute-done.9.refs_0_ = bf16[25,16,128]{2,1,0:T(8,128)(2,1)S(1)} collective-permute-done((bf16[25,16,128]{2,1,0:T(8,128)(2,1)S(1)}, bf16[25,16,128]{2,1,0:T(8,128)(2,1)S(1)}, u32[]{:S(2)}, u32[]{:S(2)}) %collective-permute-start.9) | collective-permute-done | bytes 102432 | tf_op jit(solution)/shard_map/ppermute | solution.py:394
  38.4 0.6 collective-permute-start.10
  39.0 3.3 %collective-permute-start.8 = (bf16[32,16,128]{2,1,0:T(8,128)(2,1)S(1)}, bf16[32,16,128]{2,1,0:T(8,128)(2,1)S(1)}, u32[]{:S(2)}, u32[]{:S(2)}) collective-permute-start(bf16[32,16,128]{2,1,0:T(8,128)(2,1)S(1)} %get-tuple-element.44), channel_id=1, source_target_pairs={{0,24},{8,0},{16,8},{24,16},{1,25},{9,1},{17,9},{25,17},{2,26},{10... | collective-permute-start | bytes 393224 | tf_op jit(solution)/shard_map/ppermute | solution.py:394
  42.2 0.7 %collective-permute-done.5.refs_0_ = bf16[25,16,128]{2,1,0:T(8,128)(2,1)S(1)} collective-permute-done((bf16[25,16,128]{2,1,0:T(8,128)(2,1)S(1)}, bf16[25,16,128]{2,1,0:T(8,128)(2,1)S(1)}, u32[]{:S(2)}, u32[]{:S(2)}) %collective-permute-start.5) | collective-permute-done | bytes 102432 | tf_op jit(solution)/shard_map/ppermute | solution.py:394
  42.9 0.0 collective-permute-start.6
  42.9 4.0 %correlate.3.refs_2_ = f32[5,256,256]{2,1,0:T(8,128)S(1)} custom-call(s32[16]{0:T(128)S(1)} %bitcast.5, bf16[25,16,128]{2,1,0:T(8,128)(2,1)S(1)} %get-tuple-element.49.refs_0_, bf16[32,16,128]{2,1,0:T(8,128)(2,1)S(1)} %get-tuple-element.50.refs_1_), custom_call_target="tpu_custom_call" | custom-call | tf_op jit(solution)/shard_map/correlate/pallas_call | solution.py:278
  46.9 0.0 collective-permute-done.10.refs_1_
  46.9 4.0 %correlate.4.refs_2_ = f32[5,256,256]{2,1,0:T(8,128)S(1)} custom-call(s32[16]{0:T(128)S(1)} %bitcast.6, bf16[25,16,128]{2,1,0:T(8,128)(2,1)S(1)} %collective-permute-done.9.refs_0_, bf16[32,16,128]{2,1,0:T(8,128)(2,1)S(1)} %collective-permute-done.10.refs_1_, f32[5,256,256]{2,1,0:T(8,128)S(1)} %correlate.3.refs_2_), custom_call_target="tpu_custom_call" | custom-call | tf_op jit(solution)/shard_map/correlate/pallas_call | solution.py:278
  50.9 0.0 collective-permute-done.8.refs_1_
  50.9 4.0 %correlate.5.refs_2_ = f32[5,256,256]{2,1,0:T(8,128)S(1)} custom-call(s32[16]{0:T(128)S(1)} %bitcast.7, bf16[25,16,128]{2,1,0:T(8,128)(2,1)S(1)} %collective-permute-done.7.refs_0_, bf16[32,16,128]{2,1,0:T(8,128)(2,1)S(1)} %collective-permute-done.8.refs_1_, f32[5,256,256]{2,1,0:T(8,128)S(1)} %correlate.4.refs_2_), custom_call_target="tpu_custom_call" | custom-call | tf_op jit(solution)/shard_map/correlate/pallas_call | solution.py:278
  54.9 0.0 collective-permute-done.6.refs_1_
  54.9 7.1 %correlate_last.1 = f32[5,8,8,1001]{3,2,1,0:T(8,128)} custom-call(s32[16]{0:T(128)S(1)} %bitcast.8, bf16[25,16,128]{2,1,0:T(8,128)(2,1)S(1)} %collective-permute-done.5.refs_0_, bf16[32,16,128]{2,1,0:T(8,128)(2,1)S(1)} %collective-permute-done.6.refs_1_, f32[5,256,256]{2,1,0:T(8,128)S(1)} %correlate.5.refs_2_), custom_call_target="tpu_custom_call" | custom-call | tf_op jit(solution)/shard_map/correlate_last/pallas_call | solution.py:278
  (2 shorter events, 0.1 us)
Async XLA Ops:
  1.2 9.8 %all-to-all-start = ((s32[8,1,2]{2,1,0:T(1,128)}), s32[8,1,2]{2,1,0:T(1,128)S(1)}, u32[]{:S(2)}, u32[]{:S(2)}) async-start(s32[8,1,2]{2,1,0:T(1,128)} %broadcast_in_dim.2), calls=%async_computation | async-start | bytes 8192 | tf_op jit(solution)/shard_map/all_to_all | solution.py:302
  6.4 0.7 %copy-start.1 = (f32[255]{0:T(256)S(1)}, f32[255]{0:T(256)}, u32[]{:S(2)}) copy-start(f32[255]{0:T(256)} %param.5) | copy-start | bytes 3064
  11.0 15.9 %copy-start = (s32[16,1]{0,1:T(1,128)S(1)}, s32[16,1]{0,1:T(1,128)}, u32[]{:S(2)}) copy-start(s32[16,1]{0,1:T(1,128)} %param.7) | copy-start | bytes 196
  19.1 1.9 %collective-permute-start = (bf16[384,384]{1,0:T(8,128)(2,1)S(1)}, bf16[384,384]{1,0:T(8,128)(2,1)S(1)}, u32[]{:S(2)}, u32[]{:S(2)}) collective-permute-start(bf16[384,384]{1,0:T(8,128)(2,1)S(1)} %get-tuple-element.30), channel_id=1, source_target_pairs={{0,1},{1,0},{2,3},{3,2},{4,5},{5,4},{6,7},{7,6},{8,9},{9,8},{10,11... | collective-permute-start | bytes 884744 | tf_op jit(solution)/shard_map/ppermute | solution.py:343
  19.2 5.7 %collective-permute-start.1 = (bf16[128,384]{1,0:T(8,128)(2,1)S(1)}, bf16[128,384]{1,0:T(8,128)(2,1)S(1)}, u32[]{:S(2)}, u32[]{:S(2)}) collective-permute-start(bf16[128,384]{1,0:T(8,128)(2,1)S(1)} %get-tuple-element.32), channel_id=1, source_target_pairs={{0,2},{1,3},{2,0},{3,1},{4,6},{5,7},{6,4},{7,5},{8,10},{9,11},{10,... | collective-permute-start | bytes 294920 | tf_op jit(solution)/shard_map/ppermute | solution.py:343
  19.8 7.1 %collective-permute-start.2 = (bf16[128,384]{1,0:T(8,128)(2,1)S(1)}, bf16[128,384]{1,0:T(8,128)(2,1)S(1)}, u32[]{:S(2)}, u32[]{:S(2)}) collective-permute-start(bf16[128,384]{1,0:T(8,128)(2,1)S(1)} %get-tuple-element.34), channel_id=1, source_target_pairs={{0,3},{1,2},{2,1},{3,0},{4,7},{5,6},{6,5},{7,4},{8,11},{9,10},{10,... | collective-permute-start | bytes 294920 | tf_op jit(solution)/shard_map/ppermute | solution.py:343
  24.8 10.2 %collective-permute-start.3 = (bf16[256,384]{1,0:T(8,128)(2,1)S(1)}, bf16[256,384]{1,0:T(8,128)(2,1)S(1)}, u32[]{:S(2)}, u32[]{:S(2)}) collective-permute-start(bf16[256,384]{1,0:T(8,128)(2,1)S(1)} %get-tuple-element.35), channel_id=1, source_target_pairs={{0,4},{1,5},{2,6},{3,7},{4,0},{5,1},{6,2},{7,3},{8,12},{9,13},{10,... | collective-permute-start | bytes 589832 | tf_op jit(solution)/shard_map/ppermute | solution.py:343
  25.4 9.7 %collective-permute-start.4 = (bf16[256,384]{1,0:T(8,128)(2,1)S(1)}, bf16[256,384]{1,0:T(8,128)(2,1)S(1)}, u32[]{:S(2)}, u32[]{:S(2)}) collective-permute-start(bf16[256,384]{1,0:T(8,128)(2,1)S(1)} %get-tuple-element.36), channel_id=1, source_target_pairs={{0,6},{1,7},{2,4},{3,5},{4,2},{5,3},{6,0},{7,1},{8,14},{9,15},{10,... | collective-permute-start | bytes 589832 | tf_op jit(solution)/shard_map/ppermute | solution.py:343
  27.8 8.4 %collective-permute-start.7 = (bf16[25,16,128]{2,1,0:T(8,128)(2,1)S(1)}, bf16[25,16,128]{2,1,0:T(8,128)(2,1)S(1)}, u32[]{:S(2)}, u32[]{:S(2)}) collective-permute-start(bf16[25,16,128]{2,1,0:T(8,128)(2,1)S(1)} %get-tuple-element.42), channel_id=1, source_target_pairs={{0,24},{8,0},{16,8},{24,16},{1,25},{9,1},{17,9},{25,17},{2,26},{10... | collective-permute-start | bytes 307208 | tf_op jit(solution)/shard_map/ppermute | solution.py:394
  31.4 7.0 %collective-permute-start.9 = (bf16[25,16,128]{2,1,0:T(8,128)(2,1)S(1)}, bf16[25,16,128]{2,1,0:T(8,128)(2,1)S(1)}, u32[]{:S(2)}, u32[]{:S(2)}) collective-permute-start(bf16[25,16,128]{2,1,0:T(8,128)(2,1)S(1)} %get-tuple-element.46), channel_id=1, source_target_pairs={{0,8},{8,16},{16,24},{24,0},{1,9},{9,17},{17,25},{25,1},{2,10},{10... | collective-permute-start | bytes 307208 | tf_op jit(solution)/shard_map/ppermute | solution.py:394
  31.4 11.5 %collective-permute-start.5 = (bf16[25,16,128]{2,1,0:T(8,128)(2,1)S(1)}, bf16[25,16,128]{2,1,0:T(8,128)(2,1)S(1)}, u32[]{:S(2)}, u32[]{:S(2)}) collective-permute-start(bf16[25,16,128]{2,1,0:T(8,128)(2,1)S(1)} %get-tuple-element.38), channel_id=1, source_target_pairs={{0,16},{8,24},{16,0},{24,8},{1,17},{9,25},{17,1},{25,9},{2,18},{10... | collective-permute-start | bytes 307208 | tf_op jit(solution)/shard_map/ppermute | solution.py:394
  38.4 8.5 %collective-permute-start.10 = (bf16[32,16,128]{2,1,0:T(8,128)(2,1)S(1)}, bf16[32,16,128]{2,1,0:T(8,128)(2,1)S(1)}, u32[]{:S(2)}, u32[]{:S(2)}) collective-permute-start(bf16[32,16,128]{2,1,0:T(8,128)(2,1)S(1)} %get-tuple-element.48), channel_id=1, source_target_pairs={{0,8},{8,16},{16,24},{24,0},{1,9},{9,17},{17,25},{25,1},{2,10},{10... | collective-permute-start | bytes 393224 | tf_op jit(solution)/shard_map/ppermute | solution.py:394
  39.0 11.9 %collective-permute-start.8 = (bf16[32,16,128]{2,1,0:T(8,128)(2,1)S(1)}, bf16[32,16,128]{2,1,0:T(8,128)(2,1)S(1)}, u32[]{:S(2)}, u32[]{:S(2)}) collective-permute-start(bf16[32,16,128]{2,1,0:T(8,128)(2,1)S(1)} %get-tuple-element.44), channel_id=1, source_target_pairs={{0,24},{8,0},{16,8},{24,16},{1,25},{9,1},{17,9},{25,17},{2,26},{10... | collective-permute-start | bytes 393224 | tf_op jit(solution)/shard_map/ppermute | solution.py:394
  42.9 12.0 %collective-permute-start.6 = (bf16[32,16,128]{2,1,0:T(8,128)(2,1)S(1)}, bf16[32,16,128]{2,1,0:T(8,128)(2,1)S(1)}, u32[]{:S(2)}, u32[]{:S(2)}) collective-permute-start(bf16[32,16,128]{2,1,0:T(8,128)(2,1)S(1)} %get-tuple-element.40), channel_id=1, source_target_pairs={{0,16},{8,24},{16,0},{24,8},{1,17},{9,25},{17,1},{25,9},{2,18},{10... | collective-permute-start | bytes 393224 | tf_op jit(solution)/shard_map/ppermute | solution.py:394

commit v8 on v5

--- a/solution.py
+++ b/solution.py
@@ -60,41 +60,52 @@
     steps = [k for group in groups for k in group]
     stripes = n_chan * STRIPES
     blocks_per = channels // n_chan // CB
-    span = window.shape[2]
     me = lax.axis_index("chan")
 
     def place(p):
         c, k = me ^ steps[p // STRIPES], p % STRIPES
         start = (firsts[c, k] + c * blocks_per) * CB
-        base = jnp.minimum(start - lax.rem(start, LANES), channels - span)
-        return start, pl.multiple_of(base, LANES)
-
-    def copy(p):
-        base = place(p)[1]
-        return pltpu.make_async_copy(raw.at[:, pl.ds(base, span)], window.at[p], sems.at[p])
+        return start, start - lax.rem(start, LANES)
+
+    def copy(p, tile):
+        base = jnp.minimum(place(p)[1] + tile * LANES, channels - LANES)
+        return pltpu.make_async_copy(
+            raw.at[:, pl.ds(pl.multiple_of(base, LANES), LANES)], window.at[p, tile], sems.at[p, tile]
+        )
 
     for p in range(stripes):
-        copy(p).start()
-
-    row = lax.broadcasted_iota(jnp.int32, (WIDE, span), 0)
-    lane = lax.broadcasted_iota(jnp.int32, (WIDE, span), 1)
-    batch = 2 * STRIPES
-    for first in range(0, stripes, batch):
-        for p in range(first, first + batch):
-            copy(p).wait()
-            start, base = place(p)
-            hot = (lane == row + (start - base)) & (row < channels - start)
-            hot = jnp.where(hot, 1.0, 0.0).astype(jnp.bfloat16)
-            block = window[p].astype(jnp.bfloat16)
-            chosen = lax.dot_general(hot, block, NT, preferred_element_type=jnp.float32)
-            picked[p * WIDE : (p + 1) * WIDE, :] = chosen.astype(jnp.bfloat16)
-        part = slice(first * WIDE, (first + batch) * WIDE)
+        for tile in range(2):
+            copy(p, tile).start()
+
+    lane = lax.broadcasted_iota(jnp.int32, (rows, LANES), 1)
+    row = lax.broadcasted_iota(jnp.int32, (LANES, LANES), 0)
+    column = lax.broadcasted_iota(jnp.int32, (LANES, LANES), 1)
+    height = STRIPES * WIDE
+    batch = 2
+    for first in range(0, len(steps), batch):
+        for at in range(first, first + batch):
+            sides, limits = [], []
+            for i in range(STRIPES):
+                p = at * STRIPES + i
+                start, base = place(p)
+                shift = start - base - i * WIDE
+                turn = lax.rem(2 * LANES - shift, LANES)
+                for tile in range(2):
+                    copy(p, tile).wait()
+                turned = [pltpu.roll(window[p, tile], turn, 1) for tile in range(2)]
+                sides.append(jnp.where(lane < LANES - shift, turned[0], turned[1]))
+                limits.append(channels - start + i * WIDE)
+            both = jnp.where(lane < WIDE, sides[0], sides[1]).astype(jnp.bfloat16)
+            limit = jnp.where(row < WIDE, limits[0], limits[1])
+            unit = jnp.where((row == column) & (row < limit), 1.0, 0.0).astype(jnp.bfloat16)
+            chosen = lax.dot_general(unit, both, NT, preferred_element_type=jnp.float32)
+            picked[at * height : (at + 1) * height, :] = chosen.astype(jnp.bfloat16)
+        part = slice(first * height, (first + batch) * height)
         result = lax.dot_general(
             picked[part, :], weights[...], NT, preferred_element_type=jnp.float32
         ).astype(jnp.bfloat16)
-        height = STRIPES * WIDE
-        for at in range(batch // STRIPES):
-            k = steps[first // STRIPES + at]
+        for at in range(batch):
+            k = steps[first + at]
             out, where = [(o, g.index(k)) for o, g in enumerate(groups) if k in g][0]
             sends[out][where * height : (where + 1) * height, :] = result[at * height : (at + 1) * height]
 
@@ -148,7 +159,7 @@
         owner = owners[q]
         slot = (counts >> (3 * owner)) & 7
         counts = counts + (jnp.int32(1) << (3 * owner))
-        pairs[lax.rem(owner - me + n_tgroup, n_tgroup) * SLOTS + slot] = q
+        pairs[(owner ^ me) * SLOTS + slot] = q
 
     base, per = tile_of(group, own_half(n_chan), total.shape[1] // LANES)
 
@@ -171,12 +182,12 @@
             sends[shift][at // 2] = value.astype(jnp.bfloat16)
 
 
-def correlate_kernel(n_chan, factor, last, owners, *refs):
+def correlate_kernel(n_chan, count, factor, last, owners, *refs):
     lead, window_a, window_b, whole = refs[-4:]
     out = refs[-5]
-    arrived, before = refs[:2], (refs[2] if len(refs) == 8 else None)
+    arrived, before = refs[: 2 * count], (refs[2 * count] if len(refs) > 2 * count + 5 else None)
     windows = (window_a, window_b)
-    span = lead.shape[2]
+    span = lead.shape[2] // count
     samples = span - LANES
     cols = span // LANES
     high = STEP * CB
@@ -186,50 +197,62 @@
     for q in range(K):
         first_count += jnp.where(owners[q] == me, 1, 0)
 
-    for group in range(2):
-        base, per = tile_of(group, own_half(n_chan), samples // LANES)
-        for at in range(arrived[group].shape[0]):
-            value = arrived[group][at].astype(jnp.float32)
-            for part in range(2):
-                block, j = (2 * at + part) // per, (2 * at + part) % per
-                if block < BLOCKS:
-                    lanes = pl.ds(pl.multiple_of((base + j) * LANES, LANES), LANES)
-                    whole[block, :, lanes] = value[part * CB : (part + 1) * CB]
-
-    def series(block):
-        return jnp.concatenate([whole[block], jnp.zeros((CB, LANES), jnp.float32)], 1)
+    for at_segment in range(count):
+        for group in range(2):
+            ref = arrived[2 * at_segment + group]
+            base, per = tile_of(group, own_half(n_chan), samples // LANES)
+            for at in range(ref.shape[0]):
+                value = ref[at].astype(jnp.float32)
+                for part in range(2):
+                    block, j = (2 * at + part) // per, (2 * at + part) % per
+                    if block < BLOCKS:
+                        lanes = pl.ds(pl.multiple_of((base + j) * LANES, LANES), LANES)
+                        whole[at_segment, block, :, lanes] = value[part * CB : (part + 1) * CB]
+
+    def series(at_segment, block):
+        return jnp.concatenate([whole[at_segment, block], jnp.zeros((CB, LANES), jnp.float32)], 1)
 
     for p in range(STRIPES):
-        value = series(p)
-        for a in range(CB):
-            spread = jnp.broadcast_to(value[a : a + 1], (SHIFTS, span))
-            turned = pltpu.roll(spread, 0, 1, stride=1, stride_axis=0)
-            lead[p, a * SHIFTS : (a + 1) * SHIFTS, :] = turned.astype(jnp.bfloat16)
+        for g in range(count):
+            value = series(g, p)
+            for a in range(CB):
+                spread = jnp.broadcast_to(value[a : a + 1], (SHIFTS, span))
+                turned = pltpu.roll(spread, 0, 1, stride=1, stride_axis=0)
+                rows = slice(a * SHIFTS, (a + 1) * SHIFTS)
+                lead[p, rows, g * span : (g + 1) * span] = turned.astype(jnp.bfloat16)
 
     def bounds(i):
         return max(0, ahead - i), min(cols, ahead + cols - i)
 
     for window in windows:
-        for i in range(LAG_BLOCKS):
-            first, end = bounds(i)
-            rows = slice(i * high, (i + 1) * high)
-            if first > 0:
-                window[rows, : first * LANES] = jnp.zeros((high, first * LANES), jnp.bfloat16)
-            if end < cols:
-                window[rows, end * LANES :] = jnp.zeros((high, (cols - end) * LANES), jnp.bfloat16)
+        for g in range(count):
+            for i in range(LAG_BLOCKS):
+                first, end = bounds(i)
+                rows = slice(i * high, (i + 1) * high)
+                if first > 0:
+                    window[rows, g * span : g * span + first * LANES] = jnp.zeros(
+                        (high, first * LANES), jnp.bfloat16
+                    )
+                if end < cols:
+                    window[rows, g * span + end * LANES : (g + 1) * span] = jnp.zeros(
+                        (high, (cols - end) * LANES), jnp.bfloat16
+                    )
 
     group = lax.broadcasted_iota(jnp.int32, (CB, LANES), 1) // SHIFTS
     for s in range(SLOTS):
         window = windows[s % 2]
-        value = series(STRIPES + s)
-        turned = [pltpu.roll(value, span - (FRONT - MAXLAG + SHIFTS * n), 1) for n in range(STEP)]
-        stacked = jnp.concatenate(turned, 0).astype(jnp.bfloat16)
-        stacked = jnp.concatenate([stacked[:, samples:], stacked[:, :samples]], 1)
-        for i in range(LAG_BLOCKS):
-            first, end = bounds(i)
-            window[i * high : (i + 1) * high, first * LANES : end * LANES] = stacked[
-                :, (first + i - ahead) * LANES : (end + i - ahead) * LANES
+        for g in range(count):
+            value = series(g, STRIPES + s)
+            turned = [
+                pltpu.roll(value, span - (FRONT - MAXLAG + SHIFTS * n), 1) for n in range(STEP)
             ]
+            stacked = jnp.concatenate(turned, 0).astype(jnp.bfloat16)
+            stacked = jnp.concatenate([stacked[:, samples:], stacked[:, :samples]], 1)
+            for i in range(LAG_BLOCKS):
+                first, end = bounds(i)
+                window[
+                    i * high : (i + 1) * high, g * span + first * LANES : g * span + end * LANES
+                ] = stacked[:, (first + i - ahead) * LANES : (end + i - ahead) * LANES]
         which = jnp.where(s < first_count, 0, 1)
         summed = lax.dot_general(window[...], lead[which], NT, preferred_element_type=jnp.float32)
         if before is not None:
@@ -255,22 +278,23 @@
 
 
 def correlate(n_chan, owners, arrived, before, factor, last, samples):
-    high, wide = STEP * LAG_BLOCKS * CB, CB * SHIFTS
+    high, wide, count = STEP * LAG_BLOCKS * CB, CB * SHIFTS, len(arrived) // 2
     if last:
         shape = jax.ShapeDtypeStruct((SLOTS, CB, CB, LAGS), jnp.float32)
     else:
         shape = jax.ShapeDtypeStruct((SLOTS, high, wide), jnp.float32)
     operands = (owners,) + arrived + (() if before is None else (before,))
+    depth = count * (samples + LANES)
     return pl.pallas_call(
-        functools.partial(correlate_kernel, n_chan, factor, last),
+        functools.partial(correlate_kernel, n_chan, count, factor, last),
         out_shape=shape,
         in_specs=[smem()] + [vmem()] * (len(operands) - 1),
         out_specs=vmem(),
         scratch_shapes=[
-            pltpu.VMEM((STRIPES, wide, samples + LANES), jnp.bfloat16),
-            pltpu.VMEM((high, samples + LANES), jnp.bfloat16),
-            pltpu.VMEM((high, samples + LANES), jnp.bfloat16),
-            pltpu.VMEM((BLOCKS, CB, samples), jnp.float32),
+            pltpu.VMEM((STRIPES, wide, depth), jnp.bfloat16),
+            pltpu.VMEM((high, depth), jnp.bfloat16),
+            pltpu.VMEM((high, depth), jnp.bfloat16),
+            pltpu.VMEM((count, BLOCKS, CB, samples), jnp.float32),
         ],
         compiler_params=params(40),
         name="correlate_last" if last else "correlate",
@@ -318,9 +342,9 @@
         in_specs=[smem(), pl.BlockSpec(memory_space=pl.ANY), vmem()],
         out_specs=[vmem()] * len(groups),
         scratch_shapes=[
-            pltpu.VMEM((n_chan * STRIPES, rows, 2 * LANES), jnp.float32),
+            pltpu.VMEM((n_chan * STRIPES, 2, rows, LANES), jnp.float32),
             pltpu.VMEM((n_chan * count, rows), jnp.bfloat16),
-            pltpu.SemaphoreType.DMA((n_chan * STRIPES,)),
+            pltpu.SemaphoreType.DMA((n_chan * STRIPES, 2)),
         ],
         compiler_params=params(40),
         name="select_filter",
@@ -354,7 +378,7 @@
         added = wide[:, :, :outs] + jnp.concatenate([right, none], 2) + jnp.concatenate([none, left], 2)
         early = late = [added.transpose(1, 0, 2).reshape(count, samples)]
 
-    order = sorted(range(1, n_tgroup), key=lambda s: min(s, n_tgroup - s))
+    order = sorted(range(1, n_tgroup), key=lambda s: (s.bit_length(), -s))
     arrived = [[] for _ in range(n_tgroup)]
     for group in range(2):
         use, steps = (early, early_steps) if group == 0 else (late, late_steps)
@@ -373,8 +397,8 @@
             name="place_first" if group == 0 else "place_second",
         )(owners, *use)
         arrived[0].append(sends[0])
-        for at, shift in enumerate(order):
-            route = [(g, (g + shift) % n_tgroup) for g in range(n_tgroup)]
+        for shift in order:
+            route = [(g, g ^ shift) for g in range(n_tgroup)]
             value = sends[shift]
             if group == 1:
                 value, arrived[shift][0] = lax.optimization_barrier((value, arrived[shift][0]))
@@ -382,9 +406,10 @@
 
     value = None
     factor = 1.0 / math.sqrt(samples)
-    for at, shift in enumerate([0] + order):
-        last = at == n_tgroup - 1
-        value = correlate(n_chan, owners, tuple(arrived[shift]), value, factor, last, samples)
+    turns = [[shift] for shift in [0] + order]
+    for at, shifts in enumerate(turns):
+        operands = tuple(sum([arrived[shift] for shift in shifts], []))
+        value = correlate(n_chan, owners, operands, value, factor, at == len(turns) - 1, samples)
     return value
 
 

time: 56.2 us -> 55.4 us (0.986)
  waiting for transfers between devices: 13.3 us -> 11.7 us
  Pallas kernels: 22.7 us -> 23.5 us
    ppermute x6, waiting for transfers between devices: 3.16 us -> 1.34 us  [local(): arrived[shift].append(lax.ppermute(value, 'tgroup', route))]
    pallas_call x1, Pallas kernels: 5.93 us -> 6.64 us  [local(): pl.pallas_call(functools.partial(select_kernel, n_chan, groups), out_shap...]
  transfers between devices with their start and end apart: 12 -> 12, of which waited for: 6 -> 4; matrix products, arithmetic and copies ran while one was open for 0% -> 0% of each run, Pallas kernels for 22% -> 22%
where the time goes in v8:
time: 55.4 us; the launch traced here: 55.2 us
  Pallas kernels  23.5 us (42%)
  starting transfers between devices  17.9 us (32%)
  waiting for transfers between devices  11.7 us (21%)
  local copies, waits for them, and re-layouts  1.95 us (4%)
    pallas_call x4, Pallas kernels, correlate(): pl.pallas_call(functools.partial(correlate_kernel, n_chan, count, factor,...  14.8 us
    ppermute x6, starting transfers between devices, local(): arrived[shift].append(lax.ppermute(value, 'tgroup', route))  8.79 us
    pallas_call x1, Pallas kernels, local(): pl.pallas_call(functools.partial(select_kernel, n_chan, groups), out_shap...  6.64 us
    ppermute x5, waiting for transfers between devices, exchange(): return lax.ppermute(value, 'chan', [(c, c ^ k) for c in range(n_chan)])  6.6 us
    all_to_all x1, starting transfers between devices, local(): lax.all_to_all(jnp.broadcast_to(first_block[None, :], (n_chan, STRIPES)),...  5.17 us
    ppermute x5, starting transfers between devices, exchange(): return lax.ppermute(value, 'chan', [(c, c ^ k) for c in range(n_chan)])  3.96 us
    all_to_all x1, waiting for transfers between devices, local(): lax.all_to_all(jnp.broadcast_to(first_block[None, :], (n_chan, STRIPES)),...  3.76 us
    pallas_call x2, Pallas kernels, local(): pl.pallas_call(functools.partial(place_kernel, n_chan, n_tgroup, outs, gr...  1.9 us
  transfers between devices with their start and end apart: 12, of which 4 were waited for; matrix products, arithmetic and copies ran while one was open for 0% of the time, Pallas kernels for 22%

profile of v8, /device:TPU:0, one launch (start us, length us, event | category | flops | bytes accessed | tf_op | source)
XLA Modules:
  0.0 55.2 jit_solution(12293377407894031401)
XLA Ops:
  0.0 1.2 %broadcast_in_dim.2 = s32[8,1,2]{2,1,0:T(1,128)} broadcast(s32[2]{0:T(128)} %param.6), dimensions={2} | broadcast | bytes 72 | tf_op jit(solution)/shard_map/broadcast_in_dim | solution.py:313
  1.2 5.2 %all-to-all-start = ((s32[8,1,2]{2,1,0:T(1,128)}), s32[8,1,2]{2,1,0:T(1,128)S(1)}, u32[]{:S(2)}, u32[]{:S(2)}) async-start(s32[8,1,2]{2,1,0:T(1,128)} %broadcast_in_dim.2), calls=%async_computation | async-start | bytes 8192 | tf_op jit(solution)/shard_map/all_to_all | solution.py:312
  6.4 0.0 copy-start.1
  6.4 0.7 %copy-done.1 = f32[255]{0:T(256)S(1)} copy-done((f32[255]{0:T(256)S(1)}, f32[255]{0:T(256)}, u32[]{:S(2)}) %copy-start.1) | copy-done | bytes 1044
  7.1 0.1 fir_weights.1.weights
  7.2 3.8 %all-to-all-done = s32[8,1,2]{2,1,0:T(1,128)S(1)} async-done(((s32[8,1,2]{2,1,0:T(1,128)}), s32[8,1,2]{2,1,0:T(1,128)S(1)}, u32[]{:S(2)}, u32[]{:S(2)}) %all-to-all-start) | async-done | bytes 96 | tf_op jit(solution)/shard_map/all_to_all | solution.py:312
  11.0 0.0 copy-start
  11.0 6.6 %select_filter.1 = (bf16[128,384]{1,0:T(8,128)(2,1)S(1)}, bf16[128,384]{1,0:T(8,128)(2,1)S(1)}, bf16[384,384]{1,0:T(8,128)(2,1)S(1)}, bf16[128,384]{1,0:T(8,128)...) custom-call(s32[8,2]{1,0:T(8,128)S(1)} %bitcast.9, f32[512,10240]{1,0:T(8,128)} %raw.1, ...), custom_call_target="tpu_custom_call" | custom-call | tf_op jit(solution)/shard_map/select_filter/pallas_call | solution.py:336
  17.7 0.1 collective-permute-start
  17.7 0.6 %collective-permute-start.1 = (bf16[128,384]{1,0:T(8,128)(2,1)S(1)}, bf16[128,384]{1,0:T(8,128)(2,1)S(1)}, u32[]{:S(2)}, u32[]{:S(2)}) collective-permute-start(bf16[128,384]{1,0:T(8,128)(2,1)S(1)} %get-tuple-element.32), channel_id=1, source_target_pairs={{0,2},{1,3},{2,0},{3,1},{4,6},{5,7},{6,4},{7,5},{8,10},{9,11},{10,... | collective-permute-start | bytes 294920 | tf_op jit(solution)/shard_map/ppermute | solution.py:354
  18.4 1.2 %collective-permute-start.2 = (bf16[128,384]{1,0:T(8,128)(2,1)S(1)}, bf16[128,384]{1,0:T(8,128)(2,1)S(1)}, u32[]{:S(2)}, u32[]{:S(2)}) collective-permute-start(bf16[128,384]{1,0:T(8,128)(2,1)S(1)} %get-tuple-element.34), channel_id=1, source_target_pairs={{0,3},{1,2},{2,1},{3,0},{4,7},{5,6},{6,5},{7,4},{8,11},{9,10},{10,... | collective-permute-start | bytes 294920 | tf_op jit(solution)/shard_map/ppermute | solution.py:354
  19.6 0.0 collective-permute-done.refs_3_
  19.7 3.7 %collective-permute-done.1.refs_1_ = bf16[128,384]{1,0:T(8,128)(2,1)S(1)} collective-permute-done((bf16[128,384]{1,0:T(8,128)(2,1)S(1)}, bf16[128,384]{1,0:T(8,128)(2,1)S(1)}, u32[]{:S(2)}, u32[]{:S(2)}) %collective-permute-start.1) | collective-permute-done | bytes 98336 | tf_op jit(solution)/shard_map/ppermute | solution.py:354
  23.4 0.6 %collective-permute-start.3 = (bf16[256,384]{1,0:T(8,128)(2,1)S(1)}, bf16[256,384]{1,0:T(8,128)(2,1)S(1)}, u32[]{:S(2)}, u32[]{:S(2)}) collective-permute-start(bf16[256,384]{1,0:T(8,128)(2,1)S(1)} %get-tuple-element.35), channel_id=1, source_target_pairs={{0,4},{1,5},{2,6},{3,7},{4,0},{5,1},{6,2},{7,3},{8,12},{9,13},{10,... | collective-permute-start | bytes 589832 | tf_op jit(solution)/shard_map/ppermute | solution.py:354
  24.0 1.5 %collective-permute-start.4 = (bf16[256,384]{1,0:T(8,128)(2,1)S(1)}, bf16[256,384]{1,0:T(8,128)(2,1)S(1)}, u32[]{:S(2)}, u32[]{:S(2)}) collective-permute-start(bf16[256,384]{1,0:T(8,128)(2,1)S(1)} %get-tuple-element.36), channel_id=1, source_target_pairs={{0,6},{1,7},{2,4},{3,5},{4,2},{5,3},{6,0},{7,1},{8,14},{9,15},{10,... | collective-permute-start | bytes 589832 | tf_op jit(solution)/shard_map/ppermute | solution.py:354
  25.4 0.0 collective-permute-done.2.refs_2_
  25.4 0.0 copy-done
  25.4 0.9 %place_first.1 = (bf16[25,16,128]{2,1,0:T(8,128)(2,1)S(1)}, bf16[25,16,128]{2,1,0:T(8,128)(2,1)S(1)}, bf16[25,16,128]{2,1,0:T(8,128)(2,1)S(1)}, bf16[25,16,128]{2,1,0:T(8,128)(2,1)S(1)}) custom-call(s32[16]{0:T(128)S(1)} %bitcast.3, bf16[128,384]{1,0:T(8,128)(2,1)S(1)} %get-tuple-element.28.refs_0_, bf16[128,384]{1,0:T(8,128)(2,1)S(1)} %collective-permute-done.1.refs_1_, ...), custom_call_target="tpu_custom_call" | custom-call | tf_op jit(solution)/shard_map/place_first/pallas_call | solution.py:387
  26.3 3.7 %collective-permute-start.7 = (bf16[25,16,128]{2,1,0:T(8,128)(2,1)S(1)}, bf16[25,16,128]{2,1,0:T(8,128)(2,1)S(1)}, u32[]{:S(2)}, u32[]{:S(2)}) collective-permute-start(bf16[25,16,128]{2,1,0:T(8,128)(2,1)S(1)} %get-tuple-element.42), channel_id=1, source_target_pairs={{0,24},{8,16},{16,8},{24,0},{1,25},{9,17},{17,9},{25,1},{2,26},{10... | collective-permute-start | bytes 307208 | tf_op jit(solution)/shard_map/ppermute | solution.py:405
  30.0 0.0 collective-permute-start.9
  30.0 0.8 %collective-permute-start.5 = (bf16[25,16,128]{2,1,0:T(8,128)(2,1)S(1)}, bf16[25,16,128]{2,1,0:T(8,128)(2,1)S(1)}, u32[]{:S(2)}, u32[]{:S(2)}) collective-permute-start(bf16[25,16,128]{2,1,0:T(8,128)(2,1)S(1)} %get-tuple-element.38), channel_id=1, source_target_pairs={{0,16},{8,24},{16,0},{24,8},{1,17},{9,25},{17,1},{25,9},{2,18},{10... | collective-permute-start | bytes 307208 | tf_op jit(solution)/shard_map/ppermute | solution.py:405
  30.8 2.9 %collective-permute-done.3.refs_4_ = bf16[256,384]{1,0:T(8,128)(2,1)S(1)} collective-permute-done((bf16[256,384]{1,0:T(8,128)(2,1)S(1)}, bf16[256,384]{1,0:T(8,128)(2,1)S(1)}, u32[]{:S(2)}, u32[]{:S(2)}) %collective-permute-start.3) | collective-permute-done | bytes 196640 | tf_op jit(solution)/shard_map/ppermute | solution.py:354
  33.6 0.0 collective-permute-done.4.refs_5_
  33.6 1.0 %place_second.1 = (bf16[32,16,128]{2,1,0:T(8,128)(2,1)S(1)}, bf16[32,16,128]{2,1,0:T(8,128)(2,1)S(1)}, bf16[32,16,128]{2,1,0:T(8,128)(2,1)S(1)}, bf16[32,16,128]{2,1,0:T(8,128)(2,1)S(1)}) custom-call(s32[16]{0:T(128)S(1)} %bitcast.4, bf16[128,384]{1,0:T(8,128)(2,1)S(1)} %get-tuple-element.28.refs_0_, bf16[128,384]{1,0:T(8,128)(2,1)S(1)} %collective-permute-done.1.refs_1_, ...), custom_call_target="tpu_custom_call" | custom-call | tf_op jit(solution)/shard_map/place_second/pallas_call | solution.py:387
  34.7 0.0 collective-permute-done.7.refs_0_
  34.7 1.3 %collective-permute-done.9.refs_0_ = bf16[25,16,128]{2,1,0:T(8,128)(2,1)S(1)} collective-permute-done((bf16[25,16,128]{2,1,0:T(8,128)(2,1)S(1)}, bf16[25,16,128]{2,1,0:T(8,128)(2,1)S(1)}, u32[]{:S(2)}, u32[]{:S(2)}) %collective-permute-start.9) | collective-permute-done | bytes 102432 | tf_op jit(solution)/shard_map/ppermute | solution.py:405
  36.0 1.5 %collective-permute-start.10 = (bf16[32,16,128]{2,1,0:T(8,128)(2,1)S(1)}, bf16[32,16,128]{2,1,0:T(8,128)(2,1)S(1)}, u32[]{:S(2)}, u32[]{:S(2)}) collective-permute-start(bf16[32,16,128]{2,1,0:T(8,128)(2,1)S(1)} %get-tuple-element.48), channel_id=1, source_target_pairs={{0,8},{8,0},{16,24},{24,16},{1,9},{9,1},{17,25},{25,17},{2,10},{10... | collective-permute-start | bytes 393224 | tf_op jit(solution)/shard_map/ppermute | solution.py:405
  37.5 1.3 %collective-permute-start.8 = (bf16[32,16,128]{2,1,0:T(8,128)(2,1)S(1)}, bf16[32,16,128]{2,1,0:T(8,128)(2,1)S(1)}, u32[]{:S(2)}, u32[]{:S(2)}) collective-permute-start(bf16[32,16,128]{2,1,0:T(8,128)(2,1)S(1)} %get-tuple-element.44), channel_id=1, source_target_pairs={{0,24},{8,16},{16,8},{24,0},{1,25},{9,17},{17,9},{25,1},{2,26},{10... | collective-permute-start | bytes 393224 | tf_op jit(solution)/shard_map/ppermute | solution.py:405
  38.8 0.0 collective-permute-done.5.refs_0_
  38.8 1.5 %collective-permute-start.6 = (bf16[32,16,128]{2,1,0:T(8,128)(2,1)S(1)}, bf16[32,16,128]{2,1,0:T(8,128)(2,1)S(1)}, u32[]{:S(2)}, u32[]{:S(2)}) collective-permute-start(bf16[32,16,128]{2,1,0:T(8,128)(2,1)S(1)} %get-tuple-element.40), channel_id=1, source_target_pairs={{0,16},{8,24},{16,0},{24,8},{1,17},{9,25},{17,1},{25,9},{2,18},{10... | collective-permute-start | bytes 393224 | tf_op jit(solution)/shard_map/ppermute | solution.py:405
  40.4 3.3 %correlate.3.refs_2_ = f32[5,256,256]{2,1,0:T(8,128)S(1)} custom-call(s32[16]{0:T(128)S(1)} %bitcast.5, bf16[25,16,128]{2,1,0:T(8,128)(2,1)S(1)} %get-tuple-element.49.refs_0_, bf16[32,16,128]{2,1,0:T(8,128)(2,1)S(1)} %get-tuple-element.50.refs_1_), custom_call_target="tpu_custom_call" | custom-call | tf_op jit(solution)/shard_map/correlate/pallas_call | solution.py:288
  43.6 0.0 collective-permute-done.10.refs_1_
  43.6 3.3 %correlate.4.refs_2_ = f32[5,256,256]{2,1,0:T(8,128)S(1)} custom-call(s32[16]{0:T(128)S(1)} %bitcast.6, bf16[25,16,128]{2,1,0:T(8,128)(2,1)S(1)} %collective-permute-done.9.refs_0_, bf16[32,16,128]{2,1,0:T(8,128)(2,1)S(1)} %collective-permute-done.10.refs_1_, f32[5,256,256]{2,1,0:T(8,128)S(1)} %correlate.3.refs_2_), custom_call_target="tpu_custom_call" | custom-call | tf_op jit(solution)/shard_map/correlate/pallas_call | solution.py:288
  47.0 0.0 collective-permute-done.8.refs_1_
  47.0 3.5 %correlate.5.refs_2_ = f32[5,256,256]{2,1,0:T(8,128)S(1)} custom-call(s32[16]{0:T(128)S(1)} %bitcast.7, bf16[25,16,128]{2,1,0:T(8,128)(2,1)S(1)} %collective-permute-done.7.refs_0_, bf16[32,16,128]{2,1,0:T(8,128)(2,1)S(1)} %collective-permute-done.8.refs_1_, f32[5,256,256]{2,1,0:T(8,128)S(1)} %correlate.4.refs_2_), custom_call_target="tpu_custom_call" | custom-call | tf_op jit(solution)/shard_map/correlate/pallas_call | solution.py:288
  50.5 0.0 collective-permute-done.6.refs_1_
  50.5 4.7 %correlate_last.1 = f32[5,8,8,1001]{3,2,1,0:T(8,128)} custom-call(s32[16]{0:T(128)S(1)} %bitcast.8, bf16[25,16,128]{2,1,0:T(8,128)(2,1)S(1)} %collective-permute-done.5.refs_0_, bf16[32,16,128]{2,1,0:T(8,128)(2,1)S(1)} %collective-permute-done.6.refs_1_, f32[5,256,256]{2,1,0:T(8,128)S(1)} %correlate.5.refs_2_), custom_call_target="tpu_custom_call" | custom-call | tf_op jit(solution)/shard_map/correlate_last/pallas_call | solution.py:288
  (2 shorter events, 0.1 us)
Async XLA Ops:
  1.2 9.8 %all-to-all-start = ((s32[8,1,2]{2,1,0:T(1,128)}), s32[8,1,2]{2,1,0:T(1,128)S(1)}, u32[]{:S(2)}, u32[]{:S(2)}) async-start(s32[8,1,2]{2,1,0:T(1,128)} %broadcast_in_dim.2), calls=%async_computation | async-start | bytes 8192 | tf_op jit(solution)/shard_map/all_to_all | solution.py:312
  6.4 0.7 %copy-start.1 = (f32[255]{0:T(256)S(1)}, f32[255]{0:T(256)}, u32[]{:S(2)}) copy-start(f32[255]{0:T(256)} %param.5) | copy-start | bytes 3064
  11.0 14.4 %copy-start = (s32[16,1]{0,1:T(1,128)S(1)}, s32[16,1]{0,1:T(1,128)}, u32[]{:S(2)}) copy-start(s32[16,1]{0,1:T(1,128)} %param.7) | copy-start | bytes 196
  17.7 1.9 %collective-permute-start = (bf16[384,384]{1,0:T(8,128)(2,1)S(1)}, bf16[384,384]{1,0:T(8,128)(2,1)S(1)}, u32[]{:S(2)}, u32[]{:S(2)}) collective-permute-start(bf16[384,384]{1,0:T(8,128)(2,1)S(1)} %get-tuple-element.30), channel_id=1, source_target_pairs={{0,1},{1,0},{2,3},{3,2},{4,5},{5,4},{6,7},{7,6},{8,9},{9,8},{10,11... | collective-permute-start | bytes 884744 | tf_op jit(solution)/shard_map/ppermute | solution.py:354
  17.7 5.7 %collective-permute-start.1 = (bf16[128,384]{1,0:T(8,128)(2,1)S(1)}, bf16[128,384]{1,0:T(8,128)(2,1)S(1)}, u32[]{:S(2)}, u32[]{:S(2)}) collective-permute-start(bf16[128,384]{1,0:T(8,128)(2,1)S(1)} %get-tuple-element.32), channel_id=1, source_target_pairs={{0,2},{1,3},{2,0},{3,1},{4,6},{5,7},{6,4},{7,5},{8,10},{9,11},{10,... | collective-permute-start | bytes 294920 | tf_op jit(solution)/shard_map/ppermute | solution.py:354
  18.4 7.1 %collective-permute-start.2 = (bf16[128,384]{1,0:T(8,128)(2,1)S(1)}, bf16[128,384]{1,0:T(8,128)(2,1)S(1)}, u32[]{:S(2)}, u32[]{:S(2)}) collective-permute-start(bf16[128,384]{1,0:T(8,128)(2,1)S(1)} %get-tuple-element.34), channel_id=1, source_target_pairs={{0,3},{1,2},{2,1},{3,0},{4,7},{5,6},{6,5},{7,4},{8,11},{9,10},{10,... | collective-permute-start | bytes 294920 | tf_op jit(solution)/shard_map/ppermute | solution.py:354
  23.4 10.2 %collective-permute-start.3 = (bf16[256,384]{1,0:T(8,128)(2,1)S(1)}, bf16[256,384]{1,0:T(8,128)(2,1)S(1)}, u32[]{:S(2)}, u32[]{:S(2)}) collective-permute-start(bf16[256,384]{1,0:T(8,128)(2,1)S(1)} %get-tuple-element.35), channel_id=1, source_target_pairs={{0,4},{1,5},{2,6},{3,7},{4,0},{5,1},{6,2},{7,3},{8,12},{9,13},{10,... | collective-permute-start | bytes 589832 | tf_op jit(solution)/shard_map/ppermute | solution.py:354
  24.0 9.7 %collective-permute-start.4 = (bf16[256,384]{1,0:T(8,128)(2,1)S(1)}, bf16[256,384]{1,0:T(8,128)(2,1)S(1)}, u32[]{:S(2)}, u32[]{:S(2)}) collective-permute-start(bf16[256,384]{1,0:T(8,128)(2,1)S(1)} %get-tuple-element.36), channel_id=1, source_target_pairs={{0,6},{1,7},{2,4},{3,5},{4,2},{5,3},{6,0},{7,1},{8,14},{9,15},{10,... | collective-permute-start | bytes 589832 | tf_op jit(solution)/shard_map/ppermute | solution.py:354
  26.3 8.4 %collective-permute-start.7 = (bf16[25,16,128]{2,1,0:T(8,128)(2,1)S(1)}, bf16[25,16,128]{2,1,0:T(8,128)(2,1)S(1)}, u32[]{:S(2)}, u32[]{:S(2)}) collective-permute-start(bf16[25,16,128]{2,1,0:T(8,128)(2,1)S(1)} %get-tuple-element.42), channel_id=1, source_target_pairs={{0,24},{8,16},{16,8},{24,0},{1,25},{9,17},{17,9},{25,1},{2,26},{10... | collective-permute-start | bytes 307208 | tf_op jit(solution)/shard_map/ppermute | solution.py:405
  30.0 6.0 %collective-permute-start.9 = (bf16[25,16,128]{2,1,0:T(8,128)(2,1)S(1)}, bf16[25,16,128]{2,1,0:T(8,128)(2,1)S(1)}, u32[]{:S(2)}, u32[]{:S(2)}) collective-permute-start(bf16[25,16,128]{2,1,0:T(8,128)(2,1)S(1)} %get-tuple-element.46), channel_id=1, source_target_pairs={{0,8},{8,0},{16,24},{24,16},{1,9},{9,1},{17,25},{25,17},{2,10},{10... | collective-permute-start | bytes 307208 | tf_op jit(solution)/shard_map/ppermute | solution.py:405
  30.0 8.8 %collective-permute-start.5 = (bf16[25,16,128]{2,1,0:T(8,128)(2,1)S(1)}, bf16[25,16,128]{2,1,0:T(8,128)(2,1)S(1)}, u32[]{:S(2)}, u32[]{:S(2)}) collective-permute-start(bf16[25,16,128]{2,1,0:T(8,128)(2,1)S(1)} %get-tuple-element.38), channel_id=1, source_target_pairs={{0,16},{8,24},{16,0},{24,8},{1,17},{9,25},{17,1},{25,9},{2,18},{10... | collective-permute-start | bytes 307208 | tf_op jit(solution)/shard_map/ppermute | solution.py:405
  36.0 7.6 %collective-permute-start.10 = (bf16[32,16,128]{2,1,0:T(8,128)(2,1)S(1)}, bf16[32,16,128]{2,1,0:T(8,128)(2,1)S(1)}, u32[]{:S(2)}, u32[]{:S(2)}) collective-permute-start(bf16[32,16,128]{2,1,0:T(8,128)(2,1)S(1)} %get-tuple-element.48), channel_id=1, source_target_pairs={{0,8},{8,0},{16,24},{24,16},{1,9},{9,1},{17,25},{25,17},{2,10},{10... | collective-permute-start | bytes 393224 | tf_op jit(solution)/shard_map/ppermute | solution.py:405
  37.5 9.4 %collective-permute-start.8 = (bf16[32,16,128]{2,1,0:T(8,128)(2,1)S(1)}, bf16[32,16,128]{2,1,0:T(8,128)(2,1)S(1)}, u32[]{:S(2)}, u32[]{:S(2)}) collective-permute-start(bf16[32,16,128]{2,1,0:T(8,128)(2,1)S(1)} %get-tuple-element.44), channel_id=1, source_target_pairs={{0,24},{8,16},{16,8},{24,0},{1,25},{9,17},{17,9},{25,1},{2,26},{10... | collective-permute-start | bytes 393224 | tf_op jit(solution)/shard_map/ppermute | solution.py:405
  38.8 11.7 %collective-permute-start.6 = (bf16[32,16,128]{2,1,0:T(8,128)(2,1)S(1)}, bf16[32,16,128]{2,1,0:T(8,128)(2,1)S(1)}, u32[]{:S(2)}, u32[]{:S(2)}) collective-permute-start(bf16[32,16,128]{2,1,0:T(8,128)(2,1)S(1)} %get-tuple-element.40), channel_id=1, source_target_pairs={{0,16},{8,24},{16,0},{24,8},{1,17},{9,25},{17,1},{25,9},{2,18},{10... | collective-permute-start | bytes 393224 | tf_op jit(solution)/shard_map/ppermute | solution.py:405

commit v9 on v5

--- a/solution.py
+++ b/solution.py
@@ -42,16 +42,14 @@
 def weights_kernel(taps, weights, held, line, sem):
     copy = pltpu.make_async_copy(taps, held, sem)
     copy.start()
-    rows, outs, width = weights.shape[1], weights.shape[0] - 2 * SPILL, line.shape[1]
+    rows, outs, width = weights.shape[0], weights.shape[1] - 2 * SPILL, line.shape[1]
     line[...] = jnp.zeros_like(line)
     copy.wait()
     line[0:1, :TAPS] = held[...]
     spread = jnp.broadcast_to(line[0:1, :], (outs + 2 * SPILL, width))
     value = pltpu.roll(spread, width - 4 * SPILL + 1, 1, stride=2, stride_axis=0)[:, :rows]
-    value = value.astype(jnp.bfloat16)
-    weights[:outs, :] = value[SPILL : SPILL + outs]
-    weights[outs : outs + SPILL, :] = value[SPILL + outs :]
-    weights[outs + SPILL :, :] = value[:SPILL]
+    value = jnp.concatenate([value[SPILL : SPILL + outs], value[SPILL + outs :], value[:SPILL]], 0)
+    weights[...] = value.T.astype(jnp.bfloat16)
 
 
 def select_kernel(n_chan, groups, firsts, raw, weights, *refs):
@@ -89,8 +87,8 @@
             chosen = lax.dot_general(hot, block, NT, preferred_element_type=jnp.float32)
             picked[p * WIDE : (p + 1) * WIDE, :] = chosen.astype(jnp.bfloat16)
         part = slice(first * WIDE, (first + batch) * WIDE)
-        result = lax.dot_general(
-            picked[part, :], weights[...], NT, preferred_element_type=jnp.float32
+        result = jnp.dot(
+            picked[part, :], weights[...], preferred_element_type=jnp.float32
         ).astype(jnp.bfloat16)
         height = STRIPES * WIDE
         for at in range(batch // STRIPES):
@@ -125,16 +123,22 @@
     half = vectors // 2
     if group == 0:
         return jnp.where(width == 0, 0, half + 1), half - 1
-    return jnp.where(width == 0, half - 1, 0), half + 1
+    if group == 1:
+        return jnp.where(width == 0, half - 1, 0), half + 1
+    return 0, vectors
+
+
+def tiles_in(group, vectors):
+    return -(-BLOCKS * tile_of(group, 0, vectors)[1] // 2)
 
 
 def own_half(n_chan):
     return jnp.where(lax.axis_index("chan") < n_chan // 2, 0, 1)
 
 
-def place_kernel(n_chan, n_tgroup, outs, group, steps, owners, *refs):
-    got, (total, pairs) = refs[: -n_tgroup - 2], refs[-2:]
-    sends = refs[-n_tgroup - 2 : -2]
+def place_kernel(n_chan, n_tgroup, outs, plan, steps, owners, *refs):
+    got, (total, pairs) = refs[: -len(plan) - 2], refs[-2:]
+    sends = refs[-len(plan) - 2 : -2]
     me = lax.axis_index("tgroup")
     if len(got) == 1:
         total[...] = got[0][...]
@@ -148,33 +152,34 @@
         owner = owners[q]
         slot = (counts >> (3 * owner)) & 7
         counts = counts + (jnp.int32(1) << (3 * owner))
-        pairs[lax.rem(owner - me + n_tgroup, n_tgroup) * SLOTS + slot] = q
-
-    base, per = tile_of(group, own_half(n_chan), total.shape[1] // LANES)
-
-    def tiles(q):
-        rows = pl.ds(pl.multiple_of(q * CB, CB), CB)
-        return [
-            total[rows, pl.ds(pl.multiple_of((base + j) * LANES, LANES), LANES)] for j in range(per)
-        ]
+        pairs[(owner ^ me) * SLOTS + slot] = q
 
     zero = jnp.zeros((CB, LANES), jnp.float32)
-    leads = sum([tiles(p * K) for p in range(STRIPES)], [])
-    for shift in range(n_tgroup):
-        parts = list(leads)
+    for send, (shift, group) in zip(sends, plan):
+        base, per = tile_of(group, own_half(n_chan), total.shape[1] // LANES)
+
+        def tiles(q):
+            rows = pl.ds(pl.multiple_of(q * CB, CB), CB)
+            return [
+                total[rows, pl.ds(pl.multiple_of((base + j) * LANES, LANES), LANES)]
+                for j in range(per)
+            ]
+
+        parts = sum([tiles(p * K) for p in range(STRIPES)], [])
         for s in range(SLOTS):
             q = pairs[shift * SLOTS + s]
             parts += [jnp.where(q >= 0, tile, 0.0) for tile in tiles(jnp.maximum(q, 0))]
         parts += [zero] * (len(parts) % 2)
         for at in range(0, len(parts), 2):
             value = jnp.concatenate(parts[at : at + 2], 0)
-            sends[shift][at // 2] = value.astype(jnp.bfloat16)
-
-
-def correlate_kernel(n_chan, factor, last, owners, *refs):
+            send[at // 2] = value.astype(jnp.bfloat16)
+
+
+def correlate_kernel(n_chan, groups, factor, last, owners, *refs):
     lead, window_a, window_b, whole = refs[-4:]
     out = refs[-5]
-    arrived, before = refs[:2], (refs[2] if len(refs) == 8 else None)
+    arrived = refs[: len(groups)]
+    before = refs[len(groups)] if len(refs) > len(groups) + 5 else None
     windows = (window_a, window_b)
     span = lead.shape[2]
     samples = span - LANES
@@ -186,10 +191,10 @@
     for q in range(K):
         first_count += jnp.where(owners[q] == me, 1, 0)
 
-    for group in range(2):
+    for ref, group in zip(arrived, groups):
         base, per = tile_of(group, own_half(n_chan), samples // LANES)
-        for at in range(arrived[group].shape[0]):
-            value = arrived[group][at].astype(jnp.float32)
+        for at in range(ref.shape[0]):
+            value = ref[at].astype(jnp.float32)
             for part in range(2):
                 block, j = (2 * at + part) // per, (2 * at + part) % per
                 if block < BLOCKS:
@@ -254,22 +259,23 @@
                     out[s, h * STEP + a, :, i * LANES : i * LANES + width] = value[:, :width]
 
 
-def correlate(n_chan, owners, arrived, before, factor, last, samples):
+def correlate(n_chan, owners, arrived, groups, before, factor, last, samples):
     high, wide = STEP * LAG_BLOCKS * CB, CB * SHIFTS
     if last:
         shape = jax.ShapeDtypeStruct((SLOTS, CB, CB, LAGS), jnp.float32)
     else:
         shape = jax.ShapeDtypeStruct((SLOTS, high, wide), jnp.float32)
     operands = (owners,) + arrived + (() if before is None else (before,))
+    depth = samples + LANES
     return pl.pallas_call(
-        functools.partial(correlate_kernel, n_chan, factor, last),
+        functools.partial(correlate_kernel, n_chan, groups, factor, last),
         out_shape=shape,
         in_specs=[smem()] + [vmem()] * (len(operands) - 1),
         out_specs=vmem(),
         scratch_shapes=[
-            pltpu.VMEM((STRIPES, wide, samples + LANES), jnp.bfloat16),
-            pltpu.VMEM((high, samples + LANES), jnp.bfloat16),
-            pltpu.VMEM((high, samples + LANES), jnp.bfloat16),
+            pltpu.VMEM((STRIPES, wide, depth), jnp.bfloat16),
+            pltpu.VMEM((high, depth), jnp.bfloat16),
+            pltpu.VMEM((high, depth), jnp.bfloat16),
             pltpu.VMEM((BLOCKS, CB, samples), jnp.float32),
         ],
         compiler_params=params(40),
@@ -295,7 +301,7 @@
     line = -(-(rows + 2 * outs + 4 * SPILL) // (2 * LANES)) * 2 * LANES
     weights = pl.pallas_call(
         weights_kernel,
-        out_shape=jax.ShapeDtypeStruct((outs + 2 * SPILL, rows), jnp.bfloat16),
+        out_shape=jax.ShapeDtypeStruct((rows, outs + 2 * SPILL), jnp.bfloat16),
         in_specs=[pl.BlockSpec(memory_space=pl.ANY)],
         out_specs=vmem(),
         scratch_shapes=[
@@ -307,8 +313,7 @@
         name="fir_weights",
     )(whitening_taps.reshape(1, TAPS))
 
-    relayed = n_chan == 8 and outs % LANES == 0
-    groups = [[2], [3], [1, 5, 7], [4], [6], [0]] if relayed else [[k] for k in range(n_chan)]
+    groups = [[k] for k in range(n_chan)]
     sends = pl.pallas_call(
         functools.partial(select_kernel, n_chan, groups),
         out_shape=[
@@ -329,21 +334,11 @@
     def exchange(value, k):
         return lax.ppermute(value, "chan", [(c, c ^ k) for c in range(n_chan)])
 
-    if relayed:
-        got = [sends[5], exchange(sends[0], 2), exchange(sends[1], 3), exchange(sends[2], 1)]
-        across = [
-            jnp.concatenate([sends[3 + at], got[3][(1 + at) * count : (2 + at) * count]], 0)
-            for at in range(2)
-        ]
-        across, got[1] = lax.optimization_barrier((across, got[1]))
-        across = [exchange(value, 4 + 2 * at) for at, value in enumerate(across)]
-        early, late = got, got + across
-        early_steps, late_steps = [[0], [2], [3], [1]], [[0], [2], [3], [1], [4, 5], [6, 7]]
-    else:
-        got = [sends[0]] + [exchange(sends[k], k) for k in range(1, n_chan)]
-        half = n_chan // 2
-        early, late = got[:half], got
-        early_steps, late_steps = [[k] for k in range(half)], [[k] for k in range(n_chan)]
+    half = n_chan // 2
+    got = [sends[0]] + [exchange(sends[k], k) for k in range(1, n_chan)]
+    steps = [[k] for k in range(n_chan)]
+    early, late = got[:half], got
+
     if outs % LANES:
         wide = jnp.stack(got).astype(jnp.float32)
         wide = jnp.take(wide, lax.axis_index("chan") ^ jnp.arange(n_chan), axis=0)
@@ -354,37 +349,50 @@
         added = wide[:, :, :outs] + jnp.concatenate([right, none], 2) + jnp.concatenate([none, left], 2)
         early = late = [added.transpose(1, 0, 2).reshape(count, samples)]
 
-    order = sorted(range(1, n_tgroup), key=lambda s: min(s, n_tgroup - s))
-    arrived = [[] for _ in range(n_tgroup)]
-    for group in range(2):
-        use, steps = (early, early_steps) if group == 0 else (late, late_steps)
-        vectors = samples // LANES // 2 + (1 if group else -1)
-        packed = jax.ShapeDtypeStruct((-(-BLOCKS * vectors // 2), 2 * CB, LANES), jnp.bfloat16)
-        sends = pl.pallas_call(
-            functools.partial(place_kernel, n_chan, n_tgroup, outs, group, steps),
-            out_shape=(packed,) * n_tgroup,
+    order = sorted(range(1, n_tgroup), key=lambda s: (s.bit_length(), -s))
+    vectors = samples // LANES
+    factor = 1.0 / math.sqrt(samples)
+
+    def place(plan, use, name):
+        return pl.pallas_call(
+            functools.partial(place_kernel, n_chan, n_tgroup, outs, plan, steps),
+            out_shape=[
+                jax.ShapeDtypeStruct((tiles_in(group, vectors), 2 * CB, LANES), jnp.bfloat16)
+                for _, group in plan
+            ],
             in_specs=[smem()] + [vmem()] * len(use),
-            out_specs=(vmem(),) * n_tgroup,
+            out_specs=[vmem()] * len(plan),
             scratch_shapes=[
                 pltpu.VMEM((count, samples), jnp.float32),
                 pltpu.SMEM((n_tgroup * SLOTS,), jnp.int32),
             ],
             compiler_params=params(40),
-            name="place_first" if group == 0 else "place_second",
+            name=name,
         )(owners, *use)
-        arrived[0].append(sends[0])
-        for at, shift in enumerate(order):
-            route = [(g, (g + shift) % n_tgroup) for g in range(n_tgroup)]
-            value = sends[shift]
-            if group == 1:
-                value, arrived[shift][0] = lax.optimization_barrier((value, arrived[shift][0]))
-            arrived[shift].append(lax.ppermute(value, "tgroup", route))
+
+    def hand_over(value, shift):
+        return lax.ppermute(value, "tgroup", [(g, g ^ shift) for g in range(n_tgroup)])
+
+    if outs % LANES == 0:
+        early, got[half] = lax.optimization_barrier((early, got[half]))
+        late = list(early) + got[half:]
+    far = order[1:]
+    first = place([(shift, 0) for shift in far], early, "place_first")
+    arrived = {shift: [hand_over(value, shift)] for shift, value in zip(far, first)}
+    plan = [(0, 2), (1, 2)] + [(shift, 1) for shift in far]
+    own, near, *second = place(plan, late, "place_second")
+    arrived[0], arrived[1] = [own], [hand_over(near, 1)]
+    for shift, value in zip(far, second):
+        value, held = lax.optimization_barrier((value, arrived[shift][0]))
+        arrived[shift] = [held, hand_over(value, shift)]
 
     value = None
-    factor = 1.0 / math.sqrt(samples)
     for at, shift in enumerate([0] + order):
+        parts = (0, 1) if shift in far else (2,)
         last = at == n_tgroup - 1
-        value = correlate(n_chan, owners, tuple(arrived[shift]), value, factor, last, samples)
+        value = correlate(
+            n_chan, owners, tuple(arrived[shift]), parts, value, factor, last, samples
+        )
     return value
 
 

time: 56.2 us -> 54.8 us (0.975)
  waiting for transfers between devices: 13.3 us -> 10.8 us
  starting transfers between devices: 17.6 us -> 19.1 us
    ppermute x5 -> x7, waiting for transfers between devices: 6.35 us -> 3.47 us  [exchange(): return lax.ppermute(value, 'chan', [(c, c ^ k) for c in range(n_chan)])]
    ppermute x5 -> x7, starting transfers between devices: 3.96 us -> 4.79 us  [exchange(): return lax.ppermute(value, 'chan', [(c, c ^ k) for c in range(n_chan)])]
    ppermute x6 -> x5, starting transfers between devices: 8.5 us -> 9.12 us  [hand_over(): lax.ppermute(value, 'tgroup', [(g, g ^ shift) for g in range(n_tgroup)])]
    ppermute x6 -> x5, waiting for transfers between devices: 3.16 us -> 3.71 us  [hand_over(): lax.ppermute(value, 'tgroup', [(g, g ^ shift) for g in range(n_tgroup)])]
  transfers between devices with their start and end apart: 12 -> 13, of which waited for: 6 -> 8; matrix products, arithmetic and copies ran while one was open for 0% -> 0% of each run, Pallas kernels for 22% -> 22%
where the time goes in v9:
time: 54.8 us; the launch traced here: 54.6 us
  Pallas kernels  22.7 us (41%)
  starting transfers between devices  19.1 us (35%)
  waiting for transfers between devices  10.8 us (20%)
  local copies, waits for them, and re-layouts  1.93 us (4%)
    pallas_call x4, Pallas kernels, correlate(): pl.pallas_call(functools.partial(correlate_kernel, n_chan, groups, factor...  14.7 us
    ppermute x5, starting transfers between devices, hand_over(): lax.ppermute(value, 'tgroup', [(g, g ^ shift) for g in range(n_tgroup)])  9.12 us
    pallas_call x1, Pallas kernels, local(): pl.pallas_call(functools.partial(select_kernel, n_chan, groups), out_shap...  5.95 us
    all_to_all x1, starting transfers between devices, local(): lax.all_to_all(jnp.broadcast_to(first_block[None, :], (n_chan, STRIPES)),...  5.17 us
    ppermute x7, starting transfers between devices, exchange(): return lax.ppermute(value, 'chan', [(c, c ^ k) for c in range(n_chan)])  4.79 us
    ppermute x5, waiting for transfers between devices, hand_over(): lax.ppermute(value, 'tgroup', [(g, g ^ shift) for g in range(n_tgroup)])  3.71 us
    all_to_all x1, waiting for transfers between devices, local(): lax.all_to_all(jnp.broadcast_to(first_block[None, :], (n_chan, STRIPES)),...  3.62 us
    ppermute x7, waiting for transfers between devices, exchange(): return lax.ppermute(value, 'chan', [(c, c ^ k) for c in range(n_chan)])  3.47 us
  transfers between devices with their start and end apart: 13, of which 8 were waited for; matrix products, arithmetic and copies ran while one was open for 0% of the time, Pallas kernels for 22%

profile of v9, /device:TPU:0, one launch (start us, length us, event | category | flops | bytes accessed | tf_op | source)
XLA Modules:
  0.0 54.6 jit_solution(16198463653341368763)
XLA Ops:
  0.0 1.2 %broadcast_in_dim.2 = s32[8,1,2]{2,1,0:T(1,128)} broadcast(s32[2]{0:T(128)} %param.6), dimensions={2} | broadcast | bytes 72 | tf_op jit(solution)/shard_map/broadcast_in_dim | solution.py:295
  1.2 5.2 %all-to-all-start = ((s32[8,1,2]{2,1,0:T(1,128)}), s32[8,1,2]{2,1,0:T(1,128)S(1)}, u32[]{:S(2)}, u32[]{:S(2)}) async-start(s32[8,1,2]{2,1,0:T(1,128)} %broadcast_in_dim.2), calls=%async_computation | async-start | bytes 8192 | tf_op jit(solution)/shard_map/all_to_all | solution.py:294
  6.4 0.0 copy-start.1
  6.4 0.7 %copy-done.1 = f32[255]{0:T(256)S(1)} copy-done((f32[255]{0:T(256)S(1)}, f32[255]{0:T(256)}, u32[]{:S(2)}) %copy-start.1) | copy-done | bytes 1044
  7.1 0.3 fir_weights.1.weights
  7.4 3.6 %all-to-all-done = s32[8,1,2]{2,1,0:T(1,128)S(1)} async-done(((s32[8,1,2]{2,1,0:T(1,128)}), s32[8,1,2]{2,1,0:T(1,128)S(1)}, u32[]{:S(2)}, u32[]{:S(2)}) %all-to-all-start) | async-done | bytes 96 | tf_op jit(solution)/shard_map/all_to_all | solution.py:294
  11.0 0.0 copy-start
  11.0 6.0 %select_filter.1 = (bf16[128,384]{1,0:T(8,128)(2,1)S(1)}, bf16[128,384]{1,0:T(8,128)(2,1)S(1)}, bf16[128,384]{1,0:T(8,128)(2,1)S(1)}, bf16[128,384]{1,0:T(8,128)...) custom-call(s32[8,2]{1,0:T(8,128)S(1)} %bitcast.9, ...), custom_call_target="tpu_custom_call" | custom-call | tf_op jit(solution)/shard_map/select_filter/pallas_call | solution.py:317
  17.0 0.1 collective-permute-start
  17.0 0.6 %collective-permute-start.1 = (bf16[128,384]{1,0:T(8,128)(2,1)S(1)}, bf16[128,384]{1,0:T(8,128)(2,1)S(1)}, u32[]{:S(2)}, u32[]{:S(2)}) collective-permute-start(bf16[128,384]{1,0:T(8,128)(2,1)S(1)} %get-tuple-element.30), channel_id=1, source_target_pairs={{0,2},{1,3},{2,0},{3,1},{4,6},{5,7},{6,4},{7,5},{8,10},{9,11},{10,... | collective-permute-start | bytes 294920 | tf_op jit(solution)/shard_map/ppermute | solution.py:335
  17.7 1.2 %collective-permute-start.2 = (bf16[128,384]{1,0:T(8,128)(2,1)S(1)}, bf16[128,384]{1,0:T(8,128)(2,1)S(1)}, u32[]{:S(2)}, u32[]{:S(2)}) collective-permute-start(bf16[128,384]{1,0:T(8,128)(2,1)S(1)} %get-tuple-element.31), channel_id=1, source_target_pairs={{0,3},{1,2},{2,1},{3,0},{4,7},{5,6},{6,5},{7,4},{8,11},{9,10},{10,... | collective-permute-start | bytes 294920 | tf_op jit(solution)/shard_map/ppermute | solution.py:335
  18.9 0.6 %collective-permute-start.3 = (bf16[128,384]{1,0:T(8,128)(2,1)S(1)}, bf16[128,384]{1,0:T(8,128)(2,1)S(1)}, u32[]{:S(2)}, u32[]{:S(2)}) collective-permute-start(bf16[128,384]{1,0:T(8,128)(2,1)S(1)} %get-tuple-element.32), channel_id=1, source_target_pairs={{0,4},{1,5},{2,6},{3,7},{4,0},{5,1},{6,2},{7,3},{8,12},{9,13},{10,... | collective-permute-start | bytes 294920 | tf_op jit(solution)/shard_map/ppermute | solution.py:335
  19.5 1.1 %collective-permute-start.4 = (bf16[128,384]{1,0:T(8,128)(2,1)S(1)}, bf16[128,384]{1,0:T(8,128)(2,1)S(1)}, u32[]{:S(2)}, u32[]{:S(2)}) collective-permute-start(bf16[128,384]{1,0:T(8,128)(2,1)S(1)} %get-tuple-element.38), channel_id=1, source_target_pairs={{0,5},{1,4},{2,7},{3,6},{4,1},{5,0},{6,3},{7,2},{8,13},{9,12},{10,... | collective-permute-start | bytes 294920 | tf_op jit(solution)/shard_map/ppermute | solution.py:335
  20.6 0.0 collective-permute-done.refs_1_
  20.6 0.6 %collective-permute-start.5 = (bf16[128,384]{1,0:T(8,128)(2,1)S(1)}, bf16[128,384]{1,0:T(8,128)(2,1)S(1)}, u32[]{:S(2)}, u32[]{:S(2)}) collective-permute-start(bf16[128,384]{1,0:T(8,128)(2,1)S(1)} %get-tuple-element.39), channel_id=1, source_target_pairs={{0,6},{1,7},{2,4},{3,5},{4,2},{5,3},{6,0},{7,1},{8,14},{9,15},{10,... | collective-permute-start | bytes 294920 | tf_op jit(solution)/shard_map/ppermute | solution.py:335
  21.2 1.5 %collective-permute-done.1.refs_2_ = bf16[128,384]{1,0:T(8,128)(2,1)S(1)} collective-permute-done((bf16[128,384]{1,0:T(8,128)(2,1)S(1)}, bf16[128,384]{1,0:T(8,128)(2,1)S(1)}, u32[]{:S(2)}, u32[]{:S(2)}) %collective-permute-start.1) | collective-permute-done | bytes 98336 | tf_op jit(solution)/shard_map/ppermute | solution.py:335
  22.7 0.6 %collective-permute-start.6 = (bf16[128,384]{1,0:T(8,128)(2,1)S(1)}, bf16[128,384]{1,0:T(8,128)(2,1)S(1)}, u32[]{:S(2)}, u32[]{:S(2)}) collective-permute-start(bf16[128,384]{1,0:T(8,128)(2,1)S(1)} %get-tuple-element.40), channel_id=1, source_target_pairs={{0,7},{1,6},{2,5},{3,4},{4,3},{5,2},{6,1},{7,0},{8,15},{9,14},{10,... | collective-permute-start | bytes 294920 | tf_op jit(solution)/shard_map/ppermute | solution.py:335
  23.3 0.6 %collective-permute-done.2.refs_3_ = bf16[128,384]{1,0:T(8,128)(2,1)S(1)} collective-permute-done((bf16[128,384]{1,0:T(8,128)(2,1)S(1)}, bf16[128,384]{1,0:T(8,128)(2,1)S(1)}, u32[]{:S(2)}, u32[]{:S(2)}) %collective-permute-start.2) | collective-permute-done | bytes 98336 | tf_op jit(solution)/shard_map/ppermute | solution.py:335
  23.9 0.6 %collective-permute-done.3.refs_4_ = bf16[128,384]{1,0:T(8,128)(2,1)S(1)} collective-permute-done((bf16[128,384]{1,0:T(8,128)(2,1)S(1)}, bf16[128,384]{1,0:T(8,128)(2,1)S(1)}, u32[]{:S(2)}, u32[]{:S(2)}) %collective-permute-start.3) | collective-permute-done | bytes 98336 | tf_op jit(solution)/shard_map/ppermute | solution.py:335
  24.5 0.0 copy-done
  24.5 0.8 %place_first.1 = (bf16[25,16,128]{2,1,0:T(8,128)(2,1)S(1)}, bf16[25,16,128]{2,1,0:T(8,128)(2,1)S(1)}) custom-call(s32[16]{0:T(128)S(1)} %bitcast.3, bf16[128,384]{1,0:T(8,128)(2,1)S(1)} %get-tuple-element.33.refs_0_, bf16[128,384]{1,0:T(8,128)(2,1)S(1)} %collective-permute-done.refs_1_, bf16[128,384]{1,0:T(8,128)(2,1)S(1)} %collective-permute-done.1.refs_2_, ...), custom_call_target="tpu_custom_call" | custom-call | tf_op jit(solution)/shard_map/place_first/pallas_call | solution.py:357
  25.3 3.7 %collective-permute-start.9 = (bf16[25,16,128]{2,1,0:T(8,128)(2,1)S(1)}, bf16[25,16,128]{2,1,0:T(8,128)(2,1)S(1)}, u32[]{:S(2)}, u32[]{:S(2)}) collective-permute-start(bf16[25,16,128]{2,1,0:T(8,128)(2,1)S(1)} %get-tuple-element.46), channel_id=1, source_target_pairs={{0,24},{8,16},{16,8},{24,0},{1,25},{9,17},{17,9},{25,1},{2,26},{10... | collective-permute-start | bytes 307208 | tf_op jit(solution)/shard_map/ppermute | solution.py:374
  29.0 0.0 collective-permute-start.7
  29.0 0.7 %collective-permute-done.4.refs_5_ = bf16[128,384]{1,0:T(8,128)(2,1)S(1)} collective-permute-done((bf16[128,384]{1,0:T(8,128)(2,1)S(1)}, bf16[128,384]{1,0:T(8,128)(2,1)S(1)}, u32[]{:S(2)}, u32[]{:S(2)}) %collective-permute-start.4) | collective-permute-done | bytes 98336 | tf_op jit(solution)/shard_map/ppermute | solution.py:335
  29.7 0.0 collective-permute-done.5.refs_6_
  29.7 0.0 collective-permute-done.6.refs_7_
  29.7 1.0 %place_second.1 = (bf16[56,16,128]{2,1,0:T(8,128)(2,1)S(1)}, bf16[56,16,128]{2,1,0:T(8,128)(2,1)S(1)}, bf16[32,16,128]{2,1,0:T(8,128)(2,1)S(1)}, bf16[32,16,128]{2,1,0:T(8,128)(2,1)S(1)}) custom-call(s32[16]{0:T(128)S(1)} %bitcast.4, bf16[128,384]{1,0:T(8,128)(2,1)S(1)} %get-tuple-element.33.refs_0_, bf16[128,384]{1,0:T(8,128)(2,1)S(1)} %collective-permute-done.refs_1_, ...), custom_call_target="tpu_custom_call" | custom-call | tf_op jit(solution)/shard_map/place_second/pallas_call | solution.py:357
  30.7 1.6 %collective-permute-start.11 = (bf16[56,16,128]{2,1,0:T(8,128)(2,1)S(1)}, bf16[56,16,128]{2,1,0:T(8,128)(2,1)S(1)}, u32[]{:S(2)}, u32[]{:S(2)}) collective-permute-start(bf16[56,16,128]{2,1,0:T(8,128)(2,1)S(1)} %get-tuple-element.49), channel_id=1, source_target_pairs={{0,8},{8,0},{16,24},{24,16},{1,9},{9,1},{17,25},{25,17},{2,10},{10... | collective-permute-start | bytes 688136 | tf_op jit(solution)/shard_map/ppermute | solution.py:374
  32.4 0.6 %collective-permute-done.9.refs_0_ = bf16[25,16,128]{2,1,0:T(8,128)(2,1)S(1)} collective-permute-done((bf16[25,16,128]{2,1,0:T(8,128)(2,1)S(1)}, bf16[25,16,128]{2,1,0:T(8,128)(2,1)S(1)}, u32[]{:S(2)}, u32[]{:S(2)}) %collective-permute-start.9) | collective-permute-done | bytes 102432 | tf_op jit(solution)/shard_map/ppermute | solution.py:374
  33.0 3.6 %collective-permute-start.10 = (bf16[32,16,128]{2,1,0:T(8,128)(2,1)S(1)}, bf16[32,16,128]{2,1,0:T(8,128)(2,1)S(1)}, u32[]{:S(2)}, u32[]{:S(2)}) collective-permute-start(bf16[32,16,128]{2,1,0:T(8,128)(2,1)S(1)} %get-tuple-element.48), channel_id=1, source_target_pairs={{0,24},{8,16},{16,8},{24,0},{1,25},{9,17},{17,9},{25,1},{2,26},{10... | collective-permute-start | bytes 393224 | tf_op jit(solution)/shard_map/ppermute | solution.py:374
  36.6 1.7 %collective-permute-done.7.refs_0_ = bf16[25,16,128]{2,1,0:T(8,128)(2,1)S(1)} collective-permute-done((bf16[25,16,128]{2,1,0:T(8,128)(2,1)S(1)}, bf16[25,16,128]{2,1,0:T(8,128)(2,1)S(1)}, u32[]{:S(2)}, u32[]{:S(2)}) %collective-permute-start.7) | collective-permute-done | bytes 102432 | tf_op jit(solution)/shard_map/ppermute | solution.py:374
  38.3 0.2 collective-permute-start.8
  38.5 3.3 %correlate.3.refs_1_ = f32[5,256,256]{2,1,0:T(8,128)S(1)} custom-call(s32[16]{0:T(128)S(1)} %bitcast.5, bf16[56,16,128]{2,1,0:T(8,128)(2,1)S(1)} %get-tuple-element.50.refs_0_), custom_call_target="tpu_custom_call" | custom-call | tf_op jit(solution)/shard_map/correlate/pallas_call | solution.py:270
  41.8 0.0 collective-permute-done.11.refs_0_
  41.8 3.3 %correlate.4.refs_2_ = f32[5,256,256]{2,1,0:T(8,128)S(1)} custom-call(s32[16]{0:T(128)S(1)} %bitcast.6, bf16[56,16,128]{2,1,0:T(8,128)(2,1)S(1)} %collective-permute-done.11.refs_0_, f32[5,256,256]{2,1,0:T(8,128)S(1)} %correlate.3.refs_1_), custom_call_target="tpu_custom_call" | custom-call | tf_op jit(solution)/shard_map/correlate/pallas_call | solution.py:270
  45.1 0.0 collective-permute-done.10.refs_1_
  45.2 3.3 %correlate.5.refs_2_ = f32[5,256,256]{2,1,0:T(8,128)S(1)} custom-call(s32[16]{0:T(128)S(1)} %bitcast.7, bf16[25,16,128]{2,1,0:T(8,128)(2,1)S(1)} %collective-permute-done.9.refs_0_, bf16[32,16,128]{2,1,0:T(8,128)(2,1)S(1)} %collective-permute-done.10.refs_1_, f32[5,256,256]{2,1,0:T(8,128)S(1)} %correlate.4.refs_2_), custom_call_target="tpu_custom_call" | custom-call | tf_op jit(solution)/shard_map/correlate/pallas_call | solution.py:270
  48.5 1.4 %collective-permute-done.8.refs_1_ = bf16[32,16,128]{2,1,0:T(8,128)(2,1)S(1)} collective-permute-done((bf16[32,16,128]{2,1,0:T(8,128)(2,1)S(1)}, bf16[32,16,128]{2,1,0:T(8,128)(2,1)S(1)}, u32[]{:S(2)}, u32[]{:S(2)}) %collective-permute-start.8) | collective-permute-done | bytes 131104 | tf_op jit(solution)/shard_map/ppermute | solution.py:374
  49.9 4.7 %correlate_last.1 = f32[5,8,8,1001]{3,2,1,0:T(8,128)} custom-call(s32[16]{0:T(128)S(1)} %bitcast.8, bf16[25,16,128]{2,1,0:T(8,128)(2,1)S(1)} %collective-permute-done.7.refs_0_, bf16[32,16,128]{2,1,0:T(8,128)(2,1)S(1)} %collective-permute-done.8.refs_1_, f32[5,256,256]{2,1,0:T(8,128)S(1)} %correlate.5.refs_2_), custom_call_target="tpu_custom_call" | custom-call | tf_op jit(solution)/shard_map/correlate_last/pallas_call | solution.py:270
Async XLA Ops:
  1.2 9.8 %all-to-all-start = ((s32[8,1,2]{2,1,0:T(1,128)}), s32[8,1,2]{2,1,0:T(1,128)S(1)}, u32[]{:S(2)}, u32[]{:S(2)}) async-start(s32[8,1,2]{2,1,0:T(1,128)} %broadcast_in_dim.2), calls=%async_computation | async-start | bytes 8192 | tf_op jit(solution)/shard_map/all_to_all | solution.py:294
  6.4 0.7 %copy-start.1 = (f32[255]{0:T(256)S(1)}, f32[255]{0:T(256)}, u32[]{:S(2)}) copy-start(f32[255]{0:T(256)} %param.5) | copy-start | bytes 3064
  11.0 13.5 %copy-start = (s32[16,1]{0,1:T(1,128)S(1)}, s32[16,1]{0,1:T(1,128)}, u32[]{:S(2)}) copy-start(s32[16,1]{0,1:T(1,128)} %param.7) | copy-start | bytes 196
  17.0 3.6 %collective-permute-start = (bf16[128,384]{1,0:T(8,128)(2,1)S(1)}, bf16[128,384]{1,0:T(8,128)(2,1)S(1)}, u32[]{:S(2)}, u32[]{:S(2)}) collective-permute-start(bf16[128,384]{1,0:T(8,128)(2,1)S(1)} %get-tuple-element.29), channel_id=1, source_target_pairs={{0,1},{1,0},{2,3},{3,2},{4,5},{5,4},{6,7},{7,6},{8,9},{9,8},{10,11... | collective-permute-start | bytes 294920 | tf_op jit(solution)/shard_map/ppermute | solution.py:335
  17.0 5.7 %collective-permute-start.1 = (bf16[128,384]{1,0:T(8,128)(2,1)S(1)}, bf16[128,384]{1,0:T(8,128)(2,1)S(1)}, u32[]{:S(2)}, u32[]{:S(2)}) collective-permute-start(bf16[128,384]{1,0:T(8,128)(2,1)S(1)} %get-tuple-element.30), channel_id=1, source_target_pairs={{0,2},{1,3},{2,0},{3,1},{4,6},{5,7},{6,4},{7,5},{8,10},{9,11},{10,... | collective-permute-start | bytes 294920 | tf_op jit(solution)/shard_map/ppermute | solution.py:335
  17.7 6.2 %collective-permute-start.2 = (bf16[128,384]{1,0:T(8,128)(2,1)S(1)}, bf16[128,384]{1,0:T(8,128)(2,1)S(1)}, u32[]{:S(2)}, u32[]{:S(2)}) collective-permute-start(bf16[128,384]{1,0:T(8,128)(2,1)S(1)} %get-tuple-element.31), channel_id=1, source_target_pairs={{0,3},{1,2},{2,1},{3,0},{4,7},{5,6},{6,5},{7,4},{8,11},{9,10},{10,... | collective-permute-start | bytes 294920 | tf_op jit(solution)/shard_map/ppermute | solution.py:335
  18.9 5.6 %collective-permute-start.3 = (bf16[128,384]{1,0:T(8,128)(2,1)S(1)}, bf16[128,384]{1,0:T(8,128)(2,1)S(1)}, u32[]{:S(2)}, u32[]{:S(2)}) collective-permute-start(bf16[128,384]{1,0:T(8,128)(2,1)S(1)} %get-tuple-element.32), channel_id=1, source_target_pairs={{0,4},{1,5},{2,6},{3,7},{4,0},{5,1},{6,2},{7,3},{8,12},{9,13},{10,... | collective-permute-start | bytes 294920 | tf_op jit(solution)/shard_map/ppermute | solution.py:335
  19.5 10.2 %collective-permute-start.4 = (bf16[128,384]{1,0:T(8,128)(2,1)S(1)}, bf16[128,384]{1,0:T(8,128)(2,1)S(1)}, u32[]{:S(2)}, u32[]{:S(2)}) collective-permute-start(bf16[128,384]{1,0:T(8,128)(2,1)S(1)} %get-tuple-element.38), channel_id=1, source_target_pairs={{0,5},{1,4},{2,7},{3,6},{4,1},{5,0},{6,3},{7,2},{8,13},{9,12},{10,... | collective-permute-start | bytes 294920 | tf_op jit(solution)/shard_map/ppermute | solution.py:335
  20.6 9.1 %collective-permute-start.5 = (bf16[128,384]{1,0:T(8,128)(2,1)S(1)}, bf16[128,384]{1,0:T(8,128)(2,1)S(1)}, u32[]{:S(2)}, u32[]{:S(2)}) collective-permute-start(bf16[128,384]{1,0:T(8,128)(2,1)S(1)} %get-tuple-element.39), channel_id=1, source_target_pairs={{0,6},{1,7},{2,4},{3,5},{4,2},{5,3},{6,0},{7,1},{8,14},{9,15},{10,... | collective-permute-start | bytes 294920 | tf_op jit(solution)/shard_map/ppermute | solution.py:335
  22.7 7.0 %collective-permute-start.6 = (bf16[128,384]{1,0:T(8,128)(2,1)S(1)}, bf16[128,384]{1,0:T(8,128)(2,1)S(1)}, u32[]{:S(2)}, u32[]{:S(2)}) collective-permute-start(bf16[128,384]{1,0:T(8,128)(2,1)S(1)} %get-tuple-element.40), channel_id=1, source_target_pairs={{0,7},{1,6},{2,5},{3,4},{4,3},{5,2},{6,1},{7,0},{8,15},{9,14},{10,... | collective-permute-start | bytes 294920 | tf_op jit(solution)/shard_map/ppermute | solution.py:335
  25.3 7.6 %collective-permute-start.9 = (bf16[25,16,128]{2,1,0:T(8,128)(2,1)S(1)}, bf16[25,16,128]{2,1,0:T(8,128)(2,1)S(1)}, u32[]{:S(2)}, u32[]{:S(2)}) collective-permute-start(bf16[25,16,128]{2,1,0:T(8,128)(2,1)S(1)} %get-tuple-element.46), channel_id=1, source_target_pairs={{0,24},{8,16},{16,8},{24,0},{1,25},{9,17},{17,9},{25,1},{2,26},{10... | collective-permute-start | bytes 307208 | tf_op jit(solution)/shard_map/ppermute | solution.py:374
  29.0 9.3 %collective-permute-start.7 = (bf16[25,16,128]{2,1,0:T(8,128)(2,1)S(1)}, bf16[25,16,128]{2,1,0:T(8,128)(2,1)S(1)}, u32[]{:S(2)}, u32[]{:S(2)}) collective-permute-start(bf16[25,16,128]{2,1,0:T(8,128)(2,1)S(1)} %get-tuple-element.42), channel_id=1, source_target_pairs={{0,16},{8,24},{16,0},{24,8},{1,17},{9,25},{17,1},{25,9},{2,18},{10... | collective-permute-start | bytes 307208 | tf_op jit(solution)/shard_map/ppermute | solution.py:374
  30.7 11.1 %collective-permute-start.11 = (bf16[56,16,128]{2,1,0:T(8,128)(2,1)S(1)}, bf16[56,16,128]{2,1,0:T(8,128)(2,1)S(1)}, u32[]{:S(2)}, u32[]{:S(2)}) collective-permute-start(bf16[56,16,128]{2,1,0:T(8,128)(2,1)S(1)} %get-tuple-element.49), channel_id=1, source_target_pairs={{0,8},{8,0},{16,24},{24,16},{1,9},{9,1},{17,25},{25,17},{2,10},{10... | collective-permute-start | bytes 688136 | tf_op jit(solution)/shard_map/ppermute | solution.py:374
  33.0 12.2 %collective-permute-start.10 = (bf16[32,16,128]{2,1,0:T(8,128)(2,1)S(1)}, bf16[32,16,128]{2,1,0:T(8,128)(2,1)S(1)}, u32[]{:S(2)}, u32[]{:S(2)}) collective-permute-start(bf16[32,16,128]{2,1,0:T(8,128)(2,1)S(1)} %get-tuple-element.48), channel_id=1, source_target_pairs={{0,24},{8,16},{16,8},{24,0},{1,25},{9,17},{17,9},{25,1},{2,26},{10... | collective-permute-start | bytes 393224 | tf_op jit(solution)/shard_map/ppermute | solution.py:374
  38.3 11.6 %collective-permute-start.8 = (bf16[32,16,128]{2,1,0:T(8,128)(2,1)S(1)}, bf16[32,16,128]{2,1,0:T(8,128)(2,1)S(1)}, u32[]{:S(2)}, u32[]{:S(2)}) collective-permute-start(bf16[32,16,128]{2,1,0:T(8,128)(2,1)S(1)} %get-tuple-element.44), channel_id=1, source_target_pairs={{0,16},{8,24},{16,0},{24,8},{1,17},{9,25},{17,1},{25,9},{2,18},{10... | collective-permute-start | bytes 393224 | tf_op jit(solution)/shard_map/ppermute | solution.py:374

commit v10 on v9

--- a/solution.py
+++ b/solution.py
@@ -62,8 +62,8 @@
     me = lax.axis_index("chan")
 
     def place(p):
-        c, k = me ^ steps[p // STRIPES], p % STRIPES
-        start = (firsts[c, k] + c * blocks_per) * CB
+        k = steps[p // STRIPES]
+        start = (firsts[k, p % STRIPES] + (me ^ k) * blocks_per) * CB
         base = jnp.minimum(start - lax.rem(start, LANES), channels - span)
         return start, pl.multiple_of(base, LANES)
 
@@ -291,13 +291,12 @@
     count = PAIRS * CB
     owners = pair_owner[:, 0]
 
-    firsts = lax.all_to_all(
-        jnp.broadcast_to(first_block[None, :], (n_chan, STRIPES)),
-        "chan",
-        split_axis=0,
-        concat_axis=0,
-        tiled=True,
-    )
+    def exchange(value, k):
+        return lax.ppermute(value, "chan", [(c, c ^ k) for c in range(n_chan)])
+
+    firsts = first_block.reshape(1, STRIPES)
+    while firsts.shape[0] < n_chan:
+        firsts = jnp.concatenate([firsts, exchange(firsts, firsts.shape[0])], 0)
     line = -(-(rows + 2 * outs + 4 * SPILL) // (2 * LANES)) * 2 * LANES
     weights = pl.pallas_call(
         weights_kernel,
@@ -331,9 +330,6 @@
         name="select_filter",
     )(firsts, raw_strain, weights)
 
-    def exchange(value, k):
-        return lax.ppermute(value, "chan", [(c, c ^ k) for c in range(n_chan)])
-
     half = n_chan // 2
     got = [sends[0]] + [exchange(sends[k], k) for k in range(1, n_chan)]
     steps = [[k] for k in range(n_chan)]
@@ -381,19 +377,19 @@
     arrived = {shift: [hand_over(value, shift)] for shift, value in zip(far, first)}
     plan = [(0, 2), (1, 2)] + [(shift, 1) for shift in far]
     own, near, *second = place(plan, late, "place_second")
-    arrived[0], arrived[1] = [own], [hand_over(near, 1)]
+    arrived[1] = [hand_over(near, 1)]
+    result = correlate(n_chan, owners, (own,), (2,), None, factor, n_tgroup == 1, samples)
     for shift, value in zip(far, second):
         value, held = lax.optimization_barrier((value, arrived[shift][0]))
+        if shift == far[-1]:
+            value, result = lax.optimization_barrier((value, result))
         arrived[shift] = [held, hand_over(value, shift)]
 
-    value = None
-    for at, shift in enumerate([0] + order):
+    for shift in order:
         parts = (0, 1) if shift in far else (2,)
-        last = at == n_tgroup - 1
-        value = correlate(
-            n_chan, owners, tuple(arrived[shift]), parts, value, factor, last, samples
-        )
-    return value
+        operands = (owners, tuple(arrived[shift]), parts, result)
+        result = correlate(n_chan, *operands, factor, shift == order[-1], samples)
+    return result
 
 
 def solution(mesh):

time: 54.8 us -> 58.2 us (1.062)
  starting transfers between devices: 19.1 us -> 23.9 us
  waiting for transfers between devices: 10.8 us -> 8.5 us
  other arithmetic: 0 us -> 2 us
  local copies, waits for them, and re-layouts: 1.93 us -> 0.68 us
    ppermute x7 -> x10, starting transfers between devices: 4.79 us -> 12.8 us  [exchange(): return lax.ppermute(value, 'chan', [(c, c ^ k) for c in range(n_chan)])]
    all_to_all x1 -> x0, starting transfers between devices: 5.17 us -> none  [local(): lax.all_to_all(jnp.broadcast_to(first_block[None, :], (n_chan, STRIPES)),...]
    all_to_all x1 -> x0, waiting for transfers between devices: 3.62 us -> none  [local(): lax.all_to_all(jnp.broadcast_to(first_block[None, :], (n_chan, STRIPES)),...]
    ppermute x5, starting transfers between devices: 9.12 us -> 11.1 us  [hand_over(): lax.ppermute(value, 'tgroup', [(g, g ^ shift) for g in range(n_tgroup)])]
    concatenate x0 -> x3, other arithmetic: none -> 2 us  [local(): firsts = jnp.concatenate([firsts, exchange(firsts, firsts.shape[0])], 0)]
    broadcast_in_dim x1 -> x0, local copies, waits for them, and re-layouts: 1.25 us -> none  [local(): jnp.broadcast_to(first_block[None, :], (n_chan, STRIPES))]
    ppermute x5, waiting for transfers between devices: 3.71 us -> 4.87 us  [hand_over(): lax.ppermute(value, 'tgroup', [(g, g ^ shift) for g in range(n_tgroup)])]
    ppermute x7 -> x10, waiting for transfers between devices: 3.47 us -> 3.63 us  [exchange(): return lax.ppermute(value, 'chan', [(c, c ^ k) for c in range(n_chan)])]
  transfers between devices with their start and end apart: 13 -> 15, of which waited for: 8 -> 6; matrix products, arithmetic and copies ran while one was open for 0% -> 0% of each run, Pallas kernels for 22% -> 21%
where the time goes in v10:
time: 58.2 us; the launch traced here: 58 us
  starting transfers between devices  23.9 us (41%)
  Pallas kernels  22.8 us (39%)
  waiting for transfers between devices  8.5 us (15%)
  other arithmetic  2 us (3%)
  local copies, waits for them, and re-layouts  0.68 us (1%)
    pallas_call x4, Pallas kernels, correlate(): pl.pallas_call(functools.partial(correlate_kernel, n_chan, groups, factor...  14.8 us
    ppermute x10, starting transfers between devices, exchange(): return lax.ppermute(value, 'chan', [(c, c ^ k) for c in range(n_chan)])  12.8 us
    ppermute x5, starting transfers between devices, hand_over(): lax.ppermute(value, 'tgroup', [(g, g ^ shift) for g in range(n_tgroup)])  11.1 us
    pallas_call x1, Pallas kernels, local(): pl.pallas_call(functools.partial(select_kernel, n_chan, groups), out_shap...  5.96 us
    ppermute x5, waiting for transfers between devices, hand_over(): lax.ppermute(value, 'tgroup', [(g, g ^ shift) for g in range(n_tgroup)])  4.87 us
    ppermute x10, waiting for transfers between devices, exchange(): return lax.ppermute(value, 'chan', [(c, c ^ k) for c in range(n_chan)])  3.63 us
    concatenate x3, other arithmetic, local(): firsts = jnp.concatenate([firsts, exchange(firsts, firsts.shape[0])], 0)  2 us
    pallas_call x2, Pallas kernels, place(): pl.pallas_call(functools.partial(place_kernel, n_chan, n_tgroup, outs, pl...  1.78 us
  transfers between devices with their start and end apart: 15, of which 6 were waited for; matrix products, arithmetic and copies ran while one was open for 0% of the time, Pallas kernels for 21%

profile of v10, /device:TPU:0, one launch (start us, length us, event | category | flops | bytes accessed | tf_op | source)
XLA Modules:
  0.0 58.0 jit_solution(8624046578144538183)
XLA Ops:
  0.0 0.5 collective-permute-start
  0.5 0.0 copy-start.1
  0.5 0.7 %copy-done.1 = f32[255]{0:T(256)S(1)} copy-done((f32[255]{0:T(256)S(1)}, f32[255]{0:T(256)}, u32[]{:S(2)}) %copy-start.1) | copy-done | bytes 1044
  1.1 0.3 fir_weights.1.weights
  1.4 0.0 collective-permute-done
  1.4 0.7 %pad_add_fusion.2 = s32[2,2]{1,0:T(2,128)S(1)} fusion(s32[1,2]{1,0:T(1,128)S(1)} %collective-permute-done, s32[1,2]{1,0:T(1,128)} %bitcast.11), kind=kLoop, calls=%fused_computation.2 | loop fusion | flops 4 | bytes 32 | tf_op jit(solution)/shard_map/concatenate | solution.py:299
  2.1 2.8 %collective-permute-start.1 = (s32[2,2]{1,0:T(2,128)S(1)}, s32[2,2]{1,0:T(2,128)S(1)}, u32[]{:S(2)}, u32[]{:S(2)}) collective-permute-start(s32[2,2]{1,0:T(2,128)S(1)} %pad_add_fusion.2), channel_id=1, source_target_pairs={{0,2},{1,3},{2,0},{3,1},{4,6},{5,7},{6,4},{7,5},{8,10},{9,11},{10,... | collective-permute-start | bytes 56 | tf_op jit(solution)/shard_map/ppermute | solution.py:295
  4.9 1.5 %collective-permute-done.1 = s32[2,2]{1,0:T(2,128)S(1)} collective-permute-done((s32[2,2]{1,0:T(2,128)S(1)}, s32[2,2]{1,0:T(2,128)S(1)}, u32[]{:S(2)}, u32[]{:S(2)}) %collective-permute-start.1) | collective-permute-done | bytes 48 | tf_op jit(solution)/shard_map/ppermute | solution.py:295
  6.4 0.7 %pad_add_fusion.1 = s32[4,2]{1,0:T(4,128)S(1)} fusion(s32[2,2]{1,0:T(2,128)S(1)} %collective-permute-done.1, s32[1,2]{1,0:T(1,128)S(1)} %collective-permute-done, s32[1,2]{1,0:T(1,128)} %bitcast.12), kind=kLoop, calls=%fused_computation.1 | loop fusion | flops 16 | bytes 64 | tf_op jit(solution)/shard_map/concatenate | solution.py:299
  7.1 2.1 %collective-permute-start.2 = (s32[4,2]{1,0:T(4,128)S(1)}, s32[4,2]{1,0:T(4,128)S(1)}, u32[]{:S(2)}, u32[]{:S(2)}) collective-permute-start(s32[4,2]{1,0:T(4,128)S(1)} %pad_add_fusion.1), channel_id=1, source_target_pairs={{0,4},{1,5},{2,6},{3,7},{4,0},{5,1},{6,2},{7,3},{8,12},{9,13},{10,... | collective-permute-start | bytes 104 | tf_op jit(solution)/shard_map/ppermute | solution.py:295
  9.1 1.6 %collective-permute-done.2 = s32[4,2]{1,0:T(4,128)S(1)} collective-permute-done((s32[4,2]{1,0:T(4,128)S(1)}, s32[4,2]{1,0:T(4,128)S(1)}, u32[]{:S(2)}, u32[]{:S(2)}) %collective-permute-start.2) | collective-permute-done | bytes 64 | tf_op jit(solution)/shard_map/ppermute | solution.py:295
  10.7 0.7 %pad_add_fusion.firsts = s32[8,2]{1,0:T(8,128)S(1)} fusion(s32[4,2]{1,0:T(4,128)S(1)} %collective-permute-done.2, s32[2,2]{1,0:T(2,128)S(1)} %collective-permute-done.1, s32[1,2]{1,0:T(1,128)S(1)} %collective-permute-done, s32[1,2]{1,0:T(1,128)} %bitcast.13), kind=kLoop, calls=%fused_computation | loop fusion | flops 48 | bytes 128 | tf_op jit(solution)/shard_map/concatenate | solution.py:299
  11.3 0.0 copy-start
  11.4 6.0 %select_filter.1 = (bf16[128,384]{1,0:T(8,128)(2,1)S(1)}, bf16[128,384]{1,0:T(8,128)(2,1)S(1)}, bf16[128,384]{1,0:T(8,128)(2,1)S(1)}, bf16[128,384]{1,0:T(8,128)...) custom-call(s32[8,2]{1,0:T(8,128)S(1)} %pad_add_fusion.firsts, ...), custom_call_target="tpu_custom_call" | custom-call | tf_op jit(solution)/shard_map/select_filter/pallas_call | solution.py:316
  17.3 0.1 collective-permute-start.3
  17.4 2.1 %collective-permute-start.4 = (bf16[128,384]{1,0:T(8,128)(2,1)S(1)}, bf16[128,384]{1,0:T(8,128)(2,1)S(1)}, u32[]{:S(2)}, u32[]{:S(2)}) collective-permute-start(bf16[128,384]{1,0:T(8,128)(2,1)S(1)} %get-tuple-element.32), channel_id=1, source_target_pairs={{0,2},{1,3},{2,0},{3,1},{4,6},{5,7},{6,4},{7,5},{8,10},{9,11},{10,... | collective-permute-start | bytes 294920 | tf_op jit(solution)/shard_map/ppermute | solution.py:295
  19.5 0.1 collective-permute-start.5
  19.5 1.8 %collective-permute-start.6 = (bf16[128,384]{1,0:T(8,128)(2,1)S(1)}, bf16[128,384]{1,0:T(8,128)(2,1)S(1)}, u32[]{:S(2)}, u32[]{:S(2)}) collective-permute-start(bf16[128,384]{1,0:T(8,128)(2,1)S(1)} %get-tuple-element.34), channel_id=1, source_target_pairs={{0,4},{1,5},{2,6},{3,7},{4,0},{5,1},{6,2},{7,3},{8,12},{9,13},{10,... | collective-permute-start | bytes 294920 | tf_op jit(solution)/shard_map/ppermute | solution.py:295
  21.3 0.0 collective-permute-start.7
  21.3 0.0 collective-permute-done.3.refs_1_
  21.3 2.6 %collective-permute-start.8 = (bf16[128,384]{1,0:T(8,128)(2,1)S(1)}, bf16[128,384]{1,0:T(8,128)(2,1)S(1)}, u32[]{:S(2)}, u32[]{:S(2)}) collective-permute-start(bf16[128,384]{1,0:T(8,128)(2,1)S(1)} %get-tuple-element.41), channel_id=1, source_target_pairs={{0,6},{1,7},{2,4},{3,5},{4,2},{5,3},{6,0},{7,1},{8,14},{9,15},{10,... | collective-permute-start | bytes 294920 | tf_op jit(solution)/shard_map/ppermute | solution.py:295
  23.9 0.0 collective-permute-done.4.refs_2_
  23.9 0.9 %collective-permute-start.9 = (bf16[128,384]{1,0:T(8,128)(2,1)S(1)}, bf16[128,384]{1,0:T(8,128)(2,1)S(1)}, u32[]{:S(2)}, u32[]{:S(2)}) collective-permute-start(bf16[128,384]{1,0:T(8,128)(2,1)S(1)} %get-tuple-element.42), channel_id=1, source_target_pairs={{0,7},{1,6},{2,5},{3,4},{4,3},{5,2},{6,1},{7,0},{8,15},{9,14},{10,... | collective-permute-start | bytes 294920 | tf_op jit(solution)/shard_map/ppermute | solution.py:295
  24.8 0.0 collective-permute-done.5.refs_3_
  24.8 0.0 collective-permute-done.6.refs_4_
  24.9 0.0 copy-done
  24.9 0.8 %place_first.1 = (bf16[25,16,128]{2,1,0:T(8,128)(2,1)S(1)}, bf16[25,16,128]{2,1,0:T(8,128)(2,1)S(1)}) custom-call(s32[16]{0:T(128)S(1)} %bitcast.3, bf16[128,384]{1,0:T(8,128)(2,1)S(1)} %get-tuple-element.35.refs_0_, bf16[128,384]{1,0:T(8,128)(2,1)S(1)} %collective-permute-done.3.refs_1_, bf16[128,384]{1,0:T(8,128)(2,1)S(1)} %collective-permute-done.4.refs_2_, ...), custom_call_target="tpu_custom_call" | custom-call | tf_op jit(solution)/shard_map/place_first/pallas_call | solution.py:353
  25.6 3.1 %collective-permute-start.10 = (bf16[25,16,128]{2,1,0:T(8,128)(2,1)S(1)}, bf16[25,16,128]{2,1,0:T(8,128)(2,1)S(1)}, u32[]{:S(2)}, u32[]{:S(2)}) collective-permute-start(bf16[25,16,128]{2,1,0:T(8,128)(2,1)S(1)} %get-tuple-element.44), channel_id=1, source_target_pairs={{0,16},{8,24},{16,0},{24,8},{1,17},{9,25},{17,1},{25,9},{2,18},{10... | collective-permute-start | bytes 307208 | tf_op jit(solution)/shard_map/ppermute | solution.py:370
  28.8 1.3 %collective-permute-start.12 = (bf16[25,16,128]{2,1,0:T(8,128)(2,1)S(1)}, bf16[25,16,128]{2,1,0:T(8,128)(2,1)S(1)}, u32[]{:S(2)}, u32[]{:S(2)}) collective-permute-start(bf16[25,16,128]{2,1,0:T(8,128)(2,1)S(1)} %get-tuple-element.50), channel_id=1, source_target_pairs={{0,24},{8,16},{16,8},{24,0},{1,25},{9,17},{17,9},{25,1},{2,26},{10... | collective-permute-start | bytes 307208 | tf_op jit(solution)/shard_map/ppermute | solution.py:370
  30.1 0.5 collective-permute-done.7.refs_5_
  30.6 0.0 collective-permute-done.8.refs_6_
  30.6 0.0 collective-permute-done.9.refs_7_
  30.6 1.0 %place_second.1 = (bf16[56,16,128]{2,1,0:T(8,128)(2,1)S(1)}, bf16[56,16,128]{2,1,0:T(8,128)(2,1)S(1)}, bf16[32,16,128]{2,1,0:T(8,128)(2,1)S(1)}, bf16[32,16,128]{2,1,0:T(8,128)(2,1)S(1)}) custom-call(s32[16]{0:T(128)S(1)} %bitcast.4, bf16[128,384]{1,0:T(8,128)(2,1)S(1)} %get-tuple-element.35.refs_0_, bf16[128,384]{1,0:T(8,128)(2,1)S(1)} %collective-permute-done.3.refs_1_, ...), custom_call_target="tpu_custom_call" | custom-call | tf_op jit(solution)/shard_map/place_second/pallas_call | solution.py:353
  31.6 1.6 %collective-permute-start.14 = (bf16[56,16,128]{2,1,0:T(8,128)(2,1)S(1)}, bf16[56,16,128]{2,1,0:T(8,128)(2,1)S(1)}, u32[]{:S(2)}, u32[]{:S(2)}) collective-permute-start(bf16[56,16,128]{2,1,0:T(8,128)(2,1)S(1)} %get-tuple-element.53), channel_id=1, source_target_pairs={{0,8},{8,0},{16,24},{24,16},{1,9},{9,1},{17,25},{25,17},{2,10},{10... | collective-permute-start | bytes 688136 | tf_op jit(solution)/shard_map/ppermute | solution.py:370
  33.2 3.3 %correlate.3.refs_1_ = f32[5,256,256]{2,1,0:T(8,128)S(1)} custom-call(s32[16]{0:T(128)S(1)} %bitcast.5, bf16[56,16,128]{2,1,0:T(8,128)(2,1)S(1)} %get-tuple-element.47.refs_0_), custom_call_target="tpu_custom_call" | custom-call | tf_op jit(solution)/shard_map/correlate/pallas_call | solution.py:270
  36.6 0.3 collective-permute-done.10.refs_0_
  36.9 0.0 collective-permute-done.12.refs_0_
  36.9 3.8 %collective-permute-start.13 = (bf16[32,16,128]{2,1,0:T(8,128)(2,1)S(1)}, bf16[32,16,128]{2,1,0:T(8,128)(2,1)S(1)}, u32[]{:S(2)}, u32[]{:S(2)}) collective-permute-start(bf16[32,16,128]{2,1,0:T(8,128)(2,1)S(1)} %get-tuple-element.52), channel_id=1, source_target_pairs={{0,24},{8,16},{16,8},{24,0},{1,25},{9,17},{17,9},{25,1},{2,26},{10... | collective-permute-start | bytes 393224 | tf_op jit(solution)/shard_map/ppermute | solution.py:370
  40.7 1.2 %collective-permute-start.11 = (bf16[32,16,128]{2,1,0:T(8,128)(2,1)S(1)}, bf16[32,16,128]{2,1,0:T(8,128)(2,1)S(1)}, u32[]{:S(2)}, u32[]{:S(2)}) collective-permute-start(bf16[32,16,128]{2,1,0:T(8,128)(2,1)S(1)} %get-tuple-element.48), channel_id=1, source_target_pairs={{0,16},{8,24},{16,0},{24,8},{1,17},{9,25},{17,1},{25,9},{2,18},{10... | collective-permute-start | bytes 393224 | tf_op jit(solution)/shard_map/ppermute | solution.py:370
  41.9 0.2 collective-permute-done.14.refs_0_
  42.1 3.3 %correlate.4.refs_2_ = f32[5,256,256]{2,1,0:T(8,128)S(1)} custom-call(s32[16]{0:T(128)S(1)} %bitcast.6, bf16[56,16,128]{2,1,0:T(8,128)(2,1)S(1)} %collective-permute-done.14.refs_0_, f32[5,256,256]{2,1,0:T(8,128)S(1)} %correlate.3.refs_1_), custom_call_target="tpu_custom_call" | custom-call | tf_op jit(solution)/shard_map/correlate/pallas_call | solution.py:270
  45.4 0.0 collective-permute-done.13.refs_1_
  45.5 3.3 %correlate.5.refs_2_ = f32[5,256,256]{2,1,0:T(8,128)S(1)} custom-call(s32[16]{0:T(128)S(1)} %bitcast.7, bf16[25,16,128]{2,1,0:T(8,128)(2,1)S(1)} %collective-permute-done.12.refs_0_, bf16[32,16,128]{2,1,0:T(8,128)(2,1)S(1)} %collective-permute-done.13.refs_1_, f32[5,256,256]{2,1,0:T(8,128)S(1)} %correlate.4.refs_2_), custom_call_target="tpu_custom_call" | custom-call | tf_op jit(solution)/shard_map/correlate/pallas_call | solution.py:270
  48.8 4.3 %collective-permute-done.11.refs_1_ = bf16[32,16,128]{2,1,0:T(8,128)(2,1)S(1)} collective-permute-done((bf16[32,16,128]{2,1,0:T(8,128)(2,1)S(1)}, bf16[32,16,128]{2,1,0:T(8,128)(2,1)S(1)}, u32[]{:S(2)}, u32[]{:S(2)}) %collective-permute-start.11) | collective-permute-done | bytes 131104 | tf_op jit(solution)/shard_map/ppermute | solution.py:370
  53.1 4.9 %correlate_last.1 = f32[5,8,8,1001]{3,2,1,0:T(8,128)} custom-call(s32[16]{0:T(128)S(1)} %bitcast.8, bf16[25,16,128]{2,1,0:T(8,128)(2,1)S(1)} %collective-permute-done.10.refs_0_, bf16[32,16,128]{2,1,0:T(8,128)(2,1)S(1)} %collective-permute-done.11.refs_1_, f32[5,256,256]{2,1,0:T(8,128)S(1)} %correlate.5.refs_2_), custom_call_target="tpu_custom_call" | custom-call | tf_op jit(solution)/shard_map/correlate_last/pallas_call | solution.py:270
Async XLA Ops:
  0.0 1.4 %collective-permute-start = (s32[1,2]{1,0:T(1,128)}, s32[1,2]{1,0:T(1,128)S(1)}, u32[]{:S(2)}, u32[]{:S(2)}) collective-permute-start(s32[1,2]{1,0:T(1,128)} %bitcast.10), channel_id=1, source_target_pairs={{0,1},{1,0},{2,3},{3,2},{4,5},{5,4},{6,7},{7,6},{8,9},{9,8},{10,11... | collective-permute-start | bytes 32 | tf_op jit(solution)/shard_map/ppermute | solution.py:295
  0.5 0.7 %copy-start.1 = (f32[255]{0:T(256)S(1)}, f32[255]{0:T(256)}, u32[]{:S(2)}) copy-start(f32[255]{0:T(256)} %param.5) | copy-start | bytes 3064
  2.1 4.3 %collective-permute-start.1 = (s32[2,2]{1,0:T(2,128)S(1)}, s32[2,2]{1,0:T(2,128)S(1)}, u32[]{:S(2)}, u32[]{:S(2)}) collective-permute-start(s32[2,2]{1,0:T(2,128)S(1)} %pad_add_fusion.2), channel_id=1, source_target_pairs={{0,2},{1,3},{2,0},{3,1},{4,6},{5,7},{6,4},{7,5},{8,10},{9,11},{10,... | collective-permute-start | bytes 56 | tf_op jit(solution)/shard_map/ppermute | solution.py:295
  7.1 3.6 %collective-permute-start.2 = (s32[4,2]{1,0:T(4,128)S(1)}, s32[4,2]{1,0:T(4,128)S(1)}, u32[]{:S(2)}, u32[]{:S(2)}) collective-permute-start(s32[4,2]{1,0:T(4,128)S(1)} %pad_add_fusion.1), channel_id=1, source_target_pairs={{0,4},{1,5},{2,6},{3,7},{4,0},{5,1},{6,2},{7,3},{8,12},{9,13},{10,... | collective-permute-start | bytes 104 | tf_op jit(solution)/shard_map/ppermute | solution.py:295
  11.3 13.5 %copy-start = (s32[16,1]{0,1:T(1,128)S(1)}, s32[16,1]{0,1:T(1,128)}, u32[]{:S(2)}) copy-start(s32[16,1]{0,1:T(1,128)} %param.7) | copy-start | bytes 196
  17.3 4.0 %collective-permute-start.3 = (bf16[128,384]{1,0:T(8,128)(2,1)S(1)}, bf16[128,384]{1,0:T(8,128)(2,1)S(1)}, u32[]{:S(2)}, u32[]{:S(2)}) collective-permute-start(bf16[128,384]{1,0:T(8,128)(2,1)S(1)} %get-tuple-element.31), channel_id=1, source_target_pairs={{0,1},{1,0},{2,3},{3,2},{4,5},{5,4},{6,7},{7,6},{8,9},{9,8},{10,11... | collective-permute-start | bytes 294920 | tf_op jit(solution)/shard_map/ppermute | solution.py:295
  17.4 6.5 %collective-permute-start.4 = (bf16[128,384]{1,0:T(8,128)(2,1)S(1)}, bf16[128,384]{1,0:T(8,128)(2,1)S(1)}, u32[]{:S(2)}, u32[]{:S(2)}) collective-permute-start(bf16[128,384]{1,0:T(8,128)(2,1)S(1)} %get-tuple-element.32), channel_id=1, source_target_pairs={{0,2},{1,3},{2,0},{3,1},{4,6},{5,7},{6,4},{7,5},{8,10},{9,11},{10,... | collective-permute-start | bytes 294920 | tf_op jit(solution)/shard_map/ppermute | solution.py:295
  19.5 5.4 %collective-permute-start.5 = (bf16[128,384]{1,0:T(8,128)(2,1)S(1)}, bf16[128,384]{1,0:T(8,128)(2,1)S(1)}, u32[]{:S(2)}, u32[]{:S(2)}) collective-permute-start(bf16[128,384]{1,0:T(8,128)(2,1)S(1)} %get-tuple-element.33), channel_id=1, source_target_pairs={{0,3},{1,2},{2,1},{3,0},{4,7},{5,6},{6,5},{7,4},{8,11},{9,10},{10,... | collective-permute-start | bytes 294920 | tf_op jit(solution)/shard_map/ppermute | solution.py:295
  19.5 5.3 %collective-permute-start.6 = (bf16[128,384]{1,0:T(8,128)(2,1)S(1)}, bf16[128,384]{1,0:T(8,128)(2,1)S(1)}, u32[]{:S(2)}, u32[]{:S(2)}) collective-permute-start(bf16[128,384]{1,0:T(8,128)(2,1)S(1)} %get-tuple-element.34), channel_id=1, source_target_pairs={{0,4},{1,5},{2,6},{3,7},{4,0},{5,1},{6,2},{7,3},{8,12},{9,13},{10,... | collective-permute-start | bytes 294920 | tf_op jit(solution)/shard_map/ppermute | solution.py:295
  21.3 9.3 %collective-permute-start.7 = (bf16[128,384]{1,0:T(8,128)(2,1)S(1)}, bf16[128,384]{1,0:T(8,128)(2,1)S(1)}, u32[]{:S(2)}, u32[]{:S(2)}) collective-permute-start(bf16[128,384]{1,0:T(8,128)(2,1)S(1)} %get-tuple-element.40), channel_id=1, source_target_pairs={{0,5},{1,4},{2,7},{3,6},{4,1},{5,0},{6,3},{7,2},{8,13},{9,12},{10,... | collective-permute-start | bytes 294920 | tf_op jit(solution)/shard_map/ppermute | solution.py:295
  21.3 9.3 %collective-permute-start.8 = (bf16[128,384]{1,0:T(8,128)(2,1)S(1)}, bf16[128,384]{1,0:T(8,128)(2,1)S(1)}, u32[]{:S(2)}, u32[]{:S(2)}) collective-permute-start(bf16[128,384]{1,0:T(8,128)(2,1)S(1)} %get-tuple-element.41), channel_id=1, source_target_pairs={{0,6},{1,7},{2,4},{3,5},{4,2},{5,3},{6,0},{7,1},{8,14},{9,15},{10,... | collective-permute-start | bytes 294920 | tf_op jit(solution)/shard_map/ppermute | solution.py:295
  23.9 6.7 %collective-permute-start.9 = (bf16[128,384]{1,0:T(8,128)(2,1)S(1)}, bf16[128,384]{1,0:T(8,128)(2,1)S(1)}, u32[]{:S(2)}, u32[]{:S(2)}) collective-permute-start(bf16[128,384]{1,0:T(8,128)(2,1)S(1)} %get-tuple-element.42), channel_id=1, source_target_pairs={{0,7},{1,6},{2,5},{3,4},{4,3},{5,2},{6,1},{7,0},{8,15},{9,14},{10,... | collective-permute-start | bytes 294920 | tf_op jit(solution)/shard_map/ppermute | solution.py:295
  25.6 11.2 %collective-permute-start.10 = (bf16[25,16,128]{2,1,0:T(8,128)(2,1)S(1)}, bf16[25,16,128]{2,1,0:T(8,128)(2,1)S(1)}, u32[]{:S(2)}, u32[]{:S(2)}) collective-permute-start(bf16[25,16,128]{2,1,0:T(8,128)(2,1)S(1)} %get-tuple-element.44), channel_id=1, source_target_pairs={{0,16},{8,24},{16,0},{24,8},{1,17},{9,25},{17,1},{25,9},{2,18},{10... | collective-permute-start | bytes 307208 | tf_op jit(solution)/shard_map/ppermute | solution.py:370
  28.8 8.1 %collective-permute-start.12 = (bf16[25,16,128]{2,1,0:T(8,128)(2,1)S(1)}, bf16[25,16,128]{2,1,0:T(8,128)(2,1)S(1)}, u32[]{:S(2)}, u32[]{:S(2)}) collective-permute-start(bf16[25,16,128]{2,1,0:T(8,128)(2,1)S(1)} %get-tuple-element.50), channel_id=1, source_target_pairs={{0,24},{8,16},{16,8},{24,0},{1,25},{9,17},{17,9},{25,1},{2,26},{10... | collective-permute-start | bytes 307208 | tf_op jit(solution)/shard_map/ppermute | solution.py:370
  31.6 10.5 %collective-permute-start.14 = (bf16[56,16,128]{2,1,0:T(8,128)(2,1)S(1)}, bf16[56,16,128]{2,1,0:T(8,128)(2,1)S(1)}, u32[]{:S(2)}, u32[]{:S(2)}) collective-permute-start(bf16[56,16,128]{2,1,0:T(8,128)(2,1)S(1)} %get-tuple-element.53), channel_id=1, source_target_pairs={{0,8},{8,0},{16,24},{24,16},{1,9},{9,1},{17,25},{25,17},{2,10},{10... | collective-permute-start | bytes 688136 | tf_op jit(solution)/shard_map/ppermute | solution.py:370
  36.9 8.6 %collective-permute-start.13 = (bf16[32,16,128]{2,1,0:T(8,128)(2,1)S(1)}, bf16[32,16,128]{2,1,0:T(8,128)(2,1)S(1)}, u32[]{:S(2)}, u32[]{:S(2)}) collective-permute-start(bf16[32,16,128]{2,1,0:T(8,128)(2,1)S(1)} %get-tuple-element.52), channel_id=1, source_target_pairs={{0,24},{8,16},{16,8},{24,0},{1,25},{9,17},{17,9},{25,1},{2,26},{10... | collective-permute-start | bytes 393224 | tf_op jit(solution)/shard_map/ppermute | solution.py:370
  40.7 12.4 %collective-permute-start.11 = (bf16[32,16,128]{2,1,0:T(8,128)(2,1)S(1)}, bf16[32,16,128]{2,1,0:T(8,128)(2,1)S(1)}, u32[]{:S(2)}, u32[]{:S(2)}) collective-permute-start(bf16[32,16,128]{2,1,0:T(8,128)(2,1)S(1)} %get-tuple-element.48), channel_id=1, source_target_pairs={{0,16},{8,24},{16,0},{24,8},{1,17},{9,25},{17,1},{25,9},{2,18},{10... | collective-permute-start | bytes 393224 | tf_op jit(solution)/shard_map/ppermute | solution.py:370

commit v11 on v9

--- a/solution.py
+++ b/solution.py
@@ -56,7 +56,7 @@
     sends, (window, picked, sems) = refs[: len(groups)], refs[len(groups) :]
     rows, channels = raw.shape
     steps = [k for group in groups for k in group]
-    stripes = n_chan * STRIPES
+    stripes = len(steps) * STRIPES
     blocks_per = channels // n_chan // CB
     span = window.shape[2]
     me = lax.axis_index("chan")
@@ -78,7 +78,8 @@
     lane = lax.broadcasted_iota(jnp.int32, (WIDE, span), 1)
     batch = 2 * STRIPES
     for first in range(0, stripes, batch):
-        for p in range(first, first + batch):
+        last = min(first + batch, stripes)
+        for p in range(first, last):
             copy(p).wait()
             start, base = place(p)
             hot = (lane == row + (start - base)) & (row < channels - start)
@@ -86,12 +87,12 @@
             block = window[p].astype(jnp.bfloat16)
             chosen = lax.dot_general(hot, block, NT, preferred_element_type=jnp.float32)
             picked[p * WIDE : (p + 1) * WIDE, :] = chosen.astype(jnp.bfloat16)
-        part = slice(first * WIDE, (first + batch) * WIDE)
+        part = slice(first * WIDE, last * WIDE)
         result = jnp.dot(
             picked[part, :], weights[...], preferred_element_type=jnp.float32
         ).astype(jnp.bfloat16)
         height = STRIPES * WIDE
-        for at in range(batch // STRIPES):
+        for at in range((last - first) // STRIPES):
             k = steps[first // STRIPES + at]
             out, where = [(o, g.index(k)) for o, g in enumerate(groups) if k in g][0]
             sends[out][where * height : (where + 1) * height, :] = result[at * height : (at + 1) * height]
@@ -313,30 +314,40 @@
         name="fir_weights",
     )(whitening_taps.reshape(1, TAPS))
 
-    groups = [[k] for k in range(n_chan)]
-    sends = pl.pallas_call(
-        functools.partial(select_kernel, n_chan, groups),
-        out_shape=[
-            jax.ShapeDtypeStruct((len(group) * count, outs + 2 * SPILL), jnp.bfloat16)
-            for group in groups
-        ],
-        in_specs=[smem(), pl.BlockSpec(memory_space=pl.ANY), vmem()],
-        out_specs=[vmem()] * len(groups),
-        scratch_shapes=[
-            pltpu.VMEM((n_chan * STRIPES, rows, 2 * LANES), jnp.float32),
-            pltpu.VMEM((n_chan * count, rows), jnp.bfloat16),
-            pltpu.SemaphoreType.DMA((n_chan * STRIPES,)),
-        ],
-        compiler_params=params(40),
-        name="select_filter",
-    )(firsts, raw_strain, weights)
-
+    split = n_chan == 8 and outs % LANES == 0
+    pieces = {}
+    for part in ([2, 3, 4], [1, 5, 6, 7, 0]) if split else (range(n_chan),):
+        part = list(part)
+        if pieces:
+            weights, _ = lax.optimization_barrier((weights, list(pieces.values())))
+        made = pl.pallas_call(
+            functools.partial(select_kernel, n_chan, [[k] for k in part]),
+            out_shape=[jax.ShapeDtypeStruct((count, outs + 2 * SPILL), jnp.bfloat16)] * len(part),
+            in_specs=[smem(), pl.BlockSpec(memory_space=pl.ANY), vmem()],
+            out_specs=[vmem()] * len(part),
+            scratch_shapes=[
+                pltpu.VMEM((len(part) * STRIPES, rows, 2 * LANES), jnp.float32),
+                pltpu.VMEM((len(part) * count, rows), jnp.bfloat16),
+                pltpu.SemaphoreType.DMA((len(part) * STRIPES,)),
+            ],
+            compiler_params=params(40),
+            name="select_filter",
+        )(firsts, raw_strain, weights)
+        pieces.update(zip(part, made))
     def exchange(value, k):
         return lax.ppermute(value, "chan", [(c, c ^ k) for c in range(n_chan)])
 
     half = n_chan // 2
-    got = [sends[0]] + [exchange(sends[k], k) for k in range(1, n_chan)]
-    steps = [[k] for k in range(n_chan)]
+    moved = {}
+    for k, value in pieces.items():
+        if split and k in (1, 5):
+            held = 2 if k == 1 else 3
+            value, moved[held] = lax.optimization_barrier((value, moved[held]))
+        if k:
+            moved[k] = exchange(value, k)
+    got = [pieces[0]] + [moved[k] for k in range(1, n_chan)]
+    steps = [[k] for k in ([2, 3, 1, 0, 4, 5, 6, 7] if split else range(n_chan))]
+    got = [got[k] for (k,) in steps]
     early, late = got[:half], got
 
     if outs % LANES:
@@ -374,8 +385,10 @@
         return lax.ppermute(value, "tgroup", [(g, g ^ shift) for g in range(n_tgroup)])
 
     if outs % LANES == 0:
-        early, got[half] = lax.optimization_barrier((early, got[half]))
-        late = list(early) + got[half:]
+        held = early[:2] + got[half : half + 1] + early[2:]
+        held = lax.optimization_barrier(held)
+        early = held[:2] + held[3:]
+        late = early + held[2:3] + got[half + 1 :]
     far = order[1:]
     first = place([(shift, 0) for shift in far], early, "place_first")
     arrived = {shift: [hand_over(value, shift)] for shift, value in zip(far, first)}

time: 54.8 us -> 56.8 us (1.036)
  waiting for transfers between devices: 10.8 us -> 8.64 us
  starting transfers between devices: 19.1 us -> 21.2 us
  Pallas kernels: 22.7 us -> 24.7 us
    ppermute x7, waiting for transfers between devices: 3.47 us -> 1.22 us  [exchange(): return lax.ppermute(value, 'chan', [(c, c ^ k) for c in range(n_chan)])]
    ppermute x7, starting transfers between devices: 4.79 us -> 6.65 us  [exchange(): return lax.ppermute(value, 'chan', [(c, c ^ k) for c in range(n_chan)])]
    pallas_call x1 -> x2, Pallas kernels: 5.95 us -> 7.74 us  [local(): pl.pallas_call(functools.partial(select_kernel, n_chan, [[k] for k in par...]
  transfers between devices with their start and end apart: 13 -> 13, of which waited for: 8 -> 4; matrix products, arithmetic and copies ran while one was open for 0% -> 0% of each run, Pallas kernels for 22% -> 29%
where the time goes in v11:
time: 56.8 us; the launch traced here: 56.6 us
  Pallas kernels  24.7 us (43%)
  starting transfers between devices  21.2 us (37%)
  waiting for transfers between devices  8.64 us (15%)
  local copies, waits for them, and re-layouts  1.93 us (3%)
    pallas_call x4, Pallas kernels, correlate(): pl.pallas_call(functools.partial(correlate_kernel, n_chan, groups, factor...  14.9 us
    ppermute x5, starting transfers between devices, hand_over(): lax.ppermute(value, 'tgroup', [(g, g ^ shift) for g in range(n_tgroup)])  9.43 us
    pallas_call x2, Pallas kernels, local(): pl.pallas_call(functools.partial(select_kernel, n_chan, [[k] for k in par...  7.74 us
    ppermute x7, starting transfers between devices, exchange(): return lax.ppermute(value, 'chan', [(c, c ^ k) for c in range(n_chan)])  6.65 us
    all_to_all x1, starting transfers between devices, local(): lax.all_to_all(jnp.broadcast_to(first_block[None, :], (n_chan, STRIPES)),...  5.17 us
    ppermute x5, waiting for transfers between devices, hand_over(): lax.ppermute(value, 'tgroup', [(g, g ^ shift) for g in range(n_tgroup)])  3.8 us
    all_to_all x1, waiting for transfers between devices, local(): lax.all_to_all(jnp.broadcast_to(first_block[None, :], (n_chan, STRIPES)),...  3.62 us
    pallas_call x2, Pallas kernels, place(): pl.pallas_call(functools.partial(place_kernel, n_chan, n_tgroup, outs, pl...  1.79 us
  transfers between devices with their start and end apart: 13, of which 4 were waited for; matrix products, arithmetic and copies ran while one was open for 0% of the time, Pallas kernels for 29%

profile of v11, /device:TPU:0, one launch (start us, length us, event | category | flops | bytes accessed | tf_op | source)
XLA Modules:
  0.0 56.6 jit_solution(1724646679579972192)
XLA Ops:
  0.0 1.2 %broadcast_in_dim.2 = s32[8,1,2]{2,1,0:T(1,128)} broadcast(s32[2]{0:T(128)} %param.6), dimensions={2} | broadcast | bytes 72 | tf_op jit(solution)/shard_map/broadcast_in_dim | solution.py:296
  1.2 5.2 %all-to-all-start = ((s32[8,1,2]{2,1,0:T(1,128)}), s32[8,1,2]{2,1,0:T(1,128)S(1)}, u32[]{:S(2)}, u32[]{:S(2)}) async-start(s32[8,1,2]{2,1,0:T(1,128)} %broadcast_in_dim.2), calls=%async_computation | async-start | bytes 8192 | tf_op jit(solution)/shard_map/all_to_all | solution.py:295
  6.4 0.0 copy-start.1
  6.4 0.7 %copy-done.1 = f32[255]{0:T(256)S(1)} copy-done((f32[255]{0:T(256)S(1)}, f32[255]{0:T(256)}, u32[]{:S(2)}) %copy-start.1) | copy-done | bytes 1044
  7.1 0.3 fir_weights.1.weights
  7.4 3.6 %all-to-all-done = s32[8,1,2]{2,1,0:T(1,128)S(1)} async-done(((s32[8,1,2]{2,1,0:T(1,128)}), s32[8,1,2]{2,1,0:T(1,128)S(1)}, u32[]{:S(2)}, u32[]{:S(2)}) %all-to-all-start) | async-done | bytes 96 | tf_op jit(solution)/shard_map/all_to_all | solution.py:295
  11.0 3.3 %select_filter.2 = (bf16[128,384]{1,0:T(8,128)(2,1)S(1)}, bf16[128,384]{1,0:T(8,128)(2,1)S(1)}, bf16[128,384]{1,0:T(8,128)(2,1)S(1)}) custom-call(s32[8,2]{1,0:T(8,128)S(1)} %bitcast.3, f32[512,10240]{1,0:T(8,128)} %raw.3, bf16[512,384]{1,0:T(8,128)(2,1)S(1)} %fir_weights.1.weights), custom_call_target="tpu_custom_call" | custom-call | tf_op jit(solution)/shard_map/select_filter/pallas_call | solution.py:323
  14.3 0.6 %collective-permute-start = (bf16[128,384]{1,0:T(8,128)(2,1)S(1)}, bf16[128,384]{1,0:T(8,128)(2,1)S(1)}, u32[]{:S(2)}, u32[]{:S(2)}) collective-permute-start(bf16[128,384]{1,0:T(8,128)(2,1)S(1)} %get-tuple-element.33), channel_id=1, source_target_pairs={{0,2},{1,3},{2,0},{3,1},{4,6},{5,7},{6,4},{7,5},{8,10},{9,11},{10,... | collective-permute-start | bytes 294920 | tf_op jit(solution)/shard_map/ppermute | solution.py:338
  15.0 0.6 %collective-permute-start.1 = (bf16[128,384]{1,0:T(8,128)(2,1)S(1)}, bf16[128,384]{1,0:T(8,128)(2,1)S(1)}, u32[]{:S(2)}, u32[]{:S(2)}) collective-permute-start(bf16[128,384]{1,0:T(8,128)(2,1)S(1)} %get-tuple-element.34), channel_id=1, source_target_pairs={{0,3},{1,2},{2,1},{3,0},{4,7},{5,6},{6,5},{7,4},{8,11},{9,10},{10,... | collective-permute-start | bytes 294920 | tf_op jit(solution)/shard_map/ppermute | solution.py:338
  15.6 0.0 copy-start
  15.6 0.6 collective-permute-start.2
  16.1 4.4 %select_filter.3 = (bf16[128,384]{1,0:T(8,128)(2,1)S(1)}, bf16[128,384]{1,0:T(8,128)(2,1)S(1)}, bf16[128,384]{1,0:T(8,128)(2,1)S(1)}, bf16[128,384]{1,0:T(8,128)(2,1)S(1)}, bf16[128,384]{1,0:T(8,128)(2,1)S(1)}) custom-call(s32[8,2]{1,0:T(8,128)S(1)} %bitcast.4, f32[512,10240]{1,0:T(8,128)} %raw.3, bf16[512,384]{1,0:T(8,128)(2,1)S(1)} %fir_weights.1.weights), custom_call_target="tpu_custom_call" | custom-call | tf_op jit(solution)/shard_map/select_filter/pallas_call | solution.py:323
  20.5 0.0 collective-permute-done.refs_0_
  20.6 0.8 %collective-permute-start.3 = (bf16[128,384]{1,0:T(8,128)(2,1)S(1)}, bf16[128,384]{1,0:T(8,128)(2,1)S(1)}, u32[]{:S(2)}, u32[]{:S(2)}) collective-permute-start(bf16[128,384]{1,0:T(8,128)(2,1)S(1)} %get-tuple-element.41), channel_id=1, source_target_pairs={{0,1},{1,0},{2,3},{3,2},{4,5},{5,4},{6,7},{7,6},{8,9},{9,8},{10,11... | collective-permute-start | bytes 294920 | tf_op jit(solution)/shard_map/ppermute | solution.py:338
  21.3 1.5 %collective-permute-start.5 = (bf16[128,384]{1,0:T(8,128)(2,1)S(1)}, bf16[128,384]{1,0:T(8,128)(2,1)S(1)}, u32[]{:S(2)}, u32[]{:S(2)}) collective-permute-start(bf16[128,384]{1,0:T(8,128)(2,1)S(1)} %get-tuple-element.49), channel_id=1, source_target_pairs={{0,6},{1,7},{2,4},{3,5},{4,2},{5,3},{6,0},{7,1},{8,14},{9,15},{10,... | collective-permute-start | bytes 294920 | tf_op jit(solution)/shard_map/ppermute | solution.py:338
  22.8 0.9 %collective-permute-start.6 = (bf16[128,384]{1,0:T(8,128)(2,1)S(1)}, bf16[128,384]{1,0:T(8,128)(2,1)S(1)}, u32[]{:S(2)}, u32[]{:S(2)}) collective-permute-start(bf16[128,384]{1,0:T(8,128)(2,1)S(1)} %get-tuple-element.50), channel_id=1, source_target_pairs={{0,7},{1,6},{2,5},{3,4},{4,3},{5,2},{6,1},{7,0},{8,15},{9,14},{10,... | collective-permute-start | bytes 294920 | tf_op jit(solution)/shard_map/ppermute | solution.py:338
  23.6 0.0 collective-permute-done.1.refs_1_
  23.6 1.8 %collective-permute-start.4 = (bf16[128,384]{1,0:T(8,128)(2,1)S(1)}, bf16[128,384]{1,0:T(8,128)(2,1)S(1)}, u32[]{:S(2)}, u32[]{:S(2)}) collective-permute-start(bf16[128,384]{1,0:T(8,128)(2,1)S(1)} %get-tuple-element.48), channel_id=1, source_target_pairs={{0,5},{1,4},{2,7},{3,6},{4,1},{5,0},{6,3},{7,2},{8,13},{9,12},{10,... | collective-permute-start | bytes 294920 | tf_op jit(solution)/shard_map/ppermute | solution.py:338
  25.4 0.0 collective-permute-done.2.refs_4_
  25.4 0.0 collective-permute-done.3.refs_2_
  25.4 0.0 copy-done
  25.4 0.8 %place_first.1 = (bf16[25,16,128]{2,1,0:T(8,128)(2,1)S(1)}, bf16[25,16,128]{2,1,0:T(8,128)(2,1)S(1)}) custom-call(s32[16]{0:T(128)S(1)} %bitcast.5, bf16[128,384]{1,0:T(8,128)(2,1)S(1)} %collective-permute-done.refs_0_, bf16[128,384]{1,0:T(8,128)(2,1)S(1)} %collective-permute-done.1.refs_1_, bf16[128,384]{1,0:T(8,128)(2,1)S(1)} %collective-permute-done.3.refs_2_, ...), custom_call_target="tpu_custom_call" | custom-call | tf_op jit(solution)/shard_map/place_first/pallas_call | solution.py:368
  26.2 3.7 %collective-permute-start.9 = (bf16[25,16,128]{2,1,0:T(8,128)(2,1)S(1)}, bf16[25,16,128]{2,1,0:T(8,128)(2,1)S(1)}, u32[]{:S(2)}, u32[]{:S(2)}) collective-permute-start(bf16[25,16,128]{2,1,0:T(8,128)(2,1)S(1)} %get-tuple-element.56), channel_id=1, source_target_pairs={{0,24},{8,16},{16,8},{24,0},{1,25},{9,17},{17,9},{25,1},{2,26},{10... | collective-permute-start | bytes 307208 | tf_op jit(solution)/shard_map/ppermute | solution.py:385
  29.9 0.0 collective-permute-start.7
  29.9 0.0 collective-permute-done.5.refs_6_
  29.9 0.0 collective-permute-done.6.refs_7_
  29.9 1.2 %collective-permute-done.4.refs_5_ = bf16[128,384]{1,0:T(8,128)(2,1)S(1)} collective-permute-done((bf16[128,384]{1,0:T(8,128)(2,1)S(1)}, bf16[128,384]{1,0:T(8,128)(2,1)S(1)}, u32[]{:S(2)}, u32[]{:S(2)}) %collective-permute-start.4) | collective-permute-done | bytes 98336 | tf_op jit(solution)/shard_map/ppermute | solution.py:338
  31.1 1.0 %place_second.1 = (bf16[56,16,128]{2,1,0:T(8,128)(2,1)S(1)}, bf16[56,16,128]{2,1,0:T(8,128)(2,1)S(1)}, bf16[32,16,128]{2,1,0:T(8,128)(2,1)S(1)}, bf16[32,16,128]{2,1,0:T(8,128)(2,1)S(1)}) custom-call(s32[16]{0:T(128)S(1)} %bitcast.6, bf16[128,384]{1,0:T(8,128)(2,1)S(1)} %collective-permute-done.refs_0_, bf16[128,384]{1,0:T(8,128)(2,1)S(1)} %collective-permute-done.1.refs_1_, ...), custom_call_target="tpu_custom_call" | custom-call | tf_op jit(solution)/shard_map/place_second/pallas_call | solution.py:368
  32.1 1.6 %collective-permute-start.11 = (bf16[56,16,128]{2,1,0:T(8,128)(2,1)S(1)}, bf16[56,16,128]{2,1,0:T(8,128)(2,1)S(1)}, u32[]{:S(2)}, u32[]{:S(2)}) collective-permute-start(bf16[56,16,128]{2,1,0:T(8,128)(2,1)S(1)} %get-tuple-element.59), channel_id=1, source_target_pairs={{0,8},{8,0},{16,24},{24,16},{1,9},{9,1},{17,25},{25,17},{2,10},{10... | collective-permute-start | bytes 688136 | tf_op jit(solution)/shard_map/ppermute | solution.py:385
  33.8 0.0 collective-permute-done.9.refs_0_
  33.8 3.7 %collective-permute-start.10 = (bf16[32,16,128]{2,1,0:T(8,128)(2,1)S(1)}, bf16[32,16,128]{2,1,0:T(8,128)(2,1)S(1)}, u32[]{:S(2)}, u32[]{:S(2)}) collective-permute-start(bf16[32,16,128]{2,1,0:T(8,128)(2,1)S(1)} %get-tuple-element.58), channel_id=1, source_target_pairs={{0,24},{8,16},{16,8},{24,0},{1,25},{9,17},{17,9},{25,1},{2,26},{10... | collective-permute-start | bytes 393224 | tf_op jit(solution)/shard_map/ppermute | solution.py:385
  37.5 1.4 %collective-permute-done.7.refs_0_ = bf16[25,16,128]{2,1,0:T(8,128)(2,1)S(1)} collective-permute-done((bf16[25,16,128]{2,1,0:T(8,128)(2,1)S(1)}, bf16[25,16,128]{2,1,0:T(8,128)(2,1)S(1)}, u32[]{:S(2)}, u32[]{:S(2)}) %collective-permute-start.7) | collective-permute-done | bytes 102432 | tf_op jit(solution)/shard_map/ppermute | solution.py:385
  38.9 0.4 collective-permute-start.8
  39.3 3.3 %correlate.3.refs_1_ = f32[5,256,256]{2,1,0:T(8,128)S(1)} custom-call(s32[16]{0:T(128)S(1)} %bitcast.7, bf16[56,16,128]{2,1,0:T(8,128)(2,1)S(1)} %get-tuple-element.60.refs_0_), custom_call_target="tpu_custom_call" | custom-call | tf_op jit(solution)/shard_map/correlate/pallas_call | solution.py:271
  42.6 2.4 %collective-permute-done.11.refs_0_ = bf16[56,16,128]{2,1,0:T(8,128)(2,1)S(1)} collective-permute-done((bf16[56,16,128]{2,1,0:T(8,128)(2,1)S(1)}, bf16[56,16,128]{2,1,0:T(8,128)(2,1)S(1)}, u32[]{:S(2)}, u32[]{:S(2)}) %collective-permute-start.11) | collective-permute-done | bytes 229408 | tf_op jit(solution)/shard_map/ppermute | solution.py:385
  45.0 3.3 %correlate.4.refs_2_ = f32[5,256,256]{2,1,0:T(8,128)S(1)} custom-call(s32[16]{0:T(128)S(1)} %bitcast.8, bf16[56,16,128]{2,1,0:T(8,128)(2,1)S(1)} %collective-permute-done.11.refs_0_, f32[5,256,256]{2,1,0:T(8,128)S(1)} %correlate.3.refs_1_), custom_call_target="tpu_custom_call" | custom-call | tf_op jit(solution)/shard_map/correlate/pallas_call | solution.py:271
  48.3 0.0 collective-permute-done.10.refs_1_
  48.3 3.3 %correlate.5.refs_2_ = f32[5,256,256]{2,1,0:T(8,128)S(1)} custom-call(s32[16]{0:T(128)S(1)} %bitcast.9, bf16[25,16,128]{2,1,0:T(8,128)(2,1)S(1)} %collective-permute-done.9.refs_0_, bf16[32,16,128]{2,1,0:T(8,128)(2,1)S(1)} %collective-permute-done.10.refs_1_, f32[5,256,256]{2,1,0:T(8,128)S(1)} %correlate.4.refs_2_), custom_call_target="tpu_custom_call" | custom-call | tf_op jit(solution)/shard_map/correlate/pallas_call | solution.py:271
  51.6 0.0 collective-permute-done.8.refs_1_
  51.7 4.9 %correlate_last.1 = f32[5,8,8,1001]{3,2,1,0:T(8,128)} custom-call(s32[16]{0:T(128)S(1)} %bitcast.10, bf16[25,16,128]{2,1,0:T(8,128)(2,1)S(1)} %collective-permute-done.7.refs_0_, bf16[32,16,128]{2,1,0:T(8,128)(2,1)S(1)} %collective-permute-done.8.refs_1_, f32[5,256,256]{2,1,0:T(8,128)S(1)} %correlate.5.refs_2_), custom_call_target="tpu_custom_call" | custom-call | tf_op jit(solution)/shard_map/correlate_last/pallas_call | solution.py:271
Async XLA Ops:
  1.2 9.8 %all-to-all-start = ((s32[8,1,2]{2,1,0:T(1,128)}), s32[8,1,2]{2,1,0:T(1,128)S(1)}, u32[]{:S(2)}, u32[]{:S(2)}) async-start(s32[8,1,2]{2,1,0:T(1,128)} %broadcast_in_dim.2), calls=%async_computation | async-start | bytes 8192 | tf_op jit(solution)/shard_map/all_to_all | solution.py:295
  6.4 0.7 %copy-start.1 = (f32[255]{0:T(256)S(1)}, f32[255]{0:T(256)}, u32[]{:S(2)}) copy-start(f32[255]{0:T(256)} %param.5) | copy-start | bytes 3064
  14.3 6.2 %collective-permute-start = (bf16[128,384]{1,0:T(8,128)(2,1)S(1)}, bf16[128,384]{1,0:T(8,128)(2,1)S(1)}, u32[]{:S(2)}, u32[]{:S(2)}) collective-permute-start(bf16[128,384]{1,0:T(8,128)(2,1)S(1)} %get-tuple-element.33), channel_id=1, source_target_pairs={{0,2},{1,3},{2,0},{3,1},{4,6},{5,7},{6,4},{7,5},{8,10},{9,11},{10,... | collective-permute-start | bytes 294920 | tf_op jit(solution)/shard_map/ppermute | solution.py:338
  15.0 8.7 %collective-permute-start.1 = (bf16[128,384]{1,0:T(8,128)(2,1)S(1)}, bf16[128,384]{1,0:T(8,128)(2,1)S(1)}, u32[]{:S(2)}, u32[]{:S(2)}) collective-permute-start(bf16[128,384]{1,0:T(8,128)(2,1)S(1)} %get-tuple-element.34), channel_id=1, source_target_pairs={{0,3},{1,2},{2,1},{3,0},{4,7},{5,6},{6,5},{7,4},{8,11},{9,10},{10,... | collective-permute-start | bytes 294920 | tf_op jit(solution)/shard_map/ppermute | solution.py:338
  15.6 9.9 %copy-start = (s32[16,1]{0,1:T(1,128)S(1)}, s32[16,1]{0,1:T(1,128)}, u32[]{:S(2)}) copy-start(s32[16,1]{0,1:T(1,128)} %param.7) | copy-start | bytes 196
  15.6 9.9 %collective-permute-start.2 = (bf16[128,384]{1,0:T(8,128)(2,1)S(1)}, bf16[128,384]{1,0:T(8,128)(2,1)S(1)}, u32[]{:S(2)}, u32[]{:S(2)}) collective-permute-start(bf16[128,384]{1,0:T(8,128)(2,1)S(1)} %get-tuple-element.35), channel_id=1, source_target_pairs={{0,4},{1,5},{2,6},{3,7},{4,0},{5,1},{6,2},{7,3},{8,12},{9,13},{10,... | collective-permute-start | bytes 294920 | tf_op jit(solution)/shard_map/ppermute | solution.py:338
  20.6 4.9 %collective-permute-start.3 = (bf16[128,384]{1,0:T(8,128)(2,1)S(1)}, bf16[128,384]{1,0:T(8,128)(2,1)S(1)}, u32[]{:S(2)}, u32[]{:S(2)}) collective-permute-start(bf16[128,384]{1,0:T(8,128)(2,1)S(1)} %get-tuple-element.41), channel_id=1, source_target_pairs={{0,1},{1,0},{2,3},{3,2},{4,5},{5,4},{6,7},{7,6},{8,9},{9,8},{10,11... | collective-permute-start | bytes 294920 | tf_op jit(solution)/shard_map/ppermute | solution.py:338
  21.3 8.6 %collective-permute-start.5 = (bf16[128,384]{1,0:T(8,128)(2,1)S(1)}, bf16[128,384]{1,0:T(8,128)(2,1)S(1)}, u32[]{:S(2)}, u32[]{:S(2)}) collective-permute-start(bf16[128,384]{1,0:T(8,128)(2,1)S(1)} %get-tuple-element.49), channel_id=1, source_target_pairs={{0,6},{1,7},{2,4},{3,5},{4,2},{5,3},{6,0},{7,1},{8,14},{9,15},{10,... | collective-permute-start | bytes 294920 | tf_op jit(solution)/shard_map/ppermute | solution.py:338
  22.8 7.1 %collective-permute-start.6 = (bf16[128,384]{1,0:T(8,128)(2,1)S(1)}, bf16[128,384]{1,0:T(8,128)(2,1)S(1)}, u32[]{:S(2)}, u32[]{:S(2)}) collective-permute-start(bf16[128,384]{1,0:T(8,128)(2,1)S(1)} %get-tuple-element.50), channel_id=1, source_target_pairs={{0,7},{1,6},{2,5},{3,4},{4,3},{5,2},{6,1},{7,0},{8,15},{9,14},{10,... | collective-permute-start | bytes 294920 | tf_op jit(solution)/shard_map/ppermute | solution.py:338
  23.6 7.5 %collective-permute-start.4 = (bf16[128,384]{1,0:T(8,128)(2,1)S(1)}, bf16[128,384]{1,0:T(8,128)(2,1)S(1)}, u32[]{:S(2)}, u32[]{:S(2)}) collective-permute-start(bf16[128,384]{1,0:T(8,128)(2,1)S(1)} %get-tuple-element.48), channel_id=1, source_target_pairs={{0,5},{1,4},{2,7},{3,6},{4,1},{5,0},{6,3},{7,2},{8,13},{9,12},{10,... | collective-permute-start | bytes 294920 | tf_op jit(solution)/shard_map/ppermute | solution.py:338
  26.2 7.5 %collective-permute-start.9 = (bf16[25,16,128]{2,1,0:T(8,128)(2,1)S(1)}, bf16[25,16,128]{2,1,0:T(8,128)(2,1)S(1)}, u32[]{:S(2)}, u32[]{:S(2)}) collective-permute-start(bf16[25,16,128]{2,1,0:T(8,128)(2,1)S(1)} %get-tuple-element.56), channel_id=1, source_target_pairs={{0,24},{8,16},{16,8},{24,0},{1,25},{9,17},{17,9},{25,1},{2,26},{10... | collective-permute-start | bytes 307208 | tf_op jit(solution)/shard_map/ppermute | solution.py:385
  29.9 9.0 %collective-permute-start.7 = (bf16[25,16,128]{2,1,0:T(8,128)(2,1)S(1)}, bf16[25,16,128]{2,1,0:T(8,128)(2,1)S(1)}, u32[]{:S(2)}, u32[]{:S(2)}) collective-permute-start(bf16[25,16,128]{2,1,0:T(8,128)(2,1)S(1)} %get-tuple-element.52), channel_id=1, source_target_pairs={{0,16},{8,24},{16,0},{24,8},{1,17},{9,25},{17,1},{25,9},{2,18},{10... | collective-permute-start | bytes 307208 | tf_op jit(solution)/shard_map/ppermute | solution.py:385
  32.1 12.9 %collective-permute-start.11 = (bf16[56,16,128]{2,1,0:T(8,128)(2,1)S(1)}, bf16[56,16,128]{2,1,0:T(8,128)(2,1)S(1)}, u32[]{:S(2)}, u32[]{:S(2)}) collective-permute-start(bf16[56,16,128]{2,1,0:T(8,128)(2,1)S(1)} %get-tuple-element.59), channel_id=1, source_target_pairs={{0,8},{8,0},{16,24},{24,16},{1,9},{9,1},{17,25},{25,17},{2,10},{10... | collective-permute-start | bytes 688136 | tf_op jit(solution)/shard_map/ppermute | solution.py:385
  33.8 14.5 %collective-permute-start.10 = (bf16[32,16,128]{2,1,0:T(8,128)(2,1)S(1)}, bf16[32,16,128]{2,1,0:T(8,128)(2,1)S(1)}, u32[]{:S(2)}, u32[]{:S(2)}) collective-permute-start(bf16[32,16,128]{2,1,0:T(8,128)(2,1)S(1)} %get-tuple-element.58), channel_id=1, source_target_pairs={{0,24},{8,16},{16,8},{24,0},{1,25},{9,17},{17,9},{25,1},{2,26},{10... | collective-permute-start | bytes 393224 | tf_op jit(solution)/shard_map/ppermute | solution.py:385
  38.9 12.8 %collective-permute-start.8 = (bf16[32,16,128]{2,1,0:T(8,128)(2,1)S(1)}, bf16[32,16,128]{2,1,0:T(8,128)(2,1)S(1)}, u32[]{:S(2)}, u32[]{:S(2)}) collective-permute-start(bf16[32,16,128]{2,1,0:T(8,128)(2,1)S(1)} %get-tuple-element.54), channel_id=1, source_target_pairs={{0,16},{8,24},{16,0},{24,8},{1,17},{9,25},{17,1},{25,9},{2,18},{10... | collective-permute-start | bytes 393224 | tf_op jit(solution)/shard_map/ppermute | solution.py:385

commit v12 on v9

--- a/solution.py
+++ b/solution.py
@@ -176,12 +176,12 @@
 
 
 def correlate_kernel(n_chan, groups, factor, last, owners, *refs):
-    lead, window_a, window_b, whole = refs[-4:]
-    out = refs[-5]
+    near, far, windows, whole, parts_sum = refs[-5:]
+    out = refs[-6]
     arrived = refs[: len(groups)]
-    before = refs[len(groups)] if len(refs) > len(groups) + 5 else None
-    windows = (window_a, window_b)
-    span = lead.shape[2]
+    before = refs[len(groups)] if len(refs) > len(groups) + 6 else None
+    cut = near.shape[2]
+    span = cut + far.shape[2]
     samples = span - LANES
     cols = span // LANES
     high = STEP * CB
@@ -209,36 +209,46 @@
         for a in range(CB):
             spread = jnp.broadcast_to(value[a : a + 1], (SHIFTS, span))
             turned = pltpu.roll(spread, 0, 1, stride=1, stride_axis=0)
-            lead[p, a * SHIFTS : (a + 1) * SHIFTS, :] = turned.astype(jnp.bfloat16)
+            turned = turned.astype(jnp.bfloat16)
+            near[p, a * SHIFTS : (a + 1) * SHIFTS, :] = turned[:, :cut]
+            far[p, a * SHIFTS : (a + 1) * SHIFTS, :] = turned[:, cut:]
 
     def bounds(i):
         return max(0, ahead - i), min(cols, ahead + cols - i)
 
-    for window in windows:
+    def make_window(s):
         for i in range(LAG_BLOCKS):
             first, end = bounds(i)
             rows = slice(i * high, (i + 1) * high)
             if first > 0:
-                window[rows, : first * LANES] = jnp.zeros((high, first * LANES), jnp.bfloat16)
+                windows[s, rows, : first * LANES] = jnp.zeros((high, first * LANES), jnp.bfloat16)
             if end < cols:
-                window[rows, end * LANES :] = jnp.zeros((high, (cols - end) * LANES), jnp.bfloat16)
-
-    group = lax.broadcasted_iota(jnp.int32, (CB, LANES), 1) // SHIFTS
-    for s in range(SLOTS):
-        window = windows[s % 2]
+                windows[s, rows, end * LANES :] = jnp.zeros(
+                    (high, (cols - end) * LANES), jnp.bfloat16
+                )
         value = series(STRIPES + s)
         turned = [pltpu.roll(value, span - (FRONT - MAXLAG + SHIFTS * n), 1) for n in range(STEP)]
         stacked = jnp.concatenate(turned, 0).astype(jnp.bfloat16)
         stacked = jnp.concatenate([stacked[:, samples:], stacked[:, :samples]], 1)
         for i in range(LAG_BLOCKS):
             first, end = bounds(i)
-            window[i * high : (i + 1) * high, first * LANES : end * LANES] = stacked[
+            windows[s, i * high : (i + 1) * high, first * LANES : end * LANES] = stacked[
                 :, (first + i - ahead) * LANES : (end + i - ahead) * LANES
             ]
-        which = jnp.where(s < first_count, 0, 1)
-        summed = lax.dot_general(window[...], lead[which], NT, preferred_element_type=jnp.float32)
-        if before is not None:
-            summed = summed + before[s]
+
+    which = [jnp.where(s < first_count, 0, 1) for s in range(SLOTS)]
+    for s in range(SLOTS):
+        make_window(s)
+        value = lax.dot_general(
+            windows[s, :, :cut], near[which[s]], NT, preferred_element_type=jnp.float32
+        )
+        parts_sum[s] = value if before is None else value + before[s]
+
+    group = lax.broadcasted_iota(jnp.int32, (CB, LANES), 1) // SHIFTS
+    for s in range(SLOTS):
+        summed = parts_sum[s] + lax.dot_general(
+            windows[s, :, cut:], far[which[s]], NT, preferred_element_type=jnp.float32
+        )
         if not last:
             out[s] = summed
             continue
@@ -266,17 +276,18 @@
     else:
         shape = jax.ShapeDtypeStruct((SLOTS, high, wide), jnp.float32)
     operands = (owners,) + arrived + (() if before is None else (before,))
-    depth = samples + LANES
+    depth, cut = samples + LANES, samples // 2
     return pl.pallas_call(
         functools.partial(correlate_kernel, n_chan, groups, factor, last),
         out_shape=shape,
         in_specs=[smem()] + [vmem()] * (len(operands) - 1),
         out_specs=vmem(),
         scratch_shapes=[
-            pltpu.VMEM((STRIPES, wide, depth), jnp.bfloat16),
-            pltpu.VMEM((high, depth), jnp.bfloat16),
-            pltpu.VMEM((high, depth), jnp.bfloat16),
+            pltpu.VMEM((STRIPES, wide, cut), jnp.bfloat16),
+            pltpu.VMEM((STRIPES, wide, depth - cut), jnp.bfloat16),
+            pltpu.VMEM((SLOTS, high, depth), jnp.bfloat16),
             pltpu.VMEM((BLOCKS, CB, samples), jnp.float32),
+            pltpu.VMEM((SLOTS, high, wide), jnp.float32),
         ],
         compiler_params=params(40),
         name="correlate_last" if last else "correlate",

time: 54.8 us -> 54.6 us (level)
  Pallas kernels: 22.7 us -> 21.7 us
  waiting for transfers between devices: 10.8 us -> 11.7 us
    pallas_call x4, Pallas kernels: 14.7 us -> 13.7 us  [correlate(): pl.pallas_call(functools.partial(correlate_kernel, n_chan, groups, factor...]
    ppermute x5, waiting for transfers between devices: 3.71 us -> 4.56 us  [hand_over(): lax.ppermute(value, 'tgroup', [(g, g ^ shift) for g in range(n_tgroup)])]
  transfers between devices with their start and end apart: 13 -> 13, of which waited for: 8 -> 8; matrix products, arithmetic and copies ran while one was open for 0% -> 0% of each run, Pallas kernels for 22% -> 20%
where the time goes in v12:
time: 54.6 us; the launch traced here: 54.4 us
  Pallas kernels  21.7 us (40%)
  starting transfers between devices  19.1 us (35%)
  waiting for transfers between devices  11.7 us (21%)
  local copies, waits for them, and re-layouts  1.93 us (4%)
    pallas_call x4, Pallas kernels, correlate(): pl.pallas_call(functools.partial(correlate_kernel, n_chan, groups, factor...  13.7 us
    ppermute x5, starting transfers between devices, hand_over(): lax.ppermute(value, 'tgroup', [(g, g ^ shift) for g in range(n_tgroup)])  9.12 us
    pallas_call x1, Pallas kernels, local(): pl.pallas_call(functools.partial(select_kernel, n_chan, groups), out_shap...  5.95 us
    all_to_all x1, starting transfers between devices, local(): lax.all_to_all(jnp.broadcast_to(first_block[None, :], (n_chan, STRIPES)),...  5.17 us
    ppermute x7, starting transfers between devices, exchange(): return lax.ppermute(value, 'chan', [(c, c ^ k) for c in range(n_chan)])  4.79 us
    ppermute x5, waiting for transfers between devices, hand_over(): lax.ppermute(value, 'tgroup', [(g, g ^ shift) for g in range(n_tgroup)])  4.56 us
    all_to_all x1, waiting for transfers between devices, local(): lax.all_to_all(jnp.broadcast_to(first_block[None, :], (n_chan, STRIPES)),...  3.62 us
    ppermute x7, waiting for transfers between devices, exchange(): return lax.ppermute(value, 'chan', [(c, c ^ k) for c in range(n_chan)])  3.47 us
  transfers between devices with their start and end apart: 13, of which 8 were waited for; matrix products, arithmetic and copies ran while one was open for 0% of the time, Pallas kernels for 20%

profile of v12, /device:TPU:0, one launch (start us, length us, event | category | flops | bytes accessed | tf_op | source)
XLA Modules:
  0.0 54.4 jit_solution(4196233654581473431)
XLA Ops:
  0.0 1.2 %broadcast_in_dim.2 = s32[8,1,2]{2,1,0:T(1,128)} broadcast(s32[2]{0:T(128)} %param.6), dimensions={2} | broadcast | bytes 72 | tf_op jit(solution)/shard_map/broadcast_in_dim | solution.py:306
  1.2 5.2 %all-to-all-start = ((s32[8,1,2]{2,1,0:T(1,128)}), s32[8,1,2]{2,1,0:T(1,128)S(1)}, u32[]{:S(2)}, u32[]{:S(2)}) async-start(s32[8,1,2]{2,1,0:T(1,128)} %broadcast_in_dim.2), calls=%async_computation | async-start | bytes 8192 | tf_op jit(solution)/shard_map/all_to_all | solution.py:305
  6.4 0.0 copy-start.1
  6.4 0.7 %copy-done.1 = f32[255]{0:T(256)S(1)} copy-done((f32[255]{0:T(256)S(1)}, f32[255]{0:T(256)}, u32[]{:S(2)}) %copy-start.1) | copy-done | bytes 1044
  7.1 0.3 fir_weights.1.weights
  7.4 3.6 %all-to-all-done = s32[8,1,2]{2,1,0:T(1,128)S(1)} async-done(((s32[8,1,2]{2,1,0:T(1,128)}), s32[8,1,2]{2,1,0:T(1,128)S(1)}, u32[]{:S(2)}, u32[]{:S(2)}) %all-to-all-start) | async-done | bytes 96 | tf_op jit(solution)/shard_map/all_to_all | solution.py:305
  11.0 0.0 copy-start
  11.0 6.0 %select_filter.1 = (bf16[128,384]{1,0:T(8,128)(2,1)S(1)}, bf16[128,384]{1,0:T(8,128)(2,1)S(1)}, bf16[128,384]{1,0:T(8,128)(2,1)S(1)}, bf16[128,384]{1,0:T(8,128)...) custom-call(s32[8,2]{1,0:T(8,128)S(1)} %bitcast.9, ...), custom_call_target="tpu_custom_call" | custom-call | tf_op jit(solution)/shard_map/select_filter/pallas_call | solution.py:328
  17.0 0.1 collective-permute-start
  17.0 0.6 %collective-permute-start.1 = (bf16[128,384]{1,0:T(8,128)(2,1)S(1)}, bf16[128,384]{1,0:T(8,128)(2,1)S(1)}, u32[]{:S(2)}, u32[]{:S(2)}) collective-permute-start(bf16[128,384]{1,0:T(8,128)(2,1)S(1)} %get-tuple-element.30), channel_id=1, source_target_pairs={{0,2},{1,3},{2,0},{3,1},{4,6},{5,7},{6,4},{7,5},{8,10},{9,11},{10,... | collective-permute-start | bytes 294920 | tf_op jit(solution)/shard_map/ppermute | solution.py:346
  17.7 1.2 %collective-permute-start.2 = (bf16[128,384]{1,0:T(8,128)(2,1)S(1)}, bf16[128,384]{1,0:T(8,128)(2,1)S(1)}, u32[]{:S(2)}, u32[]{:S(2)}) collective-permute-start(bf16[128,384]{1,0:T(8,128)(2,1)S(1)} %get-tuple-element.31), channel_id=1, source_target_pairs={{0,3},{1,2},{2,1},{3,0},{4,7},{5,6},{6,5},{7,4},{8,11},{9,10},{10,... | collective-permute-start | bytes 294920 | tf_op jit(solution)/shard_map/ppermute | solution.py:346
  18.9 0.6 %collective-permute-start.3 = (bf16[128,384]{1,0:T(8,128)(2,1)S(1)}, bf16[128,384]{1,0:T(8,128)(2,1)S(1)}, u32[]{:S(2)}, u32[]{:S(2)}) collective-permute-start(bf16[128,384]{1,0:T(8,128)(2,1)S(1)} %get-tuple-element.32), channel_id=1, source_target_pairs={{0,4},{1,5},{2,6},{3,7},{4,0},{5,1},{6,2},{7,3},{8,12},{9,13},{10,... | collective-permute-start | bytes 294920 | tf_op jit(solution)/shard_map/ppermute | solution.py:346
  19.5 1.1 %collective-permute-start.4 = (bf16[128,384]{1,0:T(8,128)(2,1)S(1)}, bf16[128,384]{1,0:T(8,128)(2,1)S(1)}, u32[]{:S(2)}, u32[]{:S(2)}) collective-permute-start(bf16[128,384]{1,0:T(8,128)(2,1)S(1)} %get-tuple-element.38), channel_id=1, source_target_pairs={{0,5},{1,4},{2,7},{3,6},{4,1},{5,0},{6,3},{7,2},{8,13},{9,12},{10,... | collective-permute-start | bytes 294920 | tf_op jit(solution)/shard_map/ppermute | solution.py:346
  20.6 0.0 collective-permute-done.refs_1_
  20.6 0.6 %collective-permute-start.5 = (bf16[128,384]{1,0:T(8,128)(2,1)S(1)}, bf16[128,384]{1,0:T(8,128)(2,1)S(1)}, u32[]{:S(2)}, u32[]{:S(2)}) collective-permute-start(bf16[128,384]{1,0:T(8,128)(2,1)S(1)} %get-tuple-element.39), channel_id=1, source_target_pairs={{0,6},{1,7},{2,4},{3,5},{4,2},{5,3},{6,0},{7,1},{8,14},{9,15},{10,... | collective-permute-start | bytes 294920 | tf_op jit(solution)/shard_map/ppermute | solution.py:346
  21.2 1.5 %collective-permute-done.1.refs_2_ = bf16[128,384]{1,0:T(8,128)(2,1)S(1)} collective-permute-done((bf16[128,384]{1,0:T(8,128)(2,1)S(1)}, bf16[128,384]{1,0:T(8,128)(2,1)S(1)}, u32[]{:S(2)}, u32[]{:S(2)}) %collective-permute-start.1) | collective-permute-done | bytes 98336 | tf_op jit(solution)/shard_map/ppermute | solution.py:346
  22.7 0.6 %collective-permute-start.6 = (bf16[128,384]{1,0:T(8,128)(2,1)S(1)}, bf16[128,384]{1,0:T(8,128)(2,1)S(1)}, u32[]{:S(2)}, u32[]{:S(2)}) collective-permute-start(bf16[128,384]{1,0:T(8,128)(2,1)S(1)} %get-tuple-element.40), channel_id=1, source_target_pairs={{0,7},{1,6},{2,5},{3,4},{4,3},{5,2},{6,1},{7,0},{8,15},{9,14},{10,... | collective-permute-start | bytes 294920 | tf_op jit(solution)/shard_map/ppermute | solution.py:346
  23.3 0.6 %collective-permute-done.2.refs_3_ = bf16[128,384]{1,0:T(8,128)(2,1)S(1)} collective-permute-done((bf16[128,384]{1,0:T(8,128)(2,1)S(1)}, bf16[128,384]{1,0:T(8,128)(2,1)S(1)}, u32[]{:S(2)}, u32[]{:S(2)}) %collective-permute-start.2) | collective-permute-done | bytes 98336 | tf_op jit(solution)/shard_map/ppermute | solution.py:346
  23.9 0.6 %collective-permute-done.3.refs_4_ = bf16[128,384]{1,0:T(8,128)(2,1)S(1)} collective-permute-done((bf16[128,384]{1,0:T(8,128)(2,1)S(1)}, bf16[128,384]{1,0:T(8,128)(2,1)S(1)}, u32[]{:S(2)}, u32[]{:S(2)}) %collective-permute-start.3) | collective-permute-done | bytes 98336 | tf_op jit(solution)/shard_map/ppermute | solution.py:346
  24.5 0.0 copy-done
  24.5 0.8 %place_first.1 = (bf16[25,16,128]{2,1,0:T(8,128)(2,1)S(1)}, bf16[25,16,128]{2,1,0:T(8,128)(2,1)S(1)}) custom-call(s32[16]{0:T(128)S(1)} %bitcast.3, bf16[128,384]{1,0:T(8,128)(2,1)S(1)} %get-tuple-element.33.refs_0_, bf16[128,384]{1,0:T(8,128)(2,1)S(1)} %collective-permute-done.refs_1_, bf16[128,384]{1,0:T(8,128)(2,1)S(1)} %collective-permute-done.1.refs_2_, ...), custom_call_target="tpu_custom_call" | custom-call | tf_op jit(solution)/shard_map/place_first/pallas_call | solution.py:368
  25.3 3.7 %collective-permute-start.9 = (bf16[25,16,128]{2,1,0:T(8,128)(2,1)S(1)}, bf16[25,16,128]{2,1,0:T(8,128)(2,1)S(1)}, u32[]{:S(2)}, u32[]{:S(2)}) collective-permute-start(bf16[25,16,128]{2,1,0:T(8,128)(2,1)S(1)} %get-tuple-element.46), channel_id=1, source_target_pairs={{0,24},{8,16},{16,8},{24,0},{1,25},{9,17},{17,9},{25,1},{2,26},{10... | collective-permute-start | bytes 307208 | tf_op jit(solution)/shard_map/ppermute | solution.py:385
  29.0 0.0 collective-permute-start.7
  29.0 0.7 %collective-permute-done.4.refs_5_ = bf16[128,384]{1,0:T(8,128)(2,1)S(1)} collective-permute-done((bf16[128,384]{1,0:T(8,128)(2,1)S(1)}, bf16[128,384]{1,0:T(8,128)(2,1)S(1)}, u32[]{:S(2)}, u32[]{:S(2)}) %collective-permute-start.4) | collective-permute-done | bytes 98336 | tf_op jit(solution)/shard_map/ppermute | solution.py:346
  29.7 0.0 collective-permute-done.5.refs_6_
  29.7 0.0 collective-permute-done.6.refs_7_
  29.7 1.0 %place_second.1 = (bf16[56,16,128]{2,1,0:T(8,128)(2,1)S(1)}, bf16[56,16,128]{2,1,0:T(8,128)(2,1)S(1)}, bf16[32,16,128]{2,1,0:T(8,128)(2,1)S(1)}, bf16[32,16,128]{2,1,0:T(8,128)(2,1)S(1)}) custom-call(s32[16]{0:T(128)S(1)} %bitcast.4, bf16[128,384]{1,0:T(8,128)(2,1)S(1)} %get-tuple-element.33.refs_0_, bf16[128,384]{1,0:T(8,128)(2,1)S(1)} %collective-permute-done.refs_1_, ...), custom_call_target="tpu_custom_call" | custom-call | tf_op jit(solution)/shard_map/place_second/pallas_call | solution.py:368
  30.7 1.6 %collective-permute-start.11 = (bf16[56,16,128]{2,1,0:T(8,128)(2,1)S(1)}, bf16[56,16,128]{2,1,0:T(8,128)(2,1)S(1)}, u32[]{:S(2)}, u32[]{:S(2)}) collective-permute-start(bf16[56,16,128]{2,1,0:T(8,128)(2,1)S(1)} %get-tuple-element.49), channel_id=1, source_target_pairs={{0,8},{8,0},{16,24},{24,16},{1,9},{9,1},{17,25},{25,17},{2,10},{10... | collective-permute-start | bytes 688136 | tf_op jit(solution)/shard_map/ppermute | solution.py:385
  32.4 0.6 %collective-permute-done.9.refs_0_ = bf16[25,16,128]{2,1,0:T(8,128)(2,1)S(1)} collective-permute-done((bf16[25,16,128]{2,1,0:T(8,128)(2,1)S(1)}, bf16[25,16,128]{2,1,0:T(8,128)(2,1)S(1)}, u32[]{:S(2)}, u32[]{:S(2)}) %collective-permute-start.9) | collective-permute-done | bytes 102432 | tf_op jit(solution)/shard_map/ppermute | solution.py:385
  33.0 3.6 %collective-permute-start.10 = (bf16[32,16,128]{2,1,0:T(8,128)(2,1)S(1)}, bf16[32,16,128]{2,1,0:T(8,128)(2,1)S(1)}, u32[]{:S(2)}, u32[]{:S(2)}) collective-permute-start(bf16[32,16,128]{2,1,0:T(8,128)(2,1)S(1)} %get-tuple-element.48), channel_id=1, source_target_pairs={{0,24},{8,16},{16,8},{24,0},{1,25},{9,17},{17,9},{25,1},{2,26},{10... | collective-permute-start | bytes 393224 | tf_op jit(solution)/shard_map/ppermute | solution.py:385
  36.6 1.7 %collective-permute-done.7.refs_0_ = bf16[25,16,128]{2,1,0:T(8,128)(2,1)S(1)} collective-permute-done((bf16[25,16,128]{2,1,0:T(8,128)(2,1)S(1)}, bf16[25,16,128]{2,1,0:T(8,128)(2,1)S(1)}, u32[]{:S(2)}, u32[]{:S(2)}) %collective-permute-start.7) | collective-permute-done | bytes 102432 | tf_op jit(solution)/shard_map/ppermute | solution.py:385
  38.3 0.2 collective-permute-start.8
  38.5 3.0 %correlate.3.refs_1_ = f32[5,256,256]{2,1,0:T(8,128)S(1)} custom-call(s32[16]{0:T(128)S(1)} %bitcast.5, bf16[56,16,128]{2,1,0:T(8,128)(2,1)S(1)} %get-tuple-element.50.refs_0_), custom_call_target="tpu_custom_call" | custom-call | tf_op jit(solution)/shard_map/correlate/pallas_call | solution.py:280
  41.5 0.0 collective-permute-done.11.refs_0_
  41.5 3.0 %correlate.4.refs_2_ = f32[5,256,256]{2,1,0:T(8,128)S(1)} custom-call(s32[16]{0:T(128)S(1)} %bitcast.6, bf16[56,16,128]{2,1,0:T(8,128)(2,1)S(1)} %collective-permute-done.11.refs_0_, f32[5,256,256]{2,1,0:T(8,128)S(1)} %correlate.3.refs_1_), custom_call_target="tpu_custom_call" | custom-call | tf_op jit(solution)/shard_map/correlate/pallas_call | solution.py:280
  44.6 0.0 collective-permute-done.10.refs_1_
  44.6 3.0 %correlate.5.refs_2_ = f32[5,256,256]{2,1,0:T(8,128)S(1)} custom-call(s32[16]{0:T(128)S(1)} %bitcast.7, bf16[25,16,128]{2,1,0:T(8,128)(2,1)S(1)} %collective-permute-done.9.refs_0_, bf16[32,16,128]{2,1,0:T(8,128)(2,1)S(1)} %collective-permute-done.10.refs_1_, f32[5,256,256]{2,1,0:T(8,128)S(1)} %correlate.4.refs_2_), custom_call_target="tpu_custom_call" | custom-call | tf_op jit(solution)/shard_map/correlate/pallas_call | solution.py:280
  47.6 2.2 %collective-permute-done.8.refs_1_ = bf16[32,16,128]{2,1,0:T(8,128)(2,1)S(1)} collective-permute-done((bf16[32,16,128]{2,1,0:T(8,128)(2,1)S(1)}, bf16[32,16,128]{2,1,0:T(8,128)(2,1)S(1)}, u32[]{:S(2)}, u32[]{:S(2)}) %collective-permute-start.8) | collective-permute-done | bytes 131104 | tf_op jit(solution)/shard_map/ppermute | solution.py:385
  49.9 4.6 %correlate_last.1 = f32[5,8,8,1001]{3,2,1,0:T(8,128)} custom-call(s32[16]{0:T(128)S(1)} %bitcast.8, bf16[25,16,128]{2,1,0:T(8,128)(2,1)S(1)} %collective-permute-done.7.refs_0_, bf16[32,16,128]{2,1,0:T(8,128)(2,1)S(1)} %collective-permute-done.8.refs_1_, f32[5,256,256]{2,1,0:T(8,128)S(1)} %correlate.5.refs_2_), custom_call_target="tpu_custom_call" | custom-call | tf_op jit(solution)/shard_map/correlate_last/pallas_call | solution.py:280
Async XLA Ops:
  1.2 9.8 %all-to-all-start = ((s32[8,1,2]{2,1,0:T(1,128)}), s32[8,1,2]{2,1,0:T(1,128)S(1)}, u32[]{:S(2)}, u32[]{:S(2)}) async-start(s32[8,1,2]{2,1,0:T(1,128)} %broadcast_in_dim.2), calls=%async_computation | async-start | bytes 8192 | tf_op jit(solution)/shard_map/all_to_all | solution.py:305
  6.4 0.7 %copy-start.1 = (f32[255]{0:T(256)S(1)}, f32[255]{0:T(256)}, u32[]{:S(2)}) copy-start(f32[255]{0:T(256)} %param.5) | copy-start | bytes 3064
  11.0 13.5 %copy-start = (s32[16,1]{0,1:T(1,128)S(1)}, s32[16,1]{0,1:T(1,128)}, u32[]{:S(2)}) copy-start(s32[16,1]{0,1:T(1,128)} %param.7) | copy-start | bytes 196
  17.0 3.6 %collective-permute-start = (bf16[128,384]{1,0:T(8,128)(2,1)S(1)}, bf16[128,384]{1,0:T(8,128)(2,1)S(1)}, u32[]{:S(2)}, u32[]{:S(2)}) collective-permute-start(bf16[128,384]{1,0:T(8,128)(2,1)S(1)} %get-tuple-element.29), channel_id=1, source_target_pairs={{0,1},{1,0},{2,3},{3,2},{4,5},{5,4},{6,7},{7,6},{8,9},{9,8},{10,11... | collective-permute-start | bytes 294920 | tf_op jit(solution)/shard_map/ppermute | solution.py:346
  17.0 5.7 %collective-permute-start.1 = (bf16[128,384]{1,0:T(8,128)(2,1)S(1)}, bf16[128,384]{1,0:T(8,128)(2,1)S(1)}, u32[]{:S(2)}, u32[]{:S(2)}) collective-permute-start(bf16[128,384]{1,0:T(8,128)(2,1)S(1)} %get-tuple-element.30), channel_id=1, source_target_pairs={{0,2},{1,3},{2,0},{3,1},{4,6},{5,7},{6,4},{7,5},{8,10},{9,11},{10,... | collective-permute-start | bytes 294920 | tf_op jit(solution)/shard_map/ppermute | solution.py:346
  17.7 6.2 %collective-permute-start.2 = (bf16[128,384]{1,0:T(8,128)(2,1)S(1)}, bf16[128,384]{1,0:T(8,128)(2,1)S(1)}, u32[]{:S(2)}, u32[]{:S(2)}) collective-permute-start(bf16[128,384]{1,0:T(8,128)(2,1)S(1)} %get-tuple-element.31), channel_id=1, source_target_pairs={{0,3},{1,2},{2,1},{3,0},{4,7},{5,6},{6,5},{7,4},{8,11},{9,10},{10,... | collective-permute-start | bytes 294920 | tf_op jit(solution)/shard_map/ppermute | solution.py:346
  18.9 5.6 %collective-permute-start.3 = (bf16[128,384]{1,0:T(8,128)(2,1)S(1)}, bf16[128,384]{1,0:T(8,128)(2,1)S(1)}, u32[]{:S(2)}, u32[]{:S(2)}) collective-permute-start(bf16[128,384]{1,0:T(8,128)(2,1)S(1)} %get-tuple-element.32), channel_id=1, source_target_pairs={{0,4},{1,5},{2,6},{3,7},{4,0},{5,1},{6,2},{7,3},{8,12},{9,13},{10,... | collective-permute-start | bytes 294920 | tf_op jit(solution)/shard_map/ppermute | solution.py:346
  19.5 10.2 %collective-permute-start.4 = (bf16[128,384]{1,0:T(8,128)(2,1)S(1)}, bf16[128,384]{1,0:T(8,128)(2,1)S(1)}, u32[]{:S(2)}, u32[]{:S(2)}) collective-permute-start(bf16[128,384]{1,0:T(8,128)(2,1)S(1)} %get-tuple-element.38), channel_id=1, source_target_pairs={{0,5},{1,4},{2,7},{3,6},{4,1},{5,0},{6,3},{7,2},{8,13},{9,12},{10,... | collective-permute-start | bytes 294920 | tf_op jit(solution)/shard_map/ppermute | solution.py:346
  20.6 9.1 %collective-permute-start.5 = (bf16[128,384]{1,0:T(8,128)(2,1)S(1)}, bf16[128,384]{1,0:T(8,128)(2,1)S(1)}, u32[]{:S(2)}, u32[]{:S(2)}) collective-permute-start(bf16[128,384]{1,0:T(8,128)(2,1)S(1)} %get-tuple-element.39), channel_id=1, source_target_pairs={{0,6},{1,7},{2,4},{3,5},{4,2},{5,3},{6,0},{7,1},{8,14},{9,15},{10,... | collective-permute-start | bytes 294920 | tf_op jit(solution)/shard_map/ppermute | solution.py:346
  22.7 7.0 %collective-permute-start.6 = (bf16[128,384]{1,0:T(8,128)(2,1)S(1)}, bf16[128,384]{1,0:T(8,128)(2,1)S(1)}, u32[]{:S(2)}, u32[]{:S(2)}) collective-permute-start(bf16[128,384]{1,0:T(8,128)(2,1)S(1)} %get-tuple-element.40), channel_id=1, source_target_pairs={{0,7},{1,6},{2,5},{3,4},{4,3},{5,2},{6,1},{7,0},{8,15},{9,14},{10,... | collective-permute-start | bytes 294920 | tf_op jit(solution)/shard_map/ppermute | solution.py:346
  25.3 7.6 %collective-permute-start.9 = (bf16[25,16,128]{2,1,0:T(8,128)(2,1)S(1)}, bf16[25,16,128]{2,1,0:T(8,128)(2,1)S(1)}, u32[]{:S(2)}, u32[]{:S(2)}) collective-permute-start(bf16[25,16,128]{2,1,0:T(8,128)(2,1)S(1)} %get-tuple-element.46), channel_id=1, source_target_pairs={{0,24},{8,16},{16,8},{24,0},{1,25},{9,17},{17,9},{25,1},{2,26},{10... | collective-permute-start | bytes 307208 | tf_op jit(solution)/shard_map/ppermute | solution.py:385
  29.0 9.3 %collective-permute-start.7 = (bf16[25,16,128]{2,1,0:T(8,128)(2,1)S(1)}, bf16[25,16,128]{2,1,0:T(8,128)(2,1)S(1)}, u32[]{:S(2)}, u32[]{:S(2)}) collective-permute-start(bf16[25,16,128]{2,1,0:T(8,128)(2,1)S(1)} %get-tuple-element.42), channel_id=1, source_target_pairs={{0,16},{8,24},{16,0},{24,8},{1,17},{9,25},{17,1},{25,9},{2,18},{10... | collective-permute-start | bytes 307208 | tf_op jit(solution)/shard_map/ppermute | solution.py:385
  30.7 10.8 %collective-permute-start.11 = (bf16[56,16,128]{2,1,0:T(8,128)(2,1)S(1)}, bf16[56,16,128]{2,1,0:T(8,128)(2,1)S(1)}, u32[]{:S(2)}, u32[]{:S(2)}) collective-permute-start(bf16[56,16,128]{2,1,0:T(8,128)(2,1)S(1)} %get-tuple-element.49), channel_id=1, source_target_pairs={{0,8},{8,0},{16,24},{24,16},{1,9},{9,1},{17,25},{25,17},{2,10},{10... | collective-permute-start | bytes 688136 | tf_op jit(solution)/shard_map/ppermute | solution.py:385
  33.0 11.6 %collective-permute-start.10 = (bf16[32,16,128]{2,1,0:T(8,128)(2,1)S(1)}, bf16[32,16,128]{2,1,0:T(8,128)(2,1)S(1)}, u32[]{:S(2)}, u32[]{:S(2)}) collective-permute-start(bf16[32,16,128]{2,1,0:T(8,128)(2,1)S(1)} %get-tuple-element.48), channel_id=1, source_target_pairs={{0,24},{8,16},{16,8},{24,0},{1,25},{9,17},{17,9},{25,1},{2,26},{10... | collective-permute-start | bytes 393224 | tf_op jit(solution)/shard_map/ppermute | solution.py:385
  38.3 11.6 %collective-permute-start.8 = (bf16[32,16,128]{2,1,0:T(8,128)(2,1)S(1)}, bf16[32,16,128]{2,1,0:T(8,128)(2,1)S(1)}, u32[]{:S(2)}, u32[]{:S(2)}) collective-permute-start(bf16[32,16,128]{2,1,0:T(8,128)(2,1)S(1)} %get-tuple-element.44), channel_id=1, source_target_pairs={{0,16},{8,24},{16,0},{24,8},{1,17},{9,25},{17,1},{25,9},{2,18},{10... | collective-permute-start | bytes 393224 | tf_op jit(solution)/shard_map/ppermute | solution.py:385

commit v13 on v12

--- a/solution.py
+++ b/solution.py
@@ -64,24 +64,47 @@
     def place(p):
         c, k = me ^ steps[p // STRIPES], p % STRIPES
         start = (firsts[c, k] + c * blocks_per) * CB
-        base = jnp.minimum(start - lax.rem(start, LANES), channels - span)
-        return start, pl.multiple_of(base, LANES)
-
-    def copy(p):
-        base = place(p)[1]
-        return pltpu.make_async_copy(raw.at[:, pl.ds(base, span)], window.at[p], sems.at[p])
+        offset = lax.rem(start, LANES)
+        base = start - offset
+        return start, offset, base, (offset > LANES - WIDE) & (base < channels - LANES)
+
+    def copy(p, tile):
+        base = place(p)[2]
+        if tile:
+            base = jnp.minimum(base + LANES, channels - LANES)
+        return pltpu.make_async_copy(
+            raw.at[:, pl.ds(pl.multiple_of(base, LANES), LANES)],
+            window.at[p, :, pl.ds(tile * LANES, LANES)],
+            sems.at[p, tile],
+        )
 
     for p in range(stripes):
-        copy(p).start()
+        copy(p, 0).start()
+
+        @pl.when(place(p)[3])
+        def _(p=p):
+            copy(p, 1).start()
+
+    for p in range(stripes):
+
+        @pl.when(jnp.logical_not(place(p)[3]))
+        def _(p=p):
+            window[p, :, LANES:] = jnp.zeros((rows, LANES), jnp.float32)
 
     row = lax.broadcasted_iota(jnp.int32, (WIDE, span), 0)
     lane = lax.broadcasted_iota(jnp.int32, (WIDE, span), 1)
     batch = 2 * STRIPES
     for first in range(0, stripes, batch):
         for p in range(first, first + batch):
-            copy(p).wait()
-            start, base = place(p)
-            hot = (lane == row + (start - base)) & (row < channels - start)
+            copy(p, 0).wait()
+
+            @pl.when(place(p)[3])
+            def _(p=p):
+                copy(p, 1).wait()
+
+        for p in range(first, first + batch):
+            start, offset, _, _ = place(p)
+            hot = (lane == row + offset) & (row < channels - start)
             hot = jnp.where(hot, 1.0, 0.0).astype(jnp.bfloat16)
             block = window[p].astype(jnp.bfloat16)
             chosen = lax.dot_general(hot, block, NT, preferred_element_type=jnp.float32)
@@ -336,7 +359,7 @@
         scratch_shapes=[
             pltpu.VMEM((n_chan * STRIPES, rows, 2 * LANES), jnp.float32),
             pltpu.VMEM((n_chan * count, rows), jnp.bfloat16),
-            pltpu.SemaphoreType.DMA((n_chan * STRIPES,)),
+            pltpu.SemaphoreType.DMA((n_chan * STRIPES, 2)),
         ],
         compiler_params=params(40),
         name="select_filter",

time: 54.6 us -> 53.7 us (0.984)
  Pallas kernels: 21.7 us -> 20.8 us
    pallas_call x1, Pallas kernels: 5.95 us -> 5.09 us  [local(): pl.pallas_call(functools.partial(select_kernel, n_chan, groups), out_shap...]
  transfers between devices with their start and end apart: 13 -> 13, of which waited for: 8 -> 8; matrix products, arithmetic and copies ran while one was open for 0% -> 0% of each run, Pallas kernels for 20% -> 21%
where the time goes in v13:
time: 53.7 us; the launch traced here: 53.6 us
  Pallas kernels  20.8 us (39%)
  starting transfers between devices  19.1 us (36%)
  waiting for transfers between devices  11.7 us (22%)
  local copies, waits for them, and re-layouts  1.93 us (4%)
    pallas_call x4, Pallas kernels, correlate(): pl.pallas_call(functools.partial(correlate_kernel, n_chan, groups, factor...  13.7 us
    ppermute x5, starting transfers between devices, hand_over(): lax.ppermute(value, 'tgroup', [(g, g ^ shift) for g in range(n_tgroup)])  9.1 us
    all_to_all x1, starting transfers between devices, local(): lax.all_to_all(jnp.broadcast_to(first_block[None, :], (n_chan, STRIPES)),...  5.17 us
    pallas_call x1, Pallas kernels, local(): pl.pallas_call(functools.partial(select_kernel, n_chan, groups), out_shap...  5.09 us
    ppermute x7, starting transfers between devices, exchange(): return lax.ppermute(value, 'chan', [(c, c ^ k) for c in range(n_chan)])  4.81 us
    ppermute x5, waiting for transfers between devices, hand_over(): lax.ppermute(value, 'tgroup', [(g, g ^ shift) for g in range(n_tgroup)])  4.57 us
    all_to_all x1, waiting for transfers between devices, local(): lax.all_to_all(jnp.broadcast_to(first_block[None, :], (n_chan, STRIPES)),...  3.62 us
    ppermute x7, waiting for transfers between devices, exchange(): return lax.ppermute(value, 'chan', [(c, c ^ k) for c in range(n_chan)])  3.46 us
  transfers between devices with their start and end apart: 13, of which 8 were waited for; matrix products, arithmetic and copies ran while one was open for 0% of the time, Pallas kernels for 21%

profile of v13, /device:TPU:0, one launch (start us, length us, event | category | flops | bytes accessed | tf_op | source)
XLA Modules:
  0.0 53.6 jit_solution(16326418159982218963)
XLA Ops:
  0.0 1.2 %broadcast_in_dim.2 = s32[8,1,2]{2,1,0:T(1,128)} broadcast(s32[2]{0:T(128)} %param.6), dimensions={2} | broadcast | bytes 72 | tf_op jit(solution)/shard_map/broadcast_in_dim | solution.py:329
  1.2 5.2 %all-to-all-start = ((s32[8,1,2]{2,1,0:T(1,128)}), s32[8,1,2]{2,1,0:T(1,128)S(1)}, u32[]{:S(2)}, u32[]{:S(2)}) async-start(s32[8,1,2]{2,1,0:T(1,128)} %broadcast_in_dim.2), calls=%async_computation | async-start | bytes 8192 | tf_op jit(solution)/shard_map/all_to_all | solution.py:328
  6.4 0.0 copy-start.1
  6.4 0.7 %copy-done.1 = f32[255]{0:T(256)S(1)} copy-done((f32[255]{0:T(256)S(1)}, f32[255]{0:T(256)}, u32[]{:S(2)}) %copy-start.1) | copy-done | bytes 1044
  7.1 0.3 fir_weights.1.weights
  7.4 3.6 %all-to-all-done = s32[8,1,2]{2,1,0:T(1,128)S(1)} async-done(((s32[8,1,2]{2,1,0:T(1,128)}), s32[8,1,2]{2,1,0:T(1,128)S(1)}, u32[]{:S(2)}, u32[]{:S(2)}) %all-to-all-start) | async-done | bytes 96 | tf_op jit(solution)/shard_map/all_to_all | solution.py:328
  11.0 0.0 copy-start
  11.0 5.1 %select_filter.1 = (bf16[128,384]{1,0:T(8,128)(2,1)S(1)}, bf16[128,384]{1,0:T(8,128)(2,1)S(1)}, bf16[128,384]{1,0:T(8,128)(2,1)S(1)}, bf16[128,384]{1,0:T(8,128)...) custom-call(s32[8,2]{1,0:T(8,128)S(1)} %bitcast.9, ...), custom_call_target="tpu_custom_call" | custom-call | tf_op jit(solution)/shard_map/select_filter/pallas_call | solution.py:351
  16.1 0.1 collective-permute-start
  16.2 0.5 %collective-permute-start.1 = (bf16[128,384]{1,0:T(8,128)(2,1)S(1)}, bf16[128,384]{1,0:T(8,128)(2,1)S(1)}, u32[]{:S(2)}, u32[]{:S(2)}) collective-permute-start(bf16[128,384]{1,0:T(8,128)(2,1)S(1)} %get-tuple-element.30), channel_id=1, source_target_pairs={{0,2},{1,3},{2,0},{3,1},{4,6},{5,7},{6,4},{7,5},{8,10},{9,11},{10,... | collective-permute-start | bytes 294920 | tf_op jit(solution)/shard_map/ppermute | solution.py:369
  16.7 1.3 %collective-permute-start.2 = (bf16[128,384]{1,0:T(8,128)(2,1)S(1)}, bf16[128,384]{1,0:T(8,128)(2,1)S(1)}, u32[]{:S(2)}, u32[]{:S(2)}) collective-permute-start(bf16[128,384]{1,0:T(8,128)(2,1)S(1)} %get-tuple-element.31), channel_id=1, source_target_pairs={{0,3},{1,2},{2,1},{3,0},{4,7},{5,6},{6,5},{7,4},{8,11},{9,10},{10,... | collective-permute-start | bytes 294920 | tf_op jit(solution)/shard_map/ppermute | solution.py:369
  18.0 0.6 %collective-permute-start.3 = (bf16[128,384]{1,0:T(8,128)(2,1)S(1)}, bf16[128,384]{1,0:T(8,128)(2,1)S(1)}, u32[]{:S(2)}, u32[]{:S(2)}) collective-permute-start(bf16[128,384]{1,0:T(8,128)(2,1)S(1)} %get-tuple-element.32), channel_id=1, source_target_pairs={{0,4},{1,5},{2,6},{3,7},{4,0},{5,1},{6,2},{7,3},{8,12},{9,13},{10,... | collective-permute-start | bytes 294920 | tf_op jit(solution)/shard_map/ppermute | solution.py:369
  18.6 1.1 %collective-permute-start.4 = (bf16[128,384]{1,0:T(8,128)(2,1)S(1)}, bf16[128,384]{1,0:T(8,128)(2,1)S(1)}, u32[]{:S(2)}, u32[]{:S(2)}) collective-permute-start(bf16[128,384]{1,0:T(8,128)(2,1)S(1)} %get-tuple-element.38), channel_id=1, source_target_pairs={{0,5},{1,4},{2,7},{3,6},{4,1},{5,0},{6,3},{7,2},{8,13},{9,12},{10,... | collective-permute-start | bytes 294920 | tf_op jit(solution)/shard_map/ppermute | solution.py:369
  19.7 0.0 collective-permute-done.refs_1_
  19.7 0.6 %collective-permute-start.5 = (bf16[128,384]{1,0:T(8,128)(2,1)S(1)}, bf16[128,384]{1,0:T(8,128)(2,1)S(1)}, u32[]{:S(2)}, u32[]{:S(2)}) collective-permute-start(bf16[128,384]{1,0:T(8,128)(2,1)S(1)} %get-tuple-element.39), channel_id=1, source_target_pairs={{0,6},{1,7},{2,4},{3,5},{4,2},{5,3},{6,0},{7,1},{8,14},{9,15},{10,... | collective-permute-start | bytes 294920 | tf_op jit(solution)/shard_map/ppermute | solution.py:369
  20.3 1.5 %collective-permute-done.1.refs_2_ = bf16[128,384]{1,0:T(8,128)(2,1)S(1)} collective-permute-done((bf16[128,384]{1,0:T(8,128)(2,1)S(1)}, bf16[128,384]{1,0:T(8,128)(2,1)S(1)}, u32[]{:S(2)}, u32[]{:S(2)}) %collective-permute-start.1) | collective-permute-done | bytes 98336 | tf_op jit(solution)/shard_map/ppermute | solution.py:369
  21.8 0.6 %collective-permute-start.6 = (bf16[128,384]{1,0:T(8,128)(2,1)S(1)}, bf16[128,384]{1,0:T(8,128)(2,1)S(1)}, u32[]{:S(2)}, u32[]{:S(2)}) collective-permute-start(bf16[128,384]{1,0:T(8,128)(2,1)S(1)} %get-tuple-element.40), channel_id=1, source_target_pairs={{0,7},{1,6},{2,5},{3,4},{4,3},{5,2},{6,1},{7,0},{8,15},{9,14},{10,... | collective-permute-start | bytes 294920 | tf_op jit(solution)/shard_map/ppermute | solution.py:369
  22.4 0.6 %collective-permute-done.2.refs_3_ = bf16[128,384]{1,0:T(8,128)(2,1)S(1)} collective-permute-done((bf16[128,384]{1,0:T(8,128)(2,1)S(1)}, bf16[128,384]{1,0:T(8,128)(2,1)S(1)}, u32[]{:S(2)}, u32[]{:S(2)}) %collective-permute-start.2) | collective-permute-done | bytes 98336 | tf_op jit(solution)/shard_map/ppermute | solution.py:369
  23.0 0.6 %collective-permute-done.3.refs_4_ = bf16[128,384]{1,0:T(8,128)(2,1)S(1)} collective-permute-done((bf16[128,384]{1,0:T(8,128)(2,1)S(1)}, bf16[128,384]{1,0:T(8,128)(2,1)S(1)}, u32[]{:S(2)}, u32[]{:S(2)}) %collective-permute-start.3) | collective-permute-done | bytes 98336 | tf_op jit(solution)/shard_map/ppermute | solution.py:369
  23.7 0.0 copy-done
  23.7 0.8 %place_first.1 = (bf16[25,16,128]{2,1,0:T(8,128)(2,1)S(1)}, bf16[25,16,128]{2,1,0:T(8,128)(2,1)S(1)}) custom-call(s32[16]{0:T(128)S(1)} %bitcast.3, bf16[128,384]{1,0:T(8,128)(2,1)S(1)} %get-tuple-element.33.refs_0_, bf16[128,384]{1,0:T(8,128)(2,1)S(1)} %collective-permute-done.refs_1_, bf16[128,384]{1,0:T(8,128)(2,1)S(1)} %collective-permute-done.1.refs_2_, ...), custom_call_target="tpu_custom_call" | custom-call | tf_op jit(solution)/shard_map/place_first/pallas_call | solution.py:391
  24.4 3.7 %collective-permute-start.9 = (bf16[25,16,128]{2,1,0:T(8,128)(2,1)S(1)}, bf16[25,16,128]{2,1,0:T(8,128)(2,1)S(1)}, u32[]{:S(2)}, u32[]{:S(2)}) collective-permute-start(bf16[25,16,128]{2,1,0:T(8,128)(2,1)S(1)} %get-tuple-element.46), channel_id=1, source_target_pairs={{0,24},{8,16},{16,8},{24,0},{1,25},{9,17},{17,9},{25,1},{2,26},{10... | collective-permute-start | bytes 307208 | tf_op jit(solution)/shard_map/ppermute | solution.py:408
  28.1 0.0 collective-permute-start.7
  28.1 0.7 %collective-permute-done.4.refs_5_ = bf16[128,384]{1,0:T(8,128)(2,1)S(1)} collective-permute-done((bf16[128,384]{1,0:T(8,128)(2,1)S(1)}, bf16[128,384]{1,0:T(8,128)(2,1)S(1)}, u32[]{:S(2)}, u32[]{:S(2)}) %collective-permute-start.4) | collective-permute-done | bytes 98336 | tf_op jit(solution)/shard_map/ppermute | solution.py:369
  28.8 0.0 collective-permute-done.5.refs_6_
  28.8 0.0 collective-permute-done.6.refs_7_
  28.8 1.0 %place_second.1 = (bf16[56,16,128]{2,1,0:T(8,128)(2,1)S(1)}, bf16[56,16,128]{2,1,0:T(8,128)(2,1)S(1)}, bf16[32,16,128]{2,1,0:T(8,128)(2,1)S(1)}, bf16[32,16,128]{2,1,0:T(8,128)(2,1)S(1)}) custom-call(s32[16]{0:T(128)S(1)} %bitcast.4, bf16[128,384]{1,0:T(8,128)(2,1)S(1)} %get-tuple-element.33.refs_0_, bf16[128,384]{1,0:T(8,128)(2,1)S(1)} %collective-permute-done.refs_1_, ...), custom_call_target="tpu_custom_call" | custom-call | tf_op jit(solution)/shard_map/place_second/pallas_call | solution.py:391
  29.9 1.6 %collective-permute-start.11 = (bf16[56,16,128]{2,1,0:T(8,128)(2,1)S(1)}, bf16[56,16,128]{2,1,0:T(8,128)(2,1)S(1)}, u32[]{:S(2)}, u32[]{:S(2)}) collective-permute-start(bf16[56,16,128]{2,1,0:T(8,128)(2,1)S(1)} %get-tuple-element.49), channel_id=1, source_target_pairs={{0,8},{8,0},{16,24},{24,16},{1,9},{9,1},{17,25},{25,17},{2,10},{10... | collective-permute-start | bytes 688136 | tf_op jit(solution)/shard_map/ppermute | solution.py:408
  31.5 0.6 %collective-permute-done.9.refs_0_ = bf16[25,16,128]{2,1,0:T(8,128)(2,1)S(1)} collective-permute-done((bf16[25,16,128]{2,1,0:T(8,128)(2,1)S(1)}, bf16[25,16,128]{2,1,0:T(8,128)(2,1)S(1)}, u32[]{:S(2)}, u32[]{:S(2)}) %collective-permute-start.9) | collective-permute-done | bytes 102432 | tf_op jit(solution)/shard_map/ppermute | solution.py:408
  32.1 3.6 %collective-permute-start.10 = (bf16[32,16,128]{2,1,0:T(8,128)(2,1)S(1)}, bf16[32,16,128]{2,1,0:T(8,128)(2,1)S(1)}, u32[]{:S(2)}, u32[]{:S(2)}) collective-permute-start(bf16[32,16,128]{2,1,0:T(8,128)(2,1)S(1)} %get-tuple-element.48), channel_id=1, source_target_pairs={{0,24},{8,16},{16,8},{24,0},{1,25},{9,17},{17,9},{25,1},{2,26},{10... | collective-permute-start | bytes 393224 | tf_op jit(solution)/shard_map/ppermute | solution.py:408
  35.7 1.7 %collective-permute-done.7.refs_0_ = bf16[25,16,128]{2,1,0:T(8,128)(2,1)S(1)} collective-permute-done((bf16[25,16,128]{2,1,0:T(8,128)(2,1)S(1)}, bf16[25,16,128]{2,1,0:T(8,128)(2,1)S(1)}, u32[]{:S(2)}, u32[]{:S(2)}) %collective-permute-start.7) | collective-permute-done | bytes 102432 | tf_op jit(solution)/shard_map/ppermute | solution.py:408
  37.4 0.2 collective-permute-start.8
  37.6 3.0 %correlate.3.refs_1_ = f32[5,256,256]{2,1,0:T(8,128)S(1)} custom-call(s32[16]{0:T(128)S(1)} %bitcast.5, bf16[56,16,128]{2,1,0:T(8,128)(2,1)S(1)} %get-tuple-element.50.refs_0_), custom_call_target="tpu_custom_call" | custom-call | tf_op jit(solution)/shard_map/correlate/pallas_call | solution.py:303
  40.7 0.0 collective-permute-done.11.refs_0_
  40.7 3.0 %correlate.4.refs_2_ = f32[5,256,256]{2,1,0:T(8,128)S(1)} custom-call(s32[16]{0:T(128)S(1)} %bitcast.6, bf16[56,16,128]{2,1,0:T(8,128)(2,1)S(1)} %collective-permute-done.11.refs_0_, f32[5,256,256]{2,1,0:T(8,128)S(1)} %correlate.3.refs_1_), custom_call_target="tpu_custom_call" | custom-call | tf_op jit(solution)/shard_map/correlate/pallas_call | solution.py:303
  43.7 0.0 collective-permute-done.10.refs_1_
  43.7 3.0 %correlate.5.refs_2_ = f32[5,256,256]{2,1,0:T(8,128)S(1)} custom-call(s32[16]{0:T(128)S(1)} %bitcast.7, bf16[25,16,128]{2,1,0:T(8,128)(2,1)S(1)} %collective-permute-done.9.refs_0_, bf16[32,16,128]{2,1,0:T(8,128)(2,1)S(1)} %collective-permute-done.10.refs_1_, f32[5,256,256]{2,1,0:T(8,128)S(1)} %correlate.4.refs_2_), custom_call_target="tpu_custom_call" | custom-call | tf_op jit(solution)/shard_map/correlate/pallas_call | solution.py:303
  46.8 2.2 %collective-permute-done.8.refs_1_ = bf16[32,16,128]{2,1,0:T(8,128)(2,1)S(1)} collective-permute-done((bf16[32,16,128]{2,1,0:T(8,128)(2,1)S(1)}, bf16[32,16,128]{2,1,0:T(8,128)(2,1)S(1)}, u32[]{:S(2)}, u32[]{:S(2)}) %collective-permute-start.8) | collective-permute-done | bytes 131104 | tf_op jit(solution)/shard_map/ppermute | solution.py:408
  49.0 4.6 %correlate_last.1 = f32[5,8,8,1001]{3,2,1,0:T(8,128)} custom-call(s32[16]{0:T(128)S(1)} %bitcast.8, bf16[25,16,128]{2,1,0:T(8,128)(2,1)S(1)} %collective-permute-done.7.refs_0_, bf16[32,16,128]{2,1,0:T(8,128)(2,1)S(1)} %collective-permute-done.8.refs_1_, f32[5,256,256]{2,1,0:T(8,128)S(1)} %correlate.5.refs_2_), custom_call_target="tpu_custom_call" | custom-call | tf_op jit(solution)/shard_map/correlate_last/pallas_call | solution.py:303
Async XLA Ops:
  1.2 9.8 %all-to-all-start = ((s32[8,1,2]{2,1,0:T(1,128)}), s32[8,1,2]{2,1,0:T(1,128)S(1)}, u32[]{:S(2)}, u32[]{:S(2)}) async-start(s32[8,1,2]{2,1,0:T(1,128)} %broadcast_in_dim.2), calls=%async_computation | async-start | bytes 8192 | tf_op jit(solution)/shard_map/all_to_all | solution.py:328
  6.4 0.7 %copy-start.1 = (f32[255]{0:T(256)S(1)}, f32[255]{0:T(256)}, u32[]{:S(2)}) copy-start(f32[255]{0:T(256)} %param.5) | copy-start | bytes 3064
  11.0 12.7 %copy-start = (s32[16,1]{0,1:T(1,128)S(1)}, s32[16,1]{0,1:T(1,128)}, u32[]{:S(2)}) copy-start(s32[16,1]{0,1:T(1,128)} %param.7) | copy-start | bytes 196
  16.1 3.6 %collective-permute-start = (bf16[128,384]{1,0:T(8,128)(2,1)S(1)}, bf16[128,384]{1,0:T(8,128)(2,1)S(1)}, u32[]{:S(2)}, u32[]{:S(2)}) collective-permute-start(bf16[128,384]{1,0:T(8,128)(2,1)S(1)} %get-tuple-element.29), channel_id=1, source_target_pairs={{0,1},{1,0},{2,3},{3,2},{4,5},{5,4},{6,7},{7,6},{8,9},{9,8},{10,11... | collective-permute-start | bytes 294920 | tf_op jit(solution)/shard_map/ppermute | solution.py:369
  16.2 5.7 %collective-permute-start.1 = (bf16[128,384]{1,0:T(8,128)(2,1)S(1)}, bf16[128,384]{1,0:T(8,128)(2,1)S(1)}, u32[]{:S(2)}, u32[]{:S(2)}) collective-permute-start(bf16[128,384]{1,0:T(8,128)(2,1)S(1)} %get-tuple-element.30), channel_id=1, source_target_pairs={{0,2},{1,3},{2,0},{3,1},{4,6},{5,7},{6,4},{7,5},{8,10},{9,11},{10,... | collective-permute-start | bytes 294920 | tf_op jit(solution)/shard_map/ppermute | solution.py:369
  16.7 6.3 %collective-permute-start.2 = (bf16[128,384]{1,0:T(8,128)(2,1)S(1)}, bf16[128,384]{1,0:T(8,128)(2,1)S(1)}, u32[]{:S(2)}, u32[]{:S(2)}) collective-permute-start(bf16[128,384]{1,0:T(8,128)(2,1)S(1)} %get-tuple-element.31), channel_id=1, source_target_pairs={{0,3},{1,2},{2,1},{3,0},{4,7},{5,6},{6,5},{7,4},{8,11},{9,10},{10,... | collective-permute-start | bytes 294920 | tf_op jit(solution)/shard_map/ppermute | solution.py:369
  18.0 5.6 %collective-permute-start.3 = (bf16[128,384]{1,0:T(8,128)(2,1)S(1)}, bf16[128,384]{1,0:T(8,128)(2,1)S(1)}, u32[]{:S(2)}, u32[]{:S(2)}) collective-permute-start(bf16[128,384]{1,0:T(8,128)(2,1)S(1)} %get-tuple-element.32), channel_id=1, source_target_pairs={{0,4},{1,5},{2,6},{3,7},{4,0},{5,1},{6,2},{7,3},{8,12},{9,13},{10,... | collective-permute-start | bytes 294920 | tf_op jit(solution)/shard_map/ppermute | solution.py:369
  18.6 10.2 %collective-permute-start.4 = (bf16[128,384]{1,0:T(8,128)(2,1)S(1)}, bf16[128,384]{1,0:T(8,128)(2,1)S(1)}, u32[]{:S(2)}, u32[]{:S(2)}) collective-permute-start(bf16[128,384]{1,0:T(8,128)(2,1)S(1)} %get-tuple-element.38), channel_id=1, source_target_pairs={{0,5},{1,4},{2,7},{3,6},{4,1},{5,0},{6,3},{7,2},{8,13},{9,12},{10,... | collective-permute-start | bytes 294920 | tf_op jit(solution)/shard_map/ppermute | solution.py:369
  19.7 9.1 %collective-permute-start.5 = (bf16[128,384]{1,0:T(8,128)(2,1)S(1)}, bf16[128,384]{1,0:T(8,128)(2,1)S(1)}, u32[]{:S(2)}, u32[]{:S(2)}) collective-permute-start(bf16[128,384]{1,0:T(8,128)(2,1)S(1)} %get-tuple-element.39), channel_id=1, source_target_pairs={{0,6},{1,7},{2,4},{3,5},{4,2},{5,3},{6,0},{7,1},{8,14},{9,15},{10,... | collective-permute-start | bytes 294920 | tf_op jit(solution)/shard_map/ppermute | solution.py:369
  21.8 7.0 %collective-permute-start.6 = (bf16[128,384]{1,0:T(8,128)(2,1)S(1)}, bf16[128,384]{1,0:T(8,128)(2,1)S(1)}, u32[]{:S(2)}, u32[]{:S(2)}) collective-permute-start(bf16[128,384]{1,0:T(8,128)(2,1)S(1)} %get-tuple-element.40), channel_id=1, source_target_pairs={{0,7},{1,6},{2,5},{3,4},{4,3},{5,2},{6,1},{7,0},{8,15},{9,14},{10,... | collective-permute-start | bytes 294920 | tf_op jit(solution)/shard_map/ppermute | solution.py:369
  24.4 7.7 %collective-permute-start.9 = (bf16[25,16,128]{2,1,0:T(8,128)(2,1)S(1)}, bf16[25,16,128]{2,1,0:T(8,128)(2,1)S(1)}, u32[]{:S(2)}, u32[]{:S(2)}) collective-permute-start(bf16[25,16,128]{2,1,0:T(8,128)(2,1)S(1)} %get-tuple-element.46), channel_id=1, source_target_pairs={{0,24},{8,16},{16,8},{24,0},{1,25},{9,17},{17,9},{25,1},{2,26},{10... | collective-permute-start | bytes 307208 | tf_op jit(solution)/shard_map/ppermute | solution.py:408
  28.1 9.3 %collective-permute-start.7 = (bf16[25,16,128]{2,1,0:T(8,128)(2,1)S(1)}, bf16[25,16,128]{2,1,0:T(8,128)(2,1)S(1)}, u32[]{:S(2)}, u32[]{:S(2)}) collective-permute-start(bf16[25,16,128]{2,1,0:T(8,128)(2,1)S(1)} %get-tuple-element.42), channel_id=1, source_target_pairs={{0,16},{8,24},{16,0},{24,8},{1,17},{9,25},{17,1},{25,9},{2,18},{10... | collective-permute-start | bytes 307208 | tf_op jit(solution)/shard_map/ppermute | solution.py:408
  29.9 10.8 %collective-permute-start.11 = (bf16[56,16,128]{2,1,0:T(8,128)(2,1)S(1)}, bf16[56,16,128]{2,1,0:T(8,128)(2,1)S(1)}, u32[]{:S(2)}, u32[]{:S(2)}) collective-permute-start(bf16[56,16,128]{2,1,0:T(8,128)(2,1)S(1)} %get-tuple-element.49), channel_id=1, source_target_pairs={{0,8},{8,0},{16,24},{24,16},{1,9},{9,1},{17,25},{25,17},{2,10},{10... | collective-permute-start | bytes 688136 | tf_op jit(solution)/shard_map/ppermute | solution.py:408
  32.1 11.6 %collective-permute-start.10 = (bf16[32,16,128]{2,1,0:T(8,128)(2,1)S(1)}, bf16[32,16,128]{2,1,0:T(8,128)(2,1)S(1)}, u32[]{:S(2)}, u32[]{:S(2)}) collective-permute-start(bf16[32,16,128]{2,1,0:T(8,128)(2,1)S(1)} %get-tuple-element.48), channel_id=1, source_target_pairs={{0,24},{8,16},{16,8},{24,0},{1,25},{9,17},{17,9},{25,1},{2,26},{10... | collective-permute-start | bytes 393224 | tf_op jit(solution)/shard_map/ppermute | solution.py:408
  37.4 11.6 %collective-permute-start.8 = (bf16[32,16,128]{2,1,0:T(8,128)(2,1)S(1)}, bf16[32,16,128]{2,1,0:T(8,128)(2,1)S(1)}, u32[]{:S(2)}, u32[]{:S(2)}) collective-permute-start(bf16[32,16,128]{2,1,0:T(8,128)(2,1)S(1)} %get-tuple-element.44), channel_id=1, source_target_pairs={{0,16},{8,24},{16,0},{24,8},{1,17},{9,25},{17,1},{25,9},{2,18},{10... | collective-permute-start | bytes 393224 | tf_op jit(solution)/shard_map/ppermute | solution.py:408

commit v14 on v13

--- a/solution.py
+++ b/solution.py
@@ -199,6 +199,8 @@
 
 
 def correlate_kernel(n_chan, groups, factor, last, owners, *refs):
+    if last:
+        *refs, final, sems = refs
     near, far, windows, whole, parts_sum = refs[-5:]
     out = refs[-6]
     arrived = refs[: len(groups)]
@@ -266,6 +268,10 @@
             windows[s, :, :cut], near[which[s]], NT, preferred_element_type=jnp.float32
         )
         parts_sum[s] = value if before is None else value + before[s]
+
+    def leave(part):
+        slots = pl.ds(0, SLOTS // 2 + 1) if part == 0 else pl.ds(SLOTS // 2 + 1, SLOTS // 2)
+        return pltpu.make_async_copy(final.at[slots], out.at[slots], sems.at[part])
 
     group = lax.broadcasted_iota(jnp.int32, (CB, LANES), 1) // SHIFTS
     for s in range(SLOTS):
@@ -289,7 +295,13 @@
                         if n != a:
                             moved = pltpu.roll(parts[n], (SHIFTS * (n - a)) % LANES, 1)
                             value = jnp.where(group == n, moved, value)
-                    out[s, h * STEP + a, :, i * LANES : i * LANES + width] = value[:, :width]
+                    final[s, h * STEP + a, :, i * LANES : i * LANES + width] = value[:, :width]
+        if s == SLOTS // 2:
+            leave(0).start()
+    if last:
+        leave(1).start()
+        leave(0).wait()
+        leave(1).wait()
 
 
 def correlate(n_chan, owners, arrived, groups, before, factor, last, samples):
@@ -304,14 +316,15 @@
         functools.partial(correlate_kernel, n_chan, groups, factor, last),
         out_shape=shape,
         in_specs=[smem()] + [vmem()] * (len(operands) - 1),
-        out_specs=vmem(),
+        out_specs=pl.BlockSpec(memory_space=pl.ANY) if last else vmem(),
         scratch_shapes=[
             pltpu.VMEM((STRIPES, wide, cut), jnp.bfloat16),
             pltpu.VMEM((STRIPES, wide, depth - cut), jnp.bfloat16),
             pltpu.VMEM((SLOTS, high, depth), jnp.bfloat16),
             pltpu.VMEM((BLOCKS, CB, samples), jnp.float32),
             pltpu.VMEM((SLOTS, high, wide), jnp.float32),
-        ],
+        ]
+        + [pltpu.VMEM(shape.shape, jnp.float32), pltpu.SemaphoreType.DMA((2,))] * last,
         compiler_params=params(40),
         name="correlate_last" if last else "correlate",
     )(*operands)

time: 53.7 us -> 53.5 us (level)
  no operation moved by 1% of the time
where the time goes in v14:
time: 53.5 us; the launch traced here: 53.3 us
  Pallas kernels  20.6 us (39%)
  starting transfers between devices  18.9 us (35%)
  waiting for transfers between devices  11.8 us (22%)
  local copies, waits for them, and re-layouts  1.93 us (4%)
    pallas_call x4, Pallas kernels, correlate(): pl.pallas_call(functools.partial(correlate_kernel, n_chan, groups, factor...  13.4 us
    ppermute x5, starting transfers between devices, hand_over(): lax.ppermute(value, 'tgroup', [(g, g ^ shift) for g in range(n_tgroup)])  9.1 us
    all_to_all x1, starting transfers between devices, local(): lax.all_to_all(jnp.broadcast_to(first_block[None, :], (n_chan, STRIPES)),...  5.17 us
    pallas_call x1, Pallas kernels, local(): pl.pallas_call(functools.partial(select_kernel, n_chan, groups), out_shap...  5.09 us
    ppermute x7, starting transfers between devices, exchange(): return lax.ppermute(value, 'chan', [(c, c ^ k) for c in range(n_chan)])  4.62 us
    ppermute x5, waiting for transfers between devices, hand_over(): lax.ppermute(value, 'tgroup', [(g, g ^ shift) for g in range(n_tgroup)])  4.57 us
    ppermute x7, waiting for transfers between devices, exchange(): return lax.ppermute(value, 'chan', [(c, c ^ k) for c in range(n_chan)])  3.65 us
    all_to_all x1, waiting for transfers between devices, local(): lax.all_to_all(jnp.broadcast_to(first_block[None, :], (n_chan, STRIPES)),...  3.62 us
  transfers between devices with their start and end apart: 13, of which 8 were waited for; matrix products, arithmetic and copies ran while one was open for 0% of the time, Pallas kernels for 21%

profile of v14, /device:TPU:0, one launch (start us, length us, event | category | flops | bytes accessed | tf_op | source)
XLA Modules:
  0.0 53.3 jit_solution(18130687564891440354)
XLA Ops:
  0.0 1.2 %broadcast_in_dim.2 = s32[8,1,2]{2,1,0:T(1,128)} broadcast(s32[2]{0:T(128)} %param.6), dimensions={2} | broadcast | bytes 72 | tf_op jit(solution)/shard_map/broadcast_in_dim | solution.py:342
  1.2 5.2 %all-to-all-start = ((s32[8,1,2]{2,1,0:T(1,128)}), s32[8,1,2]{2,1,0:T(1,128)S(1)}, u32[]{:S(2)}, u32[]{:S(2)}) async-start(s32[8,1,2]{2,1,0:T(1,128)} %broadcast_in_dim.2), calls=%async_computation | async-start | bytes 8192 | tf_op jit(solution)/shard_map/all_to_all | solution.py:341
  6.4 0.0 copy-start.1
  6.4 0.7 %copy-done.1 = f32[255]{0:T(256)S(1)} copy-done((f32[255]{0:T(256)S(1)}, f32[255]{0:T(256)}, u32[]{:S(2)}) %copy-start.1) | copy-done | bytes 1044
  7.1 0.3 fir_weights.1.weights
  7.4 3.6 %all-to-all-done = s32[8,1,2]{2,1,0:T(1,128)S(1)} async-done(((s32[8,1,2]{2,1,0:T(1,128)}), s32[8,1,2]{2,1,0:T(1,128)S(1)}, u32[]{:S(2)}, u32[]{:S(2)}) %all-to-all-start) | async-done | bytes 96 | tf_op jit(solution)/shard_map/all_to_all | solution.py:341
  11.0 0.0 copy-start
  11.0 5.1 %select_filter.1 = (bf16[128,384]{1,0:T(8,128)(2,1)S(1)}, bf16[128,384]{1,0:T(8,128)(2,1)S(1)}, bf16[128,384]{1,0:T(8,128)(2,1)S(1)}, bf16[128,384]{1,0:T(8,128)...) custom-call(s32[8,2]{1,0:T(8,128)S(1)} %bitcast.9, ...), custom_call_target="tpu_custom_call" | custom-call | tf_op jit(solution)/shard_map/select_filter/pallas_call | solution.py:364
  16.1 0.1 collective-permute-start
  16.2 0.6 %collective-permute-start.1 = (bf16[128,384]{1,0:T(8,128)(2,1)S(1)}, bf16[128,384]{1,0:T(8,128)(2,1)S(1)}, u32[]{:S(2)}, u32[]{:S(2)}) collective-permute-start(bf16[128,384]{1,0:T(8,128)(2,1)S(1)} %get-tuple-element.30), channel_id=1, source_target_pairs={{0,2},{1,3},{2,0},{3,1},{4,6},{5,7},{6,4},{7,5},{8,10},{9,11},{10,... | collective-permute-start | bytes 294920 | tf_op jit(solution)/shard_map/ppermute | solution.py:382
  16.8 1.2 %collective-permute-start.2 = (bf16[128,384]{1,0:T(8,128)(2,1)S(1)}, bf16[128,384]{1,0:T(8,128)(2,1)S(1)}, u32[]{:S(2)}, u32[]{:S(2)}) collective-permute-start(bf16[128,384]{1,0:T(8,128)(2,1)S(1)} %get-tuple-element.31), channel_id=1, source_target_pairs={{0,3},{1,2},{2,1},{3,0},{4,7},{5,6},{6,5},{7,4},{8,11},{9,10},{10,... | collective-permute-start | bytes 294920 | tf_op jit(solution)/shard_map/ppermute | solution.py:382
  18.0 0.6 %collective-permute-start.3 = (bf16[128,384]{1,0:T(8,128)(2,1)S(1)}, bf16[128,384]{1,0:T(8,128)(2,1)S(1)}, u32[]{:S(2)}, u32[]{:S(2)}) collective-permute-start(bf16[128,384]{1,0:T(8,128)(2,1)S(1)} %get-tuple-element.32), channel_id=1, source_target_pairs={{0,4},{1,5},{2,6},{3,7},{4,0},{5,1},{6,2},{7,3},{8,12},{9,13},{10,... | collective-permute-start | bytes 294920 | tf_op jit(solution)/shard_map/ppermute | solution.py:382
  18.6 1.1 %collective-permute-start.4 = (bf16[128,384]{1,0:T(8,128)(2,1)S(1)}, bf16[128,384]{1,0:T(8,128)(2,1)S(1)}, u32[]{:S(2)}, u32[]{:S(2)}) collective-permute-start(bf16[128,384]{1,0:T(8,128)(2,1)S(1)} %get-tuple-element.38), channel_id=1, source_target_pairs={{0,5},{1,4},{2,7},{3,6},{4,1},{5,0},{6,3},{7,2},{8,13},{9,12},{10,... | collective-permute-start | bytes 294920 | tf_op jit(solution)/shard_map/ppermute | solution.py:382
  19.7 0.0 collective-permute-done.refs_1_
  19.7 0.4 collective-permute-start.5
  20.1 1.7 %collective-permute-done.1.refs_2_ = bf16[128,384]{1,0:T(8,128)(2,1)S(1)} collective-permute-done((bf16[128,384]{1,0:T(8,128)(2,1)S(1)}, bf16[128,384]{1,0:T(8,128)(2,1)S(1)}, u32[]{:S(2)}, u32[]{:S(2)}) %collective-permute-start.1) | collective-permute-done | bytes 98336 | tf_op jit(solution)/shard_map/ppermute | solution.py:382
  21.8 0.6 %collective-permute-start.6 = (bf16[128,384]{1,0:T(8,128)(2,1)S(1)}, bf16[128,384]{1,0:T(8,128)(2,1)S(1)}, u32[]{:S(2)}, u32[]{:S(2)}) collective-permute-start(bf16[128,384]{1,0:T(8,128)(2,1)S(1)} %get-tuple-element.40), channel_id=1, source_target_pairs={{0,7},{1,6},{2,5},{3,4},{4,3},{5,2},{6,1},{7,0},{8,15},{9,14},{10,... | collective-permute-start | bytes 294920 | tf_op jit(solution)/shard_map/ppermute | solution.py:382
  22.4 0.6 %collective-permute-done.2.refs_3_ = bf16[128,384]{1,0:T(8,128)(2,1)S(1)} collective-permute-done((bf16[128,384]{1,0:T(8,128)(2,1)S(1)}, bf16[128,384]{1,0:T(8,128)(2,1)S(1)}, u32[]{:S(2)}, u32[]{:S(2)}) %collective-permute-start.2) | collective-permute-done | bytes 98336 | tf_op jit(solution)/shard_map/ppermute | solution.py:382
  23.0 0.6 %collective-permute-done.3.refs_4_ = bf16[128,384]{1,0:T(8,128)(2,1)S(1)} collective-permute-done((bf16[128,384]{1,0:T(8,128)(2,1)S(1)}, bf16[128,384]{1,0:T(8,128)(2,1)S(1)}, u32[]{:S(2)}, u32[]{:S(2)}) %collective-permute-start.3) | collective-permute-done | bytes 98336 | tf_op jit(solution)/shard_map/ppermute | solution.py:382
  23.7 0.0 copy-done
  23.7 0.8 %place_first.1 = (bf16[25,16,128]{2,1,0:T(8,128)(2,1)S(1)}, bf16[25,16,128]{2,1,0:T(8,128)(2,1)S(1)}) custom-call(s32[16]{0:T(128)S(1)} %bitcast.3, bf16[128,384]{1,0:T(8,128)(2,1)S(1)} %get-tuple-element.33.refs_0_, bf16[128,384]{1,0:T(8,128)(2,1)S(1)} %collective-permute-done.refs_1_, bf16[128,384]{1,0:T(8,128)(2,1)S(1)} %collective-permute-done.1.refs_2_, ...), custom_call_target="tpu_custom_call" | custom-call | tf_op jit(solution)/shard_map/place_first/pallas_call | solution.py:404
  24.4 3.7 %collective-permute-start.9 = (bf16[25,16,128]{2,1,0:T(8,128)(2,1)S(1)}, bf16[25,16,128]{2,1,0:T(8,128)(2,1)S(1)}, u32[]{:S(2)}, u32[]{:S(2)}) collective-permute-start(bf16[25,16,128]{2,1,0:T(8,128)(2,1)S(1)} %get-tuple-element.46), channel_id=1, source_target_pairs={{0,24},{8,16},{16,8},{24,0},{1,25},{9,17},{17,9},{25,1},{2,26},{10... | collective-permute-start | bytes 307208 | tf_op jit(solution)/shard_map/ppermute | solution.py:421
  28.1 0.0 collective-permute-start.7
  28.1 0.7 %collective-permute-done.4.refs_5_ = bf16[128,384]{1,0:T(8,128)(2,1)S(1)} collective-permute-done((bf16[128,384]{1,0:T(8,128)(2,1)S(1)}, bf16[128,384]{1,0:T(8,128)(2,1)S(1)}, u32[]{:S(2)}, u32[]{:S(2)}) %collective-permute-start.4) | collective-permute-done | bytes 98336 | tf_op jit(solution)/shard_map/ppermute | solution.py:382
  28.8 0.0 collective-permute-done.5.refs_6_
  28.8 0.0 collective-permute-done.6.refs_7_
  28.8 1.0 %place_second.1 = (bf16[56,16,128]{2,1,0:T(8,128)(2,1)S(1)}, bf16[56,16,128]{2,1,0:T(8,128)(2,1)S(1)}, bf16[32,16,128]{2,1,0:T(8,128)(2,1)S(1)}, bf16[32,16,128]{2,1,0:T(8,128)(2,1)S(1)}) custom-call(s32[16]{0:T(128)S(1)} %bitcast.4, bf16[128,384]{1,0:T(8,128)(2,1)S(1)} %get-tuple-element.33.refs_0_, bf16[128,384]{1,0:T(8,128)(2,1)S(1)} %collective-permute-done.refs_1_, ...), custom_call_target="tpu_custom_call" | custom-call | tf_op jit(solution)/shard_map/place_second/pallas_call | solution.py:404
  29.9 1.6 %collective-permute-start.11 = (bf16[56,16,128]{2,1,0:T(8,128)(2,1)S(1)}, bf16[56,16,128]{2,1,0:T(8,128)(2,1)S(1)}, u32[]{:S(2)}, u32[]{:S(2)}) collective-permute-start(bf16[56,16,128]{2,1,0:T(8,128)(2,1)S(1)} %get-tuple-element.49), channel_id=1, source_target_pairs={{0,8},{8,0},{16,24},{24,16},{1,9},{9,1},{17,25},{25,17},{2,10},{10... | collective-permute-start | bytes 688136 | tf_op jit(solution)/shard_map/ppermute | solution.py:421
  31.5 0.6 %collective-permute-done.9.refs_0_ = bf16[25,16,128]{2,1,0:T(8,128)(2,1)S(1)} collective-permute-done((bf16[25,16,128]{2,1,0:T(8,128)(2,1)S(1)}, bf16[25,16,128]{2,1,0:T(8,128)(2,1)S(1)}, u32[]{:S(2)}, u32[]{:S(2)}) %collective-permute-start.9) | collective-permute-done | bytes 102432 | tf_op jit(solution)/shard_map/ppermute | solution.py:421
  32.1 3.6 %collective-permute-start.10 = (bf16[32,16,128]{2,1,0:T(8,128)(2,1)S(1)}, bf16[32,16,128]{2,1,0:T(8,128)(2,1)S(1)}, u32[]{:S(2)}, u32[]{:S(2)}) collective-permute-start(bf16[32,16,128]{2,1,0:T(8,128)(2,1)S(1)} %get-tuple-element.48), channel_id=1, source_target_pairs={{0,24},{8,16},{16,8},{24,0},{1,25},{9,17},{17,9},{25,1},{2,26},{10... | collective-permute-start | bytes 393224 | tf_op jit(solution)/shard_map/ppermute | solution.py:421
  35.7 1.7 %collective-permute-done.7.refs_0_ = bf16[25,16,128]{2,1,0:T(8,128)(2,1)S(1)} collective-permute-done((bf16[25,16,128]{2,1,0:T(8,128)(2,1)S(1)}, bf16[25,16,128]{2,1,0:T(8,128)(2,1)S(1)}, u32[]{:S(2)}, u32[]{:S(2)}) %collective-permute-start.7) | collective-permute-done | bytes 102432 | tf_op jit(solution)/shard_map/ppermute | solution.py:421
  37.4 0.2 collective-permute-start.8
  37.6 3.0 %correlate.3.refs_1_ = f32[5,256,256]{2,1,0:T(8,128)S(1)} custom-call(s32[16]{0:T(128)S(1)} %bitcast.5, bf16[56,16,128]{2,1,0:T(8,128)(2,1)S(1)} %get-tuple-element.50.refs_0_), custom_call_target="tpu_custom_call" | custom-call | tf_op jit(solution)/shard_map/correlate/pallas_call | solution.py:315
  40.7 0.0 collective-permute-done.11.refs_0_
  40.7 3.0 %correlate.4.refs_2_ = f32[5,256,256]{2,1,0:T(8,128)S(1)} custom-call(s32[16]{0:T(128)S(1)} %bitcast.6, bf16[56,16,128]{2,1,0:T(8,128)(2,1)S(1)} %collective-permute-done.11.refs_0_, f32[5,256,256]{2,1,0:T(8,128)S(1)} %correlate.3.refs_1_), custom_call_target="tpu_custom_call" | custom-call | tf_op jit(solution)/shard_map/correlate/pallas_call | solution.py:315
  43.7 0.0 collective-permute-done.10.refs_1_
  43.7 3.0 %correlate.5.refs_2_ = f32[5,256,256]{2,1,0:T(8,128)S(1)} custom-call(s32[16]{0:T(128)S(1)} %bitcast.7, bf16[25,16,128]{2,1,0:T(8,128)(2,1)S(1)} %collective-permute-done.9.refs_0_, bf16[32,16,128]{2,1,0:T(8,128)(2,1)S(1)} %collective-permute-done.10.refs_1_, f32[5,256,256]{2,1,0:T(8,128)S(1)} %correlate.4.refs_2_), custom_call_target="tpu_custom_call" | custom-call | tf_op jit(solution)/shard_map/correlate/pallas_call | solution.py:315
  46.8 2.2 %collective-permute-done.8.refs_1_ = bf16[32,16,128]{2,1,0:T(8,128)(2,1)S(1)} collective-permute-done((bf16[32,16,128]{2,1,0:T(8,128)(2,1)S(1)}, bf16[32,16,128]{2,1,0:T(8,128)(2,1)S(1)}, u32[]{:S(2)}, u32[]{:S(2)}) %collective-permute-start.8) | collective-permute-done | bytes 131104 | tf_op jit(solution)/shard_map/ppermute | solution.py:421
  49.0 4.3 %correlate_last.1 = f32[5,8,8,1001]{3,2,1,0:T(8,128)} custom-call(s32[16]{0:T(128)S(1)} %bitcast.8, bf16[25,16,128]{2,1,0:T(8,128)(2,1)S(1)} %collective-permute-done.7.refs_0_, bf16[32,16,128]{2,1,0:T(8,128)(2,1)S(1)} %collective-permute-done.8.refs_1_, f32[5,256,256]{2,1,0:T(8,128)S(1)} %correlate.5.refs_2_), custom_call_target="tpu_custom_call" | custom-call | tf_op jit(solution)/shard_map/correlate_last/pallas_call | solution.py:315
Async XLA Ops:
  1.2 9.8 %all-to-all-start = ((s32[8,1,2]{2,1,0:T(1,128)}), s32[8,1,2]{2,1,0:T(1,128)S(1)}, u32[]{:S(2)}, u32[]{:S(2)}) async-start(s32[8,1,2]{2,1,0:T(1,128)} %broadcast_in_dim.2), calls=%async_computation | async-start | bytes 8192 | tf_op jit(solution)/shard_map/all_to_all | solution.py:341
  6.4 0.7 %copy-start.1 = (f32[255]{0:T(256)S(1)}, f32[255]{0:T(256)}, u32[]{:S(2)}) copy-start(f32[255]{0:T(256)} %param.5) | copy-start | bytes 3064
  11.0 12.7 %copy-start = (s32[16,1]{0,1:T(1,128)S(1)}, s32[16,1]{0,1:T(1,128)}, u32[]{:S(2)}) copy-start(s32[16,1]{0,1:T(1,128)} %param.7) | copy-start | bytes 196
  16.1 3.6 %collective-permute-start = (bf16[128,384]{1,0:T(8,128)(2,1)S(1)}, bf16[128,384]{1,0:T(8,128)(2,1)S(1)}, u32[]{:S(2)}, u32[]{:S(2)}) collective-permute-start(bf16[128,384]{1,0:T(8,128)(2,1)S(1)} %get-tuple-element.29), channel_id=1, source_target_pairs={{0,1},{1,0},{2,3},{3,2},{4,5},{5,4},{6,7},{7,6},{8,9},{9,8},{10,11... | collective-permute-start | bytes 294920 | tf_op jit(solution)/shard_map/ppermute | solution.py:382
  16.2 5.7 %collective-permute-start.1 = (bf16[128,384]{1,0:T(8,128)(2,1)S(1)}, bf16[128,384]{1,0:T(8,128)(2,1)S(1)}, u32[]{:S(2)}, u32[]{:S(2)}) collective-permute-start(bf16[128,384]{1,0:T(8,128)(2,1)S(1)} %get-tuple-element.30), channel_id=1, source_target_pairs={{0,2},{1,3},{2,0},{3,1},{4,6},{5,7},{6,4},{7,5},{8,10},{9,11},{10,... | collective-permute-start | bytes 294920 | tf_op jit(solution)/shard_map/ppermute | solution.py:382
  16.8 6.2 %collective-permute-start.2 = (bf16[128,384]{1,0:T(8,128)(2,1)S(1)}, bf16[128,384]{1,0:T(8,128)(2,1)S(1)}, u32[]{:S(2)}, u32[]{:S(2)}) collective-permute-start(bf16[128,384]{1,0:T(8,128)(2,1)S(1)} %get-tuple-element.31), channel_id=1, source_target_pairs={{0,3},{1,2},{2,1},{3,0},{4,7},{5,6},{6,5},{7,4},{8,11},{9,10},{10,... | collective-permute-start | bytes 294920 | tf_op jit(solution)/shard_map/ppermute | solution.py:382
  18.0 5.6 %collective-permute-start.3 = (bf16[128,384]{1,0:T(8,128)(2,1)S(1)}, bf16[128,384]{1,0:T(8,128)(2,1)S(1)}, u32[]{:S(2)}, u32[]{:S(2)}) collective-permute-start(bf16[128,384]{1,0:T(8,128)(2,1)S(1)} %get-tuple-element.32), channel_id=1, source_target_pairs={{0,4},{1,5},{2,6},{3,7},{4,0},{5,1},{6,2},{7,3},{8,12},{9,13},{10,... | collective-permute-start | bytes 294920 | tf_op jit(solution)/shard_map/ppermute | solution.py:382
  18.6 10.2 %collective-permute-start.4 = (bf16[128,384]{1,0:T(8,128)(2,1)S(1)}, bf16[128,384]{1,0:T(8,128)(2,1)S(1)}, u32[]{:S(2)}, u32[]{:S(2)}) collective-permute-start(bf16[128,384]{1,0:T(8,128)(2,1)S(1)} %get-tuple-element.38), channel_id=1, source_target_pairs={{0,5},{1,4},{2,7},{3,6},{4,1},{5,0},{6,3},{7,2},{8,13},{9,12},{10,... | collective-permute-start | bytes 294920 | tf_op jit(solution)/shard_map/ppermute | solution.py:382
  19.7 9.1 %collective-permute-start.5 = (bf16[128,384]{1,0:T(8,128)(2,1)S(1)}, bf16[128,384]{1,0:T(8,128)(2,1)S(1)}, u32[]{:S(2)}, u32[]{:S(2)}) collective-permute-start(bf16[128,384]{1,0:T(8,128)(2,1)S(1)} %get-tuple-element.39), channel_id=1, source_target_pairs={{0,6},{1,7},{2,4},{3,5},{4,2},{5,3},{6,0},{7,1},{8,14},{9,15},{10,... | collective-permute-start | bytes 294920 | tf_op jit(solution)/shard_map/ppermute | solution.py:382
  21.8 7.0 %collective-permute-start.6 = (bf16[128,384]{1,0:T(8,128)(2,1)S(1)}, bf16[128,384]{1,0:T(8,128)(2,1)S(1)}, u32[]{:S(2)}, u32[]{:S(2)}) collective-permute-start(bf16[128,384]{1,0:T(8,128)(2,1)S(1)} %get-tuple-element.40), channel_id=1, source_target_pairs={{0,7},{1,6},{2,5},{3,4},{4,3},{5,2},{6,1},{7,0},{8,15},{9,14},{10,... | collective-permute-start | bytes 294920 | tf_op jit(solution)/shard_map/ppermute | solution.py:382
  24.4 7.7 %collective-permute-start.9 = (bf16[25,16,128]{2,1,0:T(8,128)(2,1)S(1)}, bf16[25,16,128]{2,1,0:T(8,128)(2,1)S(1)}, u32[]{:S(2)}, u32[]{:S(2)}) collective-permute-start(bf16[25,16,128]{2,1,0:T(8,128)(2,1)S(1)} %get-tuple-element.46), channel_id=1, source_target_pairs={{0,24},{8,16},{16,8},{24,0},{1,25},{9,17},{17,9},{25,1},{2,26},{10... | collective-permute-start | bytes 307208 | tf_op jit(solution)/shard_map/ppermute | solution.py:421
  28.1 9.3 %collective-permute-start.7 = (bf16[25,16,128]{2,1,0:T(8,128)(2,1)S(1)}, bf16[25,16,128]{2,1,0:T(8,128)(2,1)S(1)}, u32[]{:S(2)}, u32[]{:S(2)}) collective-permute-start(bf16[25,16,128]{2,1,0:T(8,128)(2,1)S(1)} %get-tuple-element.42), channel_id=1, source_target_pairs={{0,16},{8,24},{16,0},{24,8},{1,17},{9,25},{17,1},{25,9},{2,18},{10... | collective-permute-start | bytes 307208 | tf_op jit(solution)/shard_map/ppermute | solution.py:421
  29.9 10.8 %collective-permute-start.11 = (bf16[56,16,128]{2,1,0:T(8,128)(2,1)S(1)}, bf16[56,16,128]{2,1,0:T(8,128)(2,1)S(1)}, u32[]{:S(2)}, u32[]{:S(2)}) collective-permute-start(bf16[56,16,128]{2,1,0:T(8,128)(2,1)S(1)} %get-tuple-element.49), channel_id=1, source_target_pairs={{0,8},{8,0},{16,24},{24,16},{1,9},{9,1},{17,25},{25,17},{2,10},{10... | collective-permute-start | bytes 688136 | tf_op jit(solution)/shard_map/ppermute | solution.py:421
  32.1 11.6 %collective-permute-start.10 = (bf16[32,16,128]{2,1,0:T(8,128)(2,1)S(1)}, bf16[32,16,128]{2,1,0:T(8,128)(2,1)S(1)}, u32[]{:S(2)}, u32[]{:S(2)}) collective-permute-start(bf16[32,16,128]{2,1,0:T(8,128)(2,1)S(1)} %get-tuple-element.48), channel_id=1, source_target_pairs={{0,24},{8,16},{16,8},{24,0},{1,25},{9,17},{17,9},{25,1},{2,26},{10... | collective-permute-start | bytes 393224 | tf_op jit(solution)/shard_map/ppermute | solution.py:421
  37.4 11.6 %collective-permute-start.8 = (bf16[32,16,128]{2,1,0:T(8,128)(2,1)S(1)}, bf16[32,16,128]{2,1,0:T(8,128)(2,1)S(1)}, u32[]{:S(2)}, u32[]{:S(2)}) collective-permute-start(bf16[32,16,128]{2,1,0:T(8,128)(2,1)S(1)} %get-tuple-element.44), channel_id=1, source_target_pairs={{0,16},{8,24},{16,0},{24,8},{1,17},{9,25},{17,1},{25,9},{2,18},{10... | collective-permute-start | bytes 393224 | tf_op jit(solution)/shard_map/ppermute | solution.py:421

commit v15 on v14

--- a/solution.py
+++ b/solution.py
@@ -55,6 +55,7 @@
 def select_kernel(n_chan, groups, firsts, raw, weights, *refs):
     sends, (window, picked, sems) = refs[: len(groups)], refs[len(groups) :]
     rows, channels = raw.shape
+    outs = rows // 2
     steps = [k for group in groups for k in group]
     stripes = n_chan * STRIPES
     blocks_per = channels // n_chan // CB
@@ -110,9 +111,17 @@
             chosen = lax.dot_general(hot, block, NT, preferred_element_type=jnp.float32)
             picked[p * WIDE : (p + 1) * WIDE, :] = chosen.astype(jnp.bfloat16)
         part = slice(first * WIDE, (first + batch) * WIDE)
-        result = jnp.dot(
-            picked[part, :], weights[...], preferred_element_type=jnp.float32
-        ).astype(jnp.bfloat16)
+        taken = picked[part, :]
+        inner = jnp.dot(taken, weights[:, :outs], preferred_element_type=jnp.float32)
+        if rows > 4 * SPILL:
+            taken = jnp.concatenate([taken[:, : 2 * SPILL], taken[:, rows - 2 * SPILL :]], 1)
+            edge = jnp.concatenate(
+                [weights[: 2 * SPILL, outs:], weights[rows - 2 * SPILL :, outs:]], 0
+            )
+        else:
+            edge = weights[:, outs:]
+        outer = jnp.dot(taken, edge, preferred_element_type=jnp.float32)
+        result = jnp.concatenate([inner, outer], 1).astype(jnp.bfloat16)
         height = STRIPES * WIDE
         for at in range(batch // STRIPES):
             k = steps[first // STRIPES + at]

time: 53.5 us -> 53.4 us (level)
  no operation moved by 1% of the time
where the time goes in v15:
time: 53.4 us; the launch traced here: 53.3 us
  Pallas kernels  20.5 us (38%)
  starting transfers between devices  19 us (36%)
  waiting for transfers between devices  11.8 us (22%)
  local copies, waits for them, and re-layouts  1.93 us (4%)
    pallas_call x4, Pallas kernels, correlate(): pl.pallas_call(functools.partial(correlate_kernel, n_chan, groups, factor...  13.4 us
    ppermute x5, starting transfers between devices, hand_over(): lax.ppermute(value, 'tgroup', [(g, g ^ shift) for g in range(n_tgroup)])  9.12 us
    all_to_all x1, starting transfers between devices, local(): lax.all_to_all(jnp.broadcast_to(first_block[None, :], (n_chan, STRIPES)),...  5.17 us
    pallas_call x1, Pallas kernels, local(): pl.pallas_call(functools.partial(select_kernel, n_chan, groups), out_shap...  5.02 us
    ppermute x7, starting transfers between devices, exchange(): return lax.ppermute(value, 'chan', [(c, c ^ k) for c in range(n_chan)])  4.7 us
    ppermute x5, waiting for transfers between devices, hand_over(): lax.ppermute(value, 'tgroup', [(g, g ^ shift) for g in range(n_tgroup)])  4.58 us
    all_to_all x1, waiting for transfers between devices, local(): lax.all_to_all(jnp.broadcast_to(first_block[None, :], (n_chan, STRIPES)),...  3.62 us
    ppermute x7, waiting for transfers between devices, exchange(): return lax.ppermute(value, 'chan', [(c, c ^ k) for c in range(n_chan)])  3.56 us
  transfers between devices with their start and end apart: 13, of which 8 were waited for; matrix products, arithmetic and copies ran while one was open for 0% of the time, Pallas kernels for 21%

profile of v15, /device:TPU:0, one launch (start us, length us, event | category | flops | bytes accessed | tf_op | source)
XLA Modules:
  0.0 53.3 jit_solution(17706070685255800238)
XLA Ops:
  0.0 1.2 %broadcast_in_dim.2 = s32[8,1,2]{2,1,0:T(1,128)} broadcast(s32[2]{0:T(128)} %param.6), dimensions={2} | broadcast | bytes 72 | tf_op jit(solution)/shard_map/broadcast_in_dim | solution.py:351
  1.2 5.2 %all-to-all-start = ((s32[8,1,2]{2,1,0:T(1,128)}), s32[8,1,2]{2,1,0:T(1,128)S(1)}, u32[]{:S(2)}, u32[]{:S(2)}) async-start(s32[8,1,2]{2,1,0:T(1,128)} %broadcast_in_dim.2), calls=%async_computation | async-start | bytes 8192 | tf_op jit(solution)/shard_map/all_to_all | solution.py:350
  6.4 0.0 copy-start.1
  6.4 0.7 %copy-done.1 = f32[255]{0:T(256)S(1)} copy-done((f32[255]{0:T(256)S(1)}, f32[255]{0:T(256)}, u32[]{:S(2)}) %copy-start.1) | copy-done | bytes 1044
  7.1 0.3 fir_weights.1.weights
  7.4 3.6 %all-to-all-done = s32[8,1,2]{2,1,0:T(1,128)S(1)} async-done(((s32[8,1,2]{2,1,0:T(1,128)}), s32[8,1,2]{2,1,0:T(1,128)S(1)}, u32[]{:S(2)}, u32[]{:S(2)}) %all-to-all-start) | async-done | bytes 96 | tf_op jit(solution)/shard_map/all_to_all | solution.py:350
  11.0 0.0 copy-start
  11.0 5.0 %select_filter.1 = (bf16[128,384]{1,0:T(8,128)(2,1)S(1)}, bf16[128,384]{1,0:T(8,128)(2,1)S(1)}, bf16[128,384]{1,0:T(8,128)(2,1)S(1)}, bf16[128,384]{1,0:T(8,128)...) custom-call(s32[8,2]{1,0:T(8,128)S(1)} %bitcast.9, ...), custom_call_target="tpu_custom_call" | custom-call | tf_op jit(solution)/shard_map/select_filter/pallas_call | solution.py:373
  16.0 0.1 collective-permute-start
  16.1 0.6 %collective-permute-start.1 = (bf16[128,384]{1,0:T(8,128)(2,1)S(1)}, bf16[128,384]{1,0:T(8,128)(2,1)S(1)}, u32[]{:S(2)}, u32[]{:S(2)}) collective-permute-start(bf16[128,384]{1,0:T(8,128)(2,1)S(1)} %get-tuple-element.30), channel_id=1, source_target_pairs={{0,2},{1,3},{2,0},{3,1},{4,6},{5,7},{6,4},{7,5},{8,10},{9,11},{10,... | collective-permute-start | bytes 294920 | tf_op jit(solution)/shard_map/ppermute | solution.py:391
  16.7 1.2 %collective-permute-start.2 = (bf16[128,384]{1,0:T(8,128)(2,1)S(1)}, bf16[128,384]{1,0:T(8,128)(2,1)S(1)}, u32[]{:S(2)}, u32[]{:S(2)}) collective-permute-start(bf16[128,384]{1,0:T(8,128)(2,1)S(1)} %get-tuple-element.31), channel_id=1, source_target_pairs={{0,3},{1,2},{2,1},{3,0},{4,7},{5,6},{6,5},{7,4},{8,11},{9,10},{10,... | collective-permute-start | bytes 294920 | tf_op jit(solution)/shard_map/ppermute | solution.py:391
  18.0 0.6 %collective-permute-start.3 = (bf16[128,384]{1,0:T(8,128)(2,1)S(1)}, bf16[128,384]{1,0:T(8,128)(2,1)S(1)}, u32[]{:S(2)}, u32[]{:S(2)}) collective-permute-start(bf16[128,384]{1,0:T(8,128)(2,1)S(1)} %get-tuple-element.32), channel_id=1, source_target_pairs={{0,4},{1,5},{2,6},{3,7},{4,0},{5,1},{6,2},{7,3},{8,12},{9,13},{10,... | collective-permute-start | bytes 294920 | tf_op jit(solution)/shard_map/ppermute | solution.py:391
  18.6 1.1 %collective-permute-start.4 = (bf16[128,384]{1,0:T(8,128)(2,1)S(1)}, bf16[128,384]{1,0:T(8,128)(2,1)S(1)}, u32[]{:S(2)}, u32[]{:S(2)}) collective-permute-start(bf16[128,384]{1,0:T(8,128)(2,1)S(1)} %get-tuple-element.38), channel_id=1, source_target_pairs={{0,5},{1,4},{2,7},{3,6},{4,1},{5,0},{6,3},{7,2},{8,13},{9,12},{10,... | collective-permute-start | bytes 294920 | tf_op jit(solution)/shard_map/ppermute | solution.py:391
  19.7 0.0 collective-permute-done.refs_1_
  19.7 0.5 collective-permute-start.5
  20.2 1.6 %collective-permute-done.1.refs_2_ = bf16[128,384]{1,0:T(8,128)(2,1)S(1)} collective-permute-done((bf16[128,384]{1,0:T(8,128)(2,1)S(1)}, bf16[128,384]{1,0:T(8,128)(2,1)S(1)}, u32[]{:S(2)}, u32[]{:S(2)}) %collective-permute-start.1) | collective-permute-done | bytes 98336 | tf_op jit(solution)/shard_map/ppermute | solution.py:391
  21.8 0.6 %collective-permute-start.6 = (bf16[128,384]{1,0:T(8,128)(2,1)S(1)}, bf16[128,384]{1,0:T(8,128)(2,1)S(1)}, u32[]{:S(2)}, u32[]{:S(2)}) collective-permute-start(bf16[128,384]{1,0:T(8,128)(2,1)S(1)} %get-tuple-element.40), channel_id=1, source_target_pairs={{0,7},{1,6},{2,5},{3,4},{4,3},{5,2},{6,1},{7,0},{8,15},{9,14},{10,... | collective-permute-start | bytes 294920 | tf_op jit(solution)/shard_map/ppermute | solution.py:391
  22.4 0.6 %collective-permute-done.2.refs_3_ = bf16[128,384]{1,0:T(8,128)(2,1)S(1)} collective-permute-done((bf16[128,384]{1,0:T(8,128)(2,1)S(1)}, bf16[128,384]{1,0:T(8,128)(2,1)S(1)}, u32[]{:S(2)}, u32[]{:S(2)}) %collective-permute-start.2) | collective-permute-done | bytes 98336 | tf_op jit(solution)/shard_map/ppermute | solution.py:391
  23.0 0.6 %collective-permute-done.3.refs_4_ = bf16[128,384]{1,0:T(8,128)(2,1)S(1)} collective-permute-done((bf16[128,384]{1,0:T(8,128)(2,1)S(1)}, bf16[128,384]{1,0:T(8,128)(2,1)S(1)}, u32[]{:S(2)}, u32[]{:S(2)}) %collective-permute-start.3) | collective-permute-done | bytes 98336 | tf_op jit(solution)/shard_map/ppermute | solution.py:391
  23.6 0.0 copy-done
  23.6 0.8 %place_first.1 = (bf16[25,16,128]{2,1,0:T(8,128)(2,1)S(1)}, bf16[25,16,128]{2,1,0:T(8,128)(2,1)S(1)}) custom-call(s32[16]{0:T(128)S(1)} %bitcast.3, bf16[128,384]{1,0:T(8,128)(2,1)S(1)} %get-tuple-element.33.refs_0_, bf16[128,384]{1,0:T(8,128)(2,1)S(1)} %collective-permute-done.refs_1_, bf16[128,384]{1,0:T(8,128)(2,1)S(1)} %collective-permute-done.1.refs_2_, ...), custom_call_target="tpu_custom_call" | custom-call | tf_op jit(solution)/shard_map/place_first/pallas_call | solution.py:413
  24.4 3.7 %collective-permute-start.9 = (bf16[25,16,128]{2,1,0:T(8,128)(2,1)S(1)}, bf16[25,16,128]{2,1,0:T(8,128)(2,1)S(1)}, u32[]{:S(2)}, u32[]{:S(2)}) collective-permute-start(bf16[25,16,128]{2,1,0:T(8,128)(2,1)S(1)} %get-tuple-element.46), channel_id=1, source_target_pairs={{0,24},{8,16},{16,8},{24,0},{1,25},{9,17},{17,9},{25,1},{2,26},{10... | collective-permute-start | bytes 307208 | tf_op jit(solution)/shard_map/ppermute | solution.py:430
  28.1 0.0 collective-permute-start.7
  28.1 0.7 %collective-permute-done.4.refs_5_ = bf16[128,384]{1,0:T(8,128)(2,1)S(1)} collective-permute-done((bf16[128,384]{1,0:T(8,128)(2,1)S(1)}, bf16[128,384]{1,0:T(8,128)(2,1)S(1)}, u32[]{:S(2)}, u32[]{:S(2)}) %collective-permute-start.4) | collective-permute-done | bytes 98336 | tf_op jit(solution)/shard_map/ppermute | solution.py:391
  28.8 0.0 collective-permute-done.5.refs_6_
  28.8 0.0 collective-permute-done.6.refs_7_
  28.8 1.0 %place_second.1 = (bf16[56,16,128]{2,1,0:T(8,128)(2,1)S(1)}, bf16[56,16,128]{2,1,0:T(8,128)(2,1)S(1)}, bf16[32,16,128]{2,1,0:T(8,128)(2,1)S(1)}, bf16[32,16,128]{2,1,0:T(8,128)(2,1)S(1)}) custom-call(s32[16]{0:T(128)S(1)} %bitcast.4, bf16[128,384]{1,0:T(8,128)(2,1)S(1)} %get-tuple-element.33.refs_0_, bf16[128,384]{1,0:T(8,128)(2,1)S(1)} %collective-permute-done.refs_1_, ...), custom_call_target="tpu_custom_call" | custom-call | tf_op jit(solution)/shard_map/place_second/pallas_call | solution.py:413
  29.8 1.6 %collective-permute-start.11 = (bf16[56,16,128]{2,1,0:T(8,128)(2,1)S(1)}, bf16[56,16,128]{2,1,0:T(8,128)(2,1)S(1)}, u32[]{:S(2)}, u32[]{:S(2)}) collective-permute-start(bf16[56,16,128]{2,1,0:T(8,128)(2,1)S(1)} %get-tuple-element.49), channel_id=1, source_target_pairs={{0,8},{8,0},{16,24},{24,16},{1,9},{9,1},{17,25},{25,17},{2,10},{10... | collective-permute-start | bytes 688136 | tf_op jit(solution)/shard_map/ppermute | solution.py:430
  31.4 0.6 %collective-permute-done.9.refs_0_ = bf16[25,16,128]{2,1,0:T(8,128)(2,1)S(1)} collective-permute-done((bf16[25,16,128]{2,1,0:T(8,128)(2,1)S(1)}, bf16[25,16,128]{2,1,0:T(8,128)(2,1)S(1)}, u32[]{:S(2)}, u32[]{:S(2)}) %collective-permute-start.9) | collective-permute-done | bytes 102432 | tf_op jit(solution)/shard_map/ppermute | solution.py:430
  32.0 3.6 %collective-permute-start.10 = (bf16[32,16,128]{2,1,0:T(8,128)(2,1)S(1)}, bf16[32,16,128]{2,1,0:T(8,128)(2,1)S(1)}, u32[]{:S(2)}, u32[]{:S(2)}) collective-permute-start(bf16[32,16,128]{2,1,0:T(8,128)(2,1)S(1)} %get-tuple-element.48), channel_id=1, source_target_pairs={{0,24},{8,16},{16,8},{24,0},{1,25},{9,17},{17,9},{25,1},{2,26},{10... | collective-permute-start | bytes 393224 | tf_op jit(solution)/shard_map/ppermute | solution.py:430
  35.6 1.7 %collective-permute-done.7.refs_0_ = bf16[25,16,128]{2,1,0:T(8,128)(2,1)S(1)} collective-permute-done((bf16[25,16,128]{2,1,0:T(8,128)(2,1)S(1)}, bf16[25,16,128]{2,1,0:T(8,128)(2,1)S(1)}, u32[]{:S(2)}, u32[]{:S(2)}) %collective-permute-start.7) | collective-permute-done | bytes 102432 | tf_op jit(solution)/shard_map/ppermute | solution.py:430
  37.4 0.2 collective-permute-start.8
  37.6 3.0 %correlate.3.refs_1_ = f32[5,256,256]{2,1,0:T(8,128)S(1)} custom-call(s32[16]{0:T(128)S(1)} %bitcast.5, bf16[56,16,128]{2,1,0:T(8,128)(2,1)S(1)} %get-tuple-element.50.refs_0_), custom_call_target="tpu_custom_call" | custom-call | tf_op jit(solution)/shard_map/correlate/pallas_call | solution.py:324
  40.6 0.0 collective-permute-done.11.refs_0_
  40.6 3.0 %correlate.4.refs_2_ = f32[5,256,256]{2,1,0:T(8,128)S(1)} custom-call(s32[16]{0:T(128)S(1)} %bitcast.6, bf16[56,16,128]{2,1,0:T(8,128)(2,1)S(1)} %collective-permute-done.11.refs_0_, f32[5,256,256]{2,1,0:T(8,128)S(1)} %correlate.3.refs_1_), custom_call_target="tpu_custom_call" | custom-call | tf_op jit(solution)/shard_map/correlate/pallas_call | solution.py:324
  43.6 0.0 collective-permute-done.10.refs_1_
  43.6 3.0 %correlate.5.refs_2_ = f32[5,256,256]{2,1,0:T(8,128)S(1)} custom-call(s32[16]{0:T(128)S(1)} %bitcast.7, bf16[25,16,128]{2,1,0:T(8,128)(2,1)S(1)} %collective-permute-done.9.refs_0_, bf16[32,16,128]{2,1,0:T(8,128)(2,1)S(1)} %collective-permute-done.10.refs_1_, f32[5,256,256]{2,1,0:T(8,128)S(1)} %correlate.4.refs_2_), custom_call_target="tpu_custom_call" | custom-call | tf_op jit(solution)/shard_map/correlate/pallas_call | solution.py:324
  46.7 2.3 %collective-permute-done.8.refs_1_ = bf16[32,16,128]{2,1,0:T(8,128)(2,1)S(1)} collective-permute-done((bf16[32,16,128]{2,1,0:T(8,128)(2,1)S(1)}, bf16[32,16,128]{2,1,0:T(8,128)(2,1)S(1)}, u32[]{:S(2)}, u32[]{:S(2)}) %collective-permute-start.8) | collective-permute-done | bytes 131104 | tf_op jit(solution)/shard_map/ppermute | solution.py:430
  48.9 4.3 %correlate_last.1 = f32[5,8,8,1001]{3,2,1,0:T(8,128)} custom-call(s32[16]{0:T(128)S(1)} %bitcast.8, bf16[25,16,128]{2,1,0:T(8,128)(2,1)S(1)} %collective-permute-done.7.refs_0_, bf16[32,16,128]{2,1,0:T(8,128)(2,1)S(1)} %collective-permute-done.8.refs_1_, f32[5,256,256]{2,1,0:T(8,128)S(1)} %correlate.5.refs_2_), custom_call_target="tpu_custom_call" | custom-call | tf_op jit(solution)/shard_map/correlate_last/pallas_call | solution.py:324
Async XLA Ops:
  1.2 9.8 %all-to-all-start = ((s32[8,1,2]{2,1,0:T(1,128)}), s32[8,1,2]{2,1,0:T(1,128)S(1)}, u32[]{:S(2)}, u32[]{:S(2)}) async-start(s32[8,1,2]{2,1,0:T(1,128)} %broadcast_in_dim.2), calls=%async_computation | async-start | bytes 8192 | tf_op jit(solution)/shard_map/all_to_all | solution.py:350
  6.4 0.7 %copy-start.1 = (f32[255]{0:T(256)S(1)}, f32[255]{0:T(256)}, u32[]{:S(2)}) copy-start(f32[255]{0:T(256)} %param.5) | copy-start | bytes 3064
  11.0 12.6 %copy-start = (s32[16,1]{0,1:T(1,128)S(1)}, s32[16,1]{0,1:T(1,128)}, u32[]{:S(2)}) copy-start(s32[16,1]{0,1:T(1,128)} %param.7) | copy-start | bytes 196
  16.0 3.6 %collective-permute-start = (bf16[128,384]{1,0:T(8,128)(2,1)S(1)}, bf16[128,384]{1,0:T(8,128)(2,1)S(1)}, u32[]{:S(2)}, u32[]{:S(2)}) collective-permute-start(bf16[128,384]{1,0:T(8,128)(2,1)S(1)} %get-tuple-element.29), channel_id=1, source_target_pairs={{0,1},{1,0},{2,3},{3,2},{4,5},{5,4},{6,7},{7,6},{8,9},{9,8},{10,11... | collective-permute-start | bytes 294920 | tf_op jit(solution)/shard_map/ppermute | solution.py:391
  16.1 5.7 %collective-permute-start.1 = (bf16[128,384]{1,0:T(8,128)(2,1)S(1)}, bf16[128,384]{1,0:T(8,128)(2,1)S(1)}, u32[]{:S(2)}, u32[]{:S(2)}) collective-permute-start(bf16[128,384]{1,0:T(8,128)(2,1)S(1)} %get-tuple-element.30), channel_id=1, source_target_pairs={{0,2},{1,3},{2,0},{3,1},{4,6},{5,7},{6,4},{7,5},{8,10},{9,11},{10,... | collective-permute-start | bytes 294920 | tf_op jit(solution)/shard_map/ppermute | solution.py:391
  16.7 6.2 %collective-permute-start.2 = (bf16[128,384]{1,0:T(8,128)(2,1)S(1)}, bf16[128,384]{1,0:T(8,128)(2,1)S(1)}, u32[]{:S(2)}, u32[]{:S(2)}) collective-permute-start(bf16[128,384]{1,0:T(8,128)(2,1)S(1)} %get-tuple-element.31), channel_id=1, source_target_pairs={{0,3},{1,2},{2,1},{3,0},{4,7},{5,6},{6,5},{7,4},{8,11},{9,10},{10,... | collective-permute-start | bytes 294920 | tf_op jit(solution)/shard_map/ppermute | solution.py:391
  18.0 5.6 %collective-permute-start.3 = (bf16[128,384]{1,0:T(8,128)(2,1)S(1)}, bf16[128,384]{1,0:T(8,128)(2,1)S(1)}, u32[]{:S(2)}, u32[]{:S(2)}) collective-permute-start(bf16[128,384]{1,0:T(8,128)(2,1)S(1)} %get-tuple-element.32), channel_id=1, source_target_pairs={{0,4},{1,5},{2,6},{3,7},{4,0},{5,1},{6,2},{7,3},{8,12},{9,13},{10,... | collective-permute-start | bytes 294920 | tf_op jit(solution)/shard_map/ppermute | solution.py:391
  18.6 10.2 %collective-permute-start.4 = (bf16[128,384]{1,0:T(8,128)(2,1)S(1)}, bf16[128,384]{1,0:T(8,128)(2,1)S(1)}, u32[]{:S(2)}, u32[]{:S(2)}) collective-permute-start(bf16[128,384]{1,0:T(8,128)(2,1)S(1)} %get-tuple-element.38), channel_id=1, source_target_pairs={{0,5},{1,4},{2,7},{3,6},{4,1},{5,0},{6,3},{7,2},{8,13},{9,12},{10,... | collective-permute-start | bytes 294920 | tf_op jit(solution)/shard_map/ppermute | solution.py:391
  19.7 9.1 %collective-permute-start.5 = (bf16[128,384]{1,0:T(8,128)(2,1)S(1)}, bf16[128,384]{1,0:T(8,128)(2,1)S(1)}, u32[]{:S(2)}, u32[]{:S(2)}) collective-permute-start(bf16[128,384]{1,0:T(8,128)(2,1)S(1)} %get-tuple-element.39), channel_id=1, source_target_pairs={{0,6},{1,7},{2,4},{3,5},{4,2},{5,3},{6,0},{7,1},{8,14},{9,15},{10,... | collective-permute-start | bytes 294920 | tf_op jit(solution)/shard_map/ppermute | solution.py:391
  21.8 7.0 %collective-permute-start.6 = (bf16[128,384]{1,0:T(8,128)(2,1)S(1)}, bf16[128,384]{1,0:T(8,128)(2,1)S(1)}, u32[]{:S(2)}, u32[]{:S(2)}) collective-permute-start(bf16[128,384]{1,0:T(8,128)(2,1)S(1)} %get-tuple-element.40), channel_id=1, source_target_pairs={{0,7},{1,6},{2,5},{3,4},{4,3},{5,2},{6,1},{7,0},{8,15},{9,14},{10,... | collective-permute-start | bytes 294920 | tf_op jit(solution)/shard_map/ppermute | solution.py:391
  24.4 7.6 %collective-permute-start.9 = (bf16[25,16,128]{2,1,0:T(8,128)(2,1)S(1)}, bf16[25,16,128]{2,1,0:T(8,128)(2,1)S(1)}, u32[]{:S(2)}, u32[]{:S(2)}) collective-permute-start(bf16[25,16,128]{2,1,0:T(8,128)(2,1)S(1)} %get-tuple-element.46), channel_id=1, source_target_pairs={{0,24},{8,16},{16,8},{24,0},{1,25},{9,17},{17,9},{25,1},{2,26},{10... | collective-permute-start | bytes 307208 | tf_op jit(solution)/shard_map/ppermute | solution.py:430
  28.1 9.3 %collective-permute-start.7 = (bf16[25,16,128]{2,1,0:T(8,128)(2,1)S(1)}, bf16[25,16,128]{2,1,0:T(8,128)(2,1)S(1)}, u32[]{:S(2)}, u32[]{:S(2)}) collective-permute-start(bf16[25,16,128]{2,1,0:T(8,128)(2,1)S(1)} %get-tuple-element.42), channel_id=1, source_target_pairs={{0,16},{8,24},{16,0},{24,8},{1,17},{9,25},{17,1},{25,9},{2,18},{10... | collective-permute-start | bytes 307208 | tf_op jit(solution)/shard_map/ppermute | solution.py:430
  29.8 10.8 %collective-permute-start.11 = (bf16[56,16,128]{2,1,0:T(8,128)(2,1)S(1)}, bf16[56,16,128]{2,1,0:T(8,128)(2,1)S(1)}, u32[]{:S(2)}, u32[]{:S(2)}) collective-permute-start(bf16[56,16,128]{2,1,0:T(8,128)(2,1)S(1)} %get-tuple-element.49), channel_id=1, source_target_pairs={{0,8},{8,0},{16,24},{24,16},{1,9},{9,1},{17,25},{25,17},{2,10},{10... | collective-permute-start | bytes 688136 | tf_op jit(solution)/shard_map/ppermute | solution.py:430
  32.0 11.6 %collective-permute-start.10 = (bf16[32,16,128]{2,1,0:T(8,128)(2,1)S(1)}, bf16[32,16,128]{2,1,0:T(8,128)(2,1)S(1)}, u32[]{:S(2)}, u32[]{:S(2)}) collective-permute-start(bf16[32,16,128]{2,1,0:T(8,128)(2,1)S(1)} %get-tuple-element.48), channel_id=1, source_target_pairs={{0,24},{8,16},{16,8},{24,0},{1,25},{9,17},{17,9},{25,1},{2,26},{10... | collective-permute-start | bytes 393224 | tf_op jit(solution)/shard_map/ppermute | solution.py:430
  37.4 11.6 %collective-permute-start.8 = (bf16[32,16,128]{2,1,0:T(8,128)(2,1)S(1)}, bf16[32,16,128]{2,1,0:T(8,128)(2,1)S(1)}, u32[]{:S(2)}, u32[]{:S(2)}) collective-permute-start(bf16[32,16,128]{2,1,0:T(8,128)(2,1)S(1)} %get-tuple-element.44), channel_id=1, source_target_pairs={{0,16},{8,24},{16,0},{24,8},{1,17},{9,25},{17,1},{25,9},{2,18},{10... | collective-permute-start | bytes 393224 | tf_op jit(solution)/shard_map/ppermute | solution.py:430

commit v16 on v12

--- a/solution.py
+++ b/solution.py
@@ -64,7 +64,7 @@
     def place(p):
         c, k = me ^ steps[p // STRIPES], p % STRIPES
         start = (firsts[c, k] + c * blocks_per) * CB
-        base = jnp.minimum(start - lax.rem(start, LANES), channels - span)
+        base = jnp.minimum(start & -LANES, channels - span)
         return start, pl.multiple_of(base, LANES)
 
     def copy(p):
@@ -80,6 +80,7 @@
     for first in range(0, stripes, batch):
         for p in range(first, first + batch):
             copy(p).wait()
+        for p in range(first, first + batch):
             start, base = place(p)
             hot = (lane == row + (start - base)) & (row < channels - start)
             hot = jnp.where(hot, 1.0, 0.0).astype(jnp.bfloat16)
@@ -176,6 +177,8 @@
 
 
 def correlate_kernel(n_chan, groups, factor, last, owners, *refs):
+    if last:
+        *refs, final, sems = refs
     near, far, windows, whole, parts_sum = refs[-5:]
     out = refs[-6]
     arrived = refs[: len(groups)]
@@ -243,6 +246,10 @@
             windows[s, :, :cut], near[which[s]], NT, preferred_element_type=jnp.float32
         )
         parts_sum[s] = value if before is None else value + before[s]
+
+    def leave(part):
+        slots = pl.ds(0, SLOTS // 2 + 1) if part == 0 else pl.ds(SLOTS // 2 + 1, SLOTS // 2)
+        return pltpu.make_async_copy(final.at[slots], out.at[slots], sems.at[part])
 
     group = lax.broadcasted_iota(jnp.int32, (CB, LANES), 1) // SHIFTS
     for s in range(SLOTS):
@@ -266,7 +273,13 @@
                         if n != a:
                             moved = pltpu.roll(parts[n], (SHIFTS * (n - a)) % LANES, 1)
                             value = jnp.where(group == n, moved, value)
-                    out[s, h * STEP + a, :, i * LANES : i * LANES + width] = value[:, :width]
+                    final[s, h * STEP + a, :, i * LANES : i * LANES + width] = value[:, :width]
+        if s == SLOTS // 2:
+            leave(0).start()
+    if last:
+        leave(1).start()
+        leave(0).wait()
+        leave(1).wait()
 
 
 def correlate(n_chan, owners, arrived, groups, before, factor, last, samples):
@@ -281,14 +294,15 @@
         functools.partial(correlate_kernel, n_chan, groups, factor, last),
         out_shape=shape,
         in_specs=[smem()] + [vmem()] * (len(operands) - 1),
-        out_specs=vmem(),
+        out_specs=pl.BlockSpec(memory_space=pl.ANY) if last else vmem(),
         scratch_shapes=[
             pltpu.VMEM((STRIPES, wide, cut), jnp.bfloat16),
             pltpu.VMEM((STRIPES, wide, depth - cut), jnp.bfloat16),
             pltpu.VMEM((SLOTS, high, depth), jnp.bfloat16),
             pltpu.VMEM((BLOCKS, CB, samples), jnp.float32),
             pltpu.VMEM((SLOTS, high, wide), jnp.float32),
-        ],
+        ]
+        + [pltpu.VMEM(shape.shape, jnp.float32), pltpu.SemaphoreType.DMA((2,))] * last,
         compiler_params=params(40),
         name="correlate_last" if last else "correlate",
     )(*operands)

time: 54.6 us -> 53.4 us (0.978)
  Pallas kernels: 21.7 us -> 20.4 us
    pallas_call x1, Pallas kernels: 5.95 us -> 4.95 us  [local(): pl.pallas_call(functools.partial(select_kernel, n_chan, groups), out_shap...]
  transfers between devices with their start and end apart: 13 -> 13, of which waited for: 8 -> 8; matrix products, arithmetic and copies ran while one was open for 0% -> 0% of each run, Pallas kernels for 20% -> 21%
where the time goes in v16:
time: 53.4 us; the launch traced here: 53.2 us
  Pallas kernels  20.4 us (38%)
  starting transfers between devices  19.1 us (36%)
  waiting for transfers between devices  11.7 us (22%)
  local copies, waits for them, and re-layouts  1.93 us (4%)
    pallas_call x4, Pallas kernels, correlate(): pl.pallas_call(functools.partial(correlate_kernel, n_chan, groups, factor...  13.4 us
    ppermute x5, starting transfers between devices, hand_over(): lax.ppermute(value, 'tgroup', [(g, g ^ shift) for g in range(n_tgroup)])  9.12 us
    all_to_all x1, starting transfers between devices, local(): lax.all_to_all(jnp.broadcast_to(first_block[None, :], (n_chan, STRIPES)),...  5.17 us
    pallas_call x1, Pallas kernels, local(): pl.pallas_call(functools.partial(select_kernel, n_chan, groups), out_shap...  4.95 us
    ppermute x7, starting transfers between devices, exchange(): return lax.ppermute(value, 'chan', [(c, c ^ k) for c in range(n_chan)])  4.79 us
    ppermute x5, waiting for transfers between devices, hand_over(): lax.ppermute(value, 'tgroup', [(g, g ^ shift) for g in range(n_tgroup)])  4.56 us
    all_to_all x1, waiting for transfers between devices, local(): lax.all_to_all(jnp.broadcast_to(first_block[None, :], (n_chan, STRIPES)),...  3.62 us
    ppermute x7, waiting for transfers between devices, exchange(): return lax.ppermute(value, 'chan', [(c, c ^ k) for c in range(n_chan)])  3.48 us
  transfers between devices with their start and end apart: 13, of which 8 were waited for; matrix products, arithmetic and copies ran while one was open for 0% of the time, Pallas kernels for 21%

profile of v16, /device:TPU:0, one launch (start us, length us, event | category | flops | bytes accessed | tf_op | source)
XLA Modules:
  0.0 53.2 jit_solution(5979080724150514825)
XLA Ops:
  0.0 1.2 %broadcast_in_dim.2 = s32[8,1,2]{2,1,0:T(1,128)} broadcast(s32[2]{0:T(128)} %param.6), dimensions={2} | broadcast | bytes 72 | tf_op jit(solution)/shard_map/broadcast_in_dim | solution.py:320
  1.2 5.2 %all-to-all-start = ((s32[8,1,2]{2,1,0:T(1,128)}), s32[8,1,2]{2,1,0:T(1,128)S(1)}, u32[]{:S(2)}, u32[]{:S(2)}) async-start(s32[8,1,2]{2,1,0:T(1,128)} %broadcast_in_dim.2), calls=%async_computation | async-start | bytes 8192 | tf_op jit(solution)/shard_map/all_to_all | solution.py:319
  6.4 0.0 copy-start.1
  6.4 0.7 %copy-done.1 = f32[255]{0:T(256)S(1)} copy-done((f32[255]{0:T(256)S(1)}, f32[255]{0:T(256)}, u32[]{:S(2)}) %copy-start.1) | copy-done | bytes 1044
  7.1 0.3 fir_weights.1.weights
  7.4 3.6 %all-to-all-done = s32[8,1,2]{2,1,0:T(1,128)S(1)} async-done(((s32[8,1,2]{2,1,0:T(1,128)}), s32[8,1,2]{2,1,0:T(1,128)S(1)}, u32[]{:S(2)}, u32[]{:S(2)}) %all-to-all-start) | async-done | bytes 96 | tf_op jit(solution)/shard_map/all_to_all | solution.py:319
  11.0 0.0 copy-start
  11.0 5.0 %select_filter.1 = (bf16[128,384]{1,0:T(8,128)(2,1)S(1)}, bf16[128,384]{1,0:T(8,128)(2,1)S(1)}, bf16[128,384]{1,0:T(8,128)(2,1)S(1)}, bf16[128,384]{1,0:T(8,128)...) custom-call(s32[8,2]{1,0:T(8,128)S(1)} %bitcast.9, ...), custom_call_target="tpu_custom_call" | custom-call | tf_op jit(solution)/shard_map/select_filter/pallas_call | solution.py:342
  16.0 0.1 collective-permute-start
  16.0 0.7 %collective-permute-start.1 = (bf16[128,384]{1,0:T(8,128)(2,1)S(1)}, bf16[128,384]{1,0:T(8,128)(2,1)S(1)}, u32[]{:S(2)}, u32[]{:S(2)}) collective-permute-start(bf16[128,384]{1,0:T(8,128)(2,1)S(1)} %get-tuple-element.30), channel_id=1, source_target_pairs={{0,2},{1,3},{2,0},{3,1},{4,6},{5,7},{6,4},{7,5},{8,10},{9,11},{10,... | collective-permute-start | bytes 294920 | tf_op jit(solution)/shard_map/ppermute | solution.py:360
  16.7 1.2 %collective-permute-start.2 = (bf16[128,384]{1,0:T(8,128)(2,1)S(1)}, bf16[128,384]{1,0:T(8,128)(2,1)S(1)}, u32[]{:S(2)}, u32[]{:S(2)}) collective-permute-start(bf16[128,384]{1,0:T(8,128)(2,1)S(1)} %get-tuple-element.31), channel_id=1, source_target_pairs={{0,3},{1,2},{2,1},{3,0},{4,7},{5,6},{6,5},{7,4},{8,11},{9,10},{10,... | collective-permute-start | bytes 294920 | tf_op jit(solution)/shard_map/ppermute | solution.py:360
  17.9 0.6 %collective-permute-start.3 = (bf16[128,384]{1,0:T(8,128)(2,1)S(1)}, bf16[128,384]{1,0:T(8,128)(2,1)S(1)}, u32[]{:S(2)}, u32[]{:S(2)}) collective-permute-start(bf16[128,384]{1,0:T(8,128)(2,1)S(1)} %get-tuple-element.32), channel_id=1, source_target_pairs={{0,4},{1,5},{2,6},{3,7},{4,0},{5,1},{6,2},{7,3},{8,12},{9,13},{10,... | collective-permute-start | bytes 294920 | tf_op jit(solution)/shard_map/ppermute | solution.py:360
  18.5 1.1 %collective-permute-start.4 = (bf16[128,384]{1,0:T(8,128)(2,1)S(1)}, bf16[128,384]{1,0:T(8,128)(2,1)S(1)}, u32[]{:S(2)}, u32[]{:S(2)}) collective-permute-start(bf16[128,384]{1,0:T(8,128)(2,1)S(1)} %get-tuple-element.38), channel_id=1, source_target_pairs={{0,5},{1,4},{2,7},{3,6},{4,1},{5,0},{6,3},{7,2},{8,13},{9,12},{10,... | collective-permute-start | bytes 294920 | tf_op jit(solution)/shard_map/ppermute | solution.py:360
  19.6 0.0 collective-permute-done.refs_1_
  19.6 0.6 %collective-permute-start.5 = (bf16[128,384]{1,0:T(8,128)(2,1)S(1)}, bf16[128,384]{1,0:T(8,128)(2,1)S(1)}, u32[]{:S(2)}, u32[]{:S(2)}) collective-permute-start(bf16[128,384]{1,0:T(8,128)(2,1)S(1)} %get-tuple-element.39), channel_id=1, source_target_pairs={{0,6},{1,7},{2,4},{3,5},{4,2},{5,3},{6,0},{7,1},{8,14},{9,15},{10,... | collective-permute-start | bytes 294920 | tf_op jit(solution)/shard_map/ppermute | solution.py:360
  20.2 1.5 %collective-permute-done.1.refs_2_ = bf16[128,384]{1,0:T(8,128)(2,1)S(1)} collective-permute-done((bf16[128,384]{1,0:T(8,128)(2,1)S(1)}, bf16[128,384]{1,0:T(8,128)(2,1)S(1)}, u32[]{:S(2)}, u32[]{:S(2)}) %collective-permute-start.1) | collective-permute-done | bytes 98336 | tf_op jit(solution)/shard_map/ppermute | solution.py:360
  21.7 0.6 %collective-permute-start.6 = (bf16[128,384]{1,0:T(8,128)(2,1)S(1)}, bf16[128,384]{1,0:T(8,128)(2,1)S(1)}, u32[]{:S(2)}, u32[]{:S(2)}) collective-permute-start(bf16[128,384]{1,0:T(8,128)(2,1)S(1)} %get-tuple-element.40), channel_id=1, source_target_pairs={{0,7},{1,6},{2,5},{3,4},{4,3},{5,2},{6,1},{7,0},{8,15},{9,14},{10,... | collective-permute-start | bytes 294920 | tf_op jit(solution)/shard_map/ppermute | solution.py:360
  22.3 0.6 %collective-permute-done.2.refs_3_ = bf16[128,384]{1,0:T(8,128)(2,1)S(1)} collective-permute-done((bf16[128,384]{1,0:T(8,128)(2,1)S(1)}, bf16[128,384]{1,0:T(8,128)(2,1)S(1)}, u32[]{:S(2)}, u32[]{:S(2)}) %collective-permute-start.2) | collective-permute-done | bytes 98336 | tf_op jit(solution)/shard_map/ppermute | solution.py:360
  22.9 0.6 %collective-permute-done.3.refs_4_ = bf16[128,384]{1,0:T(8,128)(2,1)S(1)} collective-permute-done((bf16[128,384]{1,0:T(8,128)(2,1)S(1)}, bf16[128,384]{1,0:T(8,128)(2,1)S(1)}, u32[]{:S(2)}, u32[]{:S(2)}) %collective-permute-start.3) | collective-permute-done | bytes 98336 | tf_op jit(solution)/shard_map/ppermute | solution.py:360
  23.5 0.0 copy-done
  23.5 0.8 %place_first.1 = (bf16[25,16,128]{2,1,0:T(8,128)(2,1)S(1)}, bf16[25,16,128]{2,1,0:T(8,128)(2,1)S(1)}) custom-call(s32[16]{0:T(128)S(1)} %bitcast.3, bf16[128,384]{1,0:T(8,128)(2,1)S(1)} %get-tuple-element.33.refs_0_, bf16[128,384]{1,0:T(8,128)(2,1)S(1)} %collective-permute-done.refs_1_, bf16[128,384]{1,0:T(8,128)(2,1)S(1)} %collective-permute-done.1.refs_2_, ...), custom_call_target="tpu_custom_call" | custom-call | tf_op jit(solution)/shard_map/place_first/pallas_call | solution.py:382
  24.3 3.7 %collective-permute-start.9 = (bf16[25,16,128]{2,1,0:T(8,128)(2,1)S(1)}, bf16[25,16,128]{2,1,0:T(8,128)(2,1)S(1)}, u32[]{:S(2)}, u32[]{:S(2)}) collective-permute-start(bf16[25,16,128]{2,1,0:T(8,128)(2,1)S(1)} %get-tuple-element.46), channel_id=1, source_target_pairs={{0,24},{8,16},{16,8},{24,0},{1,25},{9,17},{17,9},{25,1},{2,26},{10... | collective-permute-start | bytes 307208 | tf_op jit(solution)/shard_map/ppermute | solution.py:399
  28.0 0.0 collective-permute-start.7
  28.0 0.7 %collective-permute-done.4.refs_5_ = bf16[128,384]{1,0:T(8,128)(2,1)S(1)} collective-permute-done((bf16[128,384]{1,0:T(8,128)(2,1)S(1)}, bf16[128,384]{1,0:T(8,128)(2,1)S(1)}, u32[]{:S(2)}, u32[]{:S(2)}) %collective-permute-start.4) | collective-permute-done | bytes 98336 | tf_op jit(solution)/shard_map/ppermute | solution.py:360
  28.7 0.0 collective-permute-done.5.refs_6_
  28.7 0.0 collective-permute-done.6.refs_7_
  28.7 1.0 %place_second.1 = (bf16[56,16,128]{2,1,0:T(8,128)(2,1)S(1)}, bf16[56,16,128]{2,1,0:T(8,128)(2,1)S(1)}, bf16[32,16,128]{2,1,0:T(8,128)(2,1)S(1)}, bf16[32,16,128]{2,1,0:T(8,128)(2,1)S(1)}) custom-call(s32[16]{0:T(128)S(1)} %bitcast.4, bf16[128,384]{1,0:T(8,128)(2,1)S(1)} %get-tuple-element.33.refs_0_, bf16[128,384]{1,0:T(8,128)(2,1)S(1)} %collective-permute-done.refs_1_, ...), custom_call_target="tpu_custom_call" | custom-call | tf_op jit(solution)/shard_map/place_second/pallas_call | solution.py:382
  29.7 1.6 %collective-permute-start.11 = (bf16[56,16,128]{2,1,0:T(8,128)(2,1)S(1)}, bf16[56,16,128]{2,1,0:T(8,128)(2,1)S(1)}, u32[]{:S(2)}, u32[]{:S(2)}) collective-permute-start(bf16[56,16,128]{2,1,0:T(8,128)(2,1)S(1)} %get-tuple-element.49), channel_id=1, source_target_pairs={{0,8},{8,0},{16,24},{24,16},{1,9},{9,1},{17,25},{25,17},{2,10},{10... | collective-permute-start | bytes 688136 | tf_op jit(solution)/shard_map/ppermute | solution.py:399
  31.4 0.6 %collective-permute-done.9.refs_0_ = bf16[25,16,128]{2,1,0:T(8,128)(2,1)S(1)} collective-permute-done((bf16[25,16,128]{2,1,0:T(8,128)(2,1)S(1)}, bf16[25,16,128]{2,1,0:T(8,128)(2,1)S(1)}, u32[]{:S(2)}, u32[]{:S(2)}) %collective-permute-start.9) | collective-permute-done | bytes 102432 | tf_op jit(solution)/shard_map/ppermute | solution.py:399
  32.0 3.6 %collective-permute-start.10 = (bf16[32,16,128]{2,1,0:T(8,128)(2,1)S(1)}, bf16[32,16,128]{2,1,0:T(8,128)(2,1)S(1)}, u32[]{:S(2)}, u32[]{:S(2)}) collective-permute-start(bf16[32,16,128]{2,1,0:T(8,128)(2,1)S(1)} %get-tuple-element.48), channel_id=1, source_target_pairs={{0,24},{8,16},{16,8},{24,0},{1,25},{9,17},{17,9},{25,1},{2,26},{10... | collective-permute-start | bytes 393224 | tf_op jit(solution)/shard_map/ppermute | solution.py:399
  35.6 1.7 %collective-permute-done.7.refs_0_ = bf16[25,16,128]{2,1,0:T(8,128)(2,1)S(1)} collective-permute-done((bf16[25,16,128]{2,1,0:T(8,128)(2,1)S(1)}, bf16[25,16,128]{2,1,0:T(8,128)(2,1)S(1)}, u32[]{:S(2)}, u32[]{:S(2)}) %collective-permute-start.7) | collective-permute-done | bytes 102432 | tf_op jit(solution)/shard_map/ppermute | solution.py:399
  37.3 0.2 collective-permute-start.8
  37.5 3.0 %correlate.3.refs_1_ = f32[5,256,256]{2,1,0:T(8,128)S(1)} custom-call(s32[16]{0:T(128)S(1)} %bitcast.5, bf16[56,16,128]{2,1,0:T(8,128)(2,1)S(1)} %get-tuple-element.50.refs_0_), custom_call_target="tpu_custom_call" | custom-call | tf_op jit(solution)/shard_map/correlate/pallas_call | solution.py:293
  40.5 0.0 collective-permute-done.11.refs_0_
  40.5 3.0 %correlate.4.refs_2_ = f32[5,256,256]{2,1,0:T(8,128)S(1)} custom-call(s32[16]{0:T(128)S(1)} %bitcast.6, bf16[56,16,128]{2,1,0:T(8,128)(2,1)S(1)} %collective-permute-done.11.refs_0_, f32[5,256,256]{2,1,0:T(8,128)S(1)} %correlate.3.refs_1_), custom_call_target="tpu_custom_call" | custom-call | tf_op jit(solution)/shard_map/correlate/pallas_call | solution.py:293
  43.6 0.0 collective-permute-done.10.refs_1_
  43.6 3.0 %correlate.5.refs_2_ = f32[5,256,256]{2,1,0:T(8,128)S(1)} custom-call(s32[16]{0:T(128)S(1)} %bitcast.7, bf16[25,16,128]{2,1,0:T(8,128)(2,1)S(1)} %collective-permute-done.9.refs_0_, bf16[32,16,128]{2,1,0:T(8,128)(2,1)S(1)} %collective-permute-done.10.refs_1_, f32[5,256,256]{2,1,0:T(8,128)S(1)} %correlate.4.refs_2_), custom_call_target="tpu_custom_call" | custom-call | tf_op jit(solution)/shard_map/correlate/pallas_call | solution.py:293
  46.6 2.2 %collective-permute-done.8.refs_1_ = bf16[32,16,128]{2,1,0:T(8,128)(2,1)S(1)} collective-permute-done((bf16[32,16,128]{2,1,0:T(8,128)(2,1)S(1)}, bf16[32,16,128]{2,1,0:T(8,128)(2,1)S(1)}, u32[]{:S(2)}, u32[]{:S(2)}) %collective-permute-start.8) | collective-permute-done | bytes 131104 | tf_op jit(solution)/shard_map/ppermute | solution.py:399
  48.9 4.3 %correlate_last.1 = f32[5,8,8,1001]{3,2,1,0:T(8,128)} custom-call(s32[16]{0:T(128)S(1)} %bitcast.8, bf16[25,16,128]{2,1,0:T(8,128)(2,1)S(1)} %collective-permute-done.7.refs_0_, bf16[32,16,128]{2,1,0:T(8,128)(2,1)S(1)} %collective-permute-done.8.refs_1_, f32[5,256,256]{2,1,0:T(8,128)S(1)} %correlate.5.refs_2_), custom_call_target="tpu_custom_call" | custom-call | tf_op jit(solution)/shard_map/correlate_last/pallas_call | solution.py:293
Async XLA Ops:
  1.2 9.8 %all-to-all-start = ((s32[8,1,2]{2,1,0:T(1,128)}), s32[8,1,2]{2,1,0:T(1,128)S(1)}, u32[]{:S(2)}, u32[]{:S(2)}) async-start(s32[8,1,2]{2,1,0:T(1,128)} %broadcast_in_dim.2), calls=%async_computation | async-start | bytes 8192 | tf_op jit(solution)/shard_map/all_to_all | solution.py:319
  6.4 0.7 %copy-start.1 = (f32[255]{0:T(256)S(1)}, f32[255]{0:T(256)}, u32[]{:S(2)}) copy-start(f32[255]{0:T(256)} %param.5) | copy-start | bytes 3064
  11.0 12.5 %copy-start = (s32[16,1]{0,1:T(1,128)S(1)}, s32[16,1]{0,1:T(1,128)}, u32[]{:S(2)}) copy-start(s32[16,1]{0,1:T(1,128)} %param.7) | copy-start | bytes 196
  16.0 3.6 %collective-permute-start = (bf16[128,384]{1,0:T(8,128)(2,1)S(1)}, bf16[128,384]{1,0:T(8,128)(2,1)S(1)}, u32[]{:S(2)}, u32[]{:S(2)}) collective-permute-start(bf16[128,384]{1,0:T(8,128)(2,1)S(1)} %get-tuple-element.29), channel_id=1, source_target_pairs={{0,1},{1,0},{2,3},{3,2},{4,5},{5,4},{6,7},{7,6},{8,9},{9,8},{10,11... | collective-permute-start | bytes 294920 | tf_op jit(solution)/shard_map/ppermute | solution.py:360
  16.0 5.7 %collective-permute-start.1 = (bf16[128,384]{1,0:T(8,128)(2,1)S(1)}, bf16[128,384]{1,0:T(8,128)(2,1)S(1)}, u32[]{:S(2)}, u32[]{:S(2)}) collective-permute-start(bf16[128,384]{1,0:T(8,128)(2,1)S(1)} %get-tuple-element.30), channel_id=1, source_target_pairs={{0,2},{1,3},{2,0},{3,1},{4,6},{5,7},{6,4},{7,5},{8,10},{9,11},{10,... | collective-permute-start | bytes 294920 | tf_op jit(solution)/shard_map/ppermute | solution.py:360
  16.7 6.2 %collective-permute-start.2 = (bf16[128,384]{1,0:T(8,128)(2,1)S(1)}, bf16[128,384]{1,0:T(8,128)(2,1)S(1)}, u32[]{:S(2)}, u32[]{:S(2)}) collective-permute-start(bf16[128,384]{1,0:T(8,128)(2,1)S(1)} %get-tuple-element.31), channel_id=1, source_target_pairs={{0,3},{1,2},{2,1},{3,0},{4,7},{5,6},{6,5},{7,4},{8,11},{9,10},{10,... | collective-permute-start | bytes 294920 | tf_op jit(solution)/shard_map/ppermute | solution.py:360
  17.9 5.6 %collective-permute-start.3 = (bf16[128,384]{1,0:T(8,128)(2,1)S(1)}, bf16[128,384]{1,0:T(8,128)(2,1)S(1)}, u32[]{:S(2)}, u32[]{:S(2)}) collective-permute-start(bf16[128,384]{1,0:T(8,128)(2,1)S(1)} %get-tuple-element.32), channel_id=1, source_target_pairs={{0,4},{1,5},{2,6},{3,7},{4,0},{5,1},{6,2},{7,3},{8,12},{9,13},{10,... | collective-permute-start | bytes 294920 | tf_op jit(solution)/shard_map/ppermute | solution.py:360
  18.5 10.2 %collective-permute-start.4 = (bf16[128,384]{1,0:T(8,128)(2,1)S(1)}, bf16[128,384]{1,0:T(8,128)(2,1)S(1)}, u32[]{:S(2)}, u32[]{:S(2)}) collective-permute-start(bf16[128,384]{1,0:T(8,128)(2,1)S(1)} %get-tuple-element.38), channel_id=1, source_target_pairs={{0,5},{1,4},{2,7},{3,6},{4,1},{5,0},{6,3},{7,2},{8,13},{9,12},{10,... | collective-permute-start | bytes 294920 | tf_op jit(solution)/shard_map/ppermute | solution.py:360
  19.6 9.1 %collective-permute-start.5 = (bf16[128,384]{1,0:T(8,128)(2,1)S(1)}, bf16[128,384]{1,0:T(8,128)(2,1)S(1)}, u32[]{:S(2)}, u32[]{:S(2)}) collective-permute-start(bf16[128,384]{1,0:T(8,128)(2,1)S(1)} %get-tuple-element.39), channel_id=1, source_target_pairs={{0,6},{1,7},{2,4},{3,5},{4,2},{5,3},{6,0},{7,1},{8,14},{9,15},{10,... | collective-permute-start | bytes 294920 | tf_op jit(solution)/shard_map/ppermute | solution.py:360
  21.7 7.0 %collective-permute-start.6 = (bf16[128,384]{1,0:T(8,128)(2,1)S(1)}, bf16[128,384]{1,0:T(8,128)(2,1)S(1)}, u32[]{:S(2)}, u32[]{:S(2)}) collective-permute-start(bf16[128,384]{1,0:T(8,128)(2,1)S(1)} %get-tuple-element.40), channel_id=1, source_target_pairs={{0,7},{1,6},{2,5},{3,4},{4,3},{5,2},{6,1},{7,0},{8,15},{9,14},{10,... | collective-permute-start | bytes 294920 | tf_op jit(solution)/shard_map/ppermute | solution.py:360
  24.3 7.6 %collective-permute-start.9 = (bf16[25,16,128]{2,1,0:T(8,128)(2,1)S(1)}, bf16[25,16,128]{2,1,0:T(8,128)(2,1)S(1)}, u32[]{:S(2)}, u32[]{:S(2)}) collective-permute-start(bf16[25,16,128]{2,1,0:T(8,128)(2,1)S(1)} %get-tuple-element.46), channel_id=1, source_target_pairs={{0,24},{8,16},{16,8},{24,0},{1,25},{9,17},{17,9},{25,1},{2,26},{10... | collective-permute-start | bytes 307208 | tf_op jit(solution)/shard_map/ppermute | solution.py:399
  28.0 9.3 %collective-permute-start.7 = (bf16[25,16,128]{2,1,0:T(8,128)(2,1)S(1)}, bf16[25,16,128]{2,1,0:T(8,128)(2,1)S(1)}, u32[]{:S(2)}, u32[]{:S(2)}) collective-permute-start(bf16[25,16,128]{2,1,0:T(8,128)(2,1)S(1)} %get-tuple-element.42), channel_id=1, source_target_pairs={{0,16},{8,24},{16,0},{24,8},{1,17},{9,25},{17,1},{25,9},{2,18},{10... | collective-permute-start | bytes 307208 | tf_op jit(solution)/shard_map/ppermute | solution.py:399
  29.7 10.8 %collective-permute-start.11 = (bf16[56,16,128]{2,1,0:T(8,128)(2,1)S(1)}, bf16[56,16,128]{2,1,0:T(8,128)(2,1)S(1)}, u32[]{:S(2)}, u32[]{:S(2)}) collective-permute-start(bf16[56,16,128]{2,1,0:T(8,128)(2,1)S(1)} %get-tuple-element.49), channel_id=1, source_target_pairs={{0,8},{8,0},{16,24},{24,16},{1,9},{9,1},{17,25},{25,17},{2,10},{10... | collective-permute-start | bytes 688136 | tf_op jit(solution)/shard_map/ppermute | solution.py:399
  32.0 11.6 %collective-permute-start.10 = (bf16[32,16,128]{2,1,0:T(8,128)(2,1)S(1)}, bf16[32,16,128]{2,1,0:T(8,128)(2,1)S(1)}, u32[]{:S(2)}, u32[]{:S(2)}) collective-permute-start(bf16[32,16,128]{2,1,0:T(8,128)(2,1)S(1)} %get-tuple-element.48), channel_id=1, source_target_pairs={{0,24},{8,16},{16,8},{24,0},{1,25},{9,17},{17,9},{25,1},{2,26},{10... | collective-permute-start | bytes 393224 | tf_op jit(solution)/shard_map/ppermute | solution.py:399
  37.3 11.6 %collective-permute-start.8 = (bf16[32,16,128]{2,1,0:T(8,128)(2,1)S(1)}, bf16[32,16,128]{2,1,0:T(8,128)(2,1)S(1)}, u32[]{:S(2)}, u32[]{:S(2)}) collective-permute-start(bf16[32,16,128]{2,1,0:T(8,128)(2,1)S(1)} %get-tuple-element.44), channel_id=1, source_target_pairs={{0,16},{8,24},{16,0},{24,8},{1,17},{9,25},{17,1},{25,9},{2,18},{10... | collective-permute-start | bytes 393224 | tf_op jit(solution)/shard_map/ppermute | solution.py:399

commit v17 on v14

--- a/solution.py
+++ b/solution.py
@@ -93,7 +93,7 @@
 
     row = lax.broadcasted_iota(jnp.int32, (WIDE, span), 0)
     lane = lax.broadcasted_iota(jnp.int32, (WIDE, span), 1)
-    batch = 2 * STRIPES
+    batch = 4 * STRIPES
     for first in range(0, stripes, batch):
         for p in range(first, first + batch):
             copy(p, 0).wait()

time: 53.5 us -> 53.7 us (level)
  no operation moved by 1% of the time
where the time goes in v17:
time: 53.7 us; the launch traced here: 53.4 us
  Pallas kernels  20.7 us (39%)
  starting transfers between devices  19.2 us (36%)
  waiting for transfers between devices  11.6 us (22%)
  local copies, waits for them, and re-layouts  1.93 us (4%)
    pallas_call x4, Pallas kernels, correlate(): pl.pallas_call(functools.partial(correlate_kernel, n_chan, groups, factor...  13.4 us
    ppermute x5, starting transfers between devices, hand_over(): lax.ppermute(value, 'tgroup', [(g, g ^ shift) for g in range(n_tgroup)])  9.12 us
    pallas_call x1, Pallas kernels, local(): pl.pallas_call(functools.partial(select_kernel, n_chan, groups), out_shap...  5.18 us
    all_to_all x1, starting transfers between devices, local(): lax.all_to_all(jnp.broadcast_to(first_block[None, :], (n_chan, STRIPES)),...  5.17 us
    ppermute x7, starting transfers between devices, exchange(): return lax.ppermute(value, 'chan', [(c, c ^ k) for c in range(n_chan)])  4.86 us
    ppermute x5, waiting for transfers between devices, hand_over(): lax.ppermute(value, 'tgroup', [(g, g ^ shift) for g in range(n_tgroup)])  4.56 us
    all_to_all x1, waiting for transfers between devices, local(): lax.all_to_all(jnp.broadcast_to(first_block[None, :], (n_chan, STRIPES)),...  3.62 us
    ppermute x7, waiting for transfers between devices, exchange(): return lax.ppermute(value, 'chan', [(c, c ^ k) for c in range(n_chan)])  3.4 us
  transfers between devices with their start and end apart: 13, of which 8 were waited for; matrix products, arithmetic and copies ran while one was open for 0% of the time, Pallas kernels for 21%

profile of v17, /device:TPU:0, one launch (start us, length us, event | category | flops | bytes accessed | tf_op | source)
XLA Modules:
  0.0 53.4 jit_solution(11904011581454736187)
XLA Ops:
  0.0 1.2 %broadcast_in_dim.2 = s32[8,1,2]{2,1,0:T(1,128)} broadcast(s32[2]{0:T(128)} %param.6), dimensions={2} | broadcast | bytes 72 | tf_op jit(solution)/shard_map/broadcast_in_dim | solution.py:342
  1.2 5.2 %all-to-all-start = ((s32[8,1,2]{2,1,0:T(1,128)}), s32[8,1,2]{2,1,0:T(1,128)S(1)}, u32[]{:S(2)}, u32[]{:S(2)}) async-start(s32[8,1,2]{2,1,0:T(1,128)} %broadcast_in_dim.2), calls=%async_computation | async-start | bytes 8192 | tf_op jit(solution)/shard_map/all_to_all | solution.py:341
  6.4 0.0 copy-start.1
  6.4 0.7 %copy-done.1 = f32[255]{0:T(256)S(1)} copy-done((f32[255]{0:T(256)S(1)}, f32[255]{0:T(256)}, u32[]{:S(2)}) %copy-start.1) | copy-done | bytes 1044
  7.1 0.3 fir_weights.1.weights
  7.4 3.6 %all-to-all-done = s32[8,1,2]{2,1,0:T(1,128)S(1)} async-done(((s32[8,1,2]{2,1,0:T(1,128)}), s32[8,1,2]{2,1,0:T(1,128)S(1)}, u32[]{:S(2)}, u32[]{:S(2)}) %all-to-all-start) | async-done | bytes 96 | tf_op jit(solution)/shard_map/all_to_all | solution.py:341
  11.0 0.0 copy-start
  11.0 5.2 %select_filter.1 = (bf16[128,384]{1,0:T(8,128)(2,1)S(1)}, bf16[128,384]{1,0:T(8,128)(2,1)S(1)}, bf16[128,384]{1,0:T(8,128)(2,1)S(1)}, bf16[128,384]{1,0:T(8,128)...) custom-call(s32[8,2]{1,0:T(8,128)S(1)} %bitcast.9, ...), custom_call_target="tpu_custom_call" | custom-call | tf_op jit(solution)/shard_map/select_filter/pallas_call | solution.py:364
  16.2 0.1 collective-permute-start
  16.3 0.6 %collective-permute-start.1 = (bf16[128,384]{1,0:T(8,128)(2,1)S(1)}, bf16[128,384]{1,0:T(8,128)(2,1)S(1)}, u32[]{:S(2)}, u32[]{:S(2)}) collective-permute-start(bf16[128,384]{1,0:T(8,128)(2,1)S(1)} %get-tuple-element.30), channel_id=1, source_target_pairs={{0,2},{1,3},{2,0},{3,1},{4,6},{5,7},{6,4},{7,5},{8,10},{9,11},{10,... | collective-permute-start | bytes 294920 | tf_op jit(solution)/shard_map/ppermute | solution.py:382
  16.9 1.2 %collective-permute-start.2 = (bf16[128,384]{1,0:T(8,128)(2,1)S(1)}, bf16[128,384]{1,0:T(8,128)(2,1)S(1)}, u32[]{:S(2)}, u32[]{:S(2)}) collective-permute-start(bf16[128,384]{1,0:T(8,128)(2,1)S(1)} %get-tuple-element.31), channel_id=1, source_target_pairs={{0,3},{1,2},{2,1},{3,0},{4,7},{5,6},{6,5},{7,4},{8,11},{9,10},{10,... | collective-permute-start | bytes 294920 | tf_op jit(solution)/shard_map/ppermute | solution.py:382
  18.1 0.6 %collective-permute-start.3 = (bf16[128,384]{1,0:T(8,128)(2,1)S(1)}, bf16[128,384]{1,0:T(8,128)(2,1)S(1)}, u32[]{:S(2)}, u32[]{:S(2)}) collective-permute-start(bf16[128,384]{1,0:T(8,128)(2,1)S(1)} %get-tuple-element.32), channel_id=1, source_target_pairs={{0,4},{1,5},{2,6},{3,7},{4,0},{5,1},{6,2},{7,3},{8,12},{9,13},{10,... | collective-permute-start | bytes 294920 | tf_op jit(solution)/shard_map/ppermute | solution.py:382
  18.8 1.1 %collective-permute-start.4 = (bf16[128,384]{1,0:T(8,128)(2,1)S(1)}, bf16[128,384]{1,0:T(8,128)(2,1)S(1)}, u32[]{:S(2)}, u32[]{:S(2)}) collective-permute-start(bf16[128,384]{1,0:T(8,128)(2,1)S(1)} %get-tuple-element.38), channel_id=1, source_target_pairs={{0,5},{1,4},{2,7},{3,6},{4,1},{5,0},{6,3},{7,2},{8,13},{9,12},{10,... | collective-permute-start | bytes 294920 | tf_op jit(solution)/shard_map/ppermute | solution.py:382
  19.8 0.0 collective-permute-done.refs_1_
  19.8 0.6 %collective-permute-start.5 = (bf16[128,384]{1,0:T(8,128)(2,1)S(1)}, bf16[128,384]{1,0:T(8,128)(2,1)S(1)}, u32[]{:S(2)}, u32[]{:S(2)}) collective-permute-start(bf16[128,384]{1,0:T(8,128)(2,1)S(1)} %get-tuple-element.39), channel_id=1, source_target_pairs={{0,6},{1,7},{2,4},{3,5},{4,2},{5,3},{6,0},{7,1},{8,14},{9,15},{10,... | collective-permute-start | bytes 294920 | tf_op jit(solution)/shard_map/ppermute | solution.py:382
  20.5 1.5 %collective-permute-done.1.refs_2_ = bf16[128,384]{1,0:T(8,128)(2,1)S(1)} collective-permute-done((bf16[128,384]{1,0:T(8,128)(2,1)S(1)}, bf16[128,384]{1,0:T(8,128)(2,1)S(1)}, u32[]{:S(2)}, u32[]{:S(2)}) %collective-permute-start.1) | collective-permute-done | bytes 98336 | tf_op jit(solution)/shard_map/ppermute | solution.py:382
  21.9 0.6 %collective-permute-start.6 = (bf16[128,384]{1,0:T(8,128)(2,1)S(1)}, bf16[128,384]{1,0:T(8,128)(2,1)S(1)}, u32[]{:S(2)}, u32[]{:S(2)}) collective-permute-start(bf16[128,384]{1,0:T(8,128)(2,1)S(1)} %get-tuple-element.40), channel_id=1, source_target_pairs={{0,7},{1,6},{2,5},{3,4},{4,3},{5,2},{6,1},{7,0},{8,15},{9,14},{10,... | collective-permute-start | bytes 294920 | tf_op jit(solution)/shard_map/ppermute | solution.py:382
  22.5 0.6 %collective-permute-done.2.refs_3_ = bf16[128,384]{1,0:T(8,128)(2,1)S(1)} collective-permute-done((bf16[128,384]{1,0:T(8,128)(2,1)S(1)}, bf16[128,384]{1,0:T(8,128)(2,1)S(1)}, u32[]{:S(2)}, u32[]{:S(2)}) %collective-permute-start.2) | collective-permute-done | bytes 98336 | tf_op jit(solution)/shard_map/ppermute | solution.py:382
  23.1 0.6 %collective-permute-done.3.refs_4_ = bf16[128,384]{1,0:T(8,128)(2,1)S(1)} collective-permute-done((bf16[128,384]{1,0:T(8,128)(2,1)S(1)}, bf16[128,384]{1,0:T(8,128)(2,1)S(1)}, u32[]{:S(2)}, u32[]{:S(2)}) %collective-permute-start.3) | collective-permute-done | bytes 98336 | tf_op jit(solution)/shard_map/ppermute | solution.py:382
  23.8 0.0 copy-done
  23.8 0.8 %place_first.1 = (bf16[25,16,128]{2,1,0:T(8,128)(2,1)S(1)}, bf16[25,16,128]{2,1,0:T(8,128)(2,1)S(1)}) custom-call(s32[16]{0:T(128)S(1)} %bitcast.3, bf16[128,384]{1,0:T(8,128)(2,1)S(1)} %get-tuple-element.33.refs_0_, bf16[128,384]{1,0:T(8,128)(2,1)S(1)} %collective-permute-done.refs_1_, bf16[128,384]{1,0:T(8,128)(2,1)S(1)} %collective-permute-done.1.refs_2_, ...), custom_call_target="tpu_custom_call" | custom-call | tf_op jit(solution)/shard_map/place_first/pallas_call | solution.py:404
  24.5 3.7 %collective-permute-start.9 = (bf16[25,16,128]{2,1,0:T(8,128)(2,1)S(1)}, bf16[25,16,128]{2,1,0:T(8,128)(2,1)S(1)}, u32[]{:S(2)}, u32[]{:S(2)}) collective-permute-start(bf16[25,16,128]{2,1,0:T(8,128)(2,1)S(1)} %get-tuple-element.46), channel_id=1, source_target_pairs={{0,24},{8,16},{16,8},{24,0},{1,25},{9,17},{17,9},{25,1},{2,26},{10... | collective-permute-start | bytes 307208 | tf_op jit(solution)/shard_map/ppermute | solution.py:421
  28.2 0.0 collective-permute-start.7
  28.2 0.7 %collective-permute-done.4.refs_5_ = bf16[128,384]{1,0:T(8,128)(2,1)S(1)} collective-permute-done((bf16[128,384]{1,0:T(8,128)(2,1)S(1)}, bf16[128,384]{1,0:T(8,128)(2,1)S(1)}, u32[]{:S(2)}, u32[]{:S(2)}) %collective-permute-start.4) | collective-permute-done | bytes 98336 | tf_op jit(solution)/shard_map/ppermute | solution.py:382
  28.9 0.0 collective-permute-done.5.refs_6_
  28.9 0.0 collective-permute-done.6.refs_7_
  28.9 1.0 %place_second.1 = (bf16[56,16,128]{2,1,0:T(8,128)(2,1)S(1)}, bf16[56,16,128]{2,1,0:T(8,128)(2,1)S(1)}, bf16[32,16,128]{2,1,0:T(8,128)(2,1)S(1)}, bf16[32,16,128]{2,1,0:T(8,128)(2,1)S(1)}) custom-call(s32[16]{0:T(128)S(1)} %bitcast.4, bf16[128,384]{1,0:T(8,128)(2,1)S(1)} %get-tuple-element.33.refs_0_, bf16[128,384]{1,0:T(8,128)(2,1)S(1)} %collective-permute-done.refs_1_, ...), custom_call_target="tpu_custom_call" | custom-call | tf_op jit(solution)/shard_map/place_second/pallas_call | solution.py:404
  30.0 1.6 %collective-permute-start.11 = (bf16[56,16,128]{2,1,0:T(8,128)(2,1)S(1)}, bf16[56,16,128]{2,1,0:T(8,128)(2,1)S(1)}, u32[]{:S(2)}, u32[]{:S(2)}) collective-permute-start(bf16[56,16,128]{2,1,0:T(8,128)(2,1)S(1)} %get-tuple-element.49), channel_id=1, source_target_pairs={{0,8},{8,0},{16,24},{24,16},{1,9},{9,1},{17,25},{25,17},{2,10},{10... | collective-permute-start | bytes 688136 | tf_op jit(solution)/shard_map/ppermute | solution.py:421
  31.6 0.6 %collective-permute-done.9.refs_0_ = bf16[25,16,128]{2,1,0:T(8,128)(2,1)S(1)} collective-permute-done((bf16[25,16,128]{2,1,0:T(8,128)(2,1)S(1)}, bf16[25,16,128]{2,1,0:T(8,128)(2,1)S(1)}, u32[]{:S(2)}, u32[]{:S(2)}) %collective-permute-start.9) | collective-permute-done | bytes 102432 | tf_op jit(solution)/shard_map/ppermute | solution.py:421
  32.2 3.6 %collective-permute-start.10 = (bf16[32,16,128]{2,1,0:T(8,128)(2,1)S(1)}, bf16[32,16,128]{2,1,0:T(8,128)(2,1)S(1)}, u32[]{:S(2)}, u32[]{:S(2)}) collective-permute-start(bf16[32,16,128]{2,1,0:T(8,128)(2,1)S(1)} %get-tuple-element.48), channel_id=1, source_target_pairs={{0,24},{8,16},{16,8},{24,0},{1,25},{9,17},{17,9},{25,1},{2,26},{10... | collective-permute-start | bytes 393224 | tf_op jit(solution)/shard_map/ppermute | solution.py:421
  35.8 1.7 %collective-permute-done.7.refs_0_ = bf16[25,16,128]{2,1,0:T(8,128)(2,1)S(1)} collective-permute-done((bf16[25,16,128]{2,1,0:T(8,128)(2,1)S(1)}, bf16[25,16,128]{2,1,0:T(8,128)(2,1)S(1)}, u32[]{:S(2)}, u32[]{:S(2)}) %collective-permute-start.7) | collective-permute-done | bytes 102432 | tf_op jit(solution)/shard_map/ppermute | solution.py:421
  37.5 0.2 collective-permute-start.8
  37.7 3.0 %correlate.3.refs_1_ = f32[5,256,256]{2,1,0:T(8,128)S(1)} custom-call(s32[16]{0:T(128)S(1)} %bitcast.5, bf16[56,16,128]{2,1,0:T(8,128)(2,1)S(1)} %get-tuple-element.50.refs_0_), custom_call_target="tpu_custom_call" | custom-call | tf_op jit(solution)/shard_map/correlate/pallas_call | solution.py:315
  40.7 0.0 collective-permute-done.11.refs_0_
  40.8 3.0 %correlate.4.refs_2_ = f32[5,256,256]{2,1,0:T(8,128)S(1)} custom-call(s32[16]{0:T(128)S(1)} %bitcast.6, bf16[56,16,128]{2,1,0:T(8,128)(2,1)S(1)} %collective-permute-done.11.refs_0_, f32[5,256,256]{2,1,0:T(8,128)S(1)} %correlate.3.refs_1_), custom_call_target="tpu_custom_call" | custom-call | tf_op jit(solution)/shard_map/correlate/pallas_call | solution.py:315
  43.8 0.0 collective-permute-done.10.refs_1_
  43.8 3.0 %correlate.5.refs_2_ = f32[5,256,256]{2,1,0:T(8,128)S(1)} custom-call(s32[16]{0:T(128)S(1)} %bitcast.7, bf16[25,16,128]{2,1,0:T(8,128)(2,1)S(1)} %collective-permute-done.9.refs_0_, bf16[32,16,128]{2,1,0:T(8,128)(2,1)S(1)} %collective-permute-done.10.refs_1_, f32[5,256,256]{2,1,0:T(8,128)S(1)} %correlate.4.refs_2_), custom_call_target="tpu_custom_call" | custom-call | tf_op jit(solution)/shard_map/correlate/pallas_call | solution.py:315
  46.9 2.2 %collective-permute-done.8.refs_1_ = bf16[32,16,128]{2,1,0:T(8,128)(2,1)S(1)} collective-permute-done((bf16[32,16,128]{2,1,0:T(8,128)(2,1)S(1)}, bf16[32,16,128]{2,1,0:T(8,128)(2,1)S(1)}, u32[]{:S(2)}, u32[]{:S(2)}) %collective-permute-start.8) | collective-permute-done | bytes 131104 | tf_op jit(solution)/shard_map/ppermute | solution.py:421
  49.1 4.3 %correlate_last.1 = f32[5,8,8,1001]{3,2,1,0:T(8,128)} custom-call(s32[16]{0:T(128)S(1)} %bitcast.8, bf16[25,16,128]{2,1,0:T(8,128)(2,1)S(1)} %collective-permute-done.7.refs_0_, bf16[32,16,128]{2,1,0:T(8,128)(2,1)S(1)} %collective-permute-done.8.refs_1_, f32[5,256,256]{2,1,0:T(8,128)S(1)} %correlate.5.refs_2_), custom_call_target="tpu_custom_call" | custom-call | tf_op jit(solution)/shard_map/correlate_last/pallas_call | solution.py:315
Async XLA Ops:
  1.2 9.8 %all-to-all-start = ((s32[8,1,2]{2,1,0:T(1,128)}), s32[8,1,2]{2,1,0:T(1,128)S(1)}, u32[]{:S(2)}, u32[]{:S(2)}) async-start(s32[8,1,2]{2,1,0:T(1,128)} %broadcast_in_dim.2), calls=%async_computation | async-start | bytes 8192 | tf_op jit(solution)/shard_map/all_to_all | solution.py:341
  6.4 0.7 %copy-start.1 = (f32[255]{0:T(256)S(1)}, f32[255]{0:T(256)}, u32[]{:S(2)}) copy-start(f32[255]{0:T(256)} %param.5) | copy-start | bytes 3064
  11.0 12.7 %copy-start = (s32[16,1]{0,1:T(1,128)S(1)}, s32[16,1]{0,1:T(1,128)}, u32[]{:S(2)}) copy-start(s32[16,1]{0,1:T(1,128)} %param.7) | copy-start | bytes 196
  16.2 3.6 %collective-permute-start = (bf16[128,384]{1,0:T(8,128)(2,1)S(1)}, bf16[128,384]{1,0:T(8,128)(2,1)S(1)}, u32[]{:S(2)}, u32[]{:S(2)}) collective-permute-start(bf16[128,384]{1,0:T(8,128)(2,1)S(1)} %get-tuple-element.29), channel_id=1, source_target_pairs={{0,1},{1,0},{2,3},{3,2},{4,5},{5,4},{6,7},{7,6},{8,9},{9,8},{10,11... | collective-permute-start | bytes 294920 | tf_op jit(solution)/shard_map/ppermute | solution.py:382
  16.3 5.7 %collective-permute-start.1 = (bf16[128,384]{1,0:T(8,128)(2,1)S(1)}, bf16[128,384]{1,0:T(8,128)(2,1)S(1)}, u32[]{:S(2)}, u32[]{:S(2)}) collective-permute-start(bf16[128,384]{1,0:T(8,128)(2,1)S(1)} %get-tuple-element.30), channel_id=1, source_target_pairs={{0,2},{1,3},{2,0},{3,1},{4,6},{5,7},{6,4},{7,5},{8,10},{9,11},{10,... | collective-permute-start | bytes 294920 | tf_op jit(solution)/shard_map/ppermute | solution.py:382
  16.9 6.2 %collective-permute-start.2 = (bf16[128,384]{1,0:T(8,128)(2,1)S(1)}, bf16[128,384]{1,0:T(8,128)(2,1)S(1)}, u32[]{:S(2)}, u32[]{:S(2)}) collective-permute-start(bf16[128,384]{1,0:T(8,128)(2,1)S(1)} %get-tuple-element.31), channel_id=1, source_target_pairs={{0,3},{1,2},{2,1},{3,0},{4,7},{5,6},{6,5},{7,4},{8,11},{9,10},{10,... | collective-permute-start | bytes 294920 | tf_op jit(solution)/shard_map/ppermute | solution.py:382
  18.1 5.6 %collective-permute-start.3 = (bf16[128,384]{1,0:T(8,128)(2,1)S(1)}, bf16[128,384]{1,0:T(8,128)(2,1)S(1)}, u32[]{:S(2)}, u32[]{:S(2)}) collective-permute-start(bf16[128,384]{1,0:T(8,128)(2,1)S(1)} %get-tuple-element.32), channel_id=1, source_target_pairs={{0,4},{1,5},{2,6},{3,7},{4,0},{5,1},{6,2},{7,3},{8,12},{9,13},{10,... | collective-permute-start | bytes 294920 | tf_op jit(solution)/shard_map/ppermute | solution.py:382
  18.8 10.2 %collective-permute-start.4 = (bf16[128,384]{1,0:T(8,128)(2,1)S(1)}, bf16[128,384]{1,0:T(8,128)(2,1)S(1)}, u32[]{:S(2)}, u32[]{:S(2)}) collective-permute-start(bf16[128,384]{1,0:T(8,128)(2,1)S(1)} %get-tuple-element.38), channel_id=1, source_target_pairs={{0,5},{1,4},{2,7},{3,6},{4,1},{5,0},{6,3},{7,2},{8,13},{9,12},{10,... | collective-permute-start | bytes 294920 | tf_op jit(solution)/shard_map/ppermute | solution.py:382
  19.8 9.1 %collective-permute-start.5 = (bf16[128,384]{1,0:T(8,128)(2,1)S(1)}, bf16[128,384]{1,0:T(8,128)(2,1)S(1)}, u32[]{:S(2)}, u32[]{:S(2)}) collective-permute-start(bf16[128,384]{1,0:T(8,128)(2,1)S(1)} %get-tuple-element.39), channel_id=1, source_target_pairs={{0,6},{1,7},{2,4},{3,5},{4,2},{5,3},{6,0},{7,1},{8,14},{9,15},{10,... | collective-permute-start | bytes 294920 | tf_op jit(solution)/shard_map/ppermute | solution.py:382
  21.9 7.0 %collective-permute-start.6 = (bf16[128,384]{1,0:T(8,128)(2,1)S(1)}, bf16[128,384]{1,0:T(8,128)(2,1)S(1)}, u32[]{:S(2)}, u32[]{:S(2)}) collective-permute-start(bf16[128,384]{1,0:T(8,128)(2,1)S(1)} %get-tuple-element.40), channel_id=1, source_target_pairs={{0,7},{1,6},{2,5},{3,4},{4,3},{5,2},{6,1},{7,0},{8,15},{9,14},{10,... | collective-permute-start | bytes 294920 | tf_op jit(solution)/shard_map/ppermute | solution.py:382
  24.5 7.6 %collective-permute-start.9 = (bf16[25,16,128]{2,1,0:T(8,128)(2,1)S(1)}, bf16[25,16,128]{2,1,0:T(8,128)(2,1)S(1)}, u32[]{:S(2)}, u32[]{:S(2)}) collective-permute-start(bf16[25,16,128]{2,1,0:T(8,128)(2,1)S(1)} %get-tuple-element.46), channel_id=1, source_target_pairs={{0,24},{8,16},{16,8},{24,0},{1,25},{9,17},{17,9},{25,1},{2,26},{10... | collective-permute-start | bytes 307208 | tf_op jit(solution)/shard_map/ppermute | solution.py:421
  28.2 9.3 %collective-permute-start.7 = (bf16[25,16,128]{2,1,0:T(8,128)(2,1)S(1)}, bf16[25,16,128]{2,1,0:T(8,128)(2,1)S(1)}, u32[]{:S(2)}, u32[]{:S(2)}) collective-permute-start(bf16[25,16,128]{2,1,0:T(8,128)(2,1)S(1)} %get-tuple-element.42), channel_id=1, source_target_pairs={{0,16},{8,24},{16,0},{24,8},{1,17},{9,25},{17,1},{25,9},{2,18},{10... | collective-permute-start | bytes 307208 | tf_op jit(solution)/shard_map/ppermute | solution.py:421
  30.0 10.8 %collective-permute-start.11 = (bf16[56,16,128]{2,1,0:T(8,128)(2,1)S(1)}, bf16[56,16,128]{2,1,0:T(8,128)(2,1)S(1)}, u32[]{:S(2)}, u32[]{:S(2)}) collective-permute-start(bf16[56,16,128]{2,1,0:T(8,128)(2,1)S(1)} %get-tuple-element.49), channel_id=1, source_target_pairs={{0,8},{8,0},{16,24},{24,16},{1,9},{9,1},{17,25},{25,17},{2,10},{10... | collective-permute-start | bytes 688136 | tf_op jit(solution)/shard_map/ppermute | solution.py:421
  32.2 11.6 %collective-permute-start.10 = (bf16[32,16,128]{2,1,0:T(8,128)(2,1)S(1)}, bf16[32,16,128]{2,1,0:T(8,128)(2,1)S(1)}, u32[]{:S(2)}, u32[]{:S(2)}) collective-permute-start(bf16[32,16,128]{2,1,0:T(8,128)(2,1)S(1)} %get-tuple-element.48), channel_id=1, source_target_pairs={{0,24},{8,16},{16,8},{24,0},{1,25},{9,17},{17,9},{25,1},{2,26},{10... | collective-permute-start | bytes 393224 | tf_op jit(solution)/shard_map/ppermute | solution.py:421
  37.5 11.6 %collective-permute-start.8 = (bf16[32,16,128]{2,1,0:T(8,128)(2,1)S(1)}, bf16[32,16,128]{2,1,0:T(8,128)(2,1)S(1)}, u32[]{:S(2)}, u32[]{:S(2)}) collective-permute-start(bf16[32,16,128]{2,1,0:T(8,128)(2,1)S(1)} %get-tuple-element.44), channel_id=1, source_target_pairs={{0,16},{8,24},{16,0},{24,8},{1,17},{9,25},{17,1},{25,9},{2,18},{10... | collective-permute-start | bytes 393224 | tf_op jit(solution)/shard_map/ppermute | solution.py:421
